TPU v7x, 32 devices: a whole 2x2x4 slice. The times are simulated.
32 devices in a mesh: row: 2 (over x), col: 4 (over z), layer: 4 (over y, core).
Axes of the slice: x: 2, y: 2, z: 4, core: 2. Of those that a mesh axis runs over, the one named last changes fastest.
Arguments:
- blocks: float32 [16, 4, 3, 96, 96], P(('row', 'layer'), 'col'), may hold values from -2.4 to 2.4
- block_cols: int32 [16, 4, 3], replicated, may hold values from 0 to 3, as said below
- occupancy: int32 [16, 4, 3], replicated, may hold values from 0 to 1, as said below
Outputs:
- product: float32 [16, 4, 3, 96, 96], P(('row', 'layer'), 'col')
- trace: float32 [], replicated
Inputs may be any that keep to these rules, and one draw needn't show every extreme that they name: `block_cols`: within one block row and column group the 3 block columns are distinct; for block row I the column group I // 4 holds I % 4 in slot 0. `occupancy`: slot 0 of block row I in column group I // 4 is always 1.
All inputs are finite; a program needn't handle non-finite values.
Results may differ from a plain program's by a relative error of at most 0.0003.
Values sent between devices are 32-bit elements; how exact they have to be, the bound alone decides.
No kernel may reach another device: no remote copies, remote signals or barrier semaphores. Data moves between devices by JAX's collectives and lax.ppermute only.
A program may use at most 64 MiB of HBM per device.

v0:
```python
import jax
import jax.numpy as jnp
from jax import lax
from jax.sharding import PartitionSpec as P


def passed_along(value, axis, by):
    size = lax.axis_size(axis)
    return lax.ppermute(value, axis, [(i, (i + by) % size) for i in range(size)])


def pick_meta(table, first_row, row_count, group):
    slots = table.shape[2]
    piece = lax.dynamic_slice(table, (first_row, group, 0), (row_count, 1, slots))
    return piece[:, 0]


def local_product(left, left_cols, left_occ, right, right_cols, right_occ, out_cols, out_occ):
    gathered = jnp.take(right, left_cols, axis=0)
    inner_cols = jnp.take(right_cols, left_cols, axis=0)
    inner_occ = jnp.take(right_occ, left_cols, axis=0).astype(jnp.float32)
    match = (inner_cols[:, :, :, None] == out_cols[:, None, None, :]).astype(jnp.float32)
    match = match * inner_occ[:, :, :, None] * left_occ.astype(jnp.float32)[:, :, None, None]
    combined = jnp.einsum("itus,itubd->itsbd", match, gathered, precision=lax.Precision.HIGHEST)
    result = jnp.einsum("itab,itsbd->isad", left, combined, precision=lax.Precision.HIGHEST)
    return result * out_occ.astype(jnp.float32)[:, :, None, None]


def diagonal_sum(terms, cols_here, occ_here, first_row, group, width):
    rows = first_row + jnp.arange(terms.shape[0], dtype=jnp.int32)[:, None]
    hit = (group * width + cols_here == rows).astype(jnp.float32) * occ_here.astype(jnp.float32)
    return jnp.sum(hit * jnp.trace(terms, axis1=2, axis2=3))


def body(blocks, block_cols, occupancy):
    n_row = lax.axis_size("row")
    n_col = lax.axis_size("col")
    n_layer = lax.axis_size("layer")
    row_id = lax.axis_index("row")
    col_id = lax.axis_index("col")
    layer_id = lax.axis_index("layer")
    row_block = blocks.shape[0]
    tile_rows = row_block * n_layer
    width = row_block * n_row
    ratio = n_col // n_row
    group = (row_id + col_id + layer_id) % n_col
    tile = lax.all_gather(blocks, "layer", axis=0, tiled=True)
    left_tile = tile
    distance = (row_id + layer_id) % n_col
    for bit in range(max(n_col - 1, 0).bit_length()):
        moved = passed_along(left_tile, "col", -(1 << bit))
        left_tile = jnp.where(distance >> bit & 1 == 1, moved, left_tile)
    left = left_tile[:, 0]
    right_tile = tile
    source_row = group // ratio
    right_distance = (source_row - row_id) % n_row
    for bit in range(max(n_row - 1, 0).bit_length()):
        moved = passed_along(right_tile, "row", -(1 << bit))
        right_tile = jnp.where(right_distance >> bit & 1 == 1, moved, right_tile)
    right_rows = right_tile[:, 0]
    right = lax.dynamic_slice_in_dim(right_rows, group % ratio * width, width, 0)
    first_row = row_id * tile_rows
    left_cols = pick_meta(block_cols, first_row, tile_rows, group)
    left_occ = pick_meta(occupancy, first_row, tile_rows, group)
    right_cols = pick_meta(block_cols, group * width, width, col_id)
    right_occ = pick_meta(occupancy, group * width, width, col_id)
    out_cols = pick_meta(block_cols, first_row, tile_rows, col_id)
    out_occ = pick_meta(occupancy, first_row, tile_rows, col_id)
    terms = local_product(
        left, left_cols, left_occ, right, right_cols, right_occ, out_cols, out_occ
    )
    summed = lax.psum_scatter(terms, "layer", scatter_dimension=0, tiled=True)
    product = summed[:, None]
    own_row = first_row + layer_id * row_block
    own_cols = pick_meta(block_cols, own_row, row_block, col_id)
    own_occ = pick_meta(occupancy, own_row, row_block, col_id)
    local_trace = diagonal_sum(summed, own_cols, own_occ, own_row, col_id, width)
    trace = lax.psum(local_trace, ("row", "col", "layer"))
    return (product, trace)


def solution(mesh):
    in_specs = (P(("row", "layer"), "col", None, None, None), P(), P())
    out_specs = (P(("row", "layer"), "col", None, None, None), P())
    return jax.shard_map(body, mesh=mesh, in_specs=in_specs, out_specs=out_specs, check_vma=False)
```

profile of v0, /device:TPU:0, one launch (start us, length us, event | category | flops | bytes accessed | tf_op | source)
XLA Modules:
  0.0 187.6 jit_solution(13107955018616564434)
XLA Ops:
  7.2 12.4 %all_gather.3 = f32[8,1,3,96,96]{4,3,2,1,0:T(8,128)S(1)} all-gather(f32[2,1,3,96,96]{4,3,2,1,0:T(8,128)} %param.5), channel_id=1, replica_groups=mesh['row'=2,'col'=4,'layer'=4] {'layer'}, dimensions={0}, use_global_device_ids=true | all-gather | bytes 1105920 | tf_op jit(solution)/shard_map/all_gather | solution.py:47
  19.6 3.6 %collective-permute-start.1 = (f32[8,1,3,96,96]{4,3,2,1,0:T(8,128)S(1)}, f32[8,1,3,96,96]{4,3,2,1,0:T(8,128)S(1)}, u32[]{:S(2)}, u32[]{:S(2)}) collective-permute-start(f32[8,1,3,96,96]{4,3,2,1,0:T(8,128)S(1)} %all_gather.3), channel_id=1, source_target_pairs={{0,12},{4,0},{8,4},{12,8},{1,13},{5,1},{9,5},{13,9},{2,14},{6,2},{... | collective-permute-start | bytes 2654216 | tf_op jit(solution)/shard_map/ppermute | solution.py:9
  23.2 1.5 collective-permute-start
  26.7 1.4 constant_dynamic-slice_fusion.4
  28.1 1.3 pad_clamp_fusion.1
  29.4 0.7 gather_fusion.2
  30.1 0.7 reshape.103
  30.8 0.8 copy.81
  31.6 0.7 gather_fusion.1
  32.4 1.2 compare_and_fusion
  33.6 0.7 copy.80
  34.4 14.6 %collective-permute-done.1 = f32[8,1,3,96,96]{4,3,2,1,0:T(8,128)S(1)} collective-permute-done((f32[8,1,3,96,96]{4,3,2,1,0:T(8,128)S(1)}, f32[8,1,3,96,96]{4,3,2,1,0:T(8,128)S(1)}, u32[]{:S(2)}, u32[]{:S(2)}) %collective-permute-start.1) | collective-permute-done | bytes 884768 | tf_op jit(solution)/shard_map/ppermute | solution.py:9
  49.0 1.1 broadcast_select_fusion
  50.1 1.5 collective-permute-start.2
  51.7 0.7 copy.93
  52.5 0.7 copy.84
  53.2 0.7 copy.90
  54.0 0.8 fusion.28
  54.8 0.7 copy.103
  55.5 0.7 copy.104
  56.2 0.7 copy.105
  57.4 0.9 fusion.16
  58.3 2.0 %gather_fusion = f32[24,3,96,96]{3,2,1,0:T(8,128)S(1)} fusion(f32[4,3,96,96]{3,2,1,0:T(8,128)} %fusion.16, s32[1024]{0:T(1024)} %pad_clamp_fusion), kind=kCustom, calls=%fused_computation.2 | custom fusion | bytes 5308512 | tf_op jit(solution)/shard_map/jit(_take)/gather | solution.py:19
  60.3 10.9 %fusion = f32[8,3,3,96,96]{4,2,3,1,0:T(4,128)S(1)} fusion(f32[8,3,3,96,96]{4,3,2,1,0:T(8,128)S(1)} %bitcast.45, pred[8,3]{1,0:T(8,128)(4,1)} %copy-done.2, f32[8,3]{1,0:T(8,128)} %bitcast.50, f32[8,3,3]{2,1,0:T(4,128)} %copy.90, s32[8,3]{1,0:T(8,128)} %bitcast.49, s32[8,3,3]{2,1,0:T(4,128)S(1)} %copy-done), kind=kOutput, calls=%fused_computation.4 | convolution fusion | flops 24552072 | bytes 5309208 | tf_op jit(solution)/shard_map/itus,itubd->itsbd/dot_general | solution.py:24
  71.2 32.8 %collective-permute-done.2 = f32[8,1,3,96,96]{4,3,2,1,0:T(8,128)} collective-permute-done((f32[8,1,3,96,96]{4,3,2,1,0:T(8,128)}, f32[8,1,3,96,96]{4,3,2,1,0:T(8,128)}, u32[]{:S(2)}, u32[]{:S(2)}) %collective-permute-start.2) | collective-permute-done | bytes 884768 | tf_op jit(solution)/shard_map/ppermute | solution.py:9
  104.1 8.1 %fusion.11 = f32[8,3,96,96]{2,3,1,0:T(8,128)} fusion(f32[8,3,3,96,96]{4,2,3,1,0:T(4,128)S(1)} %fusion, f32[8,1,3,96,96]{4,3,2,1,0:T(8,128)} %collective-permute-done.2, f32[8,1,3,96,96]{4,3,2,1,0:T(8,128)} %broadcast_select_fusion, f32[8,3]{1,0:T(8,128)S(1)} %bitcast.51, pred[]{:T(512)S(6)} %eq.46), kind=kOutput, calls=%fused_computation.11 | convolution fusion | flops 764854272 | bytes 5308513 | tf_op jit(solution)/shard_map/itab,itsbd->isad/dot_general | solution.py:25
  112.2 0.8 constant_dynamic-slice_fusion
  113.2 24.4 %reduce-scatter.2.cloned.1.call-done = f32[2,3,96,96]{2,3,1,0:T(8,128)} async-done(((f32[8,3,96,96]{2,3,1,0:T(8,128)}), f32[2,3,96,96]{2,3,1,0:T(8,128)}) %reduce-scatter.2.cloned.1.call-update) | async-done | bytes 221200 | tf_op jit(solution)/shard_map/reduce_scatter | solution.py:72
  137.6 1.1 select_reduce_fusion
  138.7 0.7 fusion.30
  139.4 1.8 copy.99
  141.2 39.5 %psum.7 = f32[]{:T(128)} all-reduce(f32[]{:T(128)} %fusion.30), channel_id=1, replica_groups=mesh['row'=2,'col'=4,'layer'=4] {'row','col','layer'}, use_global_device_ids=true, to_apply=%region_3.5 | all-reduce | flops 1 | bytes 8 | tf_op jit(solution)/shard_map/psum | solution.py:78
  (30 shorter events, 3.2 us)
Async XLA Ops:
  7.2 17.6 %copy-start.5 = (s32[16,4,3]{0,1,2:T(4,128)S(1)}, s32[16,4,3]{0,1,2:T(4,128)}, u32[]{:S(2)}) copy-start(s32[16,4,3]{0,1,2:T(4,128)} %param.6) | copy-start | bytes 2308
  7.2 130.5 %reduce-scatter.2.cloned.1.call-start = ((), (), s32[]{:S(2)}) async-start(), calls=%async_computation.1 | async-start | bytes 1474560 | tf_op jit(solution)/shard_map/reduce_scatter | solution.py:72
  19.6 29.3 %collective-permute-start.1 = (f32[8,1,3,96,96]{4,3,2,1,0:T(8,128)S(1)}, f32[8,1,3,96,96]{4,3,2,1,0:T(8,128)S(1)}, u32[]{:S(2)}, u32[]{:S(2)}) collective-permute-start(f32[8,1,3,96,96]{4,3,2,1,0:T(8,128)S(1)} %all_gather.3), channel_id=1, source_target_pairs={{0,12},{4,0},{8,4},{12,8},{1,13},{5,1},{9,5},{13,9},{2,14},{6,2},{... | collective-permute-start | bytes 2654216 | tf_op jit(solution)/shard_map/ppermute | solution.py:9
  23.2 34.2 %collective-permute-start = (f32[8,1,3,96,96]{4,3,2,1,0:T(8,128)S(1)}, f32[8,1,3,96,96]{4,3,2,1,0:T(8,128)S(1)}, u32[]{:S(2)}, u32[]{:S(2)}) collective-permute-start(f32[8,1,3,96,96]{4,3,2,1,0:T(8,128)S(1)} %all_gather.3), channel_id=1, source_target_pairs={{0,16},{16,0},{1,17},{17,1},{2,18},{18,2},{3,19},{19,3},{4,20},{20... | collective-permute-start | bytes 2654216 | tf_op jit(solution)/shard_map/ppermute | solution.py:9
  25.4 0.6 copy-start.4
  34.4 17.2 %copy-start.2 = (pred[8,3]{1,0:T(8,128)(4,1)}, pred[8,3]{1,0:T(8,128)(4,1)S(1)}, u32[]{:S(2)}) copy-start(pred[8,3]{1,0:T(8,128)(4,1)S(1)} %copy.80) | copy-start | bytes 76
  34.4 17.2 %copy-start.1 = (s32[8,3,3]{1,0,2:T(8,128)S(1)}, s32[8,3,3]{1,0,2:T(8,128)}, u32[]{:S(2)}) copy-start(s32[8,3,3]{1,0,2:T(8,128)} %reshape.103) | copy-start | bytes 868
  50.1 53.9 %collective-permute-start.2 = (f32[8,1,3,96,96]{4,3,2,1,0:T(8,128)}, f32[8,1,3,96,96]{4,3,2,1,0:T(8,128)}, u32[]{:S(2)}, u32[]{:S(2)}) collective-permute-start(f32[8,1,3,96,96]{4,3,2,1,0:T(8,128)} %broadcast_select_fusion), channel_id=1, source_target_pairs={{0,8},{4,12},{8,0},{12,4},{1,9},{5,13},{9,1},{13,5},{2,10},{6,14},... | collective-permute-start | bytes 2654216 | tf_op jit(solution)/shard_map/ppermute | solution.py:9
  58.3 2.0 %copy-start = (s32[8,3,3]{2,1,0:T(4,128)S(1)}, s32[8,3,3]{2,1,0:T(4,128)}, u32[]{:S(2)}) copy-start(s32[8,3,3]{2,1,0:T(4,128)} %copy.84) | copy-start | bytes 868
  60.3 43.8 %copy-start.3 = (f32[8,1,3]{2,0,1:T(8,128)S(1)}, f32[8,1,3]{2,0,1:T(8,128)}, u32[]{:S(2)}) copy-start(f32[8,1,3]{2,0,1:T(8,128)} %copy.105) | copy-start | bytes 292
Sparse Core Ops, SparseCore 0:
  112.3 25.2 reduce-scatter.1
where the time goes:
time: 188 us
  waiting for transfers between devices  71.9 us (38%)
  blocking collectives  51.9 us (28%)
  matrix products  19 us (10%)
  local copies, waits for them, and re-layouts  15.6 us (8%)
  between operations  14.2 us (8%)
  other arithmetic  8.35 us (4%)
  starting transfers between devices  6.6 us (4%)
    ppermute x3, waiting for transfers between devices, passed_along(): lax.ppermute(value, axis, [(i, (i + by) % size) for i in range(size)])  47.4 us
    psum x1, blocking collectives, body(): trace = lax.psum(local_trace, ('row', 'col', 'layer'))  39.5 us
    reduce_scatter x1, waiting for transfers between devices, body(): summed = lax.psum_scatter(terms, 'layer', scatter_dimension=0, tiled=True)  24.4 us
    all_gather x1, blocking collectives, body(): tile = lax.all_gather(blocks, 'layer', axis=0, tiled=True)  12.4 us
    dot_general x1, matrix products, local_product(): jnp.einsum('itus,itubd->itsbd', match, gathered, precision=lax.Precision....  10.9 us
    dot_general x1, matrix products, local_product(): jnp.einsum('itab,itsbd->isad', left, combined, precision=lax.Precision.HI...  8.11 us
    ppermute x3, starting transfers between devices, passed_along(): lax.ppermute(value, axis, [(i, (i + by) % size) for i in range(size)])  6.56 us
  transfers between devices with their start and end apart: 4, of which 3 were waited for; matrix products, arithmetic and copies ran while one was open for 16% of the time, Pallas kernels for 0%

commit v1 on v0

v1 whole, which is shorter than its diff:
```python
import functools

import jax
import jax.numpy as jnp
from jax import lax
from jax.experimental import pallas as pl
from jax.experimental.pallas import tpu as pltpu
from jax.sharding import PartitionSpec as P

LANES = 128
AXES = ("row", "col", "layer")
LIMIT = pltpu.CompilerParams(vmem_limit_bytes=48 * 2 ** 20)
VMEM = pl.BlockSpec(memory_space=pltpu.VMEM)
SMEM = pl.BlockSpec(memory_space=pltpu.SMEM)


def tall_of(size):
    return size * size // LANES


def unpack(block, size):
    tall = block.shape[0]
    spare = LANES - size
    rest = size - tall
    pieces = [block[q * rest:(q + 1) * rest, size:] for q in range(size // spare)]
    pieces.append(jnp.zeros((rest, spare), block.dtype))
    return jnp.concatenate([block, jnp.concatenate(pieces, axis=1)], axis=0)


def parts_of(value):
    parts = []
    for _ in range(3):
        part = value.astype(jnp.bfloat16)
        parts.append(part)
        value = value - part.astype(jnp.float32)
    return parts


def found(cols_ref, occ_ref, row, group, target):
    index = jnp.int32(0)
    valid = jnp.int32(0)
    for u in range(cols_ref.shape[0]):
        hit = jnp.where((cols_ref[u, group, row] == target) & (occ_ref[u, group, row] == 1), 1, 0)
        index = index + hit * u
        valid = valid + hit
    return index, valid > 0


def place(sizes):
    n_row, n_col, n_layer = sizes
    per_group = n_row * n_layer // n_col
    pair = lax.axis_index("row") * n_layer + lax.axis_index("layer")
    return pair, lax.axis_index("col"), lax.div(pair, per_group), lax.rem(pair, per_group), per_group


def pack_kernel(sizes, cols_ref, occ_ref, x_ref, out_ref, *crossed_refs):
    rows, _, slots, size, _ = x_ref.shape
    tall = tall_of(size)
    spare = LANES - size
    rest = size - tall
    for i in range(rows):
        for t in range(slots):
            n = i * slots + t
            out_ref[n, :, :size] = x_ref[i, 0, t, :tall, :]
            for q in range(size // spare):
                out_ref[n, q * rest:(q + 1) * rest, size:] = x_ref[i, 0, t, tall:, q * spare:(q + 1) * spare]
    pair, here, group, number, per_group = place(sizes)
    for d, crossed_ref in enumerate(crossed_refs):
        shift = jnp.where(here < group, d, d + 1)
        column = lax.rem(number - shift + per_group, per_group) * rows
        for i in range(rows):
            for j in range(rows):
                index, valid = found(cols_ref, occ_ref, pair * rows + i, here, column + j)
                crossed_ref[i * rows + j] = jnp.where(valid, out_ref[i * slots + index], 0.0)


def trace_kernel(sizes, rows, size, cols_ref, occ_ref, packed_ref, *refs):
    crossed_refs, total_ref, sum_ref = refs[:-2], refs[-2], refs[-1]
    slots = packed_ref.shape[0] // rows
    pair, here, group, number, per_group = place(sizes)
    total = jnp.zeros((size, size), jnp.float32)

    def own(i, column):
        index, valid = found(cols_ref, occ_ref, pair * rows + i, here, column)
        return jnp.where(valid, unpack(packed_ref[i * slots + index], size)[:, :size], 0.0)

    def turned(block):
        return unpack(block, size)[:, :size].T

    for d, crossed_ref in enumerate(crossed_refs):
        shift = jnp.where(group < here, d, d + 1)
        column = lax.rem(number + shift, per_group) * rows
        once = (group == here) & (d + 1 == per_group // 2)
        weight = jnp.where(once, 1.0, 2.0)
        for i in range(rows):
            for j in range(rows):
                total = total + weight * own(i, column + j) * turned(crossed_ref[j * rows + i])
    sum_ref[...] = total

    @pl.when(group == here)
    def _():
        more = jnp.zeros((size, size), jnp.float32)
        for i in range(rows):
            for j in range(rows):
                more = more + own(i, number * rows + j) * own(j, number * rows + i).T
        sum_ref[...] += more

    total_ref[...] = jnp.sum(sum_ref[...], keepdims=True)


def stack_kernel(_, *refs):
    out_ref = refs[-1]
    for n, ref in enumerate(refs[:-1]):
        out_ref[n * ref.shape[0]:(n + 1) * ref.shape[0]] = ref[...]


def product_kernel(sizes, cols_ref, occ_ref, *refs):
    n_row, n_col, n_layer = sizes
    strip_refs, (mine_ref, other_ref), out_ref = refs[:n_col], refs[n_col:n_col + 2], refs[n_col + 2]
    a_refs, w_refs = refs[n_col + 3:n_col + 6], refs[n_col + 6:]
    rows, _, slots, size, _ = out_ref.shape
    pair, here, _, _, per_group = place(sizes)
    width = per_group * rows
    inner = n_col * slots
    chips = n_layer // 2
    my_row, my_layer = lax.axis_index("row"), lax.axis_index("layer")
    my_chip, my_core = lax.div(my_layer, 2), lax.rem(my_layer, 2)

    for w_ref in w_refs:
        for j in range(inner):
            w_ref[j * LANES + size:(j + 1) * LANES, :] = jnp.zeros((LANES - size, slots * LANES), jnp.bfloat16)
    for i in range(rows):
        row = pair * rows + i
        targets = [cols_ref[s, here, row] for s in range(slots)]
        for k in range(n_col):
            group = lax.rem(here + k, n_col)
            for t in range(slots):
                j = k * slots + t
                for a_ref, part in zip(a_refs, parts_of(unpack(strip_refs[k][i * slots + t], size))):
                    a_ref[:, j * LANES:(j + 1) * LANES] = part
                stored = occ_ref[t, group, row] == 1
                contracted = group * width + cols_ref[t, group, row]
                source = lax.div(contracted, rows)
                source_row, source_layer = lax.div(source, n_layer), lax.rem(source, n_layer)
                chip = lax.rem(lax.div(source_layer, 2) - my_chip + chips, chips)
                base = (lax.rem(source_row - my_row + n_row, n_row) * chips + chip) * (rows * slots)
                base = base + lax.rem(contracted, rows) * slots
                same_core = lax.rem(source_layer, 2) == my_core
                for s in range(slots):
                    index, valid = found(cols_ref, occ_ref, contracted, here, targets[s])
                    valid = valid & stored & (occ_ref[s, here, row] == 1)
                    block = jnp.where(same_core, mine_ref[base + index], other_ref[base + index])
                    block = jnp.where(valid, unpack(block, size), 0.0)
                    for w_ref, part in zip(w_refs, parts_of(block)):
                        w_ref[j * LANES:j * LANES + size, s * LANES:(s + 1) * LANES] = part

        def dot(a, w):
            return jnp.dot(a_refs[a][...], w_refs[w][...], preferred_element_type=jnp.float32)

        result = dot(0, 0) + ((dot(0, 1) + dot(1, 0)) + (dot(1, 1) + (dot(0, 2) + dot(2, 0))))
        for s in range(slots):
            out_ref[i, 0, s] = result[:, s * LANES:s * LANES + size]


def summed_over(value, axis):
    size = lax.axis_size(axis)
    step = 1
    while step < size:
        value = value + lax.ppermute(value, axis, [(i, i ^ step) for i in range(size)])
        step *= 2
    return value


def crossing(sizes, d):
    n_row, n_col, n_layer = sizes
    per_group = n_row * n_layer // n_col

    def device(group, number, column):
        pair = group * per_group + number
        return (pair // n_layer * n_col + column) * n_layer + pair % n_layer

    pairs = []
    for group in range(n_col):
        for number in range(per_group):
            for column in range(n_col):
                shift = d if group < column else d + 1
                pairs.append((device(column, (number + shift) % per_group, group), device(group, number, column)))
    return pairs


def body(blocks, block_cols, occupancy):
    rows, _, slots, size, _ = blocks.shape
    sizes = tuple(lax.axis_size(axis) for axis in AXES)
    n_row, n_col, n_layer = sizes
    per_group = n_row * n_layer // n_col
    tall = tall_of(size)
    inner = n_col * slots
    cols = jnp.transpose(block_cols, (2, 1, 0))
    occ = jnp.transpose(occupancy, (2, 1, 0))

    packed, *crossed = pl.pallas_call(
        functools.partial(pack_kernel, sizes),
        out_shape=[jax.ShapeDtypeStruct((rows * slots, tall, LANES), jnp.float32)]
        + [jax.ShapeDtypeStruct((rows * rows, tall, LANES), jnp.float32)] * (per_group // 2),
        in_specs=[SMEM, SMEM, VMEM],
        out_specs=[VMEM] * (1 + per_group // 2),
        compiler_params=LIMIT,
        name="pack",
    )(cols, occ, blocks)

    crossed = [lax.ppermute(value, AXES, crossing(sizes, d)) for d, value in enumerate(crossed)]
    strip = [packed]
    for k in range(1, n_col):
        strip.append(lax.ppermute(packed, "col", [((c + k) % n_col, c) for c in range(n_col)]))
    mine = [packed]
    for r in range(n_row):
        for y in range(0, n_layer, 2):
            if r or y:
                route = [
                    ((a + r) % n_row * n_layer + (b + y) % n_layer, a * n_layer + b)
                    for a in range(n_row) for b in range(n_layer)
                ]
                mine.append(lax.ppermute(packed, ("row", "layer"), route))

    trace = pl.pallas_call(
        functools.partial(trace_kernel, sizes, rows, size),
        out_shape=jax.ShapeDtypeStruct((1, 1), jnp.float32),
        in_specs=[SMEM, SMEM] + [VMEM] * (1 + len(crossed)),
        out_specs=VMEM,
        scratch_shapes=[pltpu.VMEM((size, size), jnp.float32)],
        compiler_params=LIMIT,
        name="trace_terms",
    )(cols, occ, packed, *crossed)
    trace = summed_over(trace, "layer")
    stacked = pl.pallas_call(
        stack_kernel,
        out_shape=jax.ShapeDtypeStruct((len(mine) * rows * slots, tall, LANES), jnp.float32),
        in_specs=[VMEM] * (1 + len(mine)),
        out_specs=VMEM,
        compiler_params=LIMIT,
        name="stack",
    )(trace, *mine)
    other = lax.ppermute(stacked, "layer", [(i, i ^ 1) for i in range(n_layer)])
    trace = summed_over(summed_over(trace, "row"), "col")

    product = pl.pallas_call(
        functools.partial(product_kernel, sizes),
        out_shape=jax.ShapeDtypeStruct(blocks.shape, jnp.float32),
        in_specs=[SMEM, SMEM] + [VMEM] * (n_col + 2),
        out_specs=VMEM,
        scratch_shapes=[pltpu.VMEM((size, inner * LANES), jnp.bfloat16)] * 3
        + [pltpu.VMEM((inner * LANES, slots * LANES), jnp.bfloat16)] * 3,
        compiler_params=LIMIT,
        name="multiply",
    )(cols, occ, *strip, stacked, other)
    return product, trace.reshape(())


def solution(mesh):
    in_specs = (P(("row", "layer"), "col", None, None, None), P(), P())
    out_specs = (P(("row", "layer"), "col", None, None, None), P())
    return jax.shard_map(body, mesh=mesh, in_specs=in_specs, out_specs=out_specs, check_vma=False)
```

time: 188 us -> 60.2 us (0.32)
  waiting for transfers between devices: 71.9 us -> 4.62 us
  blocking collectives: 51.9 us -> 0 us
  starting transfers between devices: 6.6 us -> 39.2 us
  matrix products: 19 us -> 0 us
  local copies, waits for them, and re-layouts: 15.6 us -> 2.34 us
  between operations: 14.2 us -> 5.72 us
  other arithmetic: 8.35 us -> 0 us
  Pallas kernels: 0 us -> 7.98 us
    ppermute x3 -> x13, waiting for transfers between devices: 47.4 us -> 4.62 us  [the longest x5 3.24 us: summed_over(): lax.ppermute(value, axis, [(i, i ^ step) for i in range(size)])]
    psum x1 -> x0, blocking collectives: 39.5 us -> none  [body(): trace = lax.psum(local_trace, ('row', 'col', 'layer'))]
    ppermute x3 -> x13, starting transfers between devices: 6.56 us -> 39.2 us  [the longest x5 30.7 us: summed_over(): lax.ppermute(value, axis, [(i, i ^ step) for i in range(size)])]
    reduce_scatter x1 -> x0, waiting for transfers between devices: 24.4 us -> none  [body(): summed = lax.psum_scatter(terms, 'layer', scatter_dimension=0, tiled=True)]
    dot_general x2 -> x0, matrix products: 19 us -> none  [the longest x1 10.9 us: local_product(): jnp.einsum('itus,itubd->itsbd', match, gathered, precision=lax.Precision....]
    all_gather x1 -> x0, blocking collectives: 12.4 us -> none  [body(): tile = lax.all_gather(blocks, 'layer', axis=0, tiled=True)]
    pallas_call x0 -> x4, Pallas kernels: none -> 7.98 us  [the longest x1 5.22 us: body(): pl.pallas_call(functools.partial(product_kernel, sizes), out_shape=jax.Sh...]
    gather x7 -> x0, local copies, waits for them, and re-layouts: 4.28 us -> none  [the longest x1 1.97 us: local_product(): gathered = jnp.take(right, left_cols, axis=0)]
  transfers between devices with their start and end apart: 4 -> 13, of which waited for: 3 -> 5; matrix products, arithmetic and copies ran while one was open for 16% -> 0% of each run, Pallas kernels for 0% -> 3%
where the time goes in v1:
time: 60.2 us; the launch traced here: 59.9 us
  starting transfers between devices  39.2 us (65%)
  Pallas kernels  7.98 us (13%)
  between operations  5.72 us (10%)
  waiting for transfers between devices  4.62 us (8%)
  local copies, waits for them, and re-layouts  2.34 us (4%)
    ppermute x5, starting transfers between devices, summed_over(): lax.ppermute(value, axis, [(i, i ^ step) for i in range(size)])  30.7 us
    pallas_call x1, Pallas kernels, body(): pl.pallas_call(functools.partial(product_kernel, sizes), out_shape=jax.Sh...  5.22 us
    ppermute x3, starting transfers between devices, body(): mine.append(lax.ppermute(packed, ('row', 'layer'), route))  4.6 us
    ppermute x3, starting transfers between devices, body(): lax.ppermute(packed, 'col', [((c + k) % n_col, c) for c in range(n_col)])  3.87 us
    ppermute x5, waiting for transfers between devices, summed_over(): lax.ppermute(value, axis, [(i, i ^ step) for i in range(size)])  3.24 us
    unnamed x6, local copies, waits for them, and re-layouts  2.34 us
    pallas_call x1, Pallas kernels, body(): pl.pallas_call(functools.partial(trace_kernel, sizes, rows, size), out_sh...  1.83 us
    ppermute x1, waiting for transfers between devices, body(): lax.ppermute(value, AXES, crossing(sizes, d))  1.37 us
  transfers between devices with their start and end apart: 13, of which 5 were waited for; matrix products, arithmetic and copies ran while one was open for 0% of the time, Pallas kernels for 3%

profile of v1, /device:TPU:0, one launch (start us, length us, event | category | flops | bytes accessed | tf_op | source)
XLA Modules:
  0.0 59.9 jit_solution(178643428064223428)
XLA Ops:
  0.6 1.0 %copy-done = f32[2,1,3,96,96]{4,3,2,1,0:T(8,128)S(1)} copy-done((f32[2,1,3,96,96]{4,3,2,1,0:T(8,128)S(1)}, f32[2,1,3,96,96]{4,3,2,1,0:T(8,128)}, u32[]{:S(2)}) %copy-start) | copy-done | bytes 221208
  1.6 0.7 %copy-done.1 = s32[16,4,3]{0,1,2:T(4,128)S(1)} copy-done((s32[16,4,3]{0,1,2:T(4,128)S(1)}, s32[16,4,3]{0,1,2:T(4,128)}, u32[]{:S(2)}) %copy-start.1) | copy-done | bytes 792
  2.3 0.7 %copy-done.2 = s32[16,4,3]{0,1,2:T(4,128)S(1)} copy-done((s32[16,4,3]{0,1,2:T(4,128)S(1)}, s32[16,4,3]{0,1,2:T(4,128)}, u32[]{:S(2)}) %copy-start.2) | copy-done | bytes 792
  3.0 0.9 %pack.1 = (f32[6,72,128]{2,1,0:T(8,128)S(1)}, f32[4,72,128]{2,1,0:T(8,128)S(1)}) custom-call(s32[3,4,16]{2,1,0:T(4,128)S(1)} %bitcast.3, s32[3,4,16]{2,1,0:T(4,128)S(1)} %bitcast.6, f32[2,1,3,96,96]{4,3,2,1,0:T(8,128)S(1)} %copy-done), custom_call_target="tpu_custom_call" | custom-call | tf_op jit(solution)/shard_map/pack/pallas_call | solution.py:201
  3.8 4.0 %collective-permute-start.8 = (f32[6,72,128]{2,1,0:T(8,128)S(1)}, f32[6,72,128]{2,1,0:T(8,128)S(1)}, u32[]{:S(2)}, u32[]{:S(2)}) collective-permute-start(f32[6,72,128]{2,1,0:T(8,128)S(1)} %get-tuple-element.4.packed_ref.refs_0_), channel_id=1, source_target_pairs={{18,0},{19,1},{16,2},{17,3},{2,16},{3,17},{0,18},{1,19},{22,4},{23... | collective-permute-start | bytes 663560 | tf_op jit(solution)/shard_map/ppermute | solution.py:223
  7.8 0.5 collective-permute-start.7
  8.3 0.1 collective-permute-start.6
  8.4 0.0 collective-permute-start.3
  8.5 1.4 %collective-permute-done.3.refs_0_ = f32[4,72,128]{2,1,0:T(8,128)S(1)} collective-permute-done((f32[4,72,128]{2,1,0:T(8,128)S(1)}, f32[4,72,128]{2,1,0:T(8,128)S(1)}, u32[]{:S(2)}, u32[]{:S(2)}) %collective-permute-start.3) | collective-permute-done | bytes 147488 | tf_op jit(solution)/shard_map/ppermute | solution.py:211
  9.8 1.8 %trace_terms.1 = f32[1,1]{1,0:T(1,128)} custom-call(s32[3,4,16]{2,1,0:T(4,128)S(1)} %bitcast.4, s32[3,4,16]{2,1,0:T(4,128)S(1)} %bitcast.7, f32[6,72,128]{2,1,0:T(8,128)S(1)} %get-tuple-element.4.packed_ref.refs_0_, f32[4,72,128]{2,1,0:T(8,128)S(1)} %collective-permute-done.3.refs_0_), custom_call_target="tpu_custom_call" | custom-call | tf_op jit(solution)/shard_map/trace_terms/pallas_call | solution.py:225
  11.7 0.1 collective-permute-start.4
  11.8 1.2 %collective-permute-done.4 = f32[1,1]{1,0:T(1,128)} collective-permute-done((f32[1,1]{1,0:T(1,128)}, f32[1,1]{1,0:T(1,128)}, u32[]{:S(2)}, u32[]{:S(2)}) %collective-permute-start.4) | collective-permute-done | bytes 36 | tf_op jit(solution)/shard_map/ppermute | solution.py:169
  14.3 14.3 %collective-permute-start.5 = (f32[1,1]{1,0:T(1,128)}, f32[1,1]{1,0:T(1,128)}, u32[]{:S(2)}, u32[]{:S(2)}) collective-permute-start(f32[1,1]{1,0:T(1,128)} %add.15), channel_id=1, source_target_pairs={{0,2},{1,3},{2,0},{3,1},{4,6},{5,7},{6,4},{7,5},{8,10},{9,11},{10,... | collective-permute-start | bytes 20 | tf_op jit(solution)/shard_map/ppermute | solution.py:169
  28.6 0.3 collective-permute-done.5
  29.6 0.0 collective-permute-done.8.refs_3_
  29.6 0.0 collective-permute-done.7.refs_2_
  29.6 0.0 collective-permute-done.6.refs_1_
  29.6 0.1 stack.1.refs_4_
  29.7 0.1 collective-permute-start.9
  29.7 0.1 collective-permute-start.2
  29.8 1.4 %collective-permute-start.1 = (f32[6,72,128]{2,1,0:T(8,128)S(1)}, f32[6,72,128]{2,1,0:T(8,128)S(1)}, u32[]{:S(2)}, u32[]{:S(2)}) collective-permute-start(f32[6,72,128]{2,1,0:T(8,128)S(1)} %get-tuple-element.4.packed_ref.refs_0_), channel_id=1, source_target_pairs={{8,0},{12,4},{0,8},{4,12},{9,1},{13,5},{1,9},{5,13},{10,2},{14,6},... | collective-permute-start | bytes 663560 | tf_op jit(solution)/shard_map/ppermute | solution.py:214
  31.2 2.4 %collective-permute-start = (f32[6,72,128]{2,1,0:T(8,128)S(1)}, f32[6,72,128]{2,1,0:T(8,128)S(1)}, u32[]{:S(2)}, u32[]{:S(2)}) collective-permute-start(f32[6,72,128]{2,1,0:T(8,128)S(1)} %get-tuple-element.4.packed_ref.refs_0_), channel_id=1, source_target_pairs={{4,0},{8,4},{12,8},{0,12},{5,1},{9,5},{13,9},{1,13},{6,2},{10,6},{... | collective-permute-start | bytes 663560 | tf_op jit(solution)/shard_map/ppermute | solution.py:214
  33.6 3.1 %collective-permute-start.10 = (f32[1,1]{1,0:T(1,128)}, f32[1,1]{1,0:T(1,128)}, u32[]{:S(2)}, u32[]{:S(2)}) collective-permute-start(f32[1,1]{1,0:T(1,128)} %add.16._), channel_id=1, source_target_pairs={{0,16},{16,0},{1,17},{17,1},{2,18},{18,2},{3,19},{19,3},{4,20},{20... | collective-permute-start | bytes 20 | tf_op jit(solution)/shard_map/ppermute | solution.py:169
  36.8 0.5 collective-permute-done.10
  37.9 7.0 %collective-permute-start.11 = (f32[1,1]{1,0:T(1,128)}, f32[1,1]{1,0:T(1,128)}, u32[]{:S(2)}, u32[]{:S(2)}) collective-permute-start(f32[1,1]{1,0:T(1,128)} %add.17), channel_id=1, source_target_pairs={{0,4},{4,0},{8,12},{12,8},{1,5},{5,1},{9,13},{13,9},{2,6},{6,2},{1... | collective-permute-start | bytes 20 | tf_op jit(solution)/shard_map/ppermute | solution.py:169
  45.6 6.1 %collective-permute-start.12 = (f32[1,1]{1,0:T(1,128)}, f32[1,1]{1,0:T(1,128)}, u32[]{:S(2)}, u32[]{:S(2)}) collective-permute-start(f32[1,1]{1,0:T(1,128)} %add.18), channel_id=1, source_target_pairs={{0,8},{4,12},{8,0},{12,4},{1,9},{5,13},{9,1},{13,5},{2,10},{6,14},... | collective-permute-start | bytes 20 | tf_op jit(solution)/shard_map/ppermute | solution.py:169
  51.7 1.2 %collective-permute-done.12 = f32[1,1]{1,0:T(1,128)} collective-permute-done((f32[1,1]{1,0:T(1,128)}, f32[1,1]{1,0:T(1,128)}, u32[]{:S(2)}, u32[]{:S(2)}) %collective-permute-start.12) | collective-permute-done | bytes 36 | tf_op jit(solution)/shard_map/ppermute | solution.py:169
  53.5 0.0 collective-permute-done.2.refs_3_
  53.5 0.0 collective-permute-done.1.refs_2_
  53.5 0.0 collective-permute-done.refs_1_
  53.5 0.0 collective-permute-done.9.refs_5_
  53.5 5.2 %multiply.1 = f32[2,1,3,96,96]{4,3,2,1,0:T(8,128)} custom-call(s32[3,4,16]{2,1,0:T(4,128)S(1)} %bitcast.5, s32[3,4,16]{2,1,0:T(4,128)S(1)} %bitcast.8, f32[6,72,128]{2,1,0:T(8,128)S(1)} %get-tuple-element.4.packed_ref.refs_0_, f32[6,72,128]{2,1,0:T(8,128)S(1)} %collective-permute-done.refs_1_, f32[6,72,128]{2,1,0:T(8,128)S(1)} %collective-permute-done.1.refs_2_, ...), custom_call_target="tpu_custom_call" | custom-call | tf_op jit(solution)/shard_map/multiply/pallas_call | solution.py:246
  (4 shorter events, 0.0 us)
Async XLA Ops:
  0.6 1.0 %copy-start = (f32[2,1,3,96,96]{4,3,2,1,0:T(8,128)S(1)}, f32[2,1,3,96,96]{4,3,2,1,0:T(8,128)}, u32[]{:S(2)}) copy-start(f32[2,1,3,96,96]{4,3,2,1,0:T(8,128)} %x_ref.1) | copy-start | bytes 663556
  1.6 0.7 %copy-start.1 = (s32[16,4,3]{0,1,2:T(4,128)S(1)}, s32[16,4,3]{0,1,2:T(4,128)}, u32[]{:S(2)}) copy-start(s32[16,4,3]{0,1,2:T(4,128)} %param.4) | copy-start | bytes 2308
  2.3 0.7 %copy-start.2 = (s32[16,4,3]{0,1,2:T(4,128)S(1)}, s32[16,4,3]{0,1,2:T(4,128)}, u32[]{:S(2)}) copy-start(s32[16,4,3]{0,1,2:T(4,128)} %param.5) | copy-start | bytes 2308
  3.8 25.7 %collective-permute-start.8 = (f32[6,72,128]{2,1,0:T(8,128)S(1)}, f32[6,72,128]{2,1,0:T(8,128)S(1)}, u32[]{:S(2)}, u32[]{:S(2)}) collective-permute-start(f32[6,72,128]{2,1,0:T(8,128)S(1)} %get-tuple-element.4.packed_ref.refs_0_), channel_id=1, source_target_pairs={{18,0},{19,1},{16,2},{17,3},{2,16},{3,17},{0,18},{1,19},{22,4},{23... | collective-permute-start | bytes 663560 | tf_op jit(solution)/shard_map/ppermute | solution.py:223
  7.8 21.8 %collective-permute-start.7 = (f32[6,72,128]{2,1,0:T(8,128)S(1)}, f32[6,72,128]{2,1,0:T(8,128)S(1)}, u32[]{:S(2)}, u32[]{:S(2)}) collective-permute-start(f32[6,72,128]{2,1,0:T(8,128)S(1)} %get-tuple-element.4.packed_ref.refs_0_), channel_id=1, source_target_pairs={{16,0},{17,1},{18,2},{19,3},{0,16},{1,17},{2,18},{3,19},{20,4},{21... | collective-permute-start | bytes 663560 | tf_op jit(solution)/shard_map/ppermute | solution.py:223
  8.3 21.2 %collective-permute-start.6 = (f32[6,72,128]{2,1,0:T(8,128)S(1)}, f32[6,72,128]{2,1,0:T(8,128)S(1)}, u32[]{:S(2)}, u32[]{:S(2)}) collective-permute-start(f32[6,72,128]{2,1,0:T(8,128)S(1)} %get-tuple-element.4.packed_ref.refs_0_), channel_id=1, source_target_pairs={{2,0},{3,1},{0,2},{1,3},{18,16},{19,17},{16,18},{17,19},{6,4},{7,5... | collective-permute-start | bytes 663560 | tf_op jit(solution)/shard_map/ppermute | solution.py:223
  8.4 1.4 %collective-permute-start.3 = (f32[4,72,128]{2,1,0:T(8,128)S(1)}, f32[4,72,128]{2,1,0:T(8,128)S(1)}, u32[]{:S(2)}, u32[]{:S(2)}) collective-permute-start(f32[4,72,128]{2,1,0:T(8,128)S(1)} %get-tuple-element.5), channel_id=1, source_target_pairs={{1,0},{2,4},{16,8},{18,12},{0,1},{3,5},{17,9},{19,13},{5,2},{7,6},... | collective-permute-start | bytes 442376 | tf_op jit(solution)/shard_map/ppermute | solution.py:211
  11.7 1.4 %collective-permute-start.4 = (f32[1,1]{1,0:T(1,128)}, f32[1,1]{1,0:T(1,128)}, u32[]{:S(2)}, u32[]{:S(2)}) collective-permute-start(f32[1,1]{1,0:T(1,128)} %trace_terms.1), channel_id=1, source_target_pairs={{0,1},{1,0},{2,3},{3,2},{4,5},{5,4},{6,7},{7,6},{8,9},{9,8},{10,11... | collective-permute-start | bytes 20 | tf_op jit(solution)/shard_map/ppermute | solution.py:169
  14.3 14.6 %collective-permute-start.5 = (f32[1,1]{1,0:T(1,128)}, f32[1,1]{1,0:T(1,128)}, u32[]{:S(2)}, u32[]{:S(2)}) collective-permute-start(f32[1,1]{1,0:T(1,128)} %add.15), channel_id=1, source_target_pairs={{0,2},{1,3},{2,0},{3,1},{4,6},{5,7},{6,4},{7,5},{8,10},{9,11},{10,... | collective-permute-start | bytes 20 | tf_op jit(solution)/shard_map/ppermute | solution.py:169
  29.7 23.8 %collective-permute-start.9 = (f32[24,72,128]{2,1,0:T(8,128)S(1)}, f32[24,72,128]{2,1,0:T(8,128)S(1)}, u32[]{:S(2)}, u32[]{:S(2)}) collective-permute-start(f32[24,72,128]{2,1,0:T(8,128)S(1)} %stack.1.refs_4_), channel_id=1, source_target_pairs={{0,1},{1,0},{2,3},{3,2},{4,5},{5,4},{6,7},{7,6},{8,9},{9,8},{10,11... | collective-permute-start | bytes 2654216 | tf_op jit(solution)/shard_map/ppermute | solution.py:243
  29.7 23.7 %collective-permute-start.2 = (f32[6,72,128]{2,1,0:T(8,128)S(1)}, f32[6,72,128]{2,1,0:T(8,128)S(1)}, u32[]{:S(2)}, u32[]{:S(2)}) collective-permute-start(f32[6,72,128]{2,1,0:T(8,128)S(1)} %get-tuple-element.4.packed_ref.refs_0_), channel_id=1, source_target_pairs={{12,0},{0,4},{4,8},{8,12},{13,1},{1,5},{5,9},{9,13},{14,2},{2,6},{... | collective-permute-start | bytes 663560 | tf_op jit(solution)/shard_map/ppermute | solution.py:214
  29.8 23.7 %collective-permute-start.1 = (f32[6,72,128]{2,1,0:T(8,128)S(1)}, f32[6,72,128]{2,1,0:T(8,128)S(1)}, u32[]{:S(2)}, u32[]{:S(2)}) collective-permute-start(f32[6,72,128]{2,1,0:T(8,128)S(1)} %get-tuple-element.4.packed_ref.refs_0_), channel_id=1, source_target_pairs={{8,0},{12,4},{0,8},{4,12},{9,1},{13,5},{1,9},{5,13},{10,2},{14,6},... | collective-permute-start | bytes 663560 | tf_op jit(solution)/shard_map/ppermute | solution.py:214
  31.2 22.3 %collective-permute-start = (f32[6,72,128]{2,1,0:T(8,128)S(1)}, f32[6,72,128]{2,1,0:T(8,128)S(1)}, u32[]{:S(2)}, u32[]{:S(2)}) collective-permute-start(f32[6,72,128]{2,1,0:T(8,128)S(1)} %get-tuple-element.4.packed_ref.refs_0_), channel_id=1, source_target_pairs={{4,0},{8,4},{12,8},{0,12},{5,1},{9,5},{13,9},{1,13},{6,2},{10,6},{... | collective-permute-start | bytes 663560 | tf_op jit(solution)/shard_map/ppermute | solution.py:214
  33.6 3.6 %collective-permute-start.10 = (f32[1,1]{1,0:T(1,128)}, f32[1,1]{1,0:T(1,128)}, u32[]{:S(2)}, u32[]{:S(2)}) collective-permute-start(f32[1,1]{1,0:T(1,128)} %add.16._), channel_id=1, source_target_pairs={{0,16},{16,0},{1,17},{17,1},{2,18},{18,2},{3,19},{19,3},{4,20},{20... | collective-permute-start | bytes 20 | tf_op jit(solution)/shard_map/ppermute | solution.py:169
  37.9 7.0 %collective-permute-start.11 = (f32[1,1]{1,0:T(1,128)}, f32[1,1]{1,0:T(1,128)}, u32[]{:S(2)}, u32[]{:S(2)}) collective-permute-start(f32[1,1]{1,0:T(1,128)} %add.17), channel_id=1, source_target_pairs={{0,4},{4,0},{8,12},{12,8},{1,5},{5,1},{9,13},{13,9},{2,6},{6,2},{1... | collective-permute-start | bytes 20 | tf_op jit(solution)/shard_map/ppermute | solution.py:169
  45.6 7.2 %collective-permute-start.12 = (f32[1,1]{1,0:T(1,128)}, f32[1,1]{1,0:T(1,128)}, u32[]{:S(2)}, u32[]{:S(2)}) collective-permute-start(f32[1,1]{1,0:T(1,128)} %add.18), channel_id=1, source_target_pairs={{0,8},{4,12},{8,0},{12,4},{1,9},{5,13},{9,1},{13,5},{2,10},{6,14},... | collective-permute-start | bytes 20 | tf_op jit(solution)/shard_map/ppermute | solution.py:169

commit v2 on v1

v2 whole, which is shorter than its diff:
```python
import functools

import jax
import jax.numpy as jnp
from jax import lax
from jax.experimental import pallas as pl
from jax.experimental.pallas import tpu as pltpu
from jax.sharding import PartitionSpec as P

LANES = 128
AXES = ("row", "col", "layer")
LIMIT = pltpu.CompilerParams(vmem_limit_bytes=48 * 2 ** 20)
VMEM = pl.BlockSpec(memory_space=pltpu.VMEM)
SMEM = pl.BlockSpec(memory_space=pltpu.SMEM)


def tall_of(size):
    return size * size // LANES


def unpack(block, size):
    tall = block.shape[0]
    spare = LANES - size
    rest = size - tall
    pieces = [block[q * rest:(q + 1) * rest, size:] for q in range(size // spare)]
    pieces.append(jnp.zeros((rest, spare), block.dtype))
    return jnp.concatenate([block, jnp.concatenate(pieces, axis=1)], axis=0)


def parts_of(value):
    parts = []
    for _ in range(3):
        part = value.astype(jnp.bfloat16)
        parts.append(part)
        value = value - part.astype(jnp.float32)
    return parts


def found(cols_ref, occ_ref, row, group, target):
    index = jnp.int32(0)
    valid = jnp.int32(0)
    for u in range(cols_ref.shape[0]):
        hit = jnp.where((cols_ref[u, group, row] == target) & (occ_ref[u, group, row] == 1), 1, 0)
        index = index + hit * u
        valid = valid + hit
    return index, valid > 0


def place(sizes):
    n_row, n_col, n_layer = sizes
    per_group = n_row * n_layer // n_col
    pair = lax.axis_index("row") * n_layer + lax.axis_index("layer")
    return pair, lax.axis_index("col"), lax.div(pair, per_group), lax.rem(pair, per_group), per_group


def pack_kernel(x_ref, out_ref):
    rows, _, slots, size, _ = x_ref.shape
    tall = tall_of(size)
    spare = LANES - size
    rest = size - tall
    for i in range(rows):
        for t in range(slots):
            n = i * slots + t
            out_ref[n, :, :size] = x_ref[i, 0, t, :tall, :]
            for q in range(size // spare):
                out_ref[n, q * rest:(q + 1) * rest, size:] = x_ref[i, 0, t, tall:, q * spare:(q + 1) * spare]


def cross_kernel(sizes, rows, cols_ref, occ_ref, packed_ref, *crossed_refs):
    slots = packed_ref.shape[0] // rows
    pair, here, group, number, per_group = place(sizes)
    for d, crossed_ref in enumerate(crossed_refs):
        shift = jnp.where(here < group, d, d + 1)
        column = lax.rem(number - shift + per_group, per_group) * rows
        for i in range(rows):
            for j in range(rows):
                index, valid = found(cols_ref, occ_ref, pair * rows + i, here, column + j)
                crossed_ref[i * rows + j] = jnp.where(valid, packed_ref[i * slots + index], 0.0)


def strip_block(sizes, rows, slots, mine_ref, other_ref, contracted):
    n_row, _, n_layer = sizes
    chips = n_layer // 2
    my_row, my_layer = lax.axis_index("row"), lax.axis_index("layer")
    source = lax.div(contracted, rows)
    source_row, source_layer = lax.div(source, n_layer), lax.rem(source, n_layer)
    chip = lax.rem(lax.div(source_layer, 2) - lax.div(my_layer, 2) + chips, chips)
    base = (lax.rem(source_row - my_row + n_row, n_row) * chips + chip) * (rows * slots)
    base = base + lax.rem(contracted, rows) * slots
    same_core = lax.rem(source_layer, 2) == lax.rem(my_layer, 2)
    return lambda index: jnp.where(same_core, mine_ref[base + index], other_ref[base + index])


def trace_kernel(sizes, rows, size, early, late, cols_ref, occ_ref, *refs):
    n_col = sizes[1]
    strip_refs, (mine_ref, other_ref) = refs[:len(early)], refs[len(early):len(early) + 2]
    crossed_refs, total_ref, sum_ref = refs[len(early) + 2:-2], refs[-2], refs[-1]
    packed_ref = strip_refs[0]
    slots = packed_ref.shape[0] // rows
    pair, here, group, number, per_group = place(sizes)
    width = per_group * rows
    sum_ref[...] = jnp.zeros((size, size), jnp.float32)

    def straight(block):
        return unpack(block, size)[:, :size]

    apart = lax.rem(here - group + n_col, n_col)
    is_late = functools.reduce(jnp.logical_or, [apart == k for k in late], jnp.bool_(False))

    @pl.when(is_late)
    def _():
        total = jnp.zeros((size, size), jnp.float32)
        for d, crossed_ref in enumerate(crossed_refs):
            shift = jnp.where(group < here, d, d + 1)
            column = lax.rem(number + shift, per_group) * rows
            for i in range(rows):
                for j in range(rows):
                    index, valid = found(cols_ref, occ_ref, pair * rows + i, here, column + j)
                    term = straight(packed_ref[i * slots + index]) * straight(crossed_ref[j * rows + i]).T
                    total = total + jnp.where(valid, 2.0 * term, 0.0)
        sum_ref[...] = total

    @pl.when(group == here)
    def _():
        total = jnp.zeros((size, size), jnp.float32)
        for i in range(rows):
            row = pair * rows + i
            for k, strip_ref in zip(early, strip_refs):
                contracted_group = lax.rem(here + k, n_col)
                for t in range(slots):
                    contracted = contracted_group * width + cols_ref[t, contracted_group, row]
                    index, valid = found(cols_ref, occ_ref, contracted, here, number * rows + i)
                    valid = valid & (occ_ref[t, contracted_group, row] == 1)
                    block = strip_block(sizes, rows, slots, mine_ref, other_ref, contracted)(index)
                    term = straight(strip_ref[i * slots + t]) * straight(block).T
                    total = total + jnp.where(valid, term, 0.0)
        sum_ref[...] = total

    total_ref[...] = jnp.sum(sum_ref[...], keepdims=True)


def stack_kernel(ahead, *refs):
    out_ref = refs[-1]
    for n, ref in enumerate(refs[ahead:-1]):
        out_ref[n * ref.shape[0]:(n + 1) * ref.shape[0]] = ref[...]


def product_kernel(sizes, shifts, added, cols_ref, occ_ref, *refs):
    n_row, n_col, n_layer = sizes
    count = len(shifts)
    strip_refs, (mine_ref, other_ref), refs = refs[:count], refs[count:count + 2], refs[count + 2:]
    before_ref, refs = (refs[0], refs[1:]) if added else (None, refs)
    out_ref, a_refs, w_refs = refs[0], refs[1:4], refs[4:]
    rows, _, slots, size, _ = out_ref.shape
    pair, here, _, _, per_group = place(sizes)
    width = per_group * rows

    for w_ref in w_refs:
        for j in range(count * slots):
            w_ref[j * LANES + size:(j + 1) * LANES, :] = jnp.zeros((LANES - size, slots * LANES), jnp.bfloat16)
    for i in range(rows):
        row = pair * rows + i
        targets = [cols_ref[s, here, row] for s in range(slots)]
        for k, shift in enumerate(shifts):
            group = lax.rem(here + shift, n_col)
            for t in range(slots):
                j = k * slots + t
                for a_ref, part in zip(a_refs, parts_of(unpack(strip_refs[k][i * slots + t], size))):
                    a_ref[:, j * LANES:(j + 1) * LANES] = part
                stored = occ_ref[t, group, row] == 1
                contracted = group * width + cols_ref[t, group, row]
                read = strip_block(sizes, rows, slots, mine_ref, other_ref, contracted)
                for s in range(slots):
                    index, valid = found(cols_ref, occ_ref, contracted, here, targets[s])
                    valid = valid & stored & (occ_ref[s, here, row] == 1)
                    block = jnp.where(valid, unpack(read(index), size), 0.0)
                    for w_ref, part in zip(w_refs, parts_of(block)):
                        w_ref[j * LANES:j * LANES + size, s * LANES:(s + 1) * LANES] = part

        def dot(a, w):
            return jnp.dot(a_refs[a][...], w_refs[w][...], preferred_element_type=jnp.float32)

        result = dot(0, 0) + ((dot(0, 1) + dot(1, 0)) + (dot(1, 1) + (dot(0, 2) + dot(2, 0))))
        for s in range(slots):
            block = result[:, s * LANES:s * LANES + size]
            out_ref[i, 0, s] = before_ref[i, 0, s] + block if added else block


def summed_over_all(value, sizes):
    n_row, n_col, n_layer = sizes
    total = n_row * n_col * n_layer
    bits = [1 << b for b in range((total - 1).bit_length())]
    in_layer = [b for b in bits if b < n_layer]
    in_col = [b for b in bits if n_layer <= b < n_layer * n_col]
    in_row = [b for b in bits if b >= n_layer * n_col]
    in_plane = in_layer[1:] + in_row
    stages = [in_layer[:1]]
    for some in (in_plane, in_col):
        stages += [some[n:n + 2] for n in range(0, len(some), 2)]

    def moved(mask):
        return lax.ppermute(value, AXES, [(n, n ^ mask) for n in range(total)])

    for stage in stages:
        if len(stage) == 1:
            value = value + moved(stage[0])
        elif stage:
            one, two = stage
            value = (value + moved(one)) + (moved(two) + moved(one ^ two))
    return value


def crossing(sizes, late, d):
    n_row, n_col, n_layer = sizes
    per_group = n_row * n_layer // n_col

    def device(group, number, column):
        pair = group * per_group + number
        return (pair // n_layer * n_col + column) * n_layer + pair % n_layer

    pairs = []
    for group in range(n_col):
        for number in range(per_group):
            for column in range(n_col):
                if (column - group) % n_col in late:
                    shift = d if group < column else d + 1
                    pairs.append((device(column, (number + shift) % per_group, group), device(group, number, column)))
    return pairs


def body(blocks, block_cols, occupancy):
    rows, _, slots, size, _ = blocks.shape
    sizes = tuple(lax.axis_size(axis) for axis in AXES)
    n_row, n_col, n_layer = sizes
    per_group = n_row * n_layer // n_col
    tall = tall_of(size)
    cols = jnp.transpose(block_cols, (2, 1, 0))
    occ = jnp.transpose(occupancy, (2, 1, 0))
    late = [k for k in range(n_col) if n_col < 4 * k < 3 * n_col]
    early = [k for k in range(n_col) if k not in late]

    def shape(count):
        return jax.ShapeDtypeStruct((count, tall, LANES), jnp.float32)

    packed = pl.pallas_call(
        pack_kernel,
        out_shape=shape(rows * slots),
        in_specs=[VMEM],
        out_specs=VMEM,
        compiler_params=LIMIT,
        name="pack",
    )(blocks)

    def shifted(k):
        return lax.ppermute(packed, "col", [((c + k) % n_col, c) for c in range(n_col)]) if k else packed

    strip = {k: shifted(k) for k in early}
    mine = [packed]
    for r in range(n_row):
        for y in range(0, n_layer, 2):
            if r or y:
                route = [
                    ((a + r) % n_row * n_layer + (b + y) % n_layer, a * n_layer + b)
                    for a in range(n_row) for b in range(n_layer)
                ]
                mine.append(lax.ppermute(packed, ("row", "layer"), route))
    crossed = pl.pallas_call(
        functools.partial(cross_kernel, sizes, rows),
        out_shape=[shape(rows * rows)] * (per_group // 2),
        in_specs=[SMEM, SMEM, VMEM],
        out_specs=[VMEM] * (per_group // 2),
        compiler_params=LIMIT,
        name="cross",
    )(cols, occ, packed)
    crossed = [lax.ppermute(value, AXES, crossing(sizes, late, d)) for d, value in enumerate(crossed)]

    ahead = [strip[k] for k in early if k]
    stacked = pl.pallas_call(
        functools.partial(stack_kernel, len(ahead)),
        out_shape=shape(len(mine) * rows * slots),
        in_specs=[pl.BlockSpec(memory_space=pl.ANY)] * len(ahead) + [VMEM] * len(mine),
        out_specs=VMEM,
        compiler_params=LIMIT,
        name="stack",
    )(*ahead, *mine)
    other = lax.ppermute(stacked, "layer", [(i, i ^ 1) for i in range(n_layer)])
    for k in late:
        strip[k] = shifted(k)

    trace = pl.pallas_call(
        functools.partial(trace_kernel, sizes, rows, size, early, late),
        out_shape=jax.ShapeDtypeStruct((1, 1), jnp.float32),
        in_specs=[SMEM, SMEM] + [VMEM] * (len(early) + 2 + len(crossed)),
        out_specs=VMEM,
        scratch_shapes=[pltpu.VMEM((size, size), jnp.float32)],
        compiler_params=LIMIT,
        name="trace_terms",
    )(cols, occ, *[strip[k] for k in early], stacked, other, *crossed)
    trace = summed_over_all(trace, sizes)

    product = None
    for shifts in (early, late):
        inner = len(shifts) * slots * LANES
        product = pl.pallas_call(
            functools.partial(product_kernel, sizes, shifts, product is not None),
            out_shape=jax.ShapeDtypeStruct(blocks.shape, jnp.float32),
            in_specs=[SMEM, SMEM] + [VMEM] * (len(shifts) + 2 + (product is not None)),
            out_specs=VMEM,
            scratch_shapes=[pltpu.VMEM((size, inner), jnp.bfloat16)] * 3
            + [pltpu.VMEM((inner, slots * LANES), jnp.bfloat16)] * 3,
            compiler_params=LIMIT,
            name="multiply",
        )(cols, occ, *[strip[k] for k in shifts], stacked, other, *([] if product is None else [product]))
    return product, trace.reshape(())


def solution(mesh):
    in_specs = (P(("row", "layer"), "col", None, None, None), P(), P())
    out_specs = (P(("row", "layer"), "col", None, None, None), P())
    return jax.shard_map(body, mesh=mesh, in_specs=in_specs, out_specs=out_specs, check_vma=False)
```

time: 60.2 us -> 68.6 us (1.14)
  waiting for transfers between devices: 4.62 us -> 17.3 us
  starting transfers between devices: 39.2 us -> 33.8 us
  Pallas kernels: 7.98 us -> 9.37 us
  local copies, waits for them, and re-layouts: 2.34 us -> 0.96 us
  between operations: 5.72 us -> 6.91 us
    ppermute x9 -> x11, waiting for transfers between devices: 4.61 us -> 14.7 us  [the longest x3 12.4 us: shifted(): lax.ppermute(packed, 'col', [((c + k) % n_col, c) for c in range(n_col)])]
    ppermute x9 -> x11, starting transfers between devices: 34.5 us -> 30.2 us  [the longest x7 23.6 us: moved(): return lax.ppermute(value, AXES, [(n, n ^ mask) for n in range(total)])]
    ppermute x3, waiting for transfers between devices: 0.01 us -> 2.48 us  [body(): mine.append(lax.ppermute(packed, ('row', 'layer'), route))]
    pallas_call x4 -> x6, Pallas kernels: 7.98 us -> 9.37 us  [the longest x2 6.14 us: body(): pl.pallas_call(functools.partial(product_kernel, sizes, shifts, product i...]
    unnamed x6, local copies, waits for them, and re-layouts: 2.34 us -> 0.96 us
    ppermute x3, starting transfers between devices: 4.6 us -> 3.49 us  [body(): mine.append(lax.ppermute(packed, ('row', 'layer'), route))]
  transfers between devices with their start and end apart: 13 -> 15, of which waited for: 5 -> 7; matrix products, arithmetic and copies ran while one was open for 0% -> 0% of each run, Pallas kernels for 3% -> 13%
where the time goes in v2:
time: 68.6 us; the launch traced here: 68.3 us
  starting transfers between devices  33.8 us (49%)
  waiting for transfers between devices  17.3 us (25%)
  Pallas kernels  9.37 us (14%)
  between operations  6.91 us (10%)
  local copies, waits for them, and re-layouts  0.96 us (1%)
    ppermute x7, starting transfers between devices, moved(): return lax.ppermute(value, AXES, [(n, n ^ mask) for n in range(total)])  23.6 us
    ppermute x3, waiting for transfers between devices, shifted(): lax.ppermute(packed, 'col', [((c + k) % n_col, c) for c in range(n_col)])  12.4 us
    pallas_call x2, Pallas kernels, body(): pl.pallas_call(functools.partial(product_kernel, sizes, shifts, product i...  6.14 us
    ppermute x3, starting transfers between devices, shifted(): lax.ppermute(packed, 'col', [((c + k) % n_col, c) for c in range(n_col)])  5.9 us
    ppermute x3, starting transfers between devices, body(): mine.append(lax.ppermute(packed, ('row', 'layer'), route))  3.49 us
    ppermute x3, waiting for transfers between devices, body(): mine.append(lax.ppermute(packed, ('row', 'layer'), route))  2.48 us
    ppermute x7, waiting for transfers between devices, moved(): return lax.ppermute(value, AXES, [(n, n ^ mask) for n in range(total)])  2.37 us
    pallas_call x1, Pallas kernels, body(): pl.pallas_call(functools.partial(trace_kernel, sizes, rows, size, early,...  2.27 us
  transfers between devices with their start and end apart: 15, of which 7 were waited for; matrix products, arithmetic and copies ran while one was open for 0% of the time, Pallas kernels for 13%

profile of v2, /device:TPU:0, one launch (start us, length us, event | category | flops | bytes accessed | tf_op | source)
XLA Modules:
  0.0 68.3 jit_solution(6039779391402324146)
XLA Ops:
  0.6 1.0 %copy-done = f32[2,1,3,96,96]{4,3,2,1,0:T(8,128)S(1)} copy-done((f32[2,1,3,96,96]{4,3,2,1,0:T(8,128)S(1)}, f32[2,1,3,96,96]{4,3,2,1,0:T(8,128)}, u32[]{:S(2)}) %copy-start) | copy-done | bytes 221208
  1.6 0.1 pack.1.refs_2_.refs_0_.packed_ref
  1.7 5.1 %collective-permute-start.1 = (f32[6,72,128]{2,1,0:T(8,128)S(1)}, f32[6,72,128]{2,1,0:T(8,128)S(1)}, u32[]{:S(2)}, u32[]{:S(2)}) collective-permute-start(f32[6,72,128]{2,1,0:T(8,128)S(1)} %pack.1.refs_2_.refs_0_.packed_ref), channel_id=1, source_target_pairs={{4,0},{8,4},{12,8},{0,12},{5,1},{9,5},{13,9},{1,13},{6,2},{10,6},{... | collective-permute-start | bytes 663560 | tf_op jit(solution)/shard_map/ppermute | solution.py:255
  6.8 0.0 collective-permute-start.2
  6.8 1.5 %collective-permute-start.3 = (f32[6,72,128]{2,1,0:T(8,128)S(1)}, f32[6,72,128]{2,1,0:T(8,128)S(1)}, u32[]{:S(2)}, u32[]{:S(2)}) collective-permute-start(f32[6,72,128]{2,1,0:T(8,128)S(1)} %pack.1.refs_2_.refs_0_.packed_ref), channel_id=1, source_target_pairs={{2,0},{3,1},{0,2},{1,3},{18,16},{19,17},{16,18},{17,19},{6,4},{7,5... | collective-permute-start | bytes 663560 | tf_op jit(solution)/shard_map/ppermute | solution.py:266
  8.3 1.5 %collective-permute-start.4 = (f32[6,72,128]{2,1,0:T(8,128)S(1)}, f32[6,72,128]{2,1,0:T(8,128)S(1)}, u32[]{:S(2)}, u32[]{:S(2)}) collective-permute-start(f32[6,72,128]{2,1,0:T(8,128)S(1)} %pack.1.refs_2_.refs_0_.packed_ref), channel_id=1, source_target_pairs={{16,0},{17,1},{18,2},{19,3},{0,16},{1,17},{2,18},{3,19},{20,4},{21... | collective-permute-start | bytes 663560 | tf_op jit(solution)/shard_map/ppermute | solution.py:266
  9.8 0.5 collective-permute-start.5
  10.3 2.3 %collective-permute-done.1.refs_0_.refs_1_ = f32[6,72,128]{2,1,0:T(8,128)S(1)} collective-permute-done((f32[6,72,128]{2,1,0:T(8,128)S(1)}, f32[6,72,128]{2,1,0:T(8,128)S(1)}, u32[]{:S(2)}, u32[]{:S(2)}) %collective-permute-start.1) | collective-permute-done | bytes 221216 | tf_op jit(solution)/shard_map/ppermute | solution.py:255
  12.6 4.5 %collective-permute-done.2.refs_1_.refs_2_ = f32[6,72,128]{2,1,0:T(8,128)S(1)} collective-permute-done((f32[6,72,128]{2,1,0:T(8,128)S(1)}, f32[6,72,128]{2,1,0:T(8,128)S(1)}, u32[]{:S(2)}, u32[]{:S(2)}) %collective-permute-start.2) | collective-permute-done | bytes 221216 | tf_op jit(solution)/shard_map/ppermute | solution.py:255
  17.1 0.0 collective-permute-done.3.refs_3_
  17.1 0.0 collective-permute-done.4.refs_4_
  17.1 2.5 %collective-permute-done.5.refs_5_ = f32[6,72,128]{2,1,0:T(8,128)S(1)} collective-permute-done((f32[6,72,128]{2,1,0:T(8,128)S(1)}, f32[6,72,128]{2,1,0:T(8,128)S(1)}, u32[]{:S(2)}, u32[]{:S(2)}) %collective-permute-start.5) | collective-permute-done | bytes 221216 | tf_op jit(solution)/shard_map/ppermute | solution.py:266
  19.6 0.1 stack.1.refs_3_.refs_1_
  19.7 0.1 collective-permute-start.6
  19.8 0.8 %collective-permute-start = (f32[6,72,128]{2,1,0:T(8,128)S(1)}, f32[6,72,128]{2,1,0:T(8,128)S(1)}, u32[]{:S(2)}, u32[]{:S(2)}) collective-permute-start(f32[6,72,128]{2,1,0:T(8,128)S(1)} %pack.1.refs_2_.refs_0_.packed_ref), channel_id=1, source_target_pairs={{8,0},{12,4},{0,8},{4,12},{9,1},{13,5},{1,9},{5,13},{10,2},{14,6},... | collective-permute-start | bytes 663560 | tf_op jit(solution)/shard_map/ppermute | solution.py:255
  20.6 0.8 %cross.1 = f32[4,72,128]{2,1,0:T(8,128)S(1)} custom-call(s32[3,4,16]{2,1,0:T(4,128)S(1)} %bitcast.3, s32[3,4,16]{2,1,0:T(4,128)S(1)} %bitcast.7, f32[6,72,128]{2,1,0:T(8,128)S(1)} %pack.1.refs_2_.refs_0_.packed_ref), custom_call_target="tpu_custom_call" | custom-call | tf_op jit(solution)/shard_map/cross/pallas_call | solution.py:267
  21.4 0.7 collective-permute-start.7
  22.0 0.0 collective-permute-done.7.refs_5_
  22.1 0.1 collective-permute-done.6.refs_4_.refs_2_
  22.2 2.3 %trace_terms.1 = f32[1,1]{1,0:T(1,128)} custom-call(s32[3,4,16]{2,1,0:T(4,128)S(1)} %bitcast.4, s32[3,4,16]{2,1,0:T(4,128)S(1)} %bitcast.8, f32[6,72,128]{2,1,0:T(8,128)S(1)} %pack.1.refs_2_.refs_0_.packed_ref, f32[6,72,128]{2,1,0:T(8,128)S(1)} %collective-permute-done.1.refs_0_.refs_1_, f32[6,72,128]{2,1,0:T(8,128)S(1)} %collective-permute-done.2.refs_1_.refs_2_, ...), custom_call_target="tpu_custom_call" | custom-call | tf_op jit(solution)/shard_map/trace_terms/pallas_call | solution.py:290
  24.5 0.1 collective-permute-start.8
  24.6 3.6 %multiply.2.refs_3_ = f32[2,1,3,96,96]{4,3,2,1,0:T(8,128)S(1)} custom-call(s32[3,4,16]{2,1,0:T(4,128)S(1)} %bitcast.5, s32[3,4,16]{2,1,0:T(4,128)S(1)} %bitcast.9, f32[6,72,128]{2,1,0:T(8,128)S(1)} %pack.1.refs_2_.refs_0_.packed_ref, f32[6,72,128]{2,1,0:T(8,128)S(1)} %collective-permute-done.1.refs_0_.refs_1_, ...), custom_call_target="tpu_custom_call" | custom-call | tf_op jit(solution)/shard_map/multiply/pallas_call | solution.py:304
  28.2 5.5 %collective-permute-done.refs_0_ = f32[6,72,128]{2,1,0:T(8,128)S(1)} collective-permute-done((f32[6,72,128]{2,1,0:T(8,128)S(1)}, f32[6,72,128]{2,1,0:T(8,128)S(1)}, u32[]{:S(2)}, u32[]{:S(2)}) %collective-permute-start) | collective-permute-done | bytes 221216 | tf_op jit(solution)/shard_map/ppermute | solution.py:255
  33.7 2.6 %multiply.3 = f32[2,1,3,96,96]{4,3,2,1,0:T(8,128)} custom-call(s32[3,4,16]{2,1,0:T(4,128)S(1)} %bitcast.6, s32[3,4,16]{2,1,0:T(4,128)S(1)} %bitcast.10, f32[6,72,128]{2,1,0:T(8,128)S(1)} %collective-permute-done.refs_0_, f32[24,72,128]{2,1,0:T(8,128)S(1)} %stack.1.refs_3_.refs_1_, f32[24,72,128]{2,1,0:T(8,128)S(1)} %collective-permute-done.6.refs_4_.refs_2_, ...), custom_call_target="tpu_custom_call" | custom-call | tf_op jit(solution)/shard_map/multiply/pallas_call | solution.py:304
  37.5 10.6 %collective-permute-start.10 = (f32[1,1]{1,0:T(1,128)}, f32[1,1]{1,0:T(1,128)}, u32[]{:S(2)}, u32[]{:S(2)}) collective-permute-start(f32[1,1]{1,0:T(1,128)} %add.21), channel_id=1, source_target_pairs={{0,16},{1,17},{2,18},{3,19},{4,20},{5,21},{6,22},{7,23},{8,24},{9,... | collective-permute-start | bytes 20 | tf_op jit(solution)/shard_map/ppermute | solution.py:202
  48.1 1.3 %collective-permute-start.11 = (f32[1,1]{1,0:T(1,128)}, f32[1,1]{1,0:T(1,128)}, u32[]{:S(2)}, u32[]{:S(2)}) collective-permute-start(f32[1,1]{1,0:T(1,128)} %add.21), channel_id=1, source_target_pairs={{0,18},{1,19},{2,16},{3,17},{4,22},{5,23},{6,20},{7,21},{8,26},{9,... | collective-permute-start | bytes 20 | tf_op jit(solution)/shard_map/ppermute | solution.py:202
  49.4 2.8 %collective-permute-start.9 = (f32[1,1]{1,0:T(1,128)}, f32[1,1]{1,0:T(1,128)}, u32[]{:S(2)}, u32[]{:S(2)}) collective-permute-start(f32[1,1]{1,0:T(1,128)} %add.21), channel_id=1, source_target_pairs={{0,2},{1,3},{2,0},{3,1},{4,6},{5,7},{6,4},{7,5},{8,10},{9,11},{10,... | collective-permute-start | bytes 20 | tf_op jit(solution)/shard_map/ppermute | solution.py:202
  52.1 0.7 %collective-permute-done.9 = f32[1,1]{1,0:T(1,128)} collective-permute-done((f32[1,1]{1,0:T(1,128)}, f32[1,1]{1,0:T(1,128)}, u32[]{:S(2)}, u32[]{:S(2)}) %collective-permute-start.9) | collective-permute-done | bytes 36 | tf_op jit(solution)/shard_map/ppermute | solution.py:202
  54.8 1.4 %collective-permute-start.13 = (f32[1,1]{1,0:T(1,128)}, f32[1,1]{1,0:T(1,128)}, u32[]{:S(2)}, u32[]{:S(2)}) collective-permute-start(f32[1,1]{1,0:T(1,128)} %add.24), channel_id=1, source_target_pairs={{0,8},{1,9},{2,10},{3,11},{4,12},{5,13},{6,14},{7,15},{8,0},{9,1},... | collective-permute-start | bytes 20 | tf_op jit(solution)/shard_map/ppermute | solution.py:202
  56.2 5.6 %collective-permute-start.14 = (f32[1,1]{1,0:T(1,128)}, f32[1,1]{1,0:T(1,128)}, u32[]{:S(2)}, u32[]{:S(2)}) collective-permute-start(f32[1,1]{1,0:T(1,128)} %add.24), channel_id=1, source_target_pairs={{0,12},{1,13},{2,14},{3,15},{4,8},{5,9},{6,10},{7,11},{8,4},{9,5},... | collective-permute-start | bytes 20 | tf_op jit(solution)/shard_map/ppermute | solution.py:202
  61.8 1.9 %collective-permute-start.12 = (f32[1,1]{1,0:T(1,128)}, f32[1,1]{1,0:T(1,128)}, u32[]{:S(2)}, u32[]{:S(2)}) collective-permute-start(f32[1,1]{1,0:T(1,128)} %add.24), channel_id=1, source_target_pairs={{0,4},{1,5},{2,6},{3,7},{4,0},{5,1},{6,2},{7,3},{8,12},{9,13},{10,... | collective-permute-start | bytes 20 | tf_op jit(solution)/shard_map/ppermute | solution.py:202
  63.6 1.6 %collective-permute-done.12 = f32[1,1]{1,0:T(1,128)} collective-permute-done((f32[1,1]{1,0:T(1,128)}, f32[1,1]{1,0:T(1,128)}, u32[]{:S(2)}, u32[]{:S(2)}) %collective-permute-start.12) | collective-permute-done | bytes 36 | tf_op jit(solution)/shard_map/ppermute | solution.py:202
  (10 shorter events, 0.0 us)
Async XLA Ops:
  0.6 1.0 %copy-start = (f32[2,1,3,96,96]{4,3,2,1,0:T(8,128)S(1)}, f32[2,1,3,96,96]{4,3,2,1,0:T(8,128)}, u32[]{:S(2)}) copy-start(f32[2,1,3,96,96]{4,3,2,1,0:T(8,128)} %x_ref.1) | copy-start | bytes 663556
  1.7 10.9 %collective-permute-start.1 = (f32[6,72,128]{2,1,0:T(8,128)S(1)}, f32[6,72,128]{2,1,0:T(8,128)S(1)}, u32[]{:S(2)}, u32[]{:S(2)}) collective-permute-start(f32[6,72,128]{2,1,0:T(8,128)S(1)} %pack.1.refs_2_.refs_0_.packed_ref), channel_id=1, source_target_pairs={{4,0},{8,4},{12,8},{0,12},{5,1},{9,5},{13,9},{1,13},{6,2},{10,6},{... | collective-permute-start | bytes 663560 | tf_op jit(solution)/shard_map/ppermute | solution.py:255
  6.8 10.3 %collective-permute-start.2 = (f32[6,72,128]{2,1,0:T(8,128)S(1)}, f32[6,72,128]{2,1,0:T(8,128)S(1)}, u32[]{:S(2)}, u32[]{:S(2)}) collective-permute-start(f32[6,72,128]{2,1,0:T(8,128)S(1)} %pack.1.refs_2_.refs_0_.packed_ref), channel_id=1, source_target_pairs={{12,0},{0,4},{4,8},{8,12},{13,1},{1,5},{5,9},{9,13},{14,2},{2,6},{... | collective-permute-start | bytes 663560 | tf_op jit(solution)/shard_map/ppermute | solution.py:255
  6.8 10.3 %collective-permute-start.3 = (f32[6,72,128]{2,1,0:T(8,128)S(1)}, f32[6,72,128]{2,1,0:T(8,128)S(1)}, u32[]{:S(2)}, u32[]{:S(2)}) collective-permute-start(f32[6,72,128]{2,1,0:T(8,128)S(1)} %pack.1.refs_2_.refs_0_.packed_ref), channel_id=1, source_target_pairs={{2,0},{3,1},{0,2},{1,3},{18,16},{19,17},{16,18},{17,19},{6,4},{7,5... | collective-permute-start | bytes 663560 | tf_op jit(solution)/shard_map/ppermute | solution.py:266
  8.3 8.8 %collective-permute-start.4 = (f32[6,72,128]{2,1,0:T(8,128)S(1)}, f32[6,72,128]{2,1,0:T(8,128)S(1)}, u32[]{:S(2)}, u32[]{:S(2)}) collective-permute-start(f32[6,72,128]{2,1,0:T(8,128)S(1)} %pack.1.refs_2_.refs_0_.packed_ref), channel_id=1, source_target_pairs={{16,0},{17,1},{18,2},{19,3},{0,16},{1,17},{2,18},{3,19},{20,4},{21... | collective-permute-start | bytes 663560 | tf_op jit(solution)/shard_map/ppermute | solution.py:266
  9.8 9.8 %collective-permute-start.5 = (f32[6,72,128]{2,1,0:T(8,128)S(1)}, f32[6,72,128]{2,1,0:T(8,128)S(1)}, u32[]{:S(2)}, u32[]{:S(2)}) collective-permute-start(f32[6,72,128]{2,1,0:T(8,128)S(1)} %pack.1.refs_2_.refs_0_.packed_ref), channel_id=1, source_target_pairs={{18,0},{19,1},{16,2},{17,3},{2,16},{3,17},{0,18},{1,19},{22,4},{23... | collective-permute-start | bytes 663560 | tf_op jit(solution)/shard_map/ppermute | solution.py:266
  19.6 0.9 %copy-start.1 = (s32[16,4,3]{0,1,2:T(4,128)S(1)}, s32[16,4,3]{0,1,2:T(4,128)}, u32[]{:S(2)}) copy-start(s32[16,4,3]{0,1,2:T(4,128)} %param.4) | copy-start | bytes 2308
  19.6 0.9 %copy-start.2 = (s32[16,4,3]{0,1,2:T(4,128)S(1)}, s32[16,4,3]{0,1,2:T(4,128)}, u32[]{:S(2)}) copy-start(s32[16,4,3]{0,1,2:T(4,128)} %param.5) | copy-start | bytes 2308
  19.7 2.5 %collective-permute-start.6 = (f32[24,72,128]{2,1,0:T(8,128)S(1)}, f32[24,72,128]{2,1,0:T(8,128)S(1)}, u32[]{:S(2)}, u32[]{:S(2)}) collective-permute-start(f32[24,72,128]{2,1,0:T(8,128)S(1)} %stack.1.refs_3_.refs_1_), channel_id=1, source_target_pairs={{0,1},{1,0},{2,3},{3,2},{4,5},{5,4},{6,7},{7,6},{8,9},{9,8},{10,11... | collective-permute-start | bytes 2654216 | tf_op jit(solution)/shard_map/ppermute | solution.py:286
  19.8 13.9 %collective-permute-start = (f32[6,72,128]{2,1,0:T(8,128)S(1)}, f32[6,72,128]{2,1,0:T(8,128)S(1)}, u32[]{:S(2)}, u32[]{:S(2)}) collective-permute-start(f32[6,72,128]{2,1,0:T(8,128)S(1)} %pack.1.refs_2_.refs_0_.packed_ref), channel_id=1, source_target_pairs={{8,0},{12,4},{0,8},{4,12},{9,1},{13,5},{1,9},{5,13},{10,2},{14,6},... | collective-permute-start | bytes 663560 | tf_op jit(solution)/shard_map/ppermute | solution.py:255
  21.4 0.7 collective-permute-start.7
  24.5 11.8 %collective-permute-start.8 = (f32[1,1]{1,0:T(1,128)}, f32[1,1]{1,0:T(1,128)}, u32[]{:S(2)}, u32[]{:S(2)}) collective-permute-start(f32[1,1]{1,0:T(1,128)} %trace_terms.1), channel_id=1, source_target_pairs={{0,1},{1,0},{2,3},{3,2},{4,5},{5,4},{6,7},{7,6},{8,9},{9,8},{10,11... | collective-permute-start | bytes 20 | tf_op jit(solution)/shard_map/ppermute | solution.py:202
  37.5 16.1 %collective-permute-start.10 = (f32[1,1]{1,0:T(1,128)}, f32[1,1]{1,0:T(1,128)}, u32[]{:S(2)}, u32[]{:S(2)}) collective-permute-start(f32[1,1]{1,0:T(1,128)} %add.21), channel_id=1, source_target_pairs={{0,16},{1,17},{2,18},{3,19},{4,20},{5,21},{6,22},{7,23},{8,24},{9,... | collective-permute-start | bytes 20 | tf_op jit(solution)/shard_map/ppermute | solution.py:202
  48.1 5.5 %collective-permute-start.11 = (f32[1,1]{1,0:T(1,128)}, f32[1,1]{1,0:T(1,128)}, u32[]{:S(2)}, u32[]{:S(2)}) collective-permute-start(f32[1,1]{1,0:T(1,128)} %add.21), channel_id=1, source_target_pairs={{0,18},{1,19},{2,16},{3,17},{4,22},{5,23},{6,20},{7,21},{8,26},{9,... | collective-permute-start | bytes 20 | tf_op jit(solution)/shard_map/ppermute | solution.py:202
  49.4 3.5 %collective-permute-start.9 = (f32[1,1]{1,0:T(1,128)}, f32[1,1]{1,0:T(1,128)}, u32[]{:S(2)}, u32[]{:S(2)}) collective-permute-start(f32[1,1]{1,0:T(1,128)} %add.21), channel_id=1, source_target_pairs={{0,2},{1,3},{2,0},{3,1},{4,6},{5,7},{6,4},{7,5},{8,10},{9,11},{10,... | collective-permute-start | bytes 20 | tf_op jit(solution)/shard_map/ppermute | solution.py:202
  54.8 11.2 %collective-permute-start.13 = (f32[1,1]{1,0:T(1,128)}, f32[1,1]{1,0:T(1,128)}, u32[]{:S(2)}, u32[]{:S(2)}) collective-permute-start(f32[1,1]{1,0:T(1,128)} %add.24), channel_id=1, source_target_pairs={{0,8},{1,9},{2,10},{3,11},{4,12},{5,13},{6,14},{7,15},{8,0},{9,1},... | collective-permute-start | bytes 20 | tf_op jit(solution)/shard_map/ppermute | solution.py:202
  56.2 9.8 %collective-permute-start.14 = (f32[1,1]{1,0:T(1,128)}, f32[1,1]{1,0:T(1,128)}, u32[]{:S(2)}, u32[]{:S(2)}) collective-permute-start(f32[1,1]{1,0:T(1,128)} %add.24), channel_id=1, source_target_pairs={{0,12},{1,13},{2,14},{3,15},{4,8},{5,9},{6,10},{7,11},{8,4},{9,5},... | collective-permute-start | bytes 20 | tf_op jit(solution)/shard_map/ppermute | solution.py:202
  61.8 3.5 %collective-permute-start.12 = (f32[1,1]{1,0:T(1,128)}, f32[1,1]{1,0:T(1,128)}, u32[]{:S(2)}, u32[]{:S(2)}) collective-permute-start(f32[1,1]{1,0:T(1,128)} %add.24), channel_id=1, source_target_pairs={{0,4},{1,5},{2,6},{3,7},{4,0},{5,1},{6,2},{7,3},{8,12},{9,13},{10,... | collective-permute-start | bytes 20 | tf_op jit(solution)/shard_map/ppermute | solution.py:202

commit v3 on v1

v3 whole, which is shorter than its diff:
```python
import functools

import jax
import jax.numpy as jnp
from jax import lax
from jax.experimental import pallas as pl
from jax.experimental.pallas import tpu as pltpu
from jax.sharding import PartitionSpec as P

LANES = 128
AXES = ("row", "col", "layer")
LIMIT = pltpu.CompilerParams(vmem_limit_bytes=48 * 2 ** 20)
VMEM = pl.BlockSpec(memory_space=pltpu.VMEM)
SMEM = pl.BlockSpec(memory_space=pltpu.SMEM)


def tall_of(size):
    return size * size // LANES


def unpack(block, size):
    tall = block.shape[0]
    spare = LANES - size
    rest = size - tall
    pieces = [block[q * rest:(q + 1) * rest, size:] for q in range(size // spare)]
    pieces.append(jnp.zeros((rest, spare), block.dtype))
    return jnp.concatenate([block, jnp.concatenate(pieces, axis=1)], axis=0)


def parts_of(value):
    parts = []
    for _ in range(3):
        part = value.astype(jnp.bfloat16)
        parts.append(part)
        value = value - part.astype(jnp.float32)
    return parts


def found(cols_ref, occ_ref, row, group, target):
    index = jnp.int32(0)
    valid = jnp.int32(0)
    for u in range(cols_ref.shape[0]):
        hit = jnp.where((cols_ref[u, group, row] == target) & (occ_ref[u, group, row] == 1), 1, 0)
        index = index + hit * u
        valid = valid + hit
    return index, valid > 0


def place(sizes):
    n_row, n_col, n_layer = sizes
    per_group = n_row * n_layer // n_col
    pair = lax.axis_index("row") * n_layer + lax.axis_index("layer")
    return pair, lax.axis_index("col"), lax.div(pair, per_group), lax.rem(pair, per_group), per_group


def pack_kernel(x_ref, out_ref, *more_refs):
    rows, _, slots, size, _ = x_ref.shape
    tall = tall_of(size)
    spare = LANES - size
    rest = size - tall
    for i in range(rows):
        for t in range(slots):
            n = i * slots + t
            out_ref[n, :, :size] = x_ref[i, 0, t, :tall, :]
            for q in range(size // spare):
                out_ref[n, q * rest:(q + 1) * rest, size:] = x_ref[i, 0, t, tall:, q * spare:(q + 1) * spare]
    for more_ref in more_refs:
        for n in range(more_ref.shape[0]):
            more_ref[n] = out_ref[...]


def strip_block(n_col, rows, slots, strip_ref, contracted):
    return lambda index: strip_ref[lax.div(contracted, rows), lax.rem(contracted, rows) * slots + index]


def trace_kernel(sizes, rows, size, cols_ref, occ_ref, row_ref, column_ref, total_ref, sum_ref):
    n_col = sizes[1]
    slots = row_ref.shape[1] // rows
    pair, here, group, number, per_group = place(sizes)
    width = per_group * rows
    total_ref[...] = jnp.zeros(total_ref.shape, jnp.float32)

    def straight(block):
        return unpack(block, size)[:, :size]

    @pl.when(group == here)
    def _():
        total = jnp.zeros((size, size), jnp.float32)
        for i in range(rows):
            row = pair * rows + i
            for k in range(n_col):
                for t in range(slots):
                    contracted = k * width + cols_ref[t, k, row]
                    index, valid = found(cols_ref, occ_ref, contracted, here, number * rows + i)
                    valid = valid & (occ_ref[t, k, row] == 1)
                    block = strip_block(n_col, rows, slots, column_ref, contracted)(index)
                    term = straight(row_ref[k, i * slots + t]) * straight(block).T
                    total = total + jnp.where(valid, term, 0.0)
        total_ref[...] = jnp.full(total_ref.shape, jnp.sum(total), jnp.float32)


def product_kernel(sizes, cols_ref, occ_ref, row_ref, column_ref, out_ref, *refs):
    n_row, n_col, n_layer = sizes
    a_refs, w_refs = refs[:3], refs[3:]
    rows, _, slots, size, _ = out_ref.shape
    pair, here, _, _, per_group = place(sizes)
    width = per_group * rows

    for w_ref in w_refs:
        for j in range(n_col * slots):
            w_ref[j * LANES + size:(j + 1) * LANES, :] = jnp.zeros((LANES - size, slots * LANES), jnp.bfloat16)
    for i in range(rows):
        row = pair * rows + i
        targets = [cols_ref[s, here, row] for s in range(slots)]
        for k in range(n_col):
            for t in range(slots):
                j = k * slots + t
                for a_ref, part in zip(a_refs, parts_of(unpack(row_ref[k, i * slots + t], size))):
                    a_ref[:, j * LANES:(j + 1) * LANES] = part
                stored = occ_ref[t, k, row] == 1
                contracted = k * width + cols_ref[t, k, row]
                read = strip_block(n_col, rows, slots, column_ref, contracted)
                for s in range(slots):
                    index, valid = found(cols_ref, occ_ref, contracted, here, targets[s])
                    valid = valid & stored & (occ_ref[s, here, row] == 1)
                    block = jnp.where(valid, unpack(read(index), size), 0.0)
                    for w_ref, part in zip(w_refs, parts_of(block)):
                        w_ref[j * LANES:j * LANES + size, s * LANES:(s + 1) * LANES] = part

        def dot(a, w):
            return jnp.dot(a_refs[a][...], w_refs[w][...], preferred_element_type=jnp.float32)

        result = dot(0, 0) + ((dot(0, 1) + dot(1, 0)) + (dot(1, 1) + (dot(0, 2) + dot(2, 0))))
        for s in range(slots):
            out_ref[i, 0, s] = result[:, s * LANES:s * LANES + size]


def body(blocks, block_cols, occupancy):
    rows, _, slots, size, _ = blocks.shape
    sizes = tuple(lax.axis_size(axis) for axis in AXES)
    n_row, n_col, n_layer = sizes
    n_pair = n_row * n_layer
    tall = tall_of(size)
    cols = jnp.transpose(block_cols, (2, 1, 0))
    occ = jnp.transpose(occupancy, (2, 1, 0))
    share = (rows * slots, tall, LANES)

    _, for_col, for_plane = pl.pallas_call(
        pack_kernel,
        out_shape=[jax.ShapeDtypeStruct(s, jnp.float32) for s in (share, (n_col,) + share, (n_pair,) + share)],
        in_specs=[VMEM],
        out_specs=[VMEM] * 3,
        compiler_params=LIMIT,
        name="pack",
    )(blocks)
    row_strip = lax.all_to_all(for_col, "col", 0, 0, tiled=True)
    column_strip = lax.all_to_all(for_plane, ("row", "layer"), 0, 0, tiled=True)

    trace = pl.pallas_call(
        functools.partial(trace_kernel, sizes, rows, size),
        out_shape=jax.ShapeDtypeStruct((n_col * n_pair, 1, LANES), jnp.float32),
        in_specs=[SMEM, SMEM, VMEM, VMEM],
        out_specs=VMEM,
        scratch_shapes=[pltpu.VMEM((size, size), jnp.float32)],
        compiler_params=LIMIT,
        name="trace_terms",
    )(cols, occ, row_strip, column_strip)
    trace = lax.all_to_all(trace, AXES, 0, 0, tiled=True)
    inner = n_col * slots * LANES
    product = pl.pallas_call(
        functools.partial(product_kernel, sizes),
        out_shape=jax.ShapeDtypeStruct(blocks.shape, jnp.float32),
        in_specs=[SMEM, SMEM, VMEM, VMEM],
        out_specs=VMEM,
        scratch_shapes=[pltpu.VMEM((size, inner), jnp.bfloat16)] * 3
        + [pltpu.VMEM((inner, slots * LANES), jnp.bfloat16)] * 3,
        compiler_params=LIMIT,
        name="multiply",
    )(cols, occ, row_strip, column_strip)
    return product, jnp.sum(trace[:, 0, 0])


def solution(mesh):
    in_specs = (P(("row", "layer"), "col", None, None, None), P(), P())
    out_specs = (P(("row", "layer"), "col", None, None, None), P())
    return jax.shard_map(body, mesh=mesh, in_specs=in_specs, out_specs=out_specs, check_vma=False)
```

time: 60.2 us -> 70.2 us (1.17)
  blocking collectives: 0 us -> 54.7 us
  starting transfers between devices: 39.2 us -> 2.52 us
  between operations: 5.72 us -> 0.65 us
  waiting for transfers between devices: 4.62 us -> 2.09 us
  local copies, waits for them, and re-layouts: 2.34 us -> 0.96 us
    all_to_all x0 -> x2, blocking collectives: none -> 54.7 us  [the longest x1 28.3 us: body(): row_strip = lax.all_to_all(for_col, 'col', 0, 0, tiled=True)]
    ppermute x13 -> x0, starting transfers between devices: 39.2 us -> none  [the longest x5 30.7 us: summed_over(): lax.ppermute(value, axis, [(i, i ^ step) for i in range(size)])]
    ppermute x13 -> x0, waiting for transfers between devices: 4.62 us -> none  [the longest x5 3.24 us: summed_over(): lax.ppermute(value, axis, [(i, i ^ step) for i in range(size)])]
    all_to_all x0 -> x1, starting transfers between devices: none -> 2.52 us  [body(): trace = lax.all_to_all(trace, AXES, 0, 0, tiled=True)]
    all_to_all x0 -> x1, waiting for transfers between devices: none -> 2.09 us  [body(): trace = lax.all_to_all(trace, AXES, 0, 0, tiled=True)]
    unnamed x6, local copies, waits for them, and re-layouts: 2.34 us -> 0.96 us
  transfers between devices with their start and end apart: 13 -> 1, of which waited for: 5 -> 1; matrix products, arithmetic and copies ran while one was open for 0% -> 0% of each run, Pallas kernels for 3% -> 7%
where the time goes in v3:
time: 70.2 us; the launch traced here: 70 us
  blocking collectives  54.7 us (78%)
  Pallas kernels  8.37 us (12%)
  starting transfers between devices  2.52 us (4%)
  waiting for transfers between devices  2.09 us (3%)
  local copies, waits for them, and re-layouts  0.96 us (1%)
    all_to_all x1, blocking collectives, body(): row_strip = lax.all_to_all(for_col, 'col', 0, 0, tiled=True)  28.3 us
    all_to_all x1, blocking collectives, body(): column_strip = lax.all_to_all(for_plane, ('row', 'layer'), 0, 0, tiled=True)  26.4 us
    pallas_call x1, Pallas kernels, body(): pl.pallas_call(functools.partial(product_kernel, sizes), out_shape=jax.Sh...  5.05 us
    all_to_all x1, starting transfers between devices, body(): trace = lax.all_to_all(trace, AXES, 0, 0, tiled=True)  2.52 us
    pallas_call x1, Pallas kernels, body(): pl.pallas_call(functools.partial(trace_kernel, sizes, rows, size), out_sh...  2.35 us
    all_to_all x1, waiting for transfers between devices, body(): trace = lax.all_to_all(trace, AXES, 0, 0, tiled=True)  2.09 us
  transfers between devices with their start and end apart: 1, of which 1 were waited for; matrix products, arithmetic and copies ran while one was open for 0% of the time, Pallas kernels for 7%

profile of v3, /device:TPU:0, one launch (start us, length us, event | category | flops | bytes accessed | tf_op | source)
XLA Modules:
  0.0 70.0 jit_solution(8917723754602258821)
XLA Ops:
  0.6 0.0 copy-start
  0.6 1.0 %copy-done = f32[2,1,3,96,96]{4,3,2,1,0:T(8,128)S(1)} copy-done((f32[2,1,3,96,96]{4,3,2,1,0:T(8,128)S(1)}, f32[2,1,3,96,96]{4,3,2,1,0:T(8,128)}, u32[]{:S(2)}) %copy-start) | copy-done | bytes 221208
  1.6 1.0 %pack.1 = (f32[6,72,128]{2,1,0:T(8,128)}, f32[4,6,72,128]{3,2,1,0:T(8,128)S(1)}, f32[8,6,72,128]{3,2,1,0:T(8,128)S(1)}) custom-call(f32[2,1,3,96,96]{4,3,2,1,0:T(8,128)S(1)} %copy-done), custom_call_target="tpu_custom_call" | custom-call | tf_op jit(solution)/shard_map/pack/pallas_call | solution.py:148
  2.6 28.3 %all_to_all.15.row_ref = f32[4,6,72,128]{3,2,1,0:T(8,128)S(1)} all-to-all(f32[4,6,72,128]{3,2,1,0:T(8,128)S(1)} %get-tuple-element.4), channel_id=1, replica_groups=mesh['row'=2,'col'=4,'layer'=4] {'col'}, dimensions={0} | all-to-all | bytes 1769472 | tf_op jit(solution)/shard_map/all_to_all | solution.py:156
  30.9 0.0 copy-start.1
  30.9 0.0 copy-start.2
  30.9 26.4 %all_to_all.16.column_ref = f32[8,6,72,128]{3,2,1,0:T(8,128)S(1)} all-to-all(f32[8,6,72,128]{3,2,1,0:T(8,128)S(1)} %get-tuple-element.5), channel_id=1, replica_groups=mesh['row'=2,'col'=4,'layer'=4] {'row','layer'}, dimensions={0} | all-to-all | bytes 3538944 | tf_op jit(solution)/shard_map/all_to_all | solution.py:157
  57.3 0.0 copy-done.1
  57.3 0.0 copy-done.2
  57.3 2.4 %trace_terms.1 = f32[32,1,128]{2,1,0:T(1,128)} custom-call(s32[3,4,16]{2,1,0:T(4,128)S(1)} %bitcast.2, s32[3,4,16]{2,1,0:T(4,128)S(1)} %bitcast.4, f32[4,6,72,128]{3,2,1,0:T(8,128)S(1)} %all_to_all.15.row_ref, f32[8,6,72,128]{3,2,1,0:T(8,128)S(1)} %all_to_all.16.column_ref), custom_call_target="tpu_custom_call" | custom-call | tf_op jit(solution)/shard_map/trace_terms/pallas_call | solution.py:159
  59.7 2.5 %all-to-all-start.2 = ((f32[32,1,128]{2,1,0:T(1,128)}), f32[32,1,128]{2,1,0:T(1,128)S(1)}, u32[]{:S(2)}, u32[]{:S(2)}) async-start(f32[32,1,128]{2,1,0:T(1,128)} %trace_terms.1), calls=%async_computation.2 | async-start | bytes 32768 | tf_op jit(solution)/shard_map/all_to_all | solution.py:168
  62.2 5.0 %multiply.1 = f32[2,1,3,96,96]{4,3,2,1,0:T(8,128)} custom-call(s32[3,4,16]{2,1,0:T(4,128)S(1)} %bitcast.3, s32[3,4,16]{2,1,0:T(4,128)S(1)} %bitcast.5, f32[4,6,72,128]{3,2,1,0:T(8,128)S(1)} %all_to_all.15.row_ref, f32[8,6,72,128]{3,2,1,0:T(8,128)S(1)} %all_to_all.16.column_ref), custom_call_target="tpu_custom_call" | custom-call | tf_op jit(solution)/shard_map/multiply/pallas_call | solution.py:170
  67.2 2.1 %all-to-all-done.2 = f32[32,1,128]{2,1,0:T(1,128)S(1)} async-done(((f32[32,1,128]{2,1,0:T(1,128)}), f32[32,1,128]{2,1,0:T(1,128)S(1)}, u32[]{:S(2)}, u32[]{:S(2)}) %all-to-all-start.2) | async-done | bytes 16416 | tf_op jit(solution)/shard_map/all_to_all | solution.py:168
  69.3 0.6 slice_reduce_fusion
Async XLA Ops:
  0.6 1.0 %copy-start = (f32[2,1,3,96,96]{4,3,2,1,0:T(8,128)S(1)}, f32[2,1,3,96,96]{4,3,2,1,0:T(8,128)}, u32[]{:S(2)}) copy-start(f32[2,1,3,96,96]{4,3,2,1,0:T(8,128)} %x_ref.1) | copy-start | bytes 663556
  30.9 26.4 %copy-start.1 = (s32[16,4,3]{0,1,2:T(4,128)S(1)}, s32[16,4,3]{0,1,2:T(4,128)}, u32[]{:S(2)}) copy-start(s32[16,4,3]{0,1,2:T(4,128)} %param.4) | copy-start | bytes 2308
  30.9 26.4 %copy-start.2 = (s32[16,4,3]{0,1,2:T(4,128)S(1)}, s32[16,4,3]{0,1,2:T(4,128)}, u32[]{:S(2)}) copy-start(s32[16,4,3]{0,1,2:T(4,128)} %param.5) | copy-start | bytes 2308
  59.7 9.7 %all-to-all-start.2 = ((f32[32,1,128]{2,1,0:T(1,128)}), f32[32,1,128]{2,1,0:T(1,128)S(1)}, u32[]{:S(2)}, u32[]{:S(2)}) async-start(f32[32,1,128]{2,1,0:T(1,128)} %trace_terms.1), calls=%async_computation.2 | async-start | bytes 32768 | tf_op jit(solution)/shard_map/all_to_all | solution.py:168

commit v4 on v2

--- a/solution.py
+++ b/solution.py
@@ -136,7 +136,7 @@
                     total = total + jnp.where(valid, term, 0.0)
         sum_ref[...] = total
 
-    total_ref[...] = jnp.sum(sum_ref[...], keepdims=True)
+    total_ref[...] = jnp.full(total_ref.shape, jnp.sum(sum_ref[...]), jnp.float32)
 
 
 def stack_kernel(ahead, *refs):
@@ -186,30 +186,6 @@
             out_ref[i, 0, s] = before_ref[i, 0, s] + block if added else block
 
 
-def summed_over_all(value, sizes):
-    n_row, n_col, n_layer = sizes
-    total = n_row * n_col * n_layer
-    bits = [1 << b for b in range((total - 1).bit_length())]
-    in_layer = [b for b in bits if b < n_layer]
-    in_col = [b for b in bits if n_layer <= b < n_layer * n_col]
-    in_row = [b for b in bits if b >= n_layer * n_col]
-    in_plane = in_layer[1:] + in_row
-    stages = [in_layer[:1]]
-    for some in (in_plane, in_col):
-        stages += [some[n:n + 2] for n in range(0, len(some), 2)]
-
-    def moved(mask):
-        return lax.ppermute(value, AXES, [(n, n ^ mask) for n in range(total)])
-
-    for stage in stages:
-        if len(stage) == 1:
-            value = value + moved(stage[0])
-        elif stage:
-            one, two = stage
-            value = (value + moved(one)) + (moved(two) + moved(one ^ two))
-    return value
-
-
 def crossing(sizes, late, d):
     n_row, n_col, n_layer = sizes
     per_group = n_row * n_layer // n_col
@@ -274,7 +250,7 @@
     )(cols, occ, packed)
     crossed = [lax.ppermute(value, AXES, crossing(sizes, late, d)) for d, value in enumerate(crossed)]
 
-    ahead = [strip[k] for k in early if k]
+    ahead = [strip[k] for k in early if k] + crossed
     stacked = pl.pallas_call(
         functools.partial(stack_kernel, len(ahead)),
         out_shape=shape(len(mine) * rows * slots),
@@ -289,14 +265,14 @@
 
     trace = pl.pallas_call(
         functools.partial(trace_kernel, sizes, rows, size, early, late),
-        out_shape=jax.ShapeDtypeStruct((1, 1), jnp.float32),
+        out_shape=jax.ShapeDtypeStruct((n_row * n_col * n_layer, 1, LANES), jnp.float32),
         in_specs=[SMEM, SMEM] + [VMEM] * (len(early) + 2 + len(crossed)),
         out_specs=VMEM,
         scratch_shapes=[pltpu.VMEM((size, size), jnp.float32)],
         compiler_params=LIMIT,
         name="trace_terms",
     )(cols, occ, *[strip[k] for k in early], stacked, other, *crossed)
-    trace = summed_over_all(trace, sizes)
+    trace = lax.all_to_all(trace, AXES, 0, 0, tiled=True)
 
     product = None
     for shifts in (early, late):
@@ -311,7 +287,7 @@
             compiler_params=LIMIT,
             name="multiply",
         )(cols, occ, *[strip[k] for k in shifts], stacked, other, *([] if product is None else [product]))
-    return product, trace.reshape(())
+    return product, jnp.sum(trace[:, 0, 0])
 
 
 def solution(mesh):

time: 68.6 us -> 43.9 us (0.64)
  starting transfers between devices: 33.8 us -> 18.7 us
  between operations: 6.91 us -> 0.71 us
  waiting for transfers between devices: 17.3 us -> 12.6 us
    ppermute x7 -> x0, starting transfers between devices: 23.6 us -> none  [moved(): return lax.ppermute(value, AXES, [(n, n ^ mask) for n in range(total)])]
    all_to_all x0 -> x1, starting transfers between devices: none -> 6.61 us  [body(): trace = lax.all_to_all(trace, AXES, 0, 0, tiled=True)]
    ppermute x3, waiting for transfers between devices: 12.4 us -> 8.04 us  [shifted(): lax.ppermute(packed, 'col', [((c + k) % n_col, c) for c in range(n_col)])]
    ppermute x7 -> x0, waiting for transfers between devices: 2.37 us -> none  [moved(): return lax.ppermute(value, AXES, [(n, n ^ mask) for n in range(total)])]
    ppermute x3, starting transfers between devices: 3.49 us -> 5.18 us  [body(): mine.append(lax.ppermute(packed, ('row', 'layer'), route))]
    ppermute x1, waiting for transfers between devices: 0.13 us -> 1.39 us  [body(): other = lax.ppermute(stacked, 'layer', [(i, i ^ 1) for i in range(n_layer)])]
    all_to_all x0 -> x1, waiting for transfers between devices: none -> 0.97 us  [body(): trace = lax.all_to_all(trace, AXES, 0, 0, tiled=True)]
  transfers between devices with their start and end apart: 15 -> 9, of which waited for: 7 -> 5; matrix products, arithmetic and copies ran while one was open for 0% -> 0% of each run, Pallas kernels for 13% -> 20%
where the time goes in v4:
time: 43.9 us; the launch traced here: 43.6 us
  starting transfers between devices  18.7 us (43%)
  waiting for transfers between devices  12.6 us (29%)
  Pallas kernels  9.49 us (22%)
  local copies, waits for them, and re-layouts  1.54 us (4%)
  between operations  0.71 us (2%)
  other arithmetic  0.63 us (1%)
    ppermute x3, waiting for transfers between devices, shifted(): lax.ppermute(packed, 'col', [((c + k) % n_col, c) for c in range(n_col)])  8.04 us
    all_to_all x1, starting transfers between devices, body(): trace = lax.all_to_all(trace, AXES, 0, 0, tiled=True)  6.61 us
    pallas_call x2, Pallas kernels, body(): pl.pallas_call(functools.partial(product_kernel, sizes, shifts, product i...  6.16 us
    ppermute x3, starting transfers between devices, shifted(): lax.ppermute(packed, 'col', [((c + k) % n_col, c) for c in range(n_col)])  6.12 us
    ppermute x3, starting transfers between devices, body(): mine.append(lax.ppermute(packed, ('row', 'layer'), route))  5.18 us
    pallas_call x1, Pallas kernels, body(): pl.pallas_call(functools.partial(trace_kernel, sizes, rows, size, early,...  2.37 us
    ppermute x3, waiting for transfers between devices, body(): mine.append(lax.ppermute(packed, ('row', 'layer'), route))  2.18 us
    unnamed x6, local copies, waits for them, and re-layouts  1.54 us
  transfers between devices with their start and end apart: 9, of which 5 were waited for; matrix products, arithmetic and copies ran while one was open for 0% of the time, Pallas kernels for 20%

profile of v4, /device:TPU:0, one launch (start us, length us, event | category | flops | bytes accessed | tf_op | source)
XLA Modules:
  0.0 43.6 jit_solution(10358689720207629878)
XLA Ops:
  0.6 0.0 copy-start
  0.6 1.0 %copy-done = f32[2,1,3,96,96]{4,3,2,1,0:T(8,128)S(1)} copy-done((f32[2,1,3,96,96]{4,3,2,1,0:T(8,128)S(1)}, f32[2,1,3,96,96]{4,3,2,1,0:T(8,128)}, u32[]{:S(2)}) %copy-start) | copy-done | bytes 221208
  1.6 0.0 copy-start.1
  1.6 0.0 copy-start.2
  1.6 0.1 pack.1.packed_ref.refs_3_.refs_0_
  1.7 0.6 %copy-done.1 = s32[16,4,3]{0,1,2:T(4,128)S(1)} copy-done((s32[16,4,3]{0,1,2:T(4,128)S(1)}, s32[16,4,3]{0,1,2:T(4,128)}, u32[]{:S(2)}) %copy-start.1) | copy-done | bytes 792
  2.3 0.0 copy-done.2
  2.3 0.8 %cross.1 = f32[4,72,128]{2,1,0:T(8,128)S(1)} custom-call(s32[3,4,16]{2,1,0:T(4,128)S(1)} %bitcast.2, s32[3,4,16]{2,1,0:T(4,128)S(1)} %bitcast.6, f32[6,72,128]{2,1,0:T(8,128)S(1)} %pack.1.packed_ref.refs_3_.refs_0_), custom_call_target="tpu_custom_call" | custom-call | tf_op jit(solution)/shard_map/cross/pallas_call | solution.py:243
  3.1 0.7 %collective-permute-start.3 = (f32[4,72,128]{2,1,0:T(8,128)S(1)}, f32[4,72,128]{2,1,0:T(8,128)S(1)}, u32[]{:S(2)}, u32[]{:S(2)}) collective-permute-start(f32[4,72,128]{2,1,0:T(8,128)S(1)} %cross.1), channel_id=1, source_target_pairs={{16,8},{17,9},{22,14},{23,15},{9,16},{8,17},{15,22},{14,23}} | collective-permute-start | bytes 442376 | tf_op jit(solution)/shard_map/ppermute | solution.py:251
  3.8 5.1 %collective-permute-start.1 = (f32[6,72,128]{2,1,0:T(8,128)S(1)}, f32[6,72,128]{2,1,0:T(8,128)S(1)}, u32[]{:S(2)}, u32[]{:S(2)}) collective-permute-start(f32[6,72,128]{2,1,0:T(8,128)S(1)} %pack.1.packed_ref.refs_3_.refs_0_), channel_id=1, source_target_pairs={{4,0},{8,4},{12,8},{0,12},{5,1},{9,5},{13,9},{1,13},{6,2},{10,6},{... | collective-permute-start | bytes 663560 | tf_op jit(solution)/shard_map/ppermute | solution.py:231
  8.9 0.0 collective-permute-start.2
  8.9 3.5 %collective-permute-start.4 = (f32[6,72,128]{2,1,0:T(8,128)S(1)}, f32[6,72,128]{2,1,0:T(8,128)S(1)}, u32[]{:S(2)}, u32[]{:S(2)}) collective-permute-start(f32[6,72,128]{2,1,0:T(8,128)S(1)} %pack.1.packed_ref.refs_3_.refs_0_), channel_id=1, source_target_pairs={{2,0},{3,1},{0,2},{1,3},{18,16},{19,17},{16,18},{17,19},{6,4},{7,5... | collective-permute-start | bytes 663560 | tf_op jit(solution)/shard_map/ppermute | solution.py:242
  12.3 1.4 %collective-permute-start.5 = (f32[6,72,128]{2,1,0:T(8,128)S(1)}, f32[6,72,128]{2,1,0:T(8,128)S(1)}, u32[]{:S(2)}, u32[]{:S(2)}) collective-permute-start(f32[6,72,128]{2,1,0:T(8,128)S(1)} %pack.1.packed_ref.refs_3_.refs_0_), channel_id=1, source_target_pairs={{16,0},{17,1},{18,2},{19,3},{0,16},{1,17},{2,18},{3,19},{20,4},{21... | collective-permute-start | bytes 663560 | tf_op jit(solution)/shard_map/ppermute | solution.py:242
  13.7 0.0 collective-permute-done.3.refs_2_.refs_5_
  13.7 0.3 collective-permute-start.6
  14.1 1.4 %collective-permute-done.1.refs_0_.refs_1_ = f32[6,72,128]{2,1,0:T(8,128)S(1)} collective-permute-done((f32[6,72,128]{2,1,0:T(8,128)S(1)}, f32[6,72,128]{2,1,0:T(8,128)S(1)}, u32[]{:S(2)}, u32[]{:S(2)}) %collective-permute-start.1) | collective-permute-done | bytes 221216 | tf_op jit(solution)/shard_map/ppermute | solution.py:231
  15.4 6.7 %collective-permute-done.2.refs_1_.refs_2_ = f32[6,72,128]{2,1,0:T(8,128)S(1)} collective-permute-done((f32[6,72,128]{2,1,0:T(8,128)S(1)}, f32[6,72,128]{2,1,0:T(8,128)S(1)}, u32[]{:S(2)}, u32[]{:S(2)}) %collective-permute-start.2) | collective-permute-done | bytes 221216 | tf_op jit(solution)/shard_map/ppermute | solution.py:231
  22.1 0.0 collective-permute-done.4.refs_4_
  22.1 0.0 collective-permute-done.5.refs_5_
  22.1 2.2 %collective-permute-done.6.refs_6_ = f32[6,72,128]{2,1,0:T(8,128)S(1)} collective-permute-done((f32[6,72,128]{2,1,0:T(8,128)S(1)}, f32[6,72,128]{2,1,0:T(8,128)S(1)}, u32[]{:S(2)}, u32[]{:S(2)}) %collective-permute-start.6) | collective-permute-done | bytes 221216 | tf_op jit(solution)/shard_map/ppermute | solution.py:242
  24.3 0.1 stack.1.refs_3_.refs_1_
  24.3 0.1 collective-permute-start.7
  24.4 1.0 %collective-permute-start = (f32[6,72,128]{2,1,0:T(8,128)S(1)}, f32[6,72,128]{2,1,0:T(8,128)S(1)}, u32[]{:S(2)}, u32[]{:S(2)}) collective-permute-start(f32[6,72,128]{2,1,0:T(8,128)S(1)} %pack.1.packed_ref.refs_3_.refs_0_), channel_id=1, source_target_pairs={{8,0},{12,4},{0,8},{4,12},{9,1},{13,5},{1,9},{5,13},{10,2},{14,6},... | collective-permute-start | bytes 663560 | tf_op jit(solution)/shard_map/ppermute | solution.py:231
  25.4 1.4 %collective-permute-done.7.refs_4_.refs_2_ = f32[24,72,128]{2,1,0:T(8,128)S(1)} collective-permute-done((f32[24,72,128]{2,1,0:T(8,128)S(1)}, f32[24,72,128]{2,1,0:T(8,128)S(1)}, u32[]{:S(2)}, u32[]{:S(2)}) %collective-permute-start.7) | collective-permute-done | bytes 884768 | tf_op jit(solution)/shard_map/ppermute | solution.py:262
  26.8 2.4 %trace_terms.1 = f32[32,1,128]{2,1,0:T(1,128)} custom-call(s32[3,4,16]{2,1,0:T(4,128)S(1)} %bitcast.3, s32[3,4,16]{2,1,0:T(4,128)S(1)} %bitcast.7, f32[6,72,128]{2,1,0:T(8,128)S(1)} %pack.1.packed_ref.refs_3_.refs_0_, f32[6,72,128]{2,1,0:T(8,128)S(1)} %collective-permute-done.1.refs_0_.refs_1_, f32[6,72,128]{2,1,0:T(8,128)S(1)} %collective-permute-done.2.refs_1_.refs_2_, ...), custom_call_target="tpu_custom_call" | custom-call | tf_op jit(solution)/shard_map/trace_terms/pallas_call | solution.py:266
  29.2 6.6 %all-to-all-start = ((f32[32,1,128]{2,1,0:T(1,128)}), f32[32,1,128]{2,1,0:T(1,128)S(1)}, u32[]{:S(2)}, u32[]{:S(2)}) async-start(f32[32,1,128]{2,1,0:T(1,128)} %trace_terms.1), calls=%async_computation | async-start | bytes 32768 | tf_op jit(solution)/shard_map/all_to_all | solution.py:275
  35.8 3.6 %multiply.2.refs_3_ = f32[2,1,3,96,96]{4,3,2,1,0:T(8,128)S(1)} custom-call(s32[3,4,16]{2,1,0:T(4,128)S(1)} %bitcast.4, s32[3,4,16]{2,1,0:T(4,128)S(1)} %bitcast.8, f32[6,72,128]{2,1,0:T(8,128)S(1)} %pack.1.packed_ref.refs_3_.refs_0_, f32[6,72,128]{2,1,0:T(8,128)S(1)} %collective-permute-done.1.refs_0_.refs_1_, ...), custom_call_target="tpu_custom_call" | custom-call | tf_op jit(solution)/shard_map/multiply/pallas_call | solution.py:280
  39.4 0.0 collective-permute-done.refs_0_
  39.4 2.6 %multiply.3 = f32[2,1,3,96,96]{4,3,2,1,0:T(8,128)} custom-call(s32[3,4,16]{2,1,0:T(4,128)S(1)} %bitcast.5, s32[3,4,16]{2,1,0:T(4,128)S(1)} %bitcast.9, f32[6,72,128]{2,1,0:T(8,128)S(1)} %collective-permute-done.refs_0_, f32[24,72,128]{2,1,0:T(8,128)S(1)} %stack.1.refs_3_.refs_1_, f32[24,72,128]{2,1,0:T(8,128)S(1)} %collective-permute-done.7.refs_4_.refs_2_, ...), custom_call_target="tpu_custom_call" | custom-call | tf_op jit(solution)/shard_map/multiply/pallas_call | solution.py:280
  42.0 1.0 %all-to-all-done = f32[32,1,128]{2,1,0:T(1,128)S(1)} async-done(((f32[32,1,128]{2,1,0:T(1,128)}), f32[32,1,128]{2,1,0:T(1,128)S(1)}, u32[]{:S(2)}, u32[]{:S(2)}) %all-to-all-start) | async-done | bytes 16416 | tf_op jit(solution)/shard_map/all_to_all | solution.py:275
  43.0 0.6 %slice_reduce_fusion = f32[]{:T(128)} fusion(f32[32,1,128]{2,1,0:T(1,128)S(1)} %all-to-all-done), kind=kLoop, calls=%fused_computation | loop fusion | flops 31 | bytes 132 | tf_op jit(solution)/shard_map/reduce_sum | solution.py:290
Async XLA Ops:
  0.6 1.0 %copy-start = (f32[2,1,3,96,96]{4,3,2,1,0:T(8,128)S(1)}, f32[2,1,3,96,96]{4,3,2,1,0:T(8,128)}, u32[]{:S(2)}) copy-start(f32[2,1,3,96,96]{4,3,2,1,0:T(8,128)} %x_ref.1) | copy-start | bytes 663556
  1.6 0.7 %copy-start.1 = (s32[16,4,3]{0,1,2:T(4,128)S(1)}, s32[16,4,3]{0,1,2:T(4,128)}, u32[]{:S(2)}) copy-start(s32[16,4,3]{0,1,2:T(4,128)} %param.4) | copy-start | bytes 2308
  1.6 0.7 %copy-start.2 = (s32[16,4,3]{0,1,2:T(4,128)S(1)}, s32[16,4,3]{0,1,2:T(4,128)}, u32[]{:S(2)}) copy-start(s32[16,4,3]{0,1,2:T(4,128)} %param.5) | copy-start | bytes 2308
  3.1 10.6 %collective-permute-start.3 = (f32[4,72,128]{2,1,0:T(8,128)S(1)}, f32[4,72,128]{2,1,0:T(8,128)S(1)}, u32[]{:S(2)}, u32[]{:S(2)}) collective-permute-start(f32[4,72,128]{2,1,0:T(8,128)S(1)} %cross.1), channel_id=1, source_target_pairs={{16,8},{17,9},{22,14},{23,15},{9,16},{8,17},{15,22},{14,23}} | collective-permute-start | bytes 442376 | tf_op jit(solution)/shard_map/ppermute | solution.py:251
  3.8 11.7 %collective-permute-start.1 = (f32[6,72,128]{2,1,0:T(8,128)S(1)}, f32[6,72,128]{2,1,0:T(8,128)S(1)}, u32[]{:S(2)}, u32[]{:S(2)}) collective-permute-start(f32[6,72,128]{2,1,0:T(8,128)S(1)} %pack.1.packed_ref.refs_3_.refs_0_), channel_id=1, source_target_pairs={{4,0},{8,4},{12,8},{0,12},{5,1},{9,5},{13,9},{1,13},{6,2},{10,6},{... | collective-permute-start | bytes 663560 | tf_op jit(solution)/shard_map/ppermute | solution.py:231
  8.9 13.2 %collective-permute-start.2 = (f32[6,72,128]{2,1,0:T(8,128)S(1)}, f32[6,72,128]{2,1,0:T(8,128)S(1)}, u32[]{:S(2)}, u32[]{:S(2)}) collective-permute-start(f32[6,72,128]{2,1,0:T(8,128)S(1)} %pack.1.packed_ref.refs_3_.refs_0_), channel_id=1, source_target_pairs={{12,0},{0,4},{4,8},{8,12},{13,1},{1,5},{5,9},{9,13},{14,2},{2,6},{... | collective-permute-start | bytes 663560 | tf_op jit(solution)/shard_map/ppermute | solution.py:231
  8.9 13.2 %collective-permute-start.4 = (f32[6,72,128]{2,1,0:T(8,128)S(1)}, f32[6,72,128]{2,1,0:T(8,128)S(1)}, u32[]{:S(2)}, u32[]{:S(2)}) collective-permute-start(f32[6,72,128]{2,1,0:T(8,128)S(1)} %pack.1.packed_ref.refs_3_.refs_0_), channel_id=1, source_target_pairs={{2,0},{3,1},{0,2},{1,3},{18,16},{19,17},{16,18},{17,19},{6,4},{7,5... | collective-permute-start | bytes 663560 | tf_op jit(solution)/shard_map/ppermute | solution.py:242
  12.3 9.8 %collective-permute-start.5 = (f32[6,72,128]{2,1,0:T(8,128)S(1)}, f32[6,72,128]{2,1,0:T(8,128)S(1)}, u32[]{:S(2)}, u32[]{:S(2)}) collective-permute-start(f32[6,72,128]{2,1,0:T(8,128)S(1)} %pack.1.packed_ref.refs_3_.refs_0_), channel_id=1, source_target_pairs={{16,0},{17,1},{18,2},{19,3},{0,16},{1,17},{2,18},{3,19},{20,4},{21... | collective-permute-start | bytes 663560 | tf_op jit(solution)/shard_map/ppermute | solution.py:242
  13.7 10.6 %collective-permute-start.6 = (f32[6,72,128]{2,1,0:T(8,128)S(1)}, f32[6,72,128]{2,1,0:T(8,128)S(1)}, u32[]{:S(2)}, u32[]{:S(2)}) collective-permute-start(f32[6,72,128]{2,1,0:T(8,128)S(1)} %pack.1.packed_ref.refs_3_.refs_0_), channel_id=1, source_target_pairs={{18,0},{19,1},{16,2},{17,3},{2,16},{3,17},{0,18},{1,19},{22,4},{23... | collective-permute-start | bytes 663560 | tf_op jit(solution)/shard_map/ppermute | solution.py:242
  24.3 2.5 %collective-permute-start.7 = (f32[24,72,128]{2,1,0:T(8,128)S(1)}, f32[24,72,128]{2,1,0:T(8,128)S(1)}, u32[]{:S(2)}, u32[]{:S(2)}) collective-permute-start(f32[24,72,128]{2,1,0:T(8,128)S(1)} %stack.1.refs_3_.refs_1_), channel_id=1, source_target_pairs={{0,1},{1,0},{2,3},{3,2},{4,5},{5,4},{6,7},{7,6},{8,9},{9,8},{10,11... | collective-permute-start | bytes 2654216 | tf_op jit(solution)/shard_map/ppermute | solution.py:262
  24.4 15.0 %collective-permute-start = (f32[6,72,128]{2,1,0:T(8,128)S(1)}, f32[6,72,128]{2,1,0:T(8,128)S(1)}, u32[]{:S(2)}, u32[]{:S(2)}) collective-permute-start(f32[6,72,128]{2,1,0:T(8,128)S(1)} %pack.1.packed_ref.refs_3_.refs_0_), channel_id=1, source_target_pairs={{8,0},{12,4},{0,8},{4,12},{9,1},{13,5},{1,9},{5,13},{10,2},{14,6},... | collective-permute-start | bytes 663560 | tf_op jit(solution)/shard_map/ppermute | solution.py:231
  29.2 13.8 %all-to-all-start = ((f32[32,1,128]{2,1,0:T(1,128)}), f32[32,1,128]{2,1,0:T(1,128)S(1)}, u32[]{:S(2)}, u32[]{:S(2)}) async-start(f32[32,1,128]{2,1,0:T(1,128)} %trace_terms.1), calls=%async_computation | async-start | bytes 32768 | tf_op jit(solution)/shard_map/all_to_all | solution.py:275

commit v5 on v3

v5 whole, which is shorter than its diff:
```python
import functools

import jax
import jax.numpy as jnp
from jax import lax
from jax.experimental import pallas as pl
from jax.experimental.pallas import tpu as pltpu
from jax.sharding import PartitionSpec as P

LANES = 128
AXES = ("row", "col", "layer")
LIMIT = pltpu.CompilerParams(vmem_limit_bytes=48 * 2 ** 20)
VMEM = pl.BlockSpec(memory_space=pltpu.VMEM)
SMEM = pl.BlockSpec(memory_space=pltpu.SMEM)


def tall_of(size):
    return size * size // LANES


def unpack(block, size):
    tall = block.shape[0]
    spare = LANES - size
    rest = size - tall
    pieces = [block[q * rest:(q + 1) * rest, size:] for q in range(size // spare)]
    pieces.append(jnp.zeros((rest, spare), block.dtype))
    return jnp.concatenate([block, jnp.concatenate(pieces, axis=1)], axis=0)


def parts_of(value):
    parts = []
    for _ in range(3):
        part = value.astype(jnp.bfloat16)
        parts.append(part)
        value = value - part.astype(jnp.float32)
    return parts


def found(cols_ref, occ_ref, row, group, target):
    index = jnp.int32(0)
    valid = jnp.int32(0)
    for u in range(cols_ref.shape[0]):
        hit = jnp.where((cols_ref[u, group, row] == target) & (occ_ref[u, group, row] == 1), 1, 0)
        index = index + hit * u
        valid = valid + hit
    return index, valid > 0


def place(sizes):
    n_row, n_col, n_layer = sizes
    per_group = n_row * n_layer // n_col
    pair = lax.axis_index("row") * n_layer + lax.axis_index("layer")
    return pair, lax.axis_index("col"), lax.div(pair, per_group), lax.rem(pair, per_group), per_group


def pack_kernel(x_ref, out_ref):
    rows, _, slots, size, _ = x_ref.shape
    tall = tall_of(size)
    spare = LANES - size
    rest = size - tall
    for i in range(rows):
        for t in range(slots):
            n = i * slots + t
            out_ref[n, :, :size] = x_ref[i, 0, t, :tall, :]
            for q in range(size // spare):
                out_ref[n, q * rest:(q + 1) * rest, size:] = x_ref[i, 0, t, tall:, q * spare:(q + 1) * spare]


def stack_kernel(ahead, *refs):
    out_ref = refs[-1]
    for n, ref in enumerate(refs[ahead:-1]):
        out_ref[n * ref.shape[0]:(n + 1) * ref.shape[0]] = ref[...]


def strip_block(sizes, rows, slots, mine_ref, other_ref, contracted):
    _, _, n_layer = sizes
    chips = n_layer // 2
    my_row, my_layer = lax.axis_index("row"), lax.axis_index("layer")
    source = lax.div(contracted, rows)
    source_row, source_layer = lax.div(source, n_layer), lax.rem(source, n_layer)
    chip = lax.bitwise_xor(lax.div(source_layer, 2), lax.div(my_layer, 2))
    base = (lax.bitwise_xor(source_row, my_row) * chips + chip) * (rows * slots)
    base = base + lax.rem(contracted, rows) * slots
    same_core = lax.rem(source_layer, 2) == lax.rem(my_layer, 2)
    return lambda index: jnp.where(same_core, mine_ref[base + index], other_ref[base + index])


def product_kernel(sizes, masks, last, cols_ref, occ_ref, *refs):
    n_row, n_col, n_layer = sizes
    count = len(masks)
    strip_refs, (mine_ref, other_ref), refs = refs[:count], refs[count:count + 2], refs[count + 2:]
    before_ref, refs = (refs[0], refs[1:]) if last else (None, refs)
    out_ref, refs = refs[0], refs[1:]
    total_ref, refs = (refs[0], refs[1:]) if last else (None, refs)
    a_ref, w_refs = refs[0], refs[1:]
    rows, _, slots, size, _ = out_ref.shape
    pair, here, _, _, per_group = place(sizes)
    width = per_group * rows
    total = jnp.float32(0)

    for w_ref in w_refs:
        for j in range(count * slots):
            w_ref[j * LANES + size:(j + 1) * LANES, :] = jnp.zeros((LANES - size, slots * LANES), jnp.bfloat16)
    for i in range(rows):
        row = pair * rows + i
        targets = [cols_ref[s, here, row] for s in range(slots)]
        for k, mask in enumerate(masks):
            group = lax.bitwise_xor(here, mask)
            for t in range(slots):
                j = k * slots + t
                for n, part in enumerate(parts_of(unpack(strip_refs[k][i * slots + t], size))):
                    a_ref[n * size:(n + 1) * size, j * LANES:(j + 1) * LANES] = part
                stored = occ_ref[t, group, row] == 1
                contracted = group * width + cols_ref[t, group, row]
                read = strip_block(sizes, rows, slots, mine_ref, other_ref, contracted)
                for s in range(slots):
                    index, valid = found(cols_ref, occ_ref, contracted, here, targets[s])
                    valid = valid & stored & (occ_ref[s, here, row] == 1)
                    block = jnp.where(valid, unpack(read(index), size), 0.0)
                    for w_ref, part in zip(w_refs, parts_of(block)):
                        w_ref[j * LANES:j * LANES + size, s * LANES:(s + 1) * LANES] = part

        high, low, least = [
            jnp.dot(a_ref[:(3 - n) * size], w_refs[n][...], preferred_element_type=jnp.float32) for n in range(3)
        ]
        small = low[size:] + (least + high[2 * size:])
        result = high[:size] + ((low[:size] + high[size:2 * size]) + small)
        across = lax.broadcasted_iota(jnp.int32, (size, size), 0)
        down = lax.broadcasted_iota(jnp.int32, (size, size), 1)
        for s in range(slots):
            block = result[:, s * LANES:s * LANES + size]
            if last:
                block = before_ref[i, 0, s] + block
                on_diagonal = (here * width + targets[s] == row) & (occ_ref[s, here, row] == 1)
                total = total + jnp.sum(jnp.where((across == down) & on_diagonal, block, 0.0))
            out_ref[i, 0, s] = block
    if last:
        total_ref[...] = jnp.full(total_ref.shape, total, jnp.float32)


def exchanged(value, axis, mask):
    return lax.ppermute(value, axis, [(n, n ^ mask) for n in range(lax.axis_size(axis))])


def body(blocks, block_cols, occupancy):
    rows, _, slots, size, _ = blocks.shape
    sizes = tuple(lax.axis_size(axis) for axis in AXES)
    n_row, n_col, n_layer = sizes
    tall = tall_of(size)
    cols = jnp.transpose(block_cols, (2, 1, 0))
    occ = jnp.transpose(occupancy, (2, 1, 0))

    packed = pl.pallas_call(
        pack_kernel,
        out_shape=jax.ShapeDtypeStruct((rows * slots, tall, LANES), jnp.float32),
        in_specs=[VMEM],
        out_specs=VMEM,
        compiler_params=LIMIT,
        name="pack",
    )(blocks)

    strip = {0: packed}
    bit = n_col // 2
    while bit:
        for mask in list(strip):
            strip[mask | bit] = exchanged(strip[mask], "col", bit)
        bit //= 2
    early = sorted(m for m in strip if m & (m - 1) == 0)
    late = sorted(m for m in strip if m not in early)

    mine = {0: packed}
    steps = [("row", 1 << b, (1 << b) * (n_layer // 2)) for b in range((n_row - 1).bit_length())]
    steps += [("layer", 2 << b, 1 << b) for b in range((n_layer // 2 - 1).bit_length())]
    for axis, mask, offset in steps:
        for held in list(mine):
            mine[held | offset] = exchanged(mine[held], axis, mask)
    mine = [mine[n] for n in range(len(mine))]

    ahead = [strip[m] for m in early if m]
    stacked = pl.pallas_call(
        functools.partial(stack_kernel, len(ahead)),
        out_shape=jax.ShapeDtypeStruct((len(mine) * rows * slots, tall, LANES), jnp.float32),
        in_specs=[pl.BlockSpec(memory_space=pl.ANY)] * len(ahead) + [VMEM] * len(mine),
        out_specs=VMEM,
        compiler_params=LIMIT,
        name="stack",
    )(*ahead, *mine)
    other = exchanged(stacked, "layer", 1)

    whole = jax.ShapeDtypeStruct(blocks.shape, jnp.float32)
    terms = jax.ShapeDtypeStruct((n_row * n_col * n_layer, 1, LANES), jnp.float32)

    def multiplied(masks, before):
        inner = len(masks) * slots * LANES
        return pl.pallas_call(
            functools.partial(product_kernel, sizes, masks, bool(before)),
            out_shape=(whole, terms) if before else whole,
            in_specs=[SMEM, SMEM] + [VMEM] * (len(masks) + 2 + len(before)),
            out_specs=(VMEM, VMEM) if before else VMEM,
            scratch_shapes=[pltpu.VMEM((3 * size, inner), jnp.bfloat16)]
            + [pltpu.VMEM((inner, slots * LANES), jnp.bfloat16)] * 3,
            compiler_params=LIMIT,
            name="multiply",
        )(cols, occ, *[strip[m] for m in masks], stacked, other, *before)

    product, trace = multiplied(late, [multiplied(early, [])])
    trace = lax.all_to_all(trace, AXES, 0, 0, tiled=True)
    return product, jnp.sum(trace[:, 0, 0])


def solution(mesh):
    in_specs = (P(("row", "layer"), "col", None, None, None), P(), P())
    out_specs = (P(("row", "layer"), "col", None, None, None), P())
    return jax.shard_map(body, mesh=mesh, in_specs=in_specs, out_specs=out_specs, check_vma=False)
```

time: 70.2 us -> 40.7 us (0.58)
  blocking collectives: 54.7 us -> 9.54 us
  waiting for transfers between devices: 2.09 us -> 12.1 us
  starting transfers between devices: 2.52 us -> 10.8 us
  Pallas kernels: 8.37 us -> 5.82 us
    all_to_all x2 -> x1, blocking collectives: 54.7 us -> 9.54 us  [body(): trace = lax.all_to_all(trace, AXES, 0, 0, tiled=True)]
    ppermute x0 -> x7, waiting for transfers between devices: none -> 12.1 us  [exchanged(): lax.ppermute(value, axis, [(n, n ^ mask) for n in range(lax.axis_size(axi...]
    ppermute x0 -> x7, starting transfers between devices: none -> 10.8 us  [exchanged(): lax.ppermute(value, axis, [(n, n ^ mask) for n in range(lax.axis_size(axi...]
    pallas_call x3 -> x4, Pallas kernels: 8.37 us -> 5.82 us  [the longest x2 5.65 us: multiplied(): pl.pallas_call(functools.partial(product_kernel, sizes, masks, bool(befor...]
    all_to_all x1 -> x0, starting transfers between devices: 2.52 us -> none  [body(): trace = lax.all_to_all(trace, AXES, 0, 0, tiled=True)]
    all_to_all x1 -> x0, waiting for transfers between devices: 2.09 us -> none  [body(): trace = lax.all_to_all(trace, AXES, 0, 0, tiled=True)]
  transfers between devices with their start and end apart: 1 -> 7, of which waited for: 1 -> 5; matrix products, arithmetic and copies ran while one was open for 0% -> 0% of each run, Pallas kernels for 7% -> 8%
where the time goes in v5:
time: 40.7 us; the launch traced here: 40.5 us
  waiting for transfers between devices  12.1 us (30%)
  starting transfers between devices  10.8 us (27%)
  blocking collectives  9.54 us (23%)
  Pallas kernels  5.82 us (14%)
  local copies, waits for them, and re-layouts  0.96 us (2%)
  between operations  0.67 us (2%)
  other arithmetic  0.63 us (2%)
    ppermute x7, waiting for transfers between devices, exchanged(): lax.ppermute(value, axis, [(n, n ^ mask) for n in range(lax.axis_size(axi...  12.1 us
    ppermute x7, starting transfers between devices, exchanged(): lax.ppermute(value, axis, [(n, n ^ mask) for n in range(lax.axis_size(axi...  10.8 us
    all_to_all x1, blocking collectives, body(): trace = lax.all_to_all(trace, AXES, 0, 0, tiled=True)  9.54 us
    pallas_call x2, Pallas kernels, multiplied(): pl.pallas_call(functools.partial(product_kernel, sizes, masks, bool(befor...  5.65 us
    unnamed x6, local copies, waits for them, and re-layouts  0.96 us
  transfers between devices with their start and end apart: 7, of which 5 were waited for; matrix products, arithmetic and copies ran while one was open for 0% of the time, Pallas kernels for 8%

profile of v5, /device:TPU:0, one launch (start us, length us, event | category | flops | bytes accessed | tf_op | source)
XLA Modules:
  0.0 40.5 jit_solution(15957699883985433503)
XLA Ops:
  0.6 0.0 copy-start
  0.6 1.0 %copy-done = f32[2,1,3,96,96]{4,3,2,1,0:T(8,128)S(1)} copy-done((f32[2,1,3,96,96]{4,3,2,1,0:T(8,128)S(1)}, f32[2,1,3,96,96]{4,3,2,1,0:T(8,128)}, u32[]{:S(2)}) %copy-start) | copy-done | bytes 221208
  1.6 0.1 pack.1.refs_2_.refs_0_
  1.7 3.0 %collective-permute-start.4 = (f32[6,72,128]{2,1,0:T(8,128)S(1)}, f32[6,72,128]{2,1,0:T(8,128)S(1)}, u32[]{:S(2)}, u32[]{:S(2)}) collective-permute-start(f32[6,72,128]{2,1,0:T(8,128)S(1)} %pack.1.refs_2_.refs_0_), channel_id=1, source_target_pairs={{0,16},{16,0},{1,17},{17,1},{2,18},{18,2},{3,19},{19,3},{4,20},{20... | collective-permute-start | bytes 663560 | tf_op jit(solution)/shard_map/ppermute | solution.py:142
  4.7 2.6 %collective-permute-start = (f32[6,72,128]{2,1,0:T(8,128)S(1)}, f32[6,72,128]{2,1,0:T(8,128)S(1)}, u32[]{:S(2)}, u32[]{:S(2)}) collective-permute-start(f32[6,72,128]{2,1,0:T(8,128)S(1)} %pack.1.refs_2_.refs_0_), channel_id=1, source_target_pairs={{0,8},{4,12},{8,0},{12,4},{1,9},{5,13},{9,1},{13,5},{2,10},{6,14},... | collective-permute-start | bytes 663560 | tf_op jit(solution)/shard_map/ppermute | solution.py:142
  7.3 1.6 %collective-permute-start.2 = (f32[6,72,128]{2,1,0:T(8,128)S(1)}, f32[6,72,128]{2,1,0:T(8,128)S(1)}, u32[]{:S(2)}, u32[]{:S(2)}) collective-permute-start(f32[6,72,128]{2,1,0:T(8,128)S(1)} %pack.1.refs_2_.refs_0_), channel_id=1, source_target_pairs={{0,4},{4,0},{8,12},{12,8},{1,5},{5,1},{9,13},{13,9},{2,6},{6,2},{1... | collective-permute-start | bytes 663560 | tf_op jit(solution)/shard_map/ppermute | solution.py:142
  8.9 1.5 %collective-permute-start.3 = (f32[6,72,128]{2,1,0:T(8,128)S(1)}, f32[6,72,128]{2,1,0:T(8,128)S(1)}, u32[]{:S(2)}, u32[]{:S(2)}) collective-permute-start(f32[6,72,128]{2,1,0:T(8,128)S(1)} %pack.1.refs_2_.refs_0_), channel_id=1, source_target_pairs={{0,2},{1,3},{2,0},{3,1},{4,6},{5,7},{6,4},{7,5},{8,10},{9,11},{10,... | collective-permute-start | bytes 663560 | tf_op jit(solution)/shard_map/ppermute | solution.py:142
  10.4 0.0 collective-permute-done.4.refs_4_
  10.4 1.5 %collective-permute-start.5 = (f32[6,72,128]{2,1,0:T(8,128)S(1)}, f32[6,72,128]{2,1,0:T(8,128)S(1)}, u32[]{:S(2)}, u32[]{:S(2)}) collective-permute-start(f32[6,72,128]{2,1,0:T(8,128)S(1)} %collective-permute-done.4.refs_4_), channel_id=1, source_target_pairs={{0,2},{1,3},{2,0},{3,1},{4,6},{5,7},{6,4},{7,5},{8,10},{9,11},{10,... | collective-permute-start | bytes 663560 | tf_op jit(solution)/shard_map/ppermute | solution.py:142
  11.9 5.4 %collective-permute-done.refs_1_.refs_2_ = f32[6,72,128]{2,1,0:T(8,128)S(1)} collective-permute-done((f32[6,72,128]{2,1,0:T(8,128)S(1)}, f32[6,72,128]{2,1,0:T(8,128)S(1)}, u32[]{:S(2)}, u32[]{:S(2)}) %collective-permute-start) | collective-permute-done | bytes 221216 | tf_op jit(solution)/shard_map/ppermute | solution.py:142
  17.3 0.2 collective-permute-done.2.refs_0_.refs_1_
  17.5 0.0 collective-permute-done.3.refs_3_
  17.5 2.4 %collective-permute-done.5.refs_5_ = f32[6,72,128]{2,1,0:T(8,128)S(1)} collective-permute-done((f32[6,72,128]{2,1,0:T(8,128)S(1)}, f32[6,72,128]{2,1,0:T(8,128)S(1)}, u32[]{:S(2)}, u32[]{:S(2)}) %collective-permute-start.5) | collective-permute-done | bytes 221216 | tf_op jit(solution)/shard_map/ppermute | solution.py:142
  19.9 0.0 copy-start.1
  20.0 0.0 copy-start.2
  20.0 0.1 stack.1.refs_3_.refs_1_
  20.0 0.1 collective-permute-start.6
  20.1 0.5 %collective-permute-start.1 = (f32[6,72,128]{2,1,0:T(8,128)S(1)}, f32[6,72,128]{2,1,0:T(8,128)S(1)}, u32[]{:S(2)}, u32[]{:S(2)}) collective-permute-start(f32[6,72,128]{2,1,0:T(8,128)S(1)} %collective-permute-done.refs_1_.refs_2_), channel_id=1, source_target_pairs={{0,4},{4,0},{8,12},{12,8},{1,5},{5,1},{9,13},{13,9},{2,6},{6,2},{1... | collective-permute-start | bytes 663560 | tf_op jit(solution)/shard_map/ppermute | solution.py:142
  20.6 1.9 %collective-permute-done.6.refs_4_.refs_2_ = f32[24,72,128]{2,1,0:T(8,128)S(1)} collective-permute-done((f32[24,72,128]{2,1,0:T(8,128)S(1)}, f32[24,72,128]{2,1,0:T(8,128)S(1)}, u32[]{:S(2)}, u32[]{:S(2)}) %collective-permute-start.6) | collective-permute-done | bytes 884768 | tf_op jit(solution)/shard_map/ppermute | solution.py:142
  22.5 0.0 copy-done.1
  22.5 0.0 copy-done.2
  22.5 3.2 %multiply.2.refs_3_ = f32[2,1,3,96,96]{4,3,2,1,0:T(8,128)S(1)} custom-call(s32[3,4,16]{2,1,0:T(4,128)S(1)} %bitcast.2, s32[3,4,16]{2,1,0:T(4,128)S(1)} %bitcast.4, f32[6,72,128]{2,1,0:T(8,128)S(1)} %pack.1.refs_2_.refs_0_, f32[6,72,128]{2,1,0:T(8,128)S(1)} %collective-permute-done.2.refs_0_.refs_1_, f32[6,72,128]{2,1,0:T(8,128)S(1)} %collective-permute-done.refs_1_.refs_2_, ...), custom_call_target="tpu_custom_call" | custom-call | tf_op jit(solution)/shard_map/multiply/pallas_call | solution.py:195
  25.7 2.2 %collective-permute-done.1.refs_0_ = f32[6,72,128]{2,1,0:T(8,128)S(1)} collective-permute-done((f32[6,72,128]{2,1,0:T(8,128)S(1)}, f32[6,72,128]{2,1,0:T(8,128)S(1)}, u32[]{:S(2)}, u32[]{:S(2)}) %collective-permute-start.1) | collective-permute-done | bytes 221216 | tf_op jit(solution)/shard_map/ppermute | solution.py:142
  27.9 2.4 %multiply.3 = (f32[2,1,3,96,96]{4,3,2,1,0:T(8,128)}, f32[32,1,128]{2,1,0:T(1,128)S(1)}) custom-call(s32[3,4,16]{2,1,0:T(4,128)S(1)} %bitcast.3, s32[3,4,16]{2,1,0:T(4,128)S(1)} %bitcast.5, f32[6,72,128]{2,1,0:T(8,128)S(1)} %collective-permute-done.1.refs_0_, f32[24,72,128]{2,1,0:T(8,128)S(1)} %stack.1.refs_3_.refs_1_, ...), custom_call_target="tpu_custom_call" | custom-call | tf_op jit(solution)/shard_map/multiply/pallas_call | solution.py:195
  30.4 9.5 %all_to_all.5 = f32[32,1,128]{2,1,0:T(1,128)S(1)} all-to-all(f32[32,1,128]{2,1,0:T(1,128)S(1)} %get-tuple-element.5), channel_id=1, replica_groups=mesh['row'=2,'col'=4,'layer'=4] {'row','col','layer'}, dimensions={0} | all-to-all | bytes 32768 | tf_op jit(solution)/shard_map/all_to_all | solution.py:207
  39.9 0.6 %slice_reduce_fusion = f32[]{:T(128)} fusion(f32[32,1,128]{2,1,0:T(1,128)S(1)} %all_to_all.5), kind=kLoop, calls=%fused_computation | loop fusion | flops 31 | bytes 132 | tf_op jit(solution)/shard_map/reduce_sum | solution.py:208
Async XLA Ops:
  0.6 1.0 %copy-start = (f32[2,1,3,96,96]{4,3,2,1,0:T(8,128)S(1)}, f32[2,1,3,96,96]{4,3,2,1,0:T(8,128)}, u32[]{:S(2)}) copy-start(f32[2,1,3,96,96]{4,3,2,1,0:T(8,128)} %x_ref.1) | copy-start | bytes 663556
  1.7 8.7 %collective-permute-start.4 = (f32[6,72,128]{2,1,0:T(8,128)S(1)}, f32[6,72,128]{2,1,0:T(8,128)S(1)}, u32[]{:S(2)}, u32[]{:S(2)}) collective-permute-start(f32[6,72,128]{2,1,0:T(8,128)S(1)} %pack.1.refs_2_.refs_0_), channel_id=1, source_target_pairs={{0,16},{16,0},{1,17},{17,1},{2,18},{18,2},{3,19},{19,3},{4,20},{20... | collective-permute-start | bytes 663560 | tf_op jit(solution)/shard_map/ppermute | solution.py:142
  4.7 12.6 %collective-permute-start = (f32[6,72,128]{2,1,0:T(8,128)S(1)}, f32[6,72,128]{2,1,0:T(8,128)S(1)}, u32[]{:S(2)}, u32[]{:S(2)}) collective-permute-start(f32[6,72,128]{2,1,0:T(8,128)S(1)} %pack.1.refs_2_.refs_0_), channel_id=1, source_target_pairs={{0,8},{4,12},{8,0},{12,4},{1,9},{5,13},{9,1},{13,5},{2,10},{6,14},... | collective-permute-start | bytes 663560 | tf_op jit(solution)/shard_map/ppermute | solution.py:142
  7.3 10.2 %collective-permute-start.2 = (f32[6,72,128]{2,1,0:T(8,128)S(1)}, f32[6,72,128]{2,1,0:T(8,128)S(1)}, u32[]{:S(2)}, u32[]{:S(2)}) collective-permute-start(f32[6,72,128]{2,1,0:T(8,128)S(1)} %pack.1.refs_2_.refs_0_), channel_id=1, source_target_pairs={{0,4},{4,0},{8,12},{12,8},{1,5},{5,1},{9,13},{13,9},{2,6},{6,2},{1... | collective-permute-start | bytes 663560 | tf_op jit(solution)/shard_map/ppermute | solution.py:142
  8.9 8.7 %collective-permute-start.3 = (f32[6,72,128]{2,1,0:T(8,128)S(1)}, f32[6,72,128]{2,1,0:T(8,128)S(1)}, u32[]{:S(2)}, u32[]{:S(2)}) collective-permute-start(f32[6,72,128]{2,1,0:T(8,128)S(1)} %pack.1.refs_2_.refs_0_), channel_id=1, source_target_pairs={{0,2},{1,3},{2,0},{3,1},{4,6},{5,7},{6,4},{7,5},{8,10},{9,11},{10,... | collective-permute-start | bytes 663560 | tf_op jit(solution)/shard_map/ppermute | solution.py:142
  10.4 9.5 %collective-permute-start.5 = (f32[6,72,128]{2,1,0:T(8,128)S(1)}, f32[6,72,128]{2,1,0:T(8,128)S(1)}, u32[]{:S(2)}, u32[]{:S(2)}) collective-permute-start(f32[6,72,128]{2,1,0:T(8,128)S(1)} %collective-permute-done.4.refs_4_), channel_id=1, source_target_pairs={{0,2},{1,3},{2,0},{3,1},{4,6},{5,7},{6,4},{7,5},{8,10},{9,11},{10,... | collective-permute-start | bytes 663560 | tf_op jit(solution)/shard_map/ppermute | solution.py:142
  19.9 2.6 %copy-start.1 = (s32[16,4,3]{0,1,2:T(4,128)S(1)}, s32[16,4,3]{0,1,2:T(4,128)}, u32[]{:S(2)}) copy-start(s32[16,4,3]{0,1,2:T(4,128)} %param.4) | copy-start | bytes 2308
  20.0 2.6 %copy-start.2 = (s32[16,4,3]{0,1,2:T(4,128)S(1)}, s32[16,4,3]{0,1,2:T(4,128)}, u32[]{:S(2)}) copy-start(s32[16,4,3]{0,1,2:T(4,128)} %param.5) | copy-start | bytes 2308
  20.0 2.5 %collective-permute-start.6 = (f32[24,72,128]{2,1,0:T(8,128)S(1)}, f32[24,72,128]{2,1,0:T(8,128)S(1)}, u32[]{:S(2)}, u32[]{:S(2)}) collective-permute-start(f32[24,72,128]{2,1,0:T(8,128)S(1)} %stack.1.refs_3_.refs_1_), channel_id=1, source_target_pairs={{0,1},{1,0},{2,3},{3,2},{4,5},{5,4},{6,7},{7,6},{8,9},{9,8},{10,11... | collective-permute-start | bytes 2654216 | tf_op jit(solution)/shard_map/ppermute | solution.py:142
  20.1 7.8 %collective-permute-start.1 = (f32[6,72,128]{2,1,0:T(8,128)S(1)}, f32[6,72,128]{2,1,0:T(8,128)S(1)}, u32[]{:S(2)}, u32[]{:S(2)}) collective-permute-start(f32[6,72,128]{2,1,0:T(8,128)S(1)} %collective-permute-done.refs_1_.refs_2_), channel_id=1, source_target_pairs={{0,4},{4,0},{8,12},{12,8},{1,5},{5,1},{9,13},{13,9},{2,6},{6,2},{1... | collective-permute-start | bytes 663560 | tf_op jit(solution)/shard_map/ppermute | solution.py:142

commit v6 on v5

v6 whole, which is shorter than its diff:
```python
import functools

import jax
import jax.numpy as jnp
from jax import lax
from jax.experimental import pallas as pl
from jax.experimental.pallas import tpu as pltpu
from jax.sharding import PartitionSpec as P

LANES = 128
AXES = ("row", "col", "layer")
LIMIT = pltpu.CompilerParams(vmem_limit_bytes=48 * 2 ** 20)
VMEM = pl.BlockSpec(memory_space=pltpu.VMEM)
SMEM = pl.BlockSpec(memory_space=pltpu.SMEM)


def tall_of(size):
    return size * size // LANES


def unpack(block, size):
    tall = block.shape[0]
    spare = LANES - size
    rest = size - tall
    pieces = [block[q * rest:(q + 1) * rest, size:] for q in range(size // spare)]
    pieces.append(jnp.zeros((rest, spare), block.dtype))
    return jnp.concatenate([block, jnp.concatenate(pieces, axis=1)], axis=0)


def parts_of(value):
    parts = []
    for _ in range(3):
        part = value.astype(jnp.bfloat16)
        parts.append(part)
        value = value - part.astype(jnp.float32)
    return parts


def place(sizes):
    n_row, n_col, n_layer = sizes
    per_group = n_row * n_layer // n_col
    pair = lax.axis_index("row") * n_layer + lax.axis_index("layer")
    return pair, lax.axis_index("col"), lax.div(pair, per_group), lax.rem(pair, per_group), per_group


def pack_kernel(x_ref, out_ref):
    rows, _, slots, size, _ = x_ref.shape
    tall = tall_of(size)
    spare = LANES - size
    rest = size - tall
    for i in range(rows):
        for t in range(slots):
            n = i * slots + t
            out_ref[n, :, :size] = x_ref[i, 0, t, :tall, :]
            for q in range(size // spare):
                out_ref[n, q * rest:(q + 1) * rest, size:] = x_ref[i, 0, t, tall:, q * spare:(q + 1) * spare]


def stack_kernel(count, *refs):
    out_ref = refs[-1]
    for n, ref in enumerate(refs[:count]):
        out_ref[n * ref.shape[0]:(n + 1) * ref.shape[0]] = ref[...]


def strip_block(sizes, rows, slots, mine_ref, other_ref, contracted):
    _, _, n_layer = sizes
    chips = n_layer // 2
    my_row, my_layer = lax.axis_index("row"), lax.axis_index("layer")
    source = lax.div(contracted, rows)
    source_row, source_layer = lax.div(source, n_layer), lax.rem(source, n_layer)
    chip = lax.bitwise_xor(lax.div(source_layer, 2), lax.div(my_layer, 2))
    base = (lax.bitwise_xor(source_row, my_row) * chips + chip) * (rows * slots)
    base = base + lax.rem(contracted, rows) * slots
    same_core = lax.rem(source_layer, 2) == lax.rem(my_layer, 2)
    return lambda index: jnp.where(same_core, mine_ref[base + index], other_ref[base + index])


def product_kernel(sizes, groups, added, summed, code_ref, *refs):
    n_row, n_col, n_layer = sizes
    count = len(groups)
    strip_refs, (mine_ref, other_ref), refs = refs[:count], refs[count:count + 2], refs[count + 2:]
    before_ref, refs = (refs[0], refs[1:]) if added else (None, refs)
    out_ref, refs = refs[0], refs[1:]
    total_ref, refs = (refs[0], refs[1:]) if summed else (None, refs)
    a_ref, w_refs = refs[0], refs[1:]
    rows, _, slots, size, _ = out_ref.shape
    pair, here, own_group, _, per_group = place(sizes)
    width = per_group * rows
    upper = own_group >= n_col // 2
    weights = sorted(set(weight for _, _, weight in groups))
    total = jnp.float32(0)

    for w_ref in w_refs:
        for j in range(count * slots):
            w_ref[j * LANES + size:(j + 1) * LANES, :] = jnp.zeros((LANES - size, slots * LANES), jnp.bfloat16)
    for i in range(rows):
        row = pair * rows + i
        targets = [code_ref[s, here, row] for s in range(slots)]
        for k, (value, value_upper, _) in enumerate(groups):
            group = lax.bitwise_xor(here, jnp.where(upper, value_upper, value))
            for t in range(slots):
                j = k * slots + t
                for n, part in enumerate(parts_of(unpack(strip_refs[k][i * slots + t], size))):
                    a_ref[n * size:(n + 1) * size, j * LANES:(j + 1) * LANES] = part
                column = code_ref[t, group, row]
                contracted = group * width + jnp.maximum(column, 0)
                read = strip_block(sizes, rows, slots, mine_ref, other_ref, contracted)
                sources = [jnp.where(column >= 0, code_ref[u, here, contracted], -1) for u in range(slots)]
                for s in range(slots):
                    hits = [source == targets[s] for source in sources]
                    index = functools.reduce(lambda rest, u: jnp.where(hits[u], u, rest), range(1, slots), 0)
                    valid = functools.reduce(jnp.logical_or, hits) & (targets[s] >= 0)
                    block = jnp.where(valid, unpack(read(index), size), 0.0)
                    for w_ref, part in zip(w_refs, parts_of(block)):
                        w_ref[j * LANES:j * LANES + size, s * LANES:(s + 1) * LANES] = part

        across = lax.broadcasted_iota(jnp.int32, (size, size), 0)
        down = lax.broadcasted_iota(jnp.int32, (size, size), 1)
        blocks = [before_ref[i, 0, s] if added else None for s in range(slots)]
        for weight in weights:
            inner = [k for k in range(count) if groups[k][2] == weight]
            first, end = inner[0] * slots * LANES, (inner[-1] + 1) * slots * LANES
            high, low, least = [
                jnp.dot(a_ref[:(3 - n) * size, first:end], w_refs[n][first:end], preferred_element_type=jnp.float32)
                for n in range(3)
            ]
            small = low[size:] + (least + high[2 * size:])
            result = high[:size] + ((low[:size] + high[size:2 * size]) + small)
            for s in range(slots):
                block = result[:, s * LANES:s * LANES + size]
                blocks[s] = block if blocks[s] is None else blocks[s] + block
                if summed:
                    on_diagonal = (here == own_group) & (here * width + targets[s] == row)
                    total = total + jnp.sum(jnp.where((across == down) & on_diagonal, weight * block, 0.0))
        for s in range(slots):
            out_ref[i, 0, s] = blocks[s]
    if summed:
        total_ref[...] = jnp.full(total_ref.shape, total, jnp.float32)


def exchanged(value, axis, mask):
    return lax.ppermute(value, axis, [(n, n ^ mask) for n in range(lax.axis_size(axis))])


def row_strip(packed, sizes):
    n_row, n_col, n_layer = sizes
    if n_col != 4:
        strip = {0: packed}
        bit = n_col // 2
        while bit:
            for mask in list(strip):
                strip[mask | bit] = exchanged(strip[mask], "col", bit)
            bit //= 2
        return [(strip[m], m, m, 1) for m in sorted(strip)], []
    per_group = n_row * n_layer // n_col
    route = []
    for r in range(n_row):
        for c in range(n_col):
            for y in range(n_layer):
                value = 2 if (r * n_layer + y) // per_group < n_col // 2 else 3
                route.append(((r * n_col + c) * n_layer + y, (r * n_col + (c ^ value)) * n_layer + y))
    far = lax.ppermute(packed, AXES, route)
    return [(packed, 0, 0, 1), (None, 1, 1, 1), (far, 2, 3, 2)], [(exchanged(far, "col", 1), 3, 2, 0)]


def body(blocks, block_cols, occupancy):
    rows, _, slots, size, _ = blocks.shape
    sizes = tuple(lax.axis_size(axis) for axis in AXES)
    n_row, n_col, n_layer = sizes
    chips = n_layer // 2
    tall = tall_of(size)
    code = jnp.where(occupancy == 1, block_cols, -1).transpose((2, 1, 0))

    packed = pl.pallas_call(
        pack_kernel,
        out_shape=jax.ShapeDtypeStruct((rows * slots, tall, LANES), jnp.float32),
        in_specs=[VMEM],
        out_specs=VMEM,
        compiler_params=LIMIT,
        name="pack",
    )(blocks)

    early, late = row_strip(packed, sizes)
    mine = [packed]
    for n in range(1, n_row * chips):
        row_bits, chip_bits = n // chips, n % chips
        route = [
            (a * n_layer + b, (a ^ row_bits) * n_layer + (b ^ (2 * chip_bits))) for a in range(n_row) for b in range(n_layer)
        ]
        mine.append(lax.ppermute(packed, ("row", "layer"), route))
    early = [(exchanged(packed, "col", 1) if share is None else share, *rest) for share, *rest in early]

    ahead = [share for share, value, _, _ in reversed(early) if value]
    stacked = pl.pallas_call(
        functools.partial(stack_kernel, len(mine)),
        out_shape=jax.ShapeDtypeStruct((len(mine) * rows * slots, tall, LANES), jnp.float32),
        in_specs=[VMEM] * len(mine) + [pl.BlockSpec(memory_space=pl.ANY)] * len(ahead),
        out_specs=VMEM,
        compiler_params=LIMIT,
        name="stack",
    )(*mine, *ahead)
    other = exchanged(stacked, "layer", 1)

    whole = jax.ShapeDtypeStruct(blocks.shape, jnp.float32)
    terms = jax.ShapeDtypeStruct((n_row * n_col * n_layer, 1, LANES), jnp.float32)

    def multiplied(some, before):
        inner = len(some) * slots * LANES
        summed = not before
        return pl.pallas_call(
            functools.partial(product_kernel, sizes, [tuple(rest) for _, *rest in some], bool(before), summed),
            out_shape=(whole, terms) if summed else whole,
            in_specs=[SMEM] + [VMEM] * (len(some) + 2 + len(before)),
            out_specs=(VMEM, VMEM) if summed else VMEM,
            scratch_shapes=[pltpu.VMEM((3 * size, inner), jnp.bfloat16)]
            + [pltpu.VMEM((inner, slots * LANES), jnp.bfloat16)] * 3,
            compiler_params=LIMIT,
            name="multiply",
        )(code, *[share for share, *_ in some], stacked, other, *before)

    product, trace = multiplied(early, [])
    trace = lax.all_to_all(trace, AXES, 0, 0, tiled=True)
    if late:
        product = multiplied(late, [product])
    return product, jnp.sum(trace[:, 0, 0])


def solution(mesh):
    in_specs = (P(("row", "layer"), "col", None, None, None), P(), P())
    out_specs = (P(("row", "layer"), "col", None, None, None), P())
    return jax.shard_map(body, mesh=mesh, in_specs=in_specs, out_specs=out_specs, check_vma=False)
```

time: 40.7 us -> 38.2 us (0.939)
  blocking collectives: 9.54 us -> 0 us
  starting transfers between devices: 10.8 us -> 14.2 us
  waiting for transfers between devices: 12.1 us -> 15 us
  Pallas kernels: 5.82 us -> 6.53 us
    ppermute x7 -> x3, waiting for transfers between devices: 12.1 us -> 1.32 us  [exchanged(): lax.ppermute(value, axis, [(n, n ^ mask) for n in range(lax.axis_size(axi...]
    all_to_all x1 -> x0, blocking collectives: 9.54 us -> none  [body(): trace = lax.all_to_all(trace, AXES, 0, 0, tiled=True)]
    ppermute x0 -> x4, waiting for transfers between devices: none -> 8.85 us  [the longest x1 5.21 us: row_strip(): far = lax.ppermute(packed, AXES, route)]
    ppermute x7 -> x3, starting transfers between devices: 10.8 us -> 2.92 us  [exchanged(): lax.ppermute(value, axis, [(n, n ^ mask) for n in range(lax.axis_size(axi...]
    ppermute x0 -> x4, starting transfers between devices: none -> 7.59 us  [the longest x1 4.1 us: row_strip(): far = lax.ppermute(packed, AXES, route)]
    all_to_all x0 -> x1, waiting for transfers between devices: none -> 4.81 us  [body(): trace = lax.all_to_all(trace, AXES, 0, 0, tiled=True)]
    all_to_all x0 -> x1, starting transfers between devices: none -> 3.71 us  [body(): trace = lax.all_to_all(trace, AXES, 0, 0, tiled=True)]
    pallas_call x3, Pallas kernels: 5.71 us -> 6.42 us  [the longest x2 6.36 us: multiplied(): pl.pallas_call(functools.partial(product_kernel, sizes, [tuple(rest) for...]
  transfers between devices with their start and end apart: 7 -> 8, of which waited for: 5 -> 6; matrix products, arithmetic and copies ran while one was open for 0% -> 0% of each run, Pallas kernels for 8% -> 17%
where the time goes in v6:
time: 38.2 us; the launch traced here: 38 us
  waiting for transfers between devices  15 us (39%)
  starting transfers between devices  14.2 us (37%)
  Pallas kernels  6.53 us (17%)
  local copies, waits for them, and re-layouts  0.97 us (3%)
  between operations  0.7 us (2%)
  other arithmetic  0.64 us (2%)
    pallas_call x2, Pallas kernels, multiplied(): pl.pallas_call(functools.partial(product_kernel, sizes, [tuple(rest) for...  6.36 us
    ppermute x1, waiting for transfers between devices, row_strip(): far = lax.ppermute(packed, AXES, route)  5.21 us
    all_to_all x1, waiting for transfers between devices, body(): trace = lax.all_to_all(trace, AXES, 0, 0, tiled=True)  4.81 us
    ppermute x1, starting transfers between devices, row_strip(): far = lax.ppermute(packed, AXES, route)  4.1 us
    all_to_all x1, starting transfers between devices, body(): trace = lax.all_to_all(trace, AXES, 0, 0, tiled=True)  3.71 us
    ppermute x3, waiting for transfers between devices, body(): mine.append(lax.ppermute(packed, ('row', 'layer'), route))  3.64 us
    ppermute x3, starting transfers between devices, body(): mine.append(lax.ppermute(packed, ('row', 'layer'), route))  3.49 us
    ppermute x3, starting transfers between devices, exchanged(): lax.ppermute(value, axis, [(n, n ^ mask) for n in range(lax.axis_size(axi...  2.92 us
  transfers between devices with their start and end apart: 8, of which 6 were waited for; matrix products, arithmetic and copies ran while one was open for 0% of the time, Pallas kernels for 17%

profile of v6, /device:TPU:0, one launch (start us, length us, event | category | flops | bytes accessed | tf_op | source)
XLA Modules:
  0.0 38.0 jit_solution(12933992366868673018)
XLA Ops:
  0.6 0.0 copy-start
  0.6 1.0 %copy-done = f32[2,1,3,96,96]{4,3,2,1,0:T(8,128)S(1)} copy-done((f32[2,1,3,96,96]{4,3,2,1,0:T(8,128)S(1)}, f32[2,1,3,96,96]{4,3,2,1,0:T(8,128)}, u32[]{:S(2)}) %copy-start) | copy-done | bytes 221208
  1.6 0.1 pack.1.refs_0_
  1.7 0.0 copy-start.1
  1.7 0.0 copy-start.2
  1.7 4.1 %collective-permute-start = (f32[6,72,128]{2,1,0:T(8,128)S(1)}, f32[6,72,128]{2,1,0:T(8,128)S(1)}, u32[]{:S(2)}, u32[]{:S(2)}) collective-permute-start(f32[6,72,128]{2,1,0:T(8,128)S(1)} %pack.1.refs_0_), channel_id=1, source_target_pairs={{0,8},{1,9},{2,10},{3,11},{4,12},{5,13},{6,14},{7,15},{8,0},{9,1},... | collective-permute-start | bytes 663560 | tf_op jit(solution)/shard_map/ppermute | solution.py:162
  5.8 1.6 %collective-permute-start.5 = (f32[6,72,128]{2,1,0:T(8,128)S(1)}, f32[6,72,128]{2,1,0:T(8,128)S(1)}, u32[]{:S(2)}, u32[]{:S(2)}) collective-permute-start(f32[6,72,128]{2,1,0:T(8,128)S(1)} %pack.1.refs_0_), channel_id=1, source_target_pairs={{0,4},{4,0},{8,12},{12,8},{1,5},{5,1},{9,13},{13,9},{2,6},{6,2},{1... | collective-permute-start | bytes 663560 | tf_op jit(solution)/shard_map/ppermute | solution.py:142
  7.4 1.5 %collective-permute-start.2 = (f32[6,72,128]{2,1,0:T(8,128)S(1)}, f32[6,72,128]{2,1,0:T(8,128)S(1)}, u32[]{:S(2)}, u32[]{:S(2)}) collective-permute-start(f32[6,72,128]{2,1,0:T(8,128)S(1)} %pack.1.refs_0_), channel_id=1, source_target_pairs={{0,2},{1,3},{2,0},{3,1},{16,18},{17,19},{18,16},{19,17},{4,6},{5,7... | collective-permute-start | bytes 663560 | tf_op jit(solution)/shard_map/ppermute | solution.py:190
  8.9 0.9 %collective-permute-start.3 = (f32[6,72,128]{2,1,0:T(8,128)S(1)}, f32[6,72,128]{2,1,0:T(8,128)S(1)}, u32[]{:S(2)}, u32[]{:S(2)}) collective-permute-start(f32[6,72,128]{2,1,0:T(8,128)S(1)} %pack.1.refs_0_), channel_id=1, source_target_pairs={{0,16},{1,17},{2,18},{3,19},{16,0},{17,1},{18,2},{19,3},{4,20},{5,... | collective-permute-start | bytes 663560 | tf_op jit(solution)/shard_map/ppermute | solution.py:190
  9.9 1.0 %collective-permute-start.4 = (f32[6,72,128]{2,1,0:T(8,128)S(1)}, f32[6,72,128]{2,1,0:T(8,128)S(1)}, u32[]{:S(2)}, u32[]{:S(2)}) collective-permute-start(f32[6,72,128]{2,1,0:T(8,128)S(1)} %pack.1.refs_0_), channel_id=1, source_target_pairs={{0,18},{1,19},{2,16},{3,17},{16,2},{17,3},{18,0},{19,1},{4,22},{5,... | collective-permute-start | bytes 663560 | tf_op jit(solution)/shard_map/ppermute | solution.py:190
  10.9 5.2 %collective-permute-done.refs_4_.refs_2_ = f32[6,72,128]{2,1,0:T(8,128)S(1)} collective-permute-done((f32[6,72,128]{2,1,0:T(8,128)S(1)}, f32[6,72,128]{2,1,0:T(8,128)S(1)}, u32[]{:S(2)}, u32[]{:S(2)}) %collective-permute-start) | collective-permute-done | bytes 221216 | tf_op jit(solution)/shard_map/ppermute | solution.py:162
  16.1 0.2 collective-permute-done.5.refs_5_.refs_1_
  16.3 0.0 collective-permute-done.2.refs_1_
  16.3 1.0 %collective-permute-done.3.refs_2_ = f32[6,72,128]{2,1,0:T(8,128)S(1)} collective-permute-done((f32[6,72,128]{2,1,0:T(8,128)S(1)}, f32[6,72,128]{2,1,0:T(8,128)S(1)}, u32[]{:S(2)}, u32[]{:S(2)}) %collective-permute-start.3) | collective-permute-done | bytes 221216 | tf_op jit(solution)/shard_map/ppermute | solution.py:190
  17.3 2.6 %collective-permute-done.4.refs_3_ = f32[6,72,128]{2,1,0:T(8,128)S(1)} collective-permute-done((f32[6,72,128]{2,1,0:T(8,128)S(1)}, f32[6,72,128]{2,1,0:T(8,128)S(1)}, u32[]{:S(2)}, u32[]{:S(2)}) %collective-permute-start.4) | collective-permute-done | bytes 221216 | tf_op jit(solution)/shard_map/ppermute | solution.py:190
  19.9 0.1 stack.1.refs_3_.refs_1_
  20.0 0.1 collective-permute-start.6
  20.1 1.3 %collective-permute-start.1 = (f32[6,72,128]{2,1,0:T(8,128)S(1)}, f32[6,72,128]{2,1,0:T(8,128)S(1)}, u32[]{:S(2)}, u32[]{:S(2)}) collective-permute-start(f32[6,72,128]{2,1,0:T(8,128)S(1)} %collective-permute-done.refs_4_.refs_2_), channel_id=1, source_target_pairs={{0,4},{4,0},{8,12},{12,8},{1,5},{5,1},{9,13},{13,9},{2,6},{6,2},{1... | collective-permute-start | bytes 663560 | tf_op jit(solution)/shard_map/ppermute | solution.py:142
  21.4 0.0 copy-done.1
  21.4 0.0 copy-done.2
  21.4 1.1 %collective-permute-done.6.refs_4_.refs_2_ = f32[24,72,128]{2,1,0:T(8,128)S(1)} collective-permute-done((f32[24,72,128]{2,1,0:T(8,128)S(1)}, f32[24,72,128]{2,1,0:T(8,128)S(1)}, u32[]{:S(2)}, u32[]{:S(2)}) %collective-permute-start.6) | collective-permute-done | bytes 884768 | tf_op jit(solution)/shard_map/ppermute | solution.py:142
  22.5 4.0 %multiply.2 = (f32[2,1,3,96,96]{4,3,2,1,0:T(8,128)S(1)}, f32[32,1,128]{2,1,0:T(1,128)}) custom-call(s32[3,4,16]{2,1,0:T(4,128)S(1)} %select_bitcast_fusion.code_ref, f32[6,72,128]{2,1,0:T(8,128)S(1)} %pack.1.refs_0_, f32[6,72,128]{2,1,0:T(8,128)S(1)} %collective-permute-done.5.refs_5_.refs_1_, f32[6,72,128]{2,1,0:T(8,128)S(1)} %collective-permute-done.refs_4_.refs_2_, ...), custom_call_target="tpu_custom_call" | custom-call | tf_op jit(solution)/shard_map/multiply/pallas_call | solution.py:210
  26.5 3.7 %all-to-all-start = ((f32[32,1,128]{2,1,0:T(1,128)}), f32[32,1,128]{2,1,0:T(1,128)S(1)}, u32[]{:S(2)}, u32[]{:S(2)}) async-start(f32[32,1,128]{2,1,0:T(1,128)} %get-tuple-element.5), calls=%async_computation | async-start | bytes 32768 | tf_op jit(solution)/shard_map/all_to_all | solution.py:222
  30.3 0.0 collective-permute-done.1.refs_0_
  30.3 2.3 %multiply.3 = f32[2,1,3,96,96]{4,3,2,1,0:T(8,128)} custom-call(s32[3,4,16]{2,1,0:T(4,128)S(1)} %select_bitcast_fusion.code_ref, f32[6,72,128]{2,1,0:T(8,128)S(1)} %collective-permute-done.1.refs_0_, f32[24,72,128]{2,1,0:T(8,128)S(1)} %stack.1.refs_3_.refs_1_, f32[24,72,128]{2,1,0:T(8,128)S(1)} %collective-permute-done.6.refs_4_.refs_2_, ...), custom_call_target="tpu_custom_call" | custom-call | tf_op jit(solution)/shard_map/multiply/pallas_call | solution.py:210
  32.6 4.8 %all-to-all-done = f32[32,1,128]{2,1,0:T(1,128)S(1)} async-done(((f32[32,1,128]{2,1,0:T(1,128)}), f32[32,1,128]{2,1,0:T(1,128)S(1)}, u32[]{:S(2)}, u32[]{:S(2)}) %all-to-all-start) | async-done | bytes 16416 | tf_op jit(solution)/shard_map/all_to_all | solution.py:222
  37.4 0.6 %slice_reduce_fusion = f32[]{:T(128)} fusion(f32[32,1,128]{2,1,0:T(1,128)S(1)} %all-to-all-done), kind=kLoop, calls=%fused_computation | loop fusion | flops 31 | bytes 132 | tf_op jit(solution)/shard_map/reduce_sum | solution.py:225
  (1 shorter events, 0.0 us)
Async XLA Ops:
  0.6 1.0 %copy-start = (f32[2,1,3,96,96]{4,3,2,1,0:T(8,128)S(1)}, f32[2,1,3,96,96]{4,3,2,1,0:T(8,128)}, u32[]{:S(2)}) copy-start(f32[2,1,3,96,96]{4,3,2,1,0:T(8,128)} %x_ref.1) | copy-start | bytes 663556
  1.7 19.7 %copy-start.1 = (s32[16,4,3]{0,1,2:T(4,128)S(1)}, s32[16,4,3]{0,1,2:T(4,128)}, u32[]{:S(2)}) copy-start(s32[16,4,3]{0,1,2:T(4,128)} %param.4) | copy-start | bytes 2308
  1.7 19.6 %copy-start.2 = (s32[16,4,3]{0,1,2:T(4,128)S(1)}, s32[16,4,3]{0,1,2:T(4,128)}, u32[]{:S(2)}) copy-start(s32[16,4,3]{0,1,2:T(4,128)} %param.5) | copy-start | bytes 2308
  1.7 14.4 %collective-permute-start = (f32[6,72,128]{2,1,0:T(8,128)S(1)}, f32[6,72,128]{2,1,0:T(8,128)S(1)}, u32[]{:S(2)}, u32[]{:S(2)}) collective-permute-start(f32[6,72,128]{2,1,0:T(8,128)S(1)} %pack.1.refs_0_), channel_id=1, source_target_pairs={{0,8},{1,9},{2,10},{3,11},{4,12},{5,13},{6,14},{7,15},{8,0},{9,1},... | collective-permute-start | bytes 663560 | tf_op jit(solution)/shard_map/ppermute | solution.py:162
  5.8 10.5 %collective-permute-start.5 = (f32[6,72,128]{2,1,0:T(8,128)S(1)}, f32[6,72,128]{2,1,0:T(8,128)S(1)}, u32[]{:S(2)}, u32[]{:S(2)}) collective-permute-start(f32[6,72,128]{2,1,0:T(8,128)S(1)} %pack.1.refs_0_), channel_id=1, source_target_pairs={{0,4},{4,0},{8,12},{12,8},{1,5},{5,1},{9,13},{13,9},{2,6},{6,2},{1... | collective-permute-start | bytes 663560 | tf_op jit(solution)/shard_map/ppermute | solution.py:142
  7.4 8.9 %collective-permute-start.2 = (f32[6,72,128]{2,1,0:T(8,128)S(1)}, f32[6,72,128]{2,1,0:T(8,128)S(1)}, u32[]{:S(2)}, u32[]{:S(2)}) collective-permute-start(f32[6,72,128]{2,1,0:T(8,128)S(1)} %pack.1.refs_0_), channel_id=1, source_target_pairs={{0,2},{1,3},{2,0},{3,1},{16,18},{17,19},{18,16},{19,17},{4,6},{5,7... | collective-permute-start | bytes 663560 | tf_op jit(solution)/shard_map/ppermute | solution.py:190
  8.9 8.4 %collective-permute-start.3 = (f32[6,72,128]{2,1,0:T(8,128)S(1)}, f32[6,72,128]{2,1,0:T(8,128)S(1)}, u32[]{:S(2)}, u32[]{:S(2)}) collective-permute-start(f32[6,72,128]{2,1,0:T(8,128)S(1)} %pack.1.refs_0_), channel_id=1, source_target_pairs={{0,16},{1,17},{2,18},{3,19},{16,0},{17,1},{18,2},{19,3},{4,20},{5,... | collective-permute-start | bytes 663560 | tf_op jit(solution)/shard_map/ppermute | solution.py:190
  9.9 10.1 %collective-permute-start.4 = (f32[6,72,128]{2,1,0:T(8,128)S(1)}, f32[6,72,128]{2,1,0:T(8,128)S(1)}, u32[]{:S(2)}, u32[]{:S(2)}) collective-permute-start(f32[6,72,128]{2,1,0:T(8,128)S(1)} %pack.1.refs_0_), channel_id=1, source_target_pairs={{0,18},{1,19},{2,16},{3,17},{16,2},{17,3},{18,0},{19,1},{4,22},{5,... | collective-permute-start | bytes 663560 | tf_op jit(solution)/shard_map/ppermute | solution.py:190
  20.0 2.5 %collective-permute-start.6 = (f32[24,72,128]{2,1,0:T(8,128)S(1)}, f32[24,72,128]{2,1,0:T(8,128)S(1)}, u32[]{:S(2)}, u32[]{:S(2)}) collective-permute-start(f32[24,72,128]{2,1,0:T(8,128)S(1)} %stack.1.refs_3_.refs_1_), channel_id=1, source_target_pairs={{0,1},{1,0},{2,3},{3,2},{4,5},{5,4},{6,7},{7,6},{8,9},{9,8},{10,11... | collective-permute-start | bytes 2654216 | tf_op jit(solution)/shard_map/ppermute | solution.py:142
  20.1 10.2 %collective-permute-start.1 = (f32[6,72,128]{2,1,0:T(8,128)S(1)}, f32[6,72,128]{2,1,0:T(8,128)S(1)}, u32[]{:S(2)}, u32[]{:S(2)}) collective-permute-start(f32[6,72,128]{2,1,0:T(8,128)S(1)} %collective-permute-done.refs_4_.refs_2_), channel_id=1, source_target_pairs={{0,4},{4,0},{8,12},{12,8},{1,5},{5,1},{9,13},{13,9},{2,6},{6,2},{1... | collective-permute-start | bytes 663560 | tf_op jit(solution)/shard_map/ppermute | solution.py:142
  26.5 10.9 %all-to-all-start = ((f32[32,1,128]{2,1,0:T(1,128)}), f32[32,1,128]{2,1,0:T(1,128)S(1)}, u32[]{:S(2)}, u32[]{:S(2)}) async-start(f32[32,1,128]{2,1,0:T(1,128)} %get-tuple-element.5), calls=%async_computation | async-start | bytes 32768 | tf_op jit(solution)/shard_map/all_to_all | solution.py:222

commit v7 on v6

--- a/solution.py
+++ b/solution.py
@@ -75,20 +75,57 @@
     return lambda index: jnp.where(same_core, mine_ref[base + index], other_ref[base + index])
 
 
-def product_kernel(sizes, groups, added, summed, code_ref, *refs):
-    n_row, n_col, n_layer = sizes
+def group_at(sizes, here, own_group, values):
+    return lax.bitwise_xor(here, jnp.where(own_group >= sizes[1] // 2, values[1], values[0]))
+
+
+def matched(code_ref, here, contracted, stored, target):
+    index, valid = jnp.int32(0), jnp.bool_(False)
+    for u in range(code_ref.shape[0]):
+        hit = code_ref[u, here, contracted] == target
+        index = jnp.where(hit, u, index)
+        valid = valid | hit
+    return index, valid & stored & (target >= 0)
+
+
+def trace_kernel(sizes, rows, size, groups, code_ref, *refs):
     count = len(groups)
-    strip_refs, (mine_ref, other_ref), refs = refs[:count], refs[count:count + 2], refs[count + 2:]
-    before_ref, refs = (refs[0], refs[1:]) if added else (None, refs)
-    out_ref, refs = refs[0], refs[1:]
-    total_ref, refs = (refs[0], refs[1:]) if summed else (None, refs)
-    a_ref, w_refs = refs[0], refs[1:]
+    strip_refs, (mine_ref, other_ref), total_ref = refs[:count], refs[count:count + 2], refs[-1]
+    slots = code_ref.shape[0]
+    pair, here, own_group, number, per_group = place(sizes)
+    width = per_group * rows
+
+    def straight(block):
+        return unpack(block, size)[:, :size]
+
+    @pl.when(own_group == here)
+    def _():
+        total = jnp.zeros((size, size), jnp.float32)
+        for i in range(rows):
+            row = pair * rows + i
+            for strip_ref, (value, value_upper, weight) in zip(strip_refs, groups):
+                group = group_at(sizes, here, own_group, (value, value_upper))
+                for t in range(slots):
+                    column = code_ref[t, group, row]
+                    contracted = group * width + jnp.maximum(column, 0)
+                    index, valid = matched(code_ref, here, contracted, column >= 0, number * rows + i)
+                    block = strip_block(sizes, rows, slots, mine_ref, other_ref, contracted)(index)
+                    term = straight(strip_ref[i * slots + t]) * straight(block).T
+                    total = total + jnp.where(valid, weight * term, 0.0)
+        total_ref[...] = jnp.full(total_ref.shape, jnp.sum(total), jnp.float32)
+
+    @pl.when(own_group != here)
+    def _():
+        total_ref[...] = jnp.zeros(total_ref.shape, jnp.float32)
+
+
+def product_kernel(sizes, groups, code_ref, *refs):
+    count = len(groups)
+    strip_refs, (mine_ref, other_ref), out_ref = refs[:count], refs[count:count + 2], refs[count + 2]
+    a_ref, w_refs = refs[count + 3], refs[count + 4:]
     rows, _, slots, size, _ = out_ref.shape
     pair, here, own_group, _, per_group = place(sizes)
     width = per_group * rows
-    upper = own_group >= n_col // 2
-    weights = sorted(set(weight for _, _, weight in groups))
-    total = jnp.float32(0)
 
     for w_ref in w_refs:
         for j in range(count * slots):
@@ -97,7 +134,7 @@
         row = pair * rows + i
         targets = [code_ref[s, here, row] for s in range(slots)]
         for k, (value, value_upper, _) in enumerate(groups):
-            group = lax.bitwise_xor(here, jnp.where(upper, value_upper, value))
+            group = group_at(sizes, here, own_group, (value, value_upper))
             for t in range(slots):
                 j = k * slots + t
                 for n, part in enumerate(parts_of(unpack(strip_refs[k][i * slots + t], size))):
@@ -105,37 +142,19 @@
                 column = code_ref[t, group, row]
                 contracted = group * width + jnp.maximum(column, 0)
                 read = strip_block(sizes, rows, slots, mine_ref, other_ref, contracted)
-                sources = [jnp.where(column >= 0, code_ref[u, here, contracted], -1) for u in range(slots)]
                 for s in range(slots):
-                    hits = [source == targets[s] for source in sources]
-                    index = functools.reduce(lambda rest, u: jnp.where(hits[u], u, rest), range(1, slots), 0)
-                    valid = functools.reduce(jnp.logical_or, hits) & (targets[s] >= 0)
+                    index, valid = matched(code_ref, here, contracted, column >= 0, targets[s])
                     block = jnp.where(valid, unpack(read(index), size), 0.0)
                     for w_ref, part in zip(w_refs, parts_of(block)):
                         w_ref[j * LANES:j * LANES + size, s * LANES:(s + 1) * LANES] = part
 
-        across = lax.broadcasted_iota(jnp.int32, (size, size), 0)
-        down = lax.broadcasted_iota(jnp.int32, (size, size), 1)
-        blocks = [before_ref[i, 0, s] if added else None for s in range(slots)]
-        for weight in weights:
-            inner = [k for k in range(count) if groups[k][2] == weight]
-            first, end = inner[0] * slots * LANES, (inner[-1] + 1) * slots * LANES
-            high, low, least = [
-                jnp.dot(a_ref[:(3 - n) * size, first:end], w_refs[n][first:end], preferred_element_type=jnp.float32)
-                for n in range(3)
-            ]
-            small = low[size:] + (least + high[2 * size:])
-            result = high[:size] + ((low[:size] + high[size:2 * size]) + small)
-            for s in range(slots):
-                block = result[:, s * LANES:s * LANES + size]
-                blocks[s] = block if blocks[s] is None else blocks[s] + block
-                if summed:
-                    on_diagonal = (here == own_group) & (here * width + targets[s] == row)
-                    total = total + jnp.sum(jnp.where((across == down) & on_diagonal, weight * block, 0.0))
+        high, low, least = [
+            jnp.dot(a_ref[:(3 - n) * size], w_refs[n][...], preferred_element_type=jnp.float32) for n in range(3)
+        ]
+        small = low[size:] + (least + high[2 * size:])
+        result = high[:size] + ((low[:size] + high[size:2 * size]) + small)
         for s in range(slots):
-            out_ref[i, 0, s] = blocks[s]
-    if summed:
-        total_ref[...] = jnp.full(total_ref.shape, total, jnp.float32)
+            out_ref[i, 0, s] = result[:, s * LANES:s * LANES + size]
 
 
 def exchanged(value, axis, mask):
@@ -201,27 +220,28 @@
     )(*mine, *ahead)
     other = exchanged(stacked, "layer", 1)
 
-    whole = jax.ShapeDtypeStruct(blocks.shape, jnp.float32)
-    terms = jax.ShapeDtypeStruct((n_row * n_col * n_layer, 1, LANES), jnp.float32)
-
-    def multiplied(some, before):
-        inner = len(some) * slots * LANES
-        summed = not before
-        return pl.pallas_call(
-            functools.partial(product_kernel, sizes, [tuple(rest) for _, *rest in some], bool(before), summed),
-            out_shape=(whole, terms) if summed else whole,
-            in_specs=[SMEM] + [VMEM] * (len(some) + 2 + len(before)),
-            out_specs=(VMEM, VMEM) if summed else VMEM,
-            scratch_shapes=[pltpu.VMEM((3 * size, inner), jnp.bfloat16)]
-            + [pltpu.VMEM((inner, slots * LANES), jnp.bfloat16)] * 3,
-            compiler_params=LIMIT,
-            name="multiply",
-        )(code, *[share for share, *_ in some], stacked, other, *before)
-
-    product, trace = multiplied(early, [])
+    trace = pl.pallas_call(
+        functools.partial(trace_kernel, sizes, rows, size, [tuple(rest) for _, *rest in early]),
+        out_shape=jax.ShapeDtypeStruct((n_row * n_col * n_layer, 1, LANES), jnp.float32),
+        in_specs=[SMEM] + [VMEM] * (len(early) + 2),
+        out_specs=VMEM,
+        compiler_params=LIMIT,
+        name="trace_terms",
+    )(code, *[share for share, *_ in early], stacked, other)
     trace = lax.all_to_all(trace, AXES, 0, 0, tiled=True)
-    if late:
-        product = multiplied(late, [product])
+
+    strip = early + late
+    inner = len(strip) * slots * LANES
+    product = pl.pallas_call(
+        functools.partial(product_kernel, sizes, [tuple(rest) for _, *rest in strip]),
+        out_shape=jax.ShapeDtypeStruct(blocks.shape, jnp.float32),
+        in_specs=[SMEM] + [VMEM] * (len(strip) + 2),
+        out_specs=VMEM,
+        scratch_shapes=[pltpu.VMEM((3 * size, inner), jnp.bfloat16)]
+        + [pltpu.VMEM((inner, slots * LANES), jnp.bfloat16)] * 3,
+        compiler_params=LIMIT,
+        name="multiply",
+    )(code, *[share for share, *_ in strip], stacked, other)
     return product, jnp.sum(trace[:, 0, 0])
 
 

time: 38.2 us -> 36.1 us (0.945)
  waiting for transfers between devices: 15 us -> 13.6 us
  starting transfers between devices: 14.2 us -> 13.2 us
    ppermute x3, waiting for transfers between devices: 1.32 us -> 5.86 us  [exchanged(): lax.ppermute(value, axis, [(n, n ^ mask) for n in range(lax.axis_size(axi...]
    ppermute x1, waiting for transfers between devices: 5.21 us -> 2.52 us  [row_strip(): far = lax.ppermute(packed, AXES, route)]
    all_to_all x1, waiting for transfers between devices: 4.81 us -> 2.63 us  [body(): trace = lax.all_to_all(trace, AXES, 0, 0, tiled=True)]
    ppermute x1, starting transfers between devices: 4.1 us -> 2.59 us  [row_strip(): far = lax.ppermute(packed, AXES, route)]
    ppermute x3, waiting for transfers between devices: 3.64 us -> 2.54 us  [body(): mine.append(lax.ppermute(packed, ('row', 'layer'), route))]
    ppermute x3, starting transfers between devices: 2.92 us -> 3.67 us  [exchanged(): lax.ppermute(value, axis, [(n, n ^ mask) for n in range(lax.axis_size(axi...]
  transfers between devices with their start and end apart: 8 -> 8, of which waited for: 6 -> 5; matrix products, arithmetic and copies ran while one was open for 0% -> 0% of each run, Pallas kernels for 17% -> 18%
where the time goes in v7:
time: 36.1 us; the launch traced here: 35.9 us
  waiting for transfers between devices  13.6 us (38%)
  starting transfers between devices  13.2 us (37%)
  Pallas kernels  6.81 us (19%)
  local copies, waits for them, and re-layouts  0.97 us (3%)
  between operations  0.7 us (2%)
  other arithmetic  0.64 us (2%)
    ppermute x3, waiting for transfers between devices, exchanged(): lax.ppermute(value, axis, [(n, n ^ mask) for n in range(lax.axis_size(axi...  5.86 us
    pallas_call x1, Pallas kernels, body(): pl.pallas_call(functools.partial(product_kernel, sizes, [tuple(rest) for...  4.5 us
    ppermute x3, starting transfers between devices, exchanged(): lax.ppermute(value, axis, [(n, n ^ mask) for n in range(lax.axis_size(axi...  3.67 us
    ppermute x3, starting transfers between devices, body(): mine.append(lax.ppermute(packed, ('row', 'layer'), route))  3.49 us
    all_to_all x1, starting transfers between devices, body(): trace = lax.all_to_all(trace, AXES, 0, 0, tiled=True)  3.48 us
    all_to_all x1, waiting for transfers between devices, body(): trace = lax.all_to_all(trace, AXES, 0, 0, tiled=True)  2.63 us
    ppermute x1, starting transfers between devices, row_strip(): far = lax.ppermute(packed, AXES, route)  2.59 us
    ppermute x3, waiting for transfers between devices, body(): mine.append(lax.ppermute(packed, ('row', 'layer'), route))  2.54 us
  transfers between devices with their start and end apart: 8, of which 5 were waited for; matrix products, arithmetic and copies ran while one was open for 0% of the time, Pallas kernels for 18%

profile of v7, /device:TPU:0, one launch (start us, length us, event | category | flops | bytes accessed | tf_op | source)
XLA Modules:
  0.0 35.9 jit_solution(15948277653218513655)
XLA Ops:
  0.6 0.0 copy-start
  0.6 1.0 %copy-done = f32[2,1,3,96,96]{4,3,2,1,0:T(8,128)S(1)} copy-done((f32[2,1,3,96,96]{4,3,2,1,0:T(8,128)S(1)}, f32[2,1,3,96,96]{4,3,2,1,0:T(8,128)}, u32[]{:S(2)}) %copy-start) | copy-done | bytes 221208
  1.6 0.1 pack.1.refs_0_
  1.7 0.0 copy-start.1
  1.7 0.0 copy-start.2
  1.7 3.1 %collective-permute-start = (f32[6,72,128]{2,1,0:T(8,128)S(1)}, f32[6,72,128]{2,1,0:T(8,128)S(1)}, u32[]{:S(2)}, u32[]{:S(2)}) collective-permute-start(f32[6,72,128]{2,1,0:T(8,128)S(1)} %pack.1.refs_0_), channel_id=1, source_target_pairs={{0,4},{4,0},{8,12},{12,8},{1,5},{5,1},{9,13},{13,9},{2,6},{6,2},{1... | collective-permute-start | bytes 663560 | tf_op jit(solution)/shard_map/ppermute | solution.py:161
  4.8 2.6 %collective-permute-start.1 = (f32[6,72,128]{2,1,0:T(8,128)S(1)}, f32[6,72,128]{2,1,0:T(8,128)S(1)}, u32[]{:S(2)}, u32[]{:S(2)}) collective-permute-start(f32[6,72,128]{2,1,0:T(8,128)S(1)} %pack.1.refs_0_), channel_id=1, source_target_pairs={{0,8},{1,9},{2,10},{3,11},{4,12},{5,13},{6,14},{7,15},{8,0},{9,1},... | collective-permute-start | bytes 663560 | tf_op jit(solution)/shard_map/ppermute | solution.py:181
  7.4 1.5 %collective-permute-start.3 = (f32[6,72,128]{2,1,0:T(8,128)S(1)}, f32[6,72,128]{2,1,0:T(8,128)S(1)}, u32[]{:S(2)}, u32[]{:S(2)}) collective-permute-start(f32[6,72,128]{2,1,0:T(8,128)S(1)} %pack.1.refs_0_), channel_id=1, source_target_pairs={{0,2},{1,3},{2,0},{3,1},{16,18},{17,19},{18,16},{19,17},{4,6},{5,7... | collective-permute-start | bytes 663560 | tf_op jit(solution)/shard_map/ppermute | solution.py:209
  8.9 1.4 %collective-permute-start.4 = (f32[6,72,128]{2,1,0:T(8,128)S(1)}, f32[6,72,128]{2,1,0:T(8,128)S(1)}, u32[]{:S(2)}, u32[]{:S(2)}) collective-permute-start(f32[6,72,128]{2,1,0:T(8,128)S(1)} %pack.1.refs_0_), channel_id=1, source_target_pairs={{0,16},{1,17},{2,18},{3,19},{16,0},{17,1},{18,2},{19,3},{4,20},{5,... | collective-permute-start | bytes 663560 | tf_op jit(solution)/shard_map/ppermute | solution.py:209
  10.3 0.6 %collective-permute-start.5 = (f32[6,72,128]{2,1,0:T(8,128)S(1)}, f32[6,72,128]{2,1,0:T(8,128)S(1)}, u32[]{:S(2)}, u32[]{:S(2)}) collective-permute-start(f32[6,72,128]{2,1,0:T(8,128)S(1)} %pack.1.refs_0_), channel_id=1, source_target_pairs={{0,18},{1,19},{2,16},{3,17},{16,2},{17,3},{18,0},{19,1},{4,22},{5,... | collective-permute-start | bytes 663560 | tf_op jit(solution)/shard_map/ppermute | solution.py:209
  10.9 4.0 %collective-permute-done.refs_5_.refs_1_ = f32[6,72,128]{2,1,0:T(8,128)S(1)} collective-permute-done((f32[6,72,128]{2,1,0:T(8,128)S(1)}, f32[6,72,128]{2,1,0:T(8,128)S(1)}, u32[]{:S(2)}, u32[]{:S(2)}) %collective-permute-start) | collective-permute-done | bytes 221216 | tf_op jit(solution)/shard_map/ppermute | solution.py:161
  14.9 2.5 %collective-permute-done.1.refs_4_.refs_2_ = f32[6,72,128]{2,1,0:T(8,128)S(1)} collective-permute-done((f32[6,72,128]{2,1,0:T(8,128)S(1)}, f32[6,72,128]{2,1,0:T(8,128)S(1)}, u32[]{:S(2)}, u32[]{:S(2)}) %collective-permute-start.1) | collective-permute-done | bytes 221216 | tf_op jit(solution)/shard_map/ppermute | solution.py:181
  17.4 0.0 collective-permute-done.3.refs_1_
  17.4 0.0 collective-permute-done.4.refs_2_
  17.4 2.5 %collective-permute-done.5.refs_3_ = f32[6,72,128]{2,1,0:T(8,128)S(1)} collective-permute-done((f32[6,72,128]{2,1,0:T(8,128)S(1)}, f32[6,72,128]{2,1,0:T(8,128)S(1)}, u32[]{:S(2)}, u32[]{:S(2)}) %collective-permute-start.5) | collective-permute-done | bytes 221216 | tf_op jit(solution)/shard_map/ppermute | solution.py:209
  19.9 0.1 stack.1.refs_4_.refs_3_
  20.0 0.1 collective-permute-start.6
  20.1 0.5 %collective-permute-start.2 = (f32[6,72,128]{2,1,0:T(8,128)S(1)}, f32[6,72,128]{2,1,0:T(8,128)S(1)}, u32[]{:S(2)}, u32[]{:S(2)}) collective-permute-start(f32[6,72,128]{2,1,0:T(8,128)S(1)} %collective-permute-done.1.refs_4_.refs_2_), channel_id=1, source_target_pairs={{0,4},{4,0},{8,12},{12,8},{1,5},{5,1},{9,13},{13,9},{2,6},{6,2},{1... | collective-permute-start | bytes 663560 | tf_op jit(solution)/shard_map/ppermute | solution.py:161
  20.6 0.0 copy-done.1
  20.6 0.0 copy-done.2
  20.6 1.9 %collective-permute-done.6.refs_5_.refs_4_ = f32[24,72,128]{2,1,0:T(8,128)S(1)} collective-permute-done((f32[24,72,128]{2,1,0:T(8,128)S(1)}, f32[24,72,128]{2,1,0:T(8,128)S(1)}, u32[]{:S(2)}, u32[]{:S(2)}) %collective-permute-start.6) | collective-permute-done | bytes 884768 | tf_op jit(solution)/shard_map/ppermute | solution.py:161
  22.5 2.1 %trace_terms.1 = f32[32,1,128]{2,1,0:T(1,128)} custom-call(s32[3,4,16]{2,1,0:T(4,128)S(1)} %select_bitcast_fusion.code_ref, f32[6,72,128]{2,1,0:T(8,128)S(1)} %pack.1.refs_0_, f32[6,72,128]{2,1,0:T(8,128)S(1)} %collective-permute-done.refs_5_.refs_1_, f32[6,72,128]{2,1,0:T(8,128)S(1)} %collective-permute-done.1.refs_4_.refs_2_, ...), custom_call_target="tpu_custom_call" | custom-call | tf_op jit(solution)/shard_map/trace_terms/pallas_call | solution.py:223
  24.6 3.5 %all-to-all-start = ((f32[32,1,128]{2,1,0:T(1,128)}), f32[32,1,128]{2,1,0:T(1,128)S(1)}, u32[]{:S(2)}, u32[]{:S(2)}) async-start(f32[32,1,128]{2,1,0:T(1,128)} %trace_terms.1), calls=%async_computation | async-start | bytes 32768 | tf_op jit(solution)/shard_map/all_to_all | solution.py:231
  28.1 0.0 collective-permute-done.2.refs_3_
  28.1 4.5 %multiply.1 = f32[2,1,3,96,96]{4,3,2,1,0:T(8,128)} custom-call(s32[3,4,16]{2,1,0:T(4,128)S(1)} %select_bitcast_fusion.code_ref, f32[6,72,128]{2,1,0:T(8,128)S(1)} %pack.1.refs_0_, f32[6,72,128]{2,1,0:T(8,128)S(1)} %collective-permute-done.refs_5_.refs_1_, f32[6,72,128]{2,1,0:T(8,128)S(1)} %collective-permute-done.1.refs_4_.refs_2_, ...), custom_call_target="tpu_custom_call" | custom-call | tf_op jit(solution)/shard_map/multiply/pallas_call | solution.py:235
  32.6 2.6 %all-to-all-done = f32[32,1,128]{2,1,0:T(1,128)S(1)} async-done(((f32[32,1,128]{2,1,0:T(1,128)}), f32[32,1,128]{2,1,0:T(1,128)S(1)}, u32[]{:S(2)}, u32[]{:S(2)}) %all-to-all-start) | async-done | bytes 16416 | tf_op jit(solution)/shard_map/all_to_all | solution.py:231
  35.3 0.6 %slice_reduce_fusion = f32[]{:T(128)} fusion(f32[32,1,128]{2,1,0:T(1,128)S(1)} %all-to-all-done), kind=kLoop, calls=%fused_computation | loop fusion | flops 31 | bytes 132 | tf_op jit(solution)/shard_map/reduce_sum | solution.py:245
  (1 shorter events, 0.0 us)
Async XLA Ops:
  0.6 1.0 %copy-start = (f32[2,1,3,96,96]{4,3,2,1,0:T(8,128)S(1)}, f32[2,1,3,96,96]{4,3,2,1,0:T(8,128)}, u32[]{:S(2)}) copy-start(f32[2,1,3,96,96]{4,3,2,1,0:T(8,128)} %x_ref.1) | copy-start | bytes 663556
  1.7 18.9 %copy-start.1 = (s32[16,4,3]{0,1,2:T(4,128)S(1)}, s32[16,4,3]{0,1,2:T(4,128)}, u32[]{:S(2)}) copy-start(s32[16,4,3]{0,1,2:T(4,128)} %param.4) | copy-start | bytes 2308
  1.7 18.9 %copy-start.2 = (s32[16,4,3]{0,1,2:T(4,128)S(1)}, s32[16,4,3]{0,1,2:T(4,128)}, u32[]{:S(2)}) copy-start(s32[16,4,3]{0,1,2:T(4,128)} %param.5) | copy-start | bytes 2308
  1.7 13.1 %collective-permute-start = (f32[6,72,128]{2,1,0:T(8,128)S(1)}, f32[6,72,128]{2,1,0:T(8,128)S(1)}, u32[]{:S(2)}, u32[]{:S(2)}) collective-permute-start(f32[6,72,128]{2,1,0:T(8,128)S(1)} %pack.1.refs_0_), channel_id=1, source_target_pairs={{0,4},{4,0},{8,12},{12,8},{1,5},{5,1},{9,13},{13,9},{2,6},{6,2},{1... | collective-permute-start | bytes 663560 | tf_op jit(solution)/shard_map/ppermute | solution.py:161
  4.8 12.6 %collective-permute-start.1 = (f32[6,72,128]{2,1,0:T(8,128)S(1)}, f32[6,72,128]{2,1,0:T(8,128)S(1)}, u32[]{:S(2)}, u32[]{:S(2)}) collective-permute-start(f32[6,72,128]{2,1,0:T(8,128)S(1)} %pack.1.refs_0_), channel_id=1, source_target_pairs={{0,8},{1,9},{2,10},{3,11},{4,12},{5,13},{6,14},{7,15},{8,0},{9,1},... | collective-permute-start | bytes 663560 | tf_op jit(solution)/shard_map/ppermute | solution.py:181
  7.4 10.0 %collective-permute-start.3 = (f32[6,72,128]{2,1,0:T(8,128)S(1)}, f32[6,72,128]{2,1,0:T(8,128)S(1)}, u32[]{:S(2)}, u32[]{:S(2)}) collective-permute-start(f32[6,72,128]{2,1,0:T(8,128)S(1)} %pack.1.refs_0_), channel_id=1, source_target_pairs={{0,2},{1,3},{2,0},{3,1},{16,18},{17,19},{18,16},{19,17},{4,6},{5,7... | collective-permute-start | bytes 663560 | tf_op jit(solution)/shard_map/ppermute | solution.py:209
  8.9 8.5 %collective-permute-start.4 = (f32[6,72,128]{2,1,0:T(8,128)S(1)}, f32[6,72,128]{2,1,0:T(8,128)S(1)}, u32[]{:S(2)}, u32[]{:S(2)}) collective-permute-start(f32[6,72,128]{2,1,0:T(8,128)S(1)} %pack.1.refs_0_), channel_id=1, source_target_pairs={{0,16},{1,17},{2,18},{3,19},{16,0},{17,1},{18,2},{19,3},{4,20},{5,... | collective-permute-start | bytes 663560 | tf_op jit(solution)/shard_map/ppermute | solution.py:209
  10.3 9.6 %collective-permute-start.5 = (f32[6,72,128]{2,1,0:T(8,128)S(1)}, f32[6,72,128]{2,1,0:T(8,128)S(1)}, u32[]{:S(2)}, u32[]{:S(2)}) collective-permute-start(f32[6,72,128]{2,1,0:T(8,128)S(1)} %pack.1.refs_0_), channel_id=1, source_target_pairs={{0,18},{1,19},{2,16},{3,17},{16,2},{17,3},{18,0},{19,1},{4,22},{5,... | collective-permute-start | bytes 663560 | tf_op jit(solution)/shard_map/ppermute | solution.py:209
  20.0 2.5 %collective-permute-start.6 = (f32[24,72,128]{2,1,0:T(8,128)S(1)}, f32[24,72,128]{2,1,0:T(8,128)S(1)}, u32[]{:S(2)}, u32[]{:S(2)}) collective-permute-start(f32[24,72,128]{2,1,0:T(8,128)S(1)} %stack.1.refs_4_.refs_3_), channel_id=1, source_target_pairs={{0,1},{1,0},{2,3},{3,2},{4,5},{5,4},{6,7},{7,6},{8,9},{9,8},{10,11... | collective-permute-start | bytes 2654216 | tf_op jit(solution)/shard_map/ppermute | solution.py:161
  20.1 8.0 %collective-permute-start.2 = (f32[6,72,128]{2,1,0:T(8,128)S(1)}, f32[6,72,128]{2,1,0:T(8,128)S(1)}, u32[]{:S(2)}, u32[]{:S(2)}) collective-permute-start(f32[6,72,128]{2,1,0:T(8,128)S(1)} %collective-permute-done.1.refs_4_.refs_2_), channel_id=1, source_target_pairs={{0,4},{4,0},{8,12},{12,8},{1,5},{5,1},{9,13},{13,9},{2,6},{6,2},{1... | collective-permute-start | bytes 663560 | tf_op jit(solution)/shard_map/ppermute | solution.py:161
  24.6 10.6 %all-to-all-start = ((f32[32,1,128]{2,1,0:T(1,128)}), f32[32,1,128]{2,1,0:T(1,128)S(1)}, u32[]{:S(2)}, u32[]{:S(2)}) async-start(f32[32,1,128]{2,1,0:T(1,128)} %trace_terms.1), calls=%async_computation | async-start | bytes 32768 | tf_op jit(solution)/shard_map/all_to_all | solution.py:231

commit v8 on v7

--- a/solution.py
+++ b/solution.py
@@ -12,6 +12,7 @@
 LIMIT = pltpu.CompilerParams(vmem_limit_bytes=48 * 2 ** 20)
 VMEM = pl.BlockSpec(memory_space=pltpu.VMEM)
 SMEM = pl.BlockSpec(memory_space=pltpu.SMEM)
+UNREAD = pl.BlockSpec(memory_space=pl.ANY)
 
 
 def tall_of(size):
@@ -56,9 +57,9 @@
                 out_ref[n, q * rest:(q + 1) * rest, size:] = x_ref[i, 0, t, tall:, q * spare:(q + 1) * spare]
 
 
-def stack_kernel(count, *refs):
+def stack_kernel(first, count, *refs):
     out_ref = refs[-1]
-    for n, ref in enumerate(refs[:count]):
+    for n, ref in enumerate(refs[first:first + count]):
         out_ref[n * ref.shape[0]:(n + 1) * ref.shape[0]] = ref[...]
 
 
@@ -90,7 +91,7 @@
 
 def trace_kernel(sizes, rows, size, groups, code_ref, *refs):
     count = len(groups)
-    strip_refs, (mine_ref, other_ref), total_ref = refs[:count], refs[count:count + 2], refs[-1]
+    (mine_ref, other_ref), strip_refs, total_ref = refs[:2], refs[2:2 + count], refs[-1]
     slots = code_ref.shape[0]
     pair, here, own_group, number, per_group = place(sizes)
     width = per_group * rows
@@ -121,8 +122,8 @@
 
 def product_kernel(sizes, groups, code_ref, *refs):
     count = len(groups)
-    strip_refs, (mine_ref, other_ref), out_ref = refs[:count], refs[count:count + 2], refs[count + 2]
-    a_ref, w_refs = refs[count + 3], refs[count + 4:]
+    (mine_ref, other_ref), strip_refs = refs[:2], refs[2:2 + count]
+    out_ref, a_ref, *w_refs = refs[-5:]
     rows, _, slots, size, _ = out_ref.shape
     pair, here, own_group, _, per_group = place(sizes)
     width = per_group * rows
@@ -209,25 +210,26 @@
         mine.append(lax.ppermute(packed, ("row", "layer"), route))
     early = [(exchanged(packed, "col", 1) if share is None else share, *rest) for share, *rest in early]
 
-    ahead = [share for share, value, _, _ in reversed(early) if value]
+    far = [share for share, value, _, _ in early if value > 1]
+    near = [share for share, value, _, _ in early if value == 1]
     stacked = pl.pallas_call(
-        functools.partial(stack_kernel, len(mine)),
+        functools.partial(stack_kernel, len(far), len(mine)),
         out_shape=jax.ShapeDtypeStruct((len(mine) * rows * slots, tall, LANES), jnp.float32),
-        in_specs=[VMEM] * len(mine) + [pl.BlockSpec(memory_space=pl.ANY)] * len(ahead),
+        in_specs=[UNREAD] * len(far) + [VMEM] * len(mine) + [UNREAD] * len(near),
         out_specs=VMEM,
         compiler_params=LIMIT,
         name="stack",
-    )(*mine, *ahead)
+    )(*far, *mine, *near)
     other = exchanged(stacked, "layer", 1)
 
     trace = pl.pallas_call(
         functools.partial(trace_kernel, sizes, rows, size, [tuple(rest) for _, *rest in early]),
         out_shape=jax.ShapeDtypeStruct((n_row * n_col * n_layer, 1, LANES), jnp.float32),
-        in_specs=[SMEM] + [VMEM] * (len(early) + 2),
+        in_specs=[SMEM] + [VMEM] * (len(early) + 2) + [UNREAD] * (len(mine) - 1),
         out_specs=VMEM,
         compiler_params=LIMIT,
         name="trace_terms",
-    )(code, *[share for share, *_ in early], stacked, other)
+    )(code, stacked, other, *[share for share, *_ in early], *mine[1:])
     trace = lax.all_to_all(trace, AXES, 0, 0, tiled=True)
 
     strip = early + late
@@ -235,13 +237,13 @@
     product = pl.pallas_call(
         functools.partial(product_kernel, sizes, [tuple(rest) for _, *rest in strip]),
         out_shape=jax.ShapeDtypeStruct(blocks.shape, jnp.float32),
-        in_specs=[SMEM] + [VMEM] * (len(strip) + 2),
+        in_specs=[SMEM] + [VMEM] * (len(strip) + 2) + [UNREAD] * (len(mine) - 1),
         out_specs=VMEM,
         scratch_shapes=[pltpu.VMEM((3 * size, inner), jnp.bfloat16)]
         + [pltpu.VMEM((inner, slots * LANES), jnp.bfloat16)] * 3,
         compiler_params=LIMIT,
         name="multiply",
-    )(code, *[share for share, *_ in strip], stacked, other)
+    )(code, stacked, other, *[share for share, *_ in strip], *mine[1:])
     return product, jnp.sum(trace[:, 0, 0])
 
 

time: 36.1 us -> 35.6 us (0.986)
    ppermute x3, waiting for transfers between devices: 5.86 us -> 2.26 us  [exchanged(): lax.ppermute(value, axis, [(n, n ^ mask) for n in range(lax.axis_size(axi...]
    ppermute x1, waiting for transfers between devices: 2.52 us -> 5.21 us  [row_strip(): far = lax.ppermute(packed, AXES, route)]
    ppermute x3, starting transfers between devices: 3.67 us -> 1.67 us  [exchanged(): lax.ppermute(value, axis, [(n, n ^ mask) for n in range(lax.axis_size(axi...]
    ppermute x1, starting transfers between devices: 2.59 us -> 4.1 us  [row_strip(): far = lax.ppermute(packed, AXES, route)]
    ppermute x3, waiting for transfers between devices: 2.54 us -> 3.3 us  [body(): mine.append(lax.ppermute(packed, ('row', 'layer'), route))]
    ppermute x3, starting transfers between devices: 3.49 us -> 4.03 us  [body(): mine.append(lax.ppermute(packed, ('row', 'layer'), route))]
  transfers between devices with their start and end apart: 8 -> 8, of which waited for: 5 -> 7; matrix products, arithmetic and copies ran while one was open for 0% -> 0% of each run, Pallas kernels for 18% -> 19%
where the time goes in v8:
time: 35.6 us; the launch traced here: 35.4 us
  waiting for transfers between devices  13.3 us (37%)
  starting transfers between devices  13 us (37%)
  Pallas kernels  6.81 us (19%)
  local copies, waits for them, and re-layouts  0.97 us (3%)
  between operations  0.69 us (2%)
  other arithmetic  0.64 us (2%)
    ppermute x1, waiting for transfers between devices, row_strip(): far = lax.ppermute(packed, AXES, route)  5.21 us
    pallas_call x1, Pallas kernels, body(): pl.pallas_call(functools.partial(product_kernel, sizes, [tuple(rest) for...  4.5 us
    ppermute x1, starting transfers between devices, row_strip(): far = lax.ppermute(packed, AXES, route)  4.1 us
    ppermute x3, starting transfers between devices, body(): mine.append(lax.ppermute(packed, ('row', 'layer'), route))  4.03 us
    ppermute x3, waiting for transfers between devices, body(): mine.append(lax.ppermute(packed, ('row', 'layer'), route))  3.3 us
    all_to_all x1, starting transfers between devices, body(): trace = lax.all_to_all(trace, AXES, 0, 0, tiled=True)  3.17 us
    all_to_all x1, waiting for transfers between devices, body(): trace = lax.all_to_all(trace, AXES, 0, 0, tiled=True)  2.53 us
    ppermute x3, waiting for transfers between devices, exchanged(): lax.ppermute(value, axis, [(n, n ^ mask) for n in range(lax.axis_size(axi...  2.26 us
  transfers between devices with their start and end apart: 8, of which 7 were waited for; matrix products, arithmetic and copies ran while one was open for 0% of the time, Pallas kernels for 19%

profile of v8, /device:TPU:0, one launch (start us, length us, event | category | flops | bytes accessed | tf_op | source)
XLA Modules:
  0.0 35.4 jit_solution(18210324211242911835)
XLA Ops:
  0.6 0.0 copy-start
  0.6 1.0 %copy-done = f32[2,1,3,96,96]{4,3,2,1,0:T(8,128)S(1)} copy-done((f32[2,1,3,96,96]{4,3,2,1,0:T(8,128)S(1)}, f32[2,1,3,96,96]{4,3,2,1,0:T(8,128)}, u32[]{:S(2)}) %copy-start) | copy-done | bytes 221208
  1.6 0.1 pack.1.refs_1_.refs_2_
  1.7 0.0 copy-start.1
  1.7 0.0 copy-start.2
  1.7 4.1 %collective-permute-start = (f32[6,72,128]{2,1,0:T(8,128)S(1)}, f32[6,72,128]{2,1,0:T(8,128)S(1)}, u32[]{:S(2)}, u32[]{:S(2)}) collective-permute-start(f32[6,72,128]{2,1,0:T(8,128)S(1)} %pack.1.refs_1_.refs_2_), channel_id=1, source_target_pairs={{0,8},{1,9},{2,10},{3,11},{4,12},{5,13},{6,14},{7,15},{8,0},{9,1},... | collective-permute-start | bytes 663560 | tf_op jit(solution)/shard_map/ppermute | solution.py:182
  5.8 1.5 %collective-permute-start.1 = (f32[6,72,128]{2,1,0:T(8,128)S(1)}, f32[6,72,128]{2,1,0:T(8,128)S(1)}, u32[]{:S(2)}, u32[]{:S(2)}) collective-permute-start(f32[6,72,128]{2,1,0:T(8,128)S(1)} %pack.1.refs_1_.refs_2_), channel_id=1, source_target_pairs={{0,2},{1,3},{2,0},{3,1},{16,18},{17,19},{18,16},{19,17},{4,6},{5,7... | collective-permute-start | bytes 663560 | tf_op jit(solution)/shard_map/ppermute | solution.py:210
  7.4 2.5 %collective-permute-start.2 = (f32[6,72,128]{2,1,0:T(8,128)S(1)}, f32[6,72,128]{2,1,0:T(8,128)S(1)}, u32[]{:S(2)}, u32[]{:S(2)}) collective-permute-start(f32[6,72,128]{2,1,0:T(8,128)S(1)} %pack.1.refs_1_.refs_2_), channel_id=1, source_target_pairs={{0,16},{1,17},{2,18},{3,19},{16,0},{17,1},{18,2},{19,3},{4,20},{5,... | collective-permute-start | bytes 663560 | tf_op jit(solution)/shard_map/ppermute | solution.py:210
  9.9 0.0 collective-permute-start.3
  9.9 1.0 %collective-permute-start.4 = (f32[6,72,128]{2,1,0:T(8,128)S(1)}, f32[6,72,128]{2,1,0:T(8,128)S(1)}, u32[]{:S(2)}, u32[]{:S(2)}) collective-permute-start(f32[6,72,128]{2,1,0:T(8,128)S(1)} %pack.1.refs_1_.refs_2_), channel_id=1, source_target_pairs={{0,4},{4,0},{8,12},{12,8},{1,5},{5,1},{9,13},{13,9},{2,6},{6,2},{1... | collective-permute-start | bytes 663560 | tf_op jit(solution)/shard_map/ppermute | solution.py:162
  10.9 5.2 %collective-permute-done.refs_0_.refs_4_ = f32[6,72,128]{2,1,0:T(8,128)S(1)} collective-permute-done((f32[6,72,128]{2,1,0:T(8,128)S(1)}, f32[6,72,128]{2,1,0:T(8,128)S(1)}, u32[]{:S(2)}, u32[]{:S(2)}) %collective-permute-start) | collective-permute-done | bytes 221216 | tf_op jit(solution)/shard_map/ppermute | solution.py:182
  16.1 0.0 collective-permute-done.1.refs_2_.refs_6_.refs_5_
  16.1 0.1 collective-permute-done.2.refs_3_.refs_7_.refs_6_
  16.2 3.2 %collective-permute-done.3.refs_4_.refs_8_.refs_7_ = f32[6,72,128]{2,1,0:T(8,128)S(1)} collective-permute-done((f32[6,72,128]{2,1,0:T(8,128)S(1)}, f32[6,72,128]{2,1,0:T(8,128)S(1)}, u32[]{:S(2)}, u32[]{:S(2)}) %collective-permute-start.3) | collective-permute-done | bytes 221216 | tf_op jit(solution)/shard_map/ppermute | solution.py:210
  19.4 0.3 collective-permute-done.4.refs_5_.refs_3_
  19.7 0.1 stack.1.refs_0_
  19.8 0.1 collective-permute-start.5
  19.9 0.6 %collective-permute-start.6 = (f32[6,72,128]{2,1,0:T(8,128)S(1)}, f32[6,72,128]{2,1,0:T(8,128)S(1)}, u32[]{:S(2)}, u32[]{:S(2)}) collective-permute-start(f32[6,72,128]{2,1,0:T(8,128)S(1)} %collective-permute-done.refs_0_.refs_4_), channel_id=1, source_target_pairs={{0,4},{4,0},{8,12},{12,8},{1,5},{5,1},{9,13},{13,9},{2,6},{6,2},{1... | collective-permute-start | bytes 663560 | tf_op jit(solution)/shard_map/ppermute | solution.py:162
  20.4 0.0 copy-done.1
  20.4 0.0 copy-done.2
  20.4 1.8 %collective-permute-done.5.refs_1_ = f32[24,72,128]{2,1,0:T(8,128)S(1)} collective-permute-done((f32[24,72,128]{2,1,0:T(8,128)S(1)}, f32[24,72,128]{2,1,0:T(8,128)S(1)}, u32[]{:S(2)}, u32[]{:S(2)}) %collective-permute-start.5) | collective-permute-done | bytes 884768 | tf_op jit(solution)/shard_map/ppermute | solution.py:162
  22.3 2.1 %trace_terms.1 = f32[32,1,128]{2,1,0:T(1,128)} custom-call(s32[3,4,16]{2,1,0:T(4,128)S(1)} %select_bitcast_fusion.code_ref, f32[24,72,128]{2,1,0:T(8,128)S(1)} %stack.1.refs_0_, f32[24,72,128]{2,1,0:T(8,128)S(1)} %collective-permute-done.5.refs_1_, f32[6,72,128]{2,1,0:T(8,128)S(1)} %pack.1.refs_1_.refs_2_, ...), custom_call_target="tpu_custom_call" | custom-call | tf_op jit(solution)/shard_map/trace_terms/pallas_call | solution.py:225
  24.4 3.2 %all-to-all-start = ((f32[32,1,128]{2,1,0:T(1,128)}), f32[32,1,128]{2,1,0:T(1,128)S(1)}, u32[]{:S(2)}, u32[]{:S(2)}) async-start(f32[32,1,128]{2,1,0:T(1,128)} %trace_terms.1), calls=%async_computation | async-start | bytes 32768 | tf_op jit(solution)/shard_map/all_to_all | solution.py:233
  27.6 0.1 collective-permute-done.6.refs_5_
  27.7 4.5 %multiply.1 = f32[2,1,3,96,96]{4,3,2,1,0:T(8,128)} custom-call(s32[3,4,16]{2,1,0:T(4,128)S(1)} %select_bitcast_fusion.code_ref, f32[24,72,128]{2,1,0:T(8,128)S(1)} %stack.1.refs_0_, f32[24,72,128]{2,1,0:T(8,128)S(1)} %collective-permute-done.5.refs_1_, f32[6,72,128]{2,1,0:T(8,128)S(1)} %pack.1.refs_1_.refs_2_, ...), custom_call_target="tpu_custom_call" | custom-call | tf_op jit(solution)/shard_map/multiply/pallas_call | solution.py:237
  32.2 2.5 %all-to-all-done = f32[32,1,128]{2,1,0:T(1,128)S(1)} async-done(((f32[32,1,128]{2,1,0:T(1,128)}), f32[32,1,128]{2,1,0:T(1,128)S(1)}, u32[]{:S(2)}, u32[]{:S(2)}) %all-to-all-start) | async-done | bytes 16416 | tf_op jit(solution)/shard_map/all_to_all | solution.py:233
  34.8 0.6 %slice_reduce_fusion = f32[]{:T(128)} fusion(f32[32,1,128]{2,1,0:T(1,128)S(1)} %all-to-all-done), kind=kLoop, calls=%fused_computation | loop fusion | flops 31 | bytes 132 | tf_op jit(solution)/shard_map/reduce_sum | solution.py:247
  (1 shorter events, 0.0 us)
Async XLA Ops:
  0.6 1.0 %copy-start = (f32[2,1,3,96,96]{4,3,2,1,0:T(8,128)S(1)}, f32[2,1,3,96,96]{4,3,2,1,0:T(8,128)}, u32[]{:S(2)}) copy-start(f32[2,1,3,96,96]{4,3,2,1,0:T(8,128)} %x_ref.1) | copy-start | bytes 663556
  1.7 18.7 %copy-start.1 = (s32[16,4,3]{0,1,2:T(4,128)S(1)}, s32[16,4,3]{0,1,2:T(4,128)}, u32[]{:S(2)}) copy-start(s32[16,4,3]{0,1,2:T(4,128)} %param.4) | copy-start | bytes 2308
  1.7 18.7 %copy-start.2 = (s32[16,4,3]{0,1,2:T(4,128)S(1)}, s32[16,4,3]{0,1,2:T(4,128)}, u32[]{:S(2)}) copy-start(s32[16,4,3]{0,1,2:T(4,128)} %param.5) | copy-start | bytes 2308
  1.7 14.4 %collective-permute-start = (f32[6,72,128]{2,1,0:T(8,128)S(1)}, f32[6,72,128]{2,1,0:T(8,128)S(1)}, u32[]{:S(2)}, u32[]{:S(2)}) collective-permute-start(f32[6,72,128]{2,1,0:T(8,128)S(1)} %pack.1.refs_1_.refs_2_), channel_id=1, source_target_pairs={{0,8},{1,9},{2,10},{3,11},{4,12},{5,13},{6,14},{7,15},{8,0},{9,1},... | collective-permute-start | bytes 663560 | tf_op jit(solution)/shard_map/ppermute | solution.py:182
  5.8 10.3 %collective-permute-start.1 = (f32[6,72,128]{2,1,0:T(8,128)S(1)}, f32[6,72,128]{2,1,0:T(8,128)S(1)}, u32[]{:S(2)}, u32[]{:S(2)}) collective-permute-start(f32[6,72,128]{2,1,0:T(8,128)S(1)} %pack.1.refs_1_.refs_2_), channel_id=1, source_target_pairs={{0,2},{1,3},{2,0},{3,1},{16,18},{17,19},{18,16},{19,17},{4,6},{5,7... | collective-permute-start | bytes 663560 | tf_op jit(solution)/shard_map/ppermute | solution.py:210
  7.4 8.8 %collective-permute-start.2 = (f32[6,72,128]{2,1,0:T(8,128)S(1)}, f32[6,72,128]{2,1,0:T(8,128)S(1)}, u32[]{:S(2)}, u32[]{:S(2)}) collective-permute-start(f32[6,72,128]{2,1,0:T(8,128)S(1)} %pack.1.refs_1_.refs_2_), channel_id=1, source_target_pairs={{0,16},{1,17},{2,18},{3,19},{16,0},{17,1},{18,2},{19,3},{4,20},{5,... | collective-permute-start | bytes 663560 | tf_op jit(solution)/shard_map/ppermute | solution.py:210
  9.9 9.5 %collective-permute-start.3 = (f32[6,72,128]{2,1,0:T(8,128)S(1)}, f32[6,72,128]{2,1,0:T(8,128)S(1)}, u32[]{:S(2)}, u32[]{:S(2)}) collective-permute-start(f32[6,72,128]{2,1,0:T(8,128)S(1)} %pack.1.refs_1_.refs_2_), channel_id=1, source_target_pairs={{0,18},{1,19},{2,16},{3,17},{16,2},{17,3},{18,0},{19,1},{4,22},{5,... | collective-permute-start | bytes 663560 | tf_op jit(solution)/shard_map/ppermute | solution.py:210
  9.9 9.9 %collective-permute-start.4 = (f32[6,72,128]{2,1,0:T(8,128)S(1)}, f32[6,72,128]{2,1,0:T(8,128)S(1)}, u32[]{:S(2)}, u32[]{:S(2)}) collective-permute-start(f32[6,72,128]{2,1,0:T(8,128)S(1)} %pack.1.refs_1_.refs_2_), channel_id=1, source_target_pairs={{0,4},{4,0},{8,12},{12,8},{1,5},{5,1},{9,13},{13,9},{2,6},{6,2},{1... | collective-permute-start | bytes 663560 | tf_op jit(solution)/shard_map/ppermute | solution.py:162
  19.8 2.5 %collective-permute-start.5 = (f32[24,72,128]{2,1,0:T(8,128)S(1)}, f32[24,72,128]{2,1,0:T(8,128)S(1)}, u32[]{:S(2)}, u32[]{:S(2)}) collective-permute-start(f32[24,72,128]{2,1,0:T(8,128)S(1)} %stack.1.refs_0_), channel_id=1, source_target_pairs={{0,1},{1,0},{2,3},{3,2},{4,5},{5,4},{6,7},{7,6},{8,9},{9,8},{10,11... | collective-permute-start | bytes 2654216 | tf_op jit(solution)/shard_map/ppermute | solution.py:162
  19.9 7.8 %collective-permute-start.6 = (f32[6,72,128]{2,1,0:T(8,128)S(1)}, f32[6,72,128]{2,1,0:T(8,128)S(1)}, u32[]{:S(2)}, u32[]{:S(2)}) collective-permute-start(f32[6,72,128]{2,1,0:T(8,128)S(1)} %collective-permute-done.refs_0_.refs_4_), channel_id=1, source_target_pairs={{0,4},{4,0},{8,12},{12,8},{1,5},{5,1},{9,13},{13,9},{2,6},{6,2},{1... | collective-permute-start | bytes 663560 | tf_op jit(solution)/shard_map/ppermute | solution.py:162
  24.4 10.3 %all-to-all-start = ((f32[32,1,128]{2,1,0:T(1,128)}), f32[32,1,128]{2,1,0:T(1,128)S(1)}, u32[]{:S(2)}, u32[]{:S(2)}) async-start(f32[32,1,128]{2,1,0:T(1,128)} %trace_terms.1), calls=%async_computation | async-start | bytes 32768 | tf_op jit(solution)/shard_map/all_to_all | solution.py:233

commit v9 on v8

--- a/solution.py
+++ b/solution.py
@@ -44,27 +44,24 @@
     return pair, lax.axis_index("col"), lax.div(pair, per_group), lax.rem(pair, per_group), per_group
 
 
-def pack_kernel(x_ref, out_ref):
+def pack_kernel(x_ref, out_ref, held_ref, sems):
     rows, _, slots, size, _ = x_ref.shape
     tall = tall_of(size)
     spare = LANES - size
     rest = size - tall
-    for i in range(rows):
-        for t in range(slots):
-            n = i * slots + t
-            out_ref[n, :, :size] = x_ref[i, 0, t, :tall, :]
-            for q in range(size // spare):
-                out_ref[n, q * rest:(q + 1) * rest, size:] = x_ref[i, 0, t, tall:, q * spare:(q + 1) * spare]
-
-
-def stack_kernel(first, count, *refs):
-    out_ref = refs[-1]
-    for n, ref in enumerate(refs[first:first + count]):
-        out_ref[n * ref.shape[0]:(n + 1) * ref.shape[0]] = ref[...]
-
-
-def strip_block(sizes, rows, slots, mine_ref, other_ref, contracted):
-    _, _, n_layer = sizes
+    copies = []
+    for n in range(rows * slots):
+        copies.append(pltpu.make_async_copy(x_ref.at[n // slots, 0, n % slots], held_ref.at[n], sems.at[n]))
+        copies[-1].start()
+    for n, copy in enumerate(copies):
+        copy.wait()
+        out_ref[n, :, :size] = held_ref[n, :tall, :]
+        for q in range(size // spare):
+            out_ref[n, q * rest:(q + 1) * rest, size:] = held_ref[n, tall:, q * spare:(q + 1) * spare]
+
+
+def strip_base(sizes, rows, slots, contracted):
+    n_layer = sizes[2]
     chips = n_layer // 2
     my_row, my_layer = lax.axis_index("row"), lax.axis_index("layer")
     source = lax.div(contracted, rows)
@@ -72,8 +69,8 @@
     chip = lax.bitwise_xor(lax.div(source_layer, 2), lax.div(my_layer, 2))
     base = (lax.bitwise_xor(source_row, my_row) * chips + chip) * (rows * slots)
     base = base + lax.rem(contracted, rows) * slots
-    same_core = lax.rem(source_layer, 2) == lax.rem(my_layer, 2)
-    return lambda index: jnp.where(same_core, mine_ref[base + index], other_ref[base + index])
+    other_core = lax.bitwise_xor(lax.rem(source_layer, 2), lax.rem(my_layer, 2))
+    return base + other_core * (sizes[0] * chips * rows * slots)
 
 
 def group_at(sizes, here, own_group, values):
@@ -89,12 +86,16 @@
     return index, valid & stored & (target >= 0)
 
 
-def trace_kernel(sizes, rows, size, groups, code_ref, *refs):
-    count = len(groups)
-    (mine_ref, other_ref), strip_refs, total_ref = refs[:2], refs[2:2 + count], refs[-1]
+def stack_kernel(sizes, rows, size, groups, parts, code_ref, *refs):
+    far, shares, near = parts
+    share_refs = refs[far:far + shares // 2] + refs[far + shares // 2 + near:far + shares + near]
+    strip_refs = [refs[far]] + list(refs[far + shares // 2:far + shares // 2 + near]) + list(refs[:far])
+    out_ref, total_ref = refs[-2:]
     slots = code_ref.shape[0]
     pair, here, own_group, number, per_group = place(sizes)
     width = per_group * rows
+    for n, ref in enumerate(share_refs):
+        out_ref[n * rows * slots:(n + 1) * rows * slots] = ref[...]
 
     def straight(block):
         return unpack(block, size)[:, :size]
@@ -110,7 +111,7 @@
                     column = code_ref[t, group, row]
                     contracted = group * width + jnp.maximum(column, 0)
                     index, valid = matched(code_ref, here, contracted, column >= 0, number * rows + i)
-                    block = strip_block(sizes, rows, slots, mine_ref, other_ref, contracted)(index)
+                    block = out_ref[strip_base(sizes, rows, slots, contracted) + index]
                     term = straight(strip_ref[i * slots + t]) * straight(block).T
                     total = total + jnp.where(valid, weight * term, 0.0)
         total_ref[...] = jnp.full(total_ref.shape, jnp.sum(total), jnp.float32)
@@ -120,9 +121,13 @@
         total_ref[...] = jnp.zeros(total_ref.shape, jnp.float32)
 
 
+def sum_kernel(terms_ref, out_ref):
+    out_ref[...] = jnp.sum(terms_ref[...], axis=0)[:, :1]
+
+
 def product_kernel(sizes, groups, code_ref, *refs):
     count = len(groups)
-    (mine_ref, other_ref), strip_refs = refs[:2], refs[2:2 + count]
+    column_ref, strip_refs = refs[0], refs[1:1 + count]
     out_ref, a_ref, *w_refs = refs[-5:]
     rows, _, slots, size, _ = out_ref.shape
     pair, here, own_group, _, per_group = place(sizes)
@@ -142,10 +147,10 @@
                     a_ref[n * size:(n + 1) * size, j * LANES:(j + 1) * LANES] = part
                 column = code_ref[t, group, row]
                 contracted = group * width + jnp.maximum(column, 0)
-                read = strip_block(sizes, rows, slots, mine_ref, other_ref, contracted)
+                base = strip_base(sizes, rows, slots, contracted)
                 for s in range(slots):
                     index, valid = matched(code_ref, here, contracted, column >= 0, targets[s])
-                    block = jnp.where(valid, unpack(read(index), size), 0.0)
+                    block = jnp.where(valid, unpack(column_ref[base + index], size), 0.0)
                     for w_ref, part in zip(w_refs, parts_of(block)):
                         w_ref[j * LANES:j * LANES + size, s * LANES:(s + 1) * LANES] = part
 
@@ -194,42 +199,44 @@
     packed = pl.pallas_call(
         pack_kernel,
         out_shape=jax.ShapeDtypeStruct((rows * slots, tall, LANES), jnp.float32),
-        in_specs=[VMEM],
+        in_specs=[pl.BlockSpec(memory_space=pltpu.HBM)],
         out_specs=VMEM,
+        scratch_shapes=[
+            pltpu.VMEM((rows * slots, size, size), jnp.float32),
+            pltpu.SemaphoreType.DMA((rows * slots,)),
+        ],
         compiler_params=LIMIT,
         name="pack",
     )(blocks)
 
     early, late = row_strip(packed, sizes)
-    mine = [packed]
-    for n in range(1, n_row * chips):
-        row_bits, chip_bits = n // chips, n % chips
-        route = [
-            (a * n_layer + b, (a ^ row_bits) * n_layer + (b ^ (2 * chip_bits))) for a in range(n_row) for b in range(n_layer)
-        ]
-        mine.append(lax.ppermute(packed, ("row", "layer"), route))
+    mine = {0: packed}
+    steps = [("row", 1 << b, chips << b) for b in range((n_row - 1).bit_length())]
+    steps += [("layer", 2 << b, 1 << b) for b in range((chips - 1).bit_length())]
+    for axis, mask, offset in steps:
+        for held in list(mine):
+            mine[held | offset] = exchanged(mine[held], axis, mask)
+    mine = [mine[n] for n in range(len(mine))]
     early = [(exchanged(packed, "col", 1) if share is None else share, *rest) for share, *rest in early]
+
+    others = [exchanged(share, "layer", 1) for share in mine]
 
     far = [share for share, value, _, _ in early if value > 1]
     near = [share for share, value, _, _ in early if value == 1]
-    stacked = pl.pallas_call(
-        functools.partial(stack_kernel, len(far), len(mine)),
-        out_shape=jax.ShapeDtypeStruct((len(mine) * rows * slots, tall, LANES), jnp.float32),
-        in_specs=[UNREAD] * len(far) + [VMEM] * len(mine) + [UNREAD] * len(near),
-        out_specs=VMEM,
+    operands = far + mine + near + others
+    stacked, trace = pl.pallas_call(
+        functools.partial(
+            stack_kernel, sizes, rows, size, [tuple(rest) for _, *rest in early], (len(far), 2 * len(mine), len(near))
+        ),
+        out_shape=(
+            jax.ShapeDtypeStruct((2 * len(mine) * rows * slots, tall, LANES), jnp.float32),
+            jax.ShapeDtypeStruct((n_row * n_col * n_layer, 1, LANES), jnp.float32),
+        ),
+        in_specs=[SMEM] + [VMEM] * len(operands),
+        out_specs=(VMEM, VMEM),
         compiler_params=LIMIT,
         name="stack",
-    )(*far, *mine, *near)
-    other = exchanged(stacked, "layer", 1)
-
-    trace = pl.pallas_call(
-        functools.partial(trace_kernel, sizes, rows, size, [tuple(rest) for _, *rest in early]),
-        out_shape=jax.ShapeDtypeStruct((n_row * n_col * n_layer, 1, LANES), jnp.float32),
-        in_specs=[SMEM] + [VMEM] * (len(early) + 2) + [UNREAD] * (len(mine) - 1),
-        out_specs=VMEM,
-        compiler_params=LIMIT,
-        name="trace_terms",
-    )(code, stacked, other, *[share for share, *_ in early], *mine[1:])
+    )(code, *operands)
     trace = lax.all_to_all(trace, AXES, 0, 0, tiled=True)
 
     strip = early + late
@@ -237,14 +244,22 @@
     product = pl.pallas_call(
         functools.partial(product_kernel, sizes, [tuple(rest) for _, *rest in strip]),
         out_shape=jax.ShapeDtypeStruct(blocks.shape, jnp.float32),
-        in_specs=[SMEM] + [VMEM] * (len(strip) + 2) + [UNREAD] * (len(mine) - 1),
+        in_specs=[SMEM] + [VMEM] * (len(strip) + 1),
         out_specs=VMEM,
         scratch_shapes=[pltpu.VMEM((3 * size, inner), jnp.bfloat16)]
         + [pltpu.VMEM((inner, slots * LANES), jnp.bfloat16)] * 3,
         compiler_params=LIMIT,
         name="multiply",
-    )(code, stacked, other, *[share for share, *_ in strip], *mine[1:])
-    return product, jnp.sum(trace[:, 0, 0])
+    )(code, stacked, *[share for share, *_ in strip])
+    trace = pl.pallas_call(
+        sum_kernel,
+        out_shape=jax.ShapeDtypeStruct((1, 1), jnp.float32),
+        in_specs=[VMEM],
+        out_specs=VMEM,
+        compiler_params=LIMIT,
+        name="sum",
+    )(trace)
+    return product, trace.reshape(())
 
 
 def solution(mesh):

time: 35.6 us -> 35 us (0.983)
  waiting for transfers between devices: 13.3 us -> 9.85 us
  starting transfers between devices: 13 us -> 14.5 us
  Pallas kernels: 6.81 us -> 8.06 us
    ppermute x3 -> x9, starting transfers between devices: 1.67 us -> 8.32 us  [exchanged(): lax.ppermute(value, axis, [(n, n ^ mask) for n in range(lax.axis_size(axi...]
    ppermute x3 -> x0, starting transfers between devices: 4.03 us -> none  [body(): mine.append(lax.ppermute(packed, ('row', 'layer'), route))]
    ppermute x3 -> x0, waiting for transfers between devices: 3.3 us -> none  [body(): mine.append(lax.ppermute(packed, ('row', 'layer'), route))]
    ppermute x1, starting transfers between devices: 4.1 us -> 2.59 us  [row_strip(): far = lax.ppermute(packed, AXES, route)]
    pallas_call x1, Pallas kernels: 0.11 us -> 0.87 us  [body(): pl.pallas_call(pack_kernel, out_shape=jax.ShapeDtypeStruct((rows * slots,...]
    transpose x1, other arithmetic: 0.01 us -> 0.71 us  [body(): code = jnp.where(occupancy == 1, block_cols, -1).transpose((2, 1, 0))]
    reduce_sum x1 -> x0, other arithmetic: 0.63 us -> none  [body(): return (product, jnp.sum(trace[:, 0, 0]))]
    pallas_call x2, Pallas kernels: 2.2 us -> 2.8 us  [the longest x1 2.25 us: body(): pl.pallas_call(functools.partial(stack_kernel, sizes, rows, size, [tuple(...]
  transfers between devices with their start and end apart: 8 -> 11, of which waited for: 7 -> 4; matrix products, arithmetic and copies ran while one was open for 0% -> 2% of each run, Pallas kernels for 19% -> 19%
where the time goes in v9:
time: 35 us; the launch traced here: 34.7 us
  starting transfers between devices  14.5 us (41%)
  waiting for transfers between devices  9.85 us (28%)
  Pallas kernels  8.06 us (23%)
  local copies, waits for them, and re-layouts  0.95 us (3%)
  other arithmetic  0.71 us (2%)
  between operations  0.68 us (2%)
    ppermute x9, starting transfers between devices, exchanged(): lax.ppermute(value, axis, [(n, n ^ mask) for n in range(lax.axis_size(axi...  8.32 us
    ppermute x1, waiting for transfers between devices, row_strip(): far = lax.ppermute(packed, AXES, route)  5.43 us
    pallas_call x1, Pallas kernels, body(): pl.pallas_call(functools.partial(product_kernel, sizes, [tuple(rest) for...  4.39 us
    all_to_all x1, starting transfers between devices, body(): trace = lax.all_to_all(trace, AXES, 0, 0, tiled=True)  3.56 us
    all_to_all x1, waiting for transfers between devices, body(): trace = lax.all_to_all(trace, AXES, 0, 0, tiled=True)  2.74 us
    ppermute x1, starting transfers between devices, row_strip(): far = lax.ppermute(packed, AXES, route)  2.59 us
    pallas_call x1, Pallas kernels, body(): pl.pallas_call(functools.partial(stack_kernel, sizes, rows, size, [tuple(...  2.25 us
    ppermute x9, waiting for transfers between devices, exchanged(): lax.ppermute(value, axis, [(n, n ^ mask) for n in range(lax.axis_size(axi...  1.68 us
  transfers between devices with their start and end apart: 11, of which 4 were waited for; matrix products, arithmetic and copies ran while one was open for 2% of the time, Pallas kernels for 19%

profile of v9, /device:TPU:0, one launch (start us, length us, event | category | flops | bytes accessed | tf_op | source)
XLA Modules:
  0.0 34.7 jit_solution(15835283322063590871)
XLA Ops:
  0.6 0.0 copy-start
  0.6 1.0 %copy-done = f32[2,1,3,96,96]{4,3,2,1,0:T(8,128)S(1)} copy-done((f32[2,1,3,96,96]{4,3,2,1,0:T(8,128)S(1)}, f32[2,1,3,96,96]{4,3,2,1,0:T(8,128)}, u32[]{:S(2)}) %copy-start) | copy-done | bytes 221208
  1.6 0.9 %pack.1.refs_1_ = f32[6,72,128]{2,1,0:T(8,128)S(1)} custom-call(f32[2,1,3,96,96]{4,3,2,1,0:T(8,128)S(1)} %copy-done), custom_call_target="tpu_custom_call" | custom-call | tf_op jit(solution)/shard_map/pack/pallas_call | solution.py:199
  2.5 3.0 %collective-permute-start.2 = (f32[6,72,128]{2,1,0:T(8,128)S(1)}, f32[6,72,128]{2,1,0:T(8,128)S(1)}, u32[]{:S(2)}, u32[]{:S(2)}) collective-permute-start(f32[6,72,128]{2,1,0:T(8,128)S(1)} %pack.1.refs_1_), channel_id=1, source_target_pairs={{0,16},{16,0},{1,17},{17,1},{2,18},{18,2},{3,19},{19,3},{4,20},{20... | collective-permute-start | bytes 663560 | tf_op jit(solution)/shard_map/ppermute | solution.py:167
  5.5 2.6 %collective-permute-start = (f32[6,72,128]{2,1,0:T(8,128)S(1)}, f32[6,72,128]{2,1,0:T(8,128)S(1)}, u32[]{:S(2)}, u32[]{:S(2)}) collective-permute-start(f32[6,72,128]{2,1,0:T(8,128)S(1)} %pack.1.refs_1_), channel_id=1, source_target_pairs={{0,8},{1,9},{2,10},{3,11},{4,12},{5,13},{6,14},{7,15},{8,0},{9,1},... | collective-permute-start | bytes 663560 | tf_op jit(solution)/shard_map/ppermute | solution.py:187
  8.1 1.5 %collective-permute-start.1 = (f32[6,72,128]{2,1,0:T(8,128)S(1)}, f32[6,72,128]{2,1,0:T(8,128)S(1)}, u32[]{:S(2)}, u32[]{:S(2)}) collective-permute-start(f32[6,72,128]{2,1,0:T(8,128)S(1)} %pack.1.refs_1_), channel_id=1, source_target_pairs={{0,2},{1,3},{2,0},{3,1},{4,6},{5,7},{6,4},{7,5},{8,10},{9,11},{10,... | collective-permute-start | bytes 663560 | tf_op jit(solution)/shard_map/ppermute | solution.py:167
  9.6 1.6 %collective-permute-start.4 = (f32[6,72,128]{2,1,0:T(8,128)S(1)}, f32[6,72,128]{2,1,0:T(8,128)S(1)}, u32[]{:S(2)}, u32[]{:S(2)}) collective-permute-start(f32[6,72,128]{2,1,0:T(8,128)S(1)} %pack.1.refs_1_), channel_id=1, source_target_pairs={{0,4},{4,0},{8,12},{12,8},{1,5},{5,1},{9,13},{13,9},{2,6},{6,2},{1... | collective-permute-start | bytes 663560 | tf_op jit(solution)/shard_map/ppermute | solution.py:167
  11.2 0.0 collective-permute-done.2.refs_3_
  11.2 1.5 %collective-permute-start.3 = (f32[6,72,128]{2,1,0:T(8,128)S(1)}, f32[6,72,128]{2,1,0:T(8,128)S(1)}, u32[]{:S(2)}, u32[]{:S(2)}) collective-permute-start(f32[6,72,128]{2,1,0:T(8,128)S(1)} %collective-permute-done.2.refs_3_), channel_id=1, source_target_pairs={{0,2},{1,3},{2,0},{3,1},{4,6},{5,7},{6,4},{7,5},{8,10},{9,11},{10,... | collective-permute-start | bytes 663560 | tf_op jit(solution)/shard_map/ppermute | solution.py:167
  12.7 0.0 collective-permute-start.5
  12.7 5.4 %collective-permute-done.refs_0_.refs_3_ = f32[6,72,128]{2,1,0:T(8,128)S(1)} collective-permute-done((f32[6,72,128]{2,1,0:T(8,128)S(1)}, f32[6,72,128]{2,1,0:T(8,128)S(1)}, u32[]{:S(2)}, u32[]{:S(2)}) %collective-permute-start) | collective-permute-done | bytes 221216 | tf_op jit(solution)/shard_map/ppermute | solution.py:187
  18.1 0.0 collective-permute-start.7
  18.1 0.0 collective-permute-done.1.refs_2_
  18.1 0.5 %collective-permute-start.6 = (f32[6,72,128]{2,1,0:T(8,128)S(1)}, f32[6,72,128]{2,1,0:T(8,128)S(1)}, u32[]{:S(2)}, u32[]{:S(2)}) collective-permute-start(f32[6,72,128]{2,1,0:T(8,128)S(1)} %collective-permute-done.1.refs_2_), channel_id=1, source_target_pairs={{0,1},{1,0},{2,3},{3,2},{4,5},{5,4},{6,7},{7,6},{8,9},{9,8},{10,11... | collective-permute-start | bytes 663560 | tf_op jit(solution)/shard_map/ppermute | solution.py:167
  18.6 0.9 %collective-permute-done.4.refs_5_.refs_2_ = f32[6,72,128]{2,1,0:T(8,128)S(1)} collective-permute-done((f32[6,72,128]{2,1,0:T(8,128)S(1)}, f32[6,72,128]{2,1,0:T(8,128)S(1)}, u32[]{:S(2)}, u32[]{:S(2)}) %collective-permute-start.4) | collective-permute-done | bytes 221216 | tf_op jit(solution)/shard_map/ppermute | solution.py:167
  19.5 0.2 collective-permute-start.9
  19.7 0.0 collective-permute-done.3.refs_4_
  19.7 0.0 collective-permute-start.8
  19.7 0.7 %select_bitcast_fusion.code_ref = s32[3,4,16]{2,1,0:T(4,128)S(1)} fusion(s32[16,4,3]{0,1,2:T(4,128)} %param.4, s32[16,4,3]{0,1,2:T(4,128)} %param.5), kind=kLoop, calls=%fused_computation | loop fusion | flops 384 | bytes 2304 | tf_op jit(solution)/shard_map/transpose | solution.py:197
  20.5 0.0 collective-permute-done.5.refs_6_
  20.5 0.0 collective-permute-done.7.refs_8_
  20.5 0.0 collective-permute-done.6.refs_7_
  20.5 0.7 %collective-permute-done.8.refs_9_ = f32[6,72,128]{2,1,0:T(8,128)S(1)} collective-permute-done((f32[6,72,128]{2,1,0:T(8,128)S(1)}, f32[6,72,128]{2,1,0:T(8,128)S(1)}, u32[]{:S(2)}, u32[]{:S(2)}) %collective-permute-start.8) | collective-permute-done | bytes 221216 | tf_op jit(solution)/shard_map/ppermute | solution.py:167
  21.2 2.3 %stack.1 = (f32[48,72,128]{2,1,0:T(8,128)S(1)}, f32[32,1,128]{2,1,0:T(1,128)}) custom-call(s32[3,4,16]{2,1,0:T(4,128)S(1)} %select_bitcast_fusion.code_ref, f32[6,72,128]{2,1,0:T(8,128)S(1)} %collective-permute-done.refs_0_.refs_3_, f32[6,72,128]{2,1,0:T(8,128)S(1)} %pack.1.refs_1_, f32[6,72,128]{2,1,0:T(8,128)S(1)} %collective-permute-done.1.refs_2_, ...), custom_call_target="tpu_custom_call" | custom-call | tf_op jit(solution)/shard_map/stack/pallas_call | solution.py:227
  23.5 3.6 %all-to-all-start = ((f32[32,1,128]{2,1,0:T(1,128)}), f32[32,1,128]{2,1,0:T(1,128)S(1)}, u32[]{:S(2)}, u32[]{:S(2)}) async-start(f32[32,1,128]{2,1,0:T(1,128)} %get-tuple-element.5), calls=%async_computation | async-start | bytes 32768 | tf_op jit(solution)/shard_map/all_to_all | solution.py:240
  27.0 0.0 collective-permute-done.9.refs_4_
  27.0 4.4 %multiply.1 = f32[2,1,3,96,96]{4,3,2,1,0:T(8,128)} custom-call(s32[3,4,16]{2,1,0:T(4,128)S(1)} %select_bitcast_fusion.code_ref, f32[48,72,128]{2,1,0:T(8,128)S(1)} %get-tuple-element.4.refs_0_, f32[6,72,128]{2,1,0:T(8,128)S(1)} %pack.1.refs_1_, f32[6,72,128]{2,1,0:T(8,128)S(1)} %collective-permute-done.4.refs_5_.refs_2_, ...), custom_call_target="tpu_custom_call" | custom-call | tf_op jit(solution)/shard_map/multiply/pallas_call | solution.py:244
  31.4 2.7 %all-to-all-done.terms_ref = f32[32,1,128]{2,1,0:T(1,128)S(1)} async-done(((f32[32,1,128]{2,1,0:T(1,128)}), f32[32,1,128]{2,1,0:T(1,128)S(1)}, u32[]{:S(2)}, u32[]{:S(2)}) %all-to-all-start) | async-done | bytes 16416 | tf_op jit(solution)/shard_map/all_to_all | solution.py:240
  34.2 0.5 %sum.1 = f32[1,1]{1,0:T(1,128)} custom-call(f32[32,1,128]{2,1,0:T(1,128)S(1)} %all-to-all-done.terms_ref), custom_call_target="tpu_custom_call" | custom-call | tf_op jit(solution)/shard_map/sum/pallas_call | solution.py:254
Async XLA Ops:
  0.6 1.0 %copy-start = (f32[2,1,3,96,96]{4,3,2,1,0:T(8,128)S(1)}, f32[2,1,3,96,96]{4,3,2,1,0:T(8,128)}, u32[]{:S(2)}) copy-start(f32[2,1,3,96,96]{4,3,2,1,0:T(8,128)} %x_ref.1) | copy-start | bytes 663556
  2.5 8.7 %collective-permute-start.2 = (f32[6,72,128]{2,1,0:T(8,128)S(1)}, f32[6,72,128]{2,1,0:T(8,128)S(1)}, u32[]{:S(2)}, u32[]{:S(2)}) collective-permute-start(f32[6,72,128]{2,1,0:T(8,128)S(1)} %pack.1.refs_1_), channel_id=1, source_target_pairs={{0,16},{16,0},{1,17},{17,1},{2,18},{18,2},{3,19},{19,3},{4,20},{20... | collective-permute-start | bytes 663560 | tf_op jit(solution)/shard_map/ppermute | solution.py:167
  5.5 12.6 %collective-permute-start = (f32[6,72,128]{2,1,0:T(8,128)S(1)}, f32[6,72,128]{2,1,0:T(8,128)S(1)}, u32[]{:S(2)}, u32[]{:S(2)}) collective-permute-start(f32[6,72,128]{2,1,0:T(8,128)S(1)} %pack.1.refs_1_), channel_id=1, source_target_pairs={{0,8},{1,9},{2,10},{3,11},{4,12},{5,13},{6,14},{7,15},{8,0},{9,1},... | collective-permute-start | bytes 663560 | tf_op jit(solution)/shard_map/ppermute | solution.py:187
  8.1 10.0 %collective-permute-start.1 = (f32[6,72,128]{2,1,0:T(8,128)S(1)}, f32[6,72,128]{2,1,0:T(8,128)S(1)}, u32[]{:S(2)}, u32[]{:S(2)}) collective-permute-start(f32[6,72,128]{2,1,0:T(8,128)S(1)} %pack.1.refs_1_), channel_id=1, source_target_pairs={{0,2},{1,3},{2,0},{3,1},{4,6},{5,7},{6,4},{7,5},{8,10},{9,11},{10,... | collective-permute-start | bytes 663560 | tf_op jit(solution)/shard_map/ppermute | solution.py:167
  9.6 10.0 %collective-permute-start.4 = (f32[6,72,128]{2,1,0:T(8,128)S(1)}, f32[6,72,128]{2,1,0:T(8,128)S(1)}, u32[]{:S(2)}, u32[]{:S(2)}) collective-permute-start(f32[6,72,128]{2,1,0:T(8,128)S(1)} %pack.1.refs_1_), channel_id=1, source_target_pairs={{0,4},{4,0},{8,12},{12,8},{1,5},{5,1},{9,13},{13,9},{2,6},{6,2},{1... | collective-permute-start | bytes 663560 | tf_op jit(solution)/shard_map/ppermute | solution.py:167
  11.2 8.6 %collective-permute-start.3 = (f32[6,72,128]{2,1,0:T(8,128)S(1)}, f32[6,72,128]{2,1,0:T(8,128)S(1)}, u32[]{:S(2)}, u32[]{:S(2)}) collective-permute-start(f32[6,72,128]{2,1,0:T(8,128)S(1)} %collective-permute-done.2.refs_3_), channel_id=1, source_target_pairs={{0,2},{1,3},{2,0},{3,1},{4,6},{5,7},{6,4},{7,5},{8,10},{9,11},{10,... | collective-permute-start | bytes 663560 | tf_op jit(solution)/shard_map/ppermute | solution.py:167
  12.7 7.8 %collective-permute-start.5 = (f32[6,72,128]{2,1,0:T(8,128)S(1)}, f32[6,72,128]{2,1,0:T(8,128)S(1)}, u32[]{:S(2)}, u32[]{:S(2)}) collective-permute-start(f32[6,72,128]{2,1,0:T(8,128)S(1)} %pack.1.refs_1_), channel_id=1, source_target_pairs={{0,1},{1,0},{2,3},{3,2},{4,5},{5,4},{6,7},{7,6},{8,9},{9,8},{10,11... | collective-permute-start | bytes 663560 | tf_op jit(solution)/shard_map/ppermute | solution.py:167
  18.1 2.4 %collective-permute-start.7 = (f32[6,72,128]{2,1,0:T(8,128)S(1)}, f32[6,72,128]{2,1,0:T(8,128)S(1)}, u32[]{:S(2)}, u32[]{:S(2)}) collective-permute-start(f32[6,72,128]{2,1,0:T(8,128)S(1)} %collective-permute-done.2.refs_3_), channel_id=1, source_target_pairs={{0,1},{1,0},{2,3},{3,2},{4,5},{5,4},{6,7},{7,6},{8,9},{9,8},{10,11... | collective-permute-start | bytes 663560 | tf_op jit(solution)/shard_map/ppermute | solution.py:167
  18.1 2.4 %collective-permute-start.6 = (f32[6,72,128]{2,1,0:T(8,128)S(1)}, f32[6,72,128]{2,1,0:T(8,128)S(1)}, u32[]{:S(2)}, u32[]{:S(2)}) collective-permute-start(f32[6,72,128]{2,1,0:T(8,128)S(1)} %collective-permute-done.1.refs_2_), channel_id=1, source_target_pairs={{0,1},{1,0},{2,3},{3,2},{4,5},{5,4},{6,7},{7,6},{8,9},{9,8},{10,11... | collective-permute-start | bytes 663560 | tf_op jit(solution)/shard_map/ppermute | solution.py:167
  19.5 7.5 %collective-permute-start.9 = (f32[6,72,128]{2,1,0:T(8,128)S(1)}, f32[6,72,128]{2,1,0:T(8,128)S(1)}, u32[]{:S(2)}, u32[]{:S(2)}) collective-permute-start(f32[6,72,128]{2,1,0:T(8,128)S(1)} %collective-permute-done.refs_0_.refs_3_), channel_id=1, source_target_pairs={{0,4},{4,0},{8,12},{12,8},{1,5},{5,1},{9,13},{13,9},{2,6},{6,2},{1... | collective-permute-start | bytes 663560 | tf_op jit(solution)/shard_map/ppermute | solution.py:167
  19.7 1.5 %collective-permute-start.8 = (f32[6,72,128]{2,1,0:T(8,128)S(1)}, f32[6,72,128]{2,1,0:T(8,128)S(1)}, u32[]{:S(2)}, u32[]{:S(2)}) collective-permute-start(f32[6,72,128]{2,1,0:T(8,128)S(1)} %collective-permute-done.3.refs_4_), channel_id=1, source_target_pairs={{0,1},{1,0},{2,3},{3,2},{4,5},{5,4},{6,7},{7,6},{8,9},{9,8},{10,11... | collective-permute-start | bytes 663560 | tf_op jit(solution)/shard_map/ppermute | solution.py:167
  23.5 10.7 %all-to-all-start = ((f32[32,1,128]{2,1,0:T(1,128)}), f32[32,1,128]{2,1,0:T(1,128)S(1)}, u32[]{:S(2)}, u32[]{:S(2)}) async-start(f32[32,1,128]{2,1,0:T(1,128)} %get-tuple-element.5), calls=%async_computation | async-start | bytes 32768 | tf_op jit(solution)/shard_map/all_to_all | solution.py:240

commit v10 on v8

--- a/solution.py
+++ b/solution.py
@@ -11,8 +11,8 @@
 AXES = ("row", "col", "layer")
 LIMIT = pltpu.CompilerParams(vmem_limit_bytes=48 * 2 ** 20)
 VMEM = pl.BlockSpec(memory_space=pltpu.VMEM)
+UNREAD = pl.BlockSpec(memory_space=pl.ANY)
 SMEM = pl.BlockSpec(memory_space=pltpu.SMEM)
-UNREAD = pl.BlockSpec(memory_space=pl.ANY)
 
 
 def tall_of(size):
@@ -57,23 +57,26 @@
                 out_ref[n, q * rest:(q + 1) * rest, size:] = x_ref[i, 0, t, tall:, q * spare:(q + 1) * spare]
 
 
-def stack_kernel(first, count, *refs):
-    out_ref = refs[-1]
-    for n, ref in enumerate(refs[first:first + count]):
-        out_ref[n * ref.shape[0]:(n + 1) * ref.shape[0]] = ref[...]
-
-
-def strip_block(sizes, rows, slots, mine_ref, other_ref, contracted):
-    _, _, n_layer = sizes
+def four_by_four(sizes):
+    return sizes[0] == 2 and sizes[1] == 4 and sizes[2] == 4
+
+
+def strip_base(sizes, rows, slots, shares, contracted):
+    n_row, n_col, n_layer = sizes
     chips = n_layer // 2
     my_row, my_layer = lax.axis_index("row"), lax.axis_index("layer")
     source = lax.div(contracted, rows)
     source_row, source_layer = lax.div(source, n_layer), lax.rem(source, n_layer)
-    chip = lax.bitwise_xor(lax.div(source_layer, 2), lax.div(my_layer, 2))
-    base = (lax.bitwise_xor(source_row, my_row) * chips + chip) * (rows * slots)
-    base = base + lax.rem(contracted, rows) * slots
-    same_core = lax.rem(source_layer, 2) == lax.rem(my_layer, 2)
-    return lambda index: jnp.where(same_core, mine_ref[base + index], other_ref[base + index])
+    share = lax.bitwise_xor(source_row, my_row) * chips + lax.bitwise_xor(lax.div(source_layer, 2), lax.div(my_layer, 2))
+    if four_by_four(sizes):
+        share = jnp.where((share >= 2) & (lax.axis_index("col") >= 2), 5 - share, share)
+    other_core = lax.bitwise_xor(lax.rem(source_layer, 2), lax.rem(my_layer, 2))
+    return ((share + other_core * shares) * rows + lax.rem(contracted, rows)) * slots
+
+
+def stack(share_refs, out_ref):
+    for n, ref in enumerate(share_refs):
+        out_ref[n * ref.shape[0]:(n + 1) * ref.shape[0]] = ref[...]
 
 
 def group_at(sizes, here, own_group, values):
@@ -89,18 +92,22 @@
     return index, valid & stored & (target >= 0)
 
 
-def trace_kernel(sizes, rows, size, groups, code_ref, *refs):
-    count = len(groups)
-    (mine_ref, other_ref), strip_refs, total_ref = refs[:2], refs[2:2 + count], refs[-1]
+def mark_kernel(_, out_ref):
+    out_ref[...] = jnp.zeros(out_ref.shape, jnp.float32)
+
+
+def trace_kernel(sizes, rows, size, groups, shares, code_ref, *refs):
+    strip_refs, share_refs = refs[:len(groups)], refs[len(groups):len(groups) + 2 * shares]
+    total_ref, column_ref = refs[-2:]
     slots = code_ref.shape[0]
     pair, here, own_group, number, per_group = place(sizes)
     width = per_group * rows
-
     def straight(block):
         return unpack(block, size)[:, :size]
 
     @pl.when(own_group == here)
     def _():
+        stack(share_refs, column_ref)
         total = jnp.zeros((size, size), jnp.float32)
         for i in range(rows):
             row = pair * rows + i
@@ -110,7 +117,7 @@
                     column = code_ref[t, group, row]
                     contracted = group * width + jnp.maximum(column, 0)
                     index, valid = matched(code_ref, here, contracted, column >= 0, number * rows + i)
-                    block = strip_block(sizes, rows, slots, mine_ref, other_ref, contracted)(index)
+                    block = column_ref[strip_base(sizes, rows, slots, shares, contracted) + index]
                     term = straight(strip_ref[i * slots + t]) * straight(block).T
                     total = total + jnp.where(valid, weight * term, 0.0)
         total_ref[...] = jnp.full(total_ref.shape, jnp.sum(total), jnp.float32)
@@ -120,13 +127,19 @@
         total_ref[...] = jnp.zeros(total_ref.shape, jnp.float32)
 
 
-def product_kernel(sizes, groups, code_ref, *refs):
+def sum_kernel(terms_ref, out_ref):
+    out_ref[...] = jnp.sum(terms_ref[...], axis=0)[:, :1]
+
+
+def product_kernel(sizes, groups, strip_at, share_at, code_ref, *refs):
     count = len(groups)
-    (mine_ref, other_ref), strip_refs = refs[:2], refs[2:2 + count]
-    out_ref, a_ref, *w_refs = refs[-5:]
+    strip_refs, share_refs = [refs[n] for n in strip_at], [refs[n] for n in share_at]
+    shares = len(share_at) // 2
+    out_ref, column_ref, a_ref, *w_refs = refs[-6:]
     rows, _, slots, size, _ = out_ref.shape
     pair, here, own_group, _, per_group = place(sizes)
     width = per_group * rows
+    stack(share_refs, column_ref)
 
     for w_ref in w_refs:
         for j in range(count * slots):
@@ -142,10 +155,10 @@
                     a_ref[n * size:(n + 1) * size, j * LANES:(j + 1) * LANES] = part
                 column = code_ref[t, group, row]
                 contracted = group * width + jnp.maximum(column, 0)
-                read = strip_block(sizes, rows, slots, mine_ref, other_ref, contracted)
+                base = strip_base(sizes, rows, slots, shares, contracted)
                 for s in range(slots):
                     index, valid = matched(code_ref, here, contracted, column >= 0, targets[s])
-                    block = jnp.where(valid, unpack(read(index), size), 0.0)
+                    block = jnp.where(valid, unpack(column_ref[base + index], size), 0.0)
                     for w_ref, part in zip(w_refs, parts_of(block)):
                         w_ref[j * LANES:j * LANES + size, s * LANES:(s + 1) * LANES] = part
 
@@ -201,50 +214,83 @@
     )(blocks)
 
     early, late = row_strip(packed, sizes)
-    mine = [packed]
-    for n in range(1, n_row * chips):
-        row_bits, chip_bits = n // chips, n % chips
-        route = [
-            (a * n_layer + b, (a ^ row_bits) * n_layer + (b ^ (2 * chip_bits))) for a in range(n_row) for b in range(n_layer)
-        ]
-        mine.append(lax.ppermute(packed, ("row", "layer"), route))
+    def in_plane(steps):
+        route = []
+        for a in range(n_row):
+            for c in range(n_col):
+                for b in range(n_layer):
+                    row_bits, chip_bits = steps[c >= n_col // 2]
+                    target = ((a ^ row_bits) * n_col + c) * n_layer + (b ^ (2 * chip_bits))
+                    route.append(((a * n_col + c) * n_layer + b, target))
+        return lax.ppermute(packed, AXES, route)
+
+    if four_by_four(sizes):
+        mine = [packed, in_plane([(0, 1)] * 2), in_plane([(1, 0), (1, 1)]), in_plane([(1, 1), (1, 0)])]
+        needed = 3
+    else:
+        mine = [packed] + [in_plane([(n // chips, n % chips)] * 2) for n in range(1, n_row * chips)]
+        needed = len(mine)
     early = [(exchanged(packed, "col", 1) if share is None else share, *rest) for share, *rest in early]
+    others = [exchanged(share, "layer", 1) for share in mine]
+
+    def column(count):
+        return jax.ShapeDtypeStruct((2 * count * rows * slots, tall, LANES), jnp.float32)
 
     far = [share for share, value, _, _ in early if value > 1]
-    near = [share for share, value, _, _ in early if value == 1]
-    stacked = pl.pallas_call(
-        functools.partial(stack_kernel, len(far), len(mine)),
-        out_shape=jax.ShapeDtypeStruct((len(mine) * rows * slots, tall, LANES), jnp.float32),
-        in_specs=[UNREAD] * len(far) + [VMEM] * len(mine) + [UNREAD] * len(near),
-        out_specs=VMEM,
-        compiler_params=LIMIT,
-        name="stack",
-    )(*far, *mine, *near)
-    other = exchanged(stacked, "layer", 1)
-
+    marks = [
+        pl.pallas_call(
+            mark_kernel,
+            out_shape=jax.ShapeDtypeStruct((8, LANES), jnp.float32),
+            in_specs=[UNREAD],
+            out_specs=VMEM,
+            cost_estimate=pl.CostEstimate(flops=int(5e+09), bytes_accessed=0, transcendentals=0),
+            compiler_params=LIMIT,
+            name="mark",
+        )(share)
+        for share in far
+    ]
     trace = pl.pallas_call(
-        functools.partial(trace_kernel, sizes, rows, size, [tuple(rest) for _, *rest in early]),
+        functools.partial(trace_kernel, sizes, rows, size, [tuple(rest) for _, *rest in early], needed),
         out_shape=jax.ShapeDtypeStruct((n_row * n_col * n_layer, 1, LANES), jnp.float32),
-        in_specs=[SMEM] + [VMEM] * (len(early) + 2) + [UNREAD] * (len(mine) - 1),
-        out_specs=VMEM,
+        in_specs=[SMEM] + [VMEM] * (len(early) + 2 * needed) + [UNREAD] * len(marks),
+        out_specs=VMEM,
+        scratch_shapes=[pltpu.VMEM(column(needed).shape, jnp.float32)],
         compiler_params=LIMIT,
         name="trace_terms",
-    )(code, stacked, other, *[share for share, *_ in early], *mine[1:])
+    )(code, *[share for share, *_ in early], *mine[:needed], *others[:needed], *marks)
     trace = lax.all_to_all(trace, AXES, 0, 0, tiled=True)
 
     strip = early + late
     inner = len(strip) * slots * LANES
+    near = [share for share, value, _, _ in early if value == 1]
+    operands = far + mine + near + [share for share, *_ in late] + others
+
+    def at(share):
+        return next(n for n, operand in enumerate(operands) if operand is share)
+
+    strip_at, share_at = [at(share) for share, *_ in strip], [at(share) for share in mine + others]
     product = pl.pallas_call(
-        functools.partial(product_kernel, sizes, [tuple(rest) for _, *rest in strip]),
+        functools.partial(product_kernel, sizes, [tuple(rest) for _, *rest in strip], strip_at, share_at),
         out_shape=jax.ShapeDtypeStruct(blocks.shape, jnp.float32),
-        in_specs=[SMEM] + [VMEM] * (len(strip) + 2) + [UNREAD] * (len(mine) - 1),
-        out_specs=VMEM,
-        scratch_shapes=[pltpu.VMEM((3 * size, inner), jnp.bfloat16)]
+        in_specs=[SMEM] + [VMEM] * len(operands),
+        out_specs=VMEM,
+        scratch_shapes=[
+            pltpu.VMEM(column(len(mine)).shape, jnp.float32),
+            pltpu.VMEM((3 * size, inner), jnp.bfloat16),
+        ]
         + [pltpu.VMEM((inner, slots * LANES), jnp.bfloat16)] * 3,
         compiler_params=LIMIT,
         name="multiply",
-    )(code, stacked, other, *[share for share, *_ in strip], *mine[1:])
-    return product, jnp.sum(trace[:, 0, 0])
+    )(code, *operands)
+    trace = pl.pallas_call(
+        sum_kernel,
+        out_shape=jax.ShapeDtypeStruct((1, 1), jnp.float32),
+        in_specs=[VMEM],
+        out_specs=VMEM,
+        compiler_params=LIMIT,
+        name="sum",
+    )(trace)
+    return product, trace.reshape(())
 
 
 def solution(mesh):

time: 35.6 us -> 33.8 us (0.949)
  waiting for transfers between devices: 13.3 us -> 11.7 us
  other arithmetic: 0.64 us -> 0.01 us
  Pallas kernels: 6.81 us -> 7.29 us
    ppermute x3, waiting for transfers between devices: 3.3 us -> 2.4 us  [in_plane(): return lax.ppermute(packed, AXES, route)]
    ppermute x3 -> x6, waiting for transfers between devices: 2.26 us -> 1.46 us  [exchanged(): lax.ppermute(value, axis, [(n, n ^ mask) for n in range(lax.axis_size(axi...]
    reduce_sum x1 -> x0, other arithmetic: 0.63 us -> none  [body(): return (product, jnp.sum(trace[:, 0, 0]))]
    pallas_call x1 -> x2, Pallas kernels: 0.06 us -> 0.55 us  [the longest x1 0.54 us: body(): pl.pallas_call(sum_kernel, out_shape=jax.ShapeDtypeStruct((1, 1), jnp.flo...]
    ppermute x3 -> x6, starting transfers between devices: 1.67 us -> 1.94 us  [exchanged(): lax.ppermute(value, axis, [(n, n ^ mask) for n in range(lax.axis_size(axi...]
  transfers between devices with their start and end apart: 8 -> 11, of which waited for: 7 -> 5; matrix products, arithmetic and copies ran while one was open for 0% -> 0% of each run, Pallas kernels for 19% -> 20%
where the time goes in v10:
time: 33.8 us; the launch traced here: 33.6 us
  starting transfers between devices  13 us (38%)
  waiting for transfers between devices  11.7 us (35%)
  Pallas kernels  7.29 us (22%)
  local copies, waits for them, and re-layouts  0.96 us (3%)
  between operations  0.7 us (2%)
    ppermute x1, waiting for transfers between devices, row_strip(): far = lax.ppermute(packed, AXES, route)  5.2 us
    pallas_call x1, Pallas kernels, body(): pl.pallas_call(functools.partial(product_kernel, sizes, [tuple(rest) for...  4.47 us
    ppermute x1, starting transfers between devices, row_strip(): far = lax.ppermute(packed, AXES, route)  4.1 us
    ppermute x3, starting transfers between devices, in_plane(): return lax.ppermute(packed, AXES, route)  4.03 us
    all_to_all x1, starting transfers between devices, body(): trace = lax.all_to_all(trace, AXES, 0, 0, tiled=True)  2.91 us
    all_to_all x1, waiting for transfers between devices, body(): trace = lax.all_to_all(trace, AXES, 0, 0, tiled=True)  2.65 us
    ppermute x3, waiting for transfers between devices, in_plane(): return lax.ppermute(packed, AXES, route)  2.4 us
    pallas_call x1, Pallas kernels, body(): pl.pallas_call(functools.partial(trace_kernel, sizes, rows, size, [tuple(...  2.16 us
  transfers between devices with their start and end apart: 11, of which 5 were waited for; matrix products, arithmetic and copies ran while one was open for 0% of the time, Pallas kernels for 20%

profile of v10, /device:TPU:0, one launch (start us, length us, event | category | flops | bytes accessed | tf_op | source)
XLA Modules:
  0.0 33.6 jit_solution(5345746683002567637)
XLA Ops:
  0.6 0.0 copy-start
  0.6 1.0 %copy-done = f32[2,1,3,96,96]{4,3,2,1,0:T(8,128)S(1)} copy-done((f32[2,1,3,96,96]{4,3,2,1,0:T(8,128)S(1)}, f32[2,1,3,96,96]{4,3,2,1,0:T(8,128)}, u32[]{:S(2)}) %copy-start) | copy-done | bytes 221208
  1.6 0.0 copy-start.1
  1.6 0.0 copy-start.2
  1.6 0.1 pack.1.refs_1_.refs_0_.refs_3_
  1.7 4.1 %collective-permute-start = (f32[6,72,128]{2,1,0:T(8,128)S(1)}, f32[6,72,128]{2,1,0:T(8,128)S(1)}, u32[]{:S(2)}, u32[]{:S(2)}) collective-permute-start(f32[6,72,128]{2,1,0:T(8,128)S(1)} %pack.1.refs_1_.refs_0_.refs_3_), channel_id=1, source_target_pairs={{0,8},{1,9},{2,10},{3,11},{4,12},{5,13},{6,14},{7,15},{8,0},{9,1},... | collective-permute-start | bytes 663560 | tf_op jit(solution)/shard_map/ppermute | solution.py:195
  5.8 1.5 %collective-permute-start.1 = (f32[6,72,128]{2,1,0:T(8,128)S(1)}, f32[6,72,128]{2,1,0:T(8,128)S(1)}, u32[]{:S(2)}, u32[]{:S(2)}) collective-permute-start(f32[6,72,128]{2,1,0:T(8,128)S(1)} %pack.1.refs_1_.refs_0_.refs_3_), channel_id=1, source_target_pairs={{0,2},{1,3},{2,0},{3,1},{4,6},{5,7},{6,4},{7,5},{8,10},{9,11},{10,... | collective-permute-start | bytes 663560 | tf_op jit(solution)/shard_map/ppermute | solution.py:225
  7.3 2.5 %collective-permute-start.2 = (f32[6,72,128]{2,1,0:T(8,128)S(1)}, f32[6,72,128]{2,1,0:T(8,128)S(1)}, u32[]{:S(2)}, u32[]{:S(2)}) collective-permute-start(f32[6,72,128]{2,1,0:T(8,128)S(1)} %pack.1.refs_1_.refs_0_.refs_3_), channel_id=1, source_target_pairs={{0,16},{1,17},{2,18},{3,19},{4,20},{5,21},{6,22},{7,23},{8,26},{9,... | collective-permute-start | bytes 663560 | tf_op jit(solution)/shard_map/ppermute | solution.py:225
  9.8 0.0 collective-permute-start.3
  9.8 1.0 %collective-permute-start.4 = (f32[6,72,128]{2,1,0:T(8,128)S(1)}, f32[6,72,128]{2,1,0:T(8,128)S(1)}, u32[]{:S(2)}, u32[]{:S(2)}) collective-permute-start(f32[6,72,128]{2,1,0:T(8,128)S(1)} %pack.1.refs_1_.refs_0_.refs_3_), channel_id=1, source_target_pairs={{0,4},{4,0},{8,12},{12,8},{1,5},{5,1},{9,13},{13,9},{2,6},{6,2},{1... | collective-permute-start | bytes 663560 | tf_op jit(solution)/shard_map/ppermute | solution.py:175
  10.9 0.0 copy-done.1
  10.9 0.0 copy-done.2
  10.9 5.2 %collective-permute-done.refs_0_._.refs_2_ = f32[6,72,128]{2,1,0:T(8,128)S(1)} collective-permute-done((f32[6,72,128]{2,1,0:T(8,128)S(1)}, f32[6,72,128]{2,1,0:T(8,128)S(1)}, u32[]{:S(2)}, u32[]{:S(2)}) %collective-permute-start) | collective-permute-done | bytes 221216 | tf_op jit(solution)/shard_map/ppermute | solution.py:195
  16.1 0.0 collective-permute-start.6
  16.1 0.0 collective-permute-done.1.refs_2_.refs_4_
  16.1 0.7 %collective-permute-start.5 = (f32[6,72,128]{2,1,0:T(8,128)S(1)}, f32[6,72,128]{2,1,0:T(8,128)S(1)}, u32[]{:S(2)}, u32[]{:S(2)}) collective-permute-start(f32[6,72,128]{2,1,0:T(8,128)S(1)} %collective-permute-done.refs_0_._.refs_2_), channel_id=1, source_target_pairs={{0,4},{4,0},{8,12},{12,8},{1,5},{5,1},{9,13},{13,9},{2,6},{6,2},{1... | collective-permute-start | bytes 663560 | tf_op jit(solution)/shard_map/ppermute | solution.py:175
  16.8 0.0 collective-permute-done.2.refs_3_.refs_5_
  16.8 0.2 collective-permute-start.7
  17.0 2.4 %collective-permute-done.3.refs_4_ = f32[6,72,128]{2,1,0:T(8,128)S(1)} collective-permute-done((f32[6,72,128]{2,1,0:T(8,128)S(1)}, f32[6,72,128]{2,1,0:T(8,128)S(1)}, u32[]{:S(2)}, u32[]{:S(2)}) %collective-permute-start.3) | collective-permute-done | bytes 221216 | tf_op jit(solution)/shard_map/ppermute | solution.py:225
  19.4 0.0 collective-permute-start.8
  19.4 0.8 %collective-permute-done.4.refs_5_.refs_1_ = f32[6,72,128]{2,1,0:T(8,128)S(1)} collective-permute-done((f32[6,72,128]{2,1,0:T(8,128)S(1)}, f32[6,72,128]{2,1,0:T(8,128)S(1)}, u32[]{:S(2)}, u32[]{:S(2)}) %collective-permute-start.4) | collective-permute-done | bytes 221216 | tf_op jit(solution)/shard_map/ppermute | solution.py:175
  20.2 0.0 collective-permute-start.9
  20.2 0.0 collective-permute-done.6.refs_7_.refs_6_
  20.2 0.0 collective-permute-done.7.refs_8_.refs_7_
  20.2 0.7 %collective-permute-done.8.refs_9_.refs_8_ = f32[6,72,128]{2,1,0:T(8,128)S(1)} collective-permute-done((f32[6,72,128]{2,1,0:T(8,128)S(1)}, f32[6,72,128]{2,1,0:T(8,128)S(1)}, u32[]{:S(2)}, u32[]{:S(2)}) %collective-permute-start.8) | collective-permute-done | bytes 221216 | tf_op jit(solution)/shard_map/ppermute | solution.py:175
  20.9 2.2 %trace_terms.1 = f32[32,1,128]{2,1,0:T(1,128)} custom-call(s32[3,4,16]{2,1,0:T(4,128)S(1)} %select_bitcast_fusion.code_ref, f32[6,72,128]{2,1,0:T(8,128)S(1)} %pack.1.refs_1_.refs_0_.refs_3_, f32[6,72,128]{2,1,0:T(8,128)S(1)} %collective-permute-done.4.refs_5_.refs_1_, f32[6,72,128]{2,1,0:T(8,128)S(1)} %collective-permute-done.refs_0_._.refs_2_, ...), custom_call_target="tpu_custom_call" | custom-call | tf_op jit(solution)/shard_map/trace_terms/pallas_call | solution.py:252
  23.0 2.9 %all-to-all-start = ((f32[32,1,128]{2,1,0:T(1,128)}), f32[32,1,128]{2,1,0:T(1,128)S(1)}, u32[]{:S(2)}, u32[]{:S(2)}) async-start(f32[32,1,128]{2,1,0:T(1,128)} %trace_terms.1), calls=%async_computation | async-start | bytes 32768 | tf_op jit(solution)/shard_map/all_to_all | solution.py:261
  25.9 0.0 collective-permute-done.5.refs_6_
  26.0 0.0 collective-permute-done.9.refs_10_
  26.0 4.5 %multiply.1 = f32[2,1,3,96,96]{4,3,2,1,0:T(8,128)} custom-call(s32[3,4,16]{2,1,0:T(4,128)S(1)} %select_bitcast_fusion.code_ref, f32[6,72,128]{2,1,0:T(8,128)S(1)} %collective-permute-done.refs_0_._.refs_2_, f32[6,72,128]{2,1,0:T(8,128)S(1)} %pack.1.refs_1_.refs_0_.refs_3_, f32[6,72,128]{2,1,0:T(8,128)S(1)} %collective-permute-done.1.refs_2_.refs_4_, ...), custom_call_target="tpu_custom_call" | custom-call | tf_op jit(solution)/shard_map/multiply/pallas_call | solution.py:272
  30.4 2.7 %all-to-all-done.terms_ref = f32[32,1,128]{2,1,0:T(1,128)S(1)} async-done(((f32[32,1,128]{2,1,0:T(1,128)}), f32[32,1,128]{2,1,0:T(1,128)S(1)}, u32[]{:S(2)}, u32[]{:S(2)}) %all-to-all-start) | async-done | bytes 16416 | tf_op jit(solution)/shard_map/all_to_all | solution.py:261
  33.1 0.5 %sum.1 = f32[1,1]{1,0:T(1,128)} custom-call(f32[32,1,128]{2,1,0:T(1,128)S(1)} %all-to-all-done.terms_ref), custom_call_target="tpu_custom_call" | custom-call | tf_op jit(solution)/shard_map/sum/pallas_call | solution.py:285
  (2 shorter events, 0.0 us)
Async XLA Ops:
  0.6 1.0 %copy-start = (f32[2,1,3,96,96]{4,3,2,1,0:T(8,128)S(1)}, f32[2,1,3,96,96]{4,3,2,1,0:T(8,128)}, u32[]{:S(2)}) copy-start(f32[2,1,3,96,96]{4,3,2,1,0:T(8,128)} %x_ref.1) | copy-start | bytes 663556
  1.6 9.3 %copy-start.1 = (s32[16,4,3]{0,1,2:T(4,128)S(1)}, s32[16,4,3]{0,1,2:T(4,128)}, u32[]{:S(2)}) copy-start(s32[16,4,3]{0,1,2:T(4,128)} %param.4) | copy-start | bytes 2308
  1.6 9.3 %copy-start.2 = (s32[16,4,3]{0,1,2:T(4,128)S(1)}, s32[16,4,3]{0,1,2:T(4,128)}, u32[]{:S(2)}) copy-start(s32[16,4,3]{0,1,2:T(4,128)} %param.5) | copy-start | bytes 2308
  1.7 14.4 %collective-permute-start = (f32[6,72,128]{2,1,0:T(8,128)S(1)}, f32[6,72,128]{2,1,0:T(8,128)S(1)}, u32[]{:S(2)}, u32[]{:S(2)}) collective-permute-start(f32[6,72,128]{2,1,0:T(8,128)S(1)} %pack.1.refs_1_.refs_0_.refs_3_), channel_id=1, source_target_pairs={{0,8},{1,9},{2,10},{3,11},{4,12},{5,13},{6,14},{7,15},{8,0},{9,1},... | collective-permute-start | bytes 663560 | tf_op jit(solution)/shard_map/ppermute | solution.py:195
  5.8 10.3 %collective-permute-start.1 = (f32[6,72,128]{2,1,0:T(8,128)S(1)}, f32[6,72,128]{2,1,0:T(8,128)S(1)}, u32[]{:S(2)}, u32[]{:S(2)}) collective-permute-start(f32[6,72,128]{2,1,0:T(8,128)S(1)} %pack.1.refs_1_.refs_0_.refs_3_), channel_id=1, source_target_pairs={{0,2},{1,3},{2,0},{3,1},{4,6},{5,7},{6,4},{7,5},{8,10},{9,11},{10,... | collective-permute-start | bytes 663560 | tf_op jit(solution)/shard_map/ppermute | solution.py:225
  7.3 9.4 %collective-permute-start.2 = (f32[6,72,128]{2,1,0:T(8,128)S(1)}, f32[6,72,128]{2,1,0:T(8,128)S(1)}, u32[]{:S(2)}, u32[]{:S(2)}) collective-permute-start(f32[6,72,128]{2,1,0:T(8,128)S(1)} %pack.1.refs_1_.refs_0_.refs_3_), channel_id=1, source_target_pairs={{0,16},{1,17},{2,18},{3,19},{4,20},{5,21},{6,22},{7,23},{8,26},{9,... | collective-permute-start | bytes 663560 | tf_op jit(solution)/shard_map/ppermute | solution.py:225
  9.8 9.5 %collective-permute-start.3 = (f32[6,72,128]{2,1,0:T(8,128)S(1)}, f32[6,72,128]{2,1,0:T(8,128)S(1)}, u32[]{:S(2)}, u32[]{:S(2)}) collective-permute-start(f32[6,72,128]{2,1,0:T(8,128)S(1)} %pack.1.refs_1_.refs_0_.refs_3_), channel_id=1, source_target_pairs={{0,18},{1,19},{2,16},{3,17},{4,22},{5,23},{6,20},{7,21},{8,24},{9,... | collective-permute-start | bytes 663560 | tf_op jit(solution)/shard_map/ppermute | solution.py:225
  9.8 10.3 %collective-permute-start.4 = (f32[6,72,128]{2,1,0:T(8,128)S(1)}, f32[6,72,128]{2,1,0:T(8,128)S(1)}, u32[]{:S(2)}, u32[]{:S(2)}) collective-permute-start(f32[6,72,128]{2,1,0:T(8,128)S(1)} %pack.1.refs_1_.refs_0_.refs_3_), channel_id=1, source_target_pairs={{0,4},{4,0},{8,12},{12,8},{1,5},{5,1},{9,13},{13,9},{2,6},{6,2},{1... | collective-permute-start | bytes 663560 | tf_op jit(solution)/shard_map/ppermute | solution.py:175
  16.1 4.1 %collective-permute-start.6 = (f32[6,72,128]{2,1,0:T(8,128)S(1)}, f32[6,72,128]{2,1,0:T(8,128)S(1)}, u32[]{:S(2)}, u32[]{:S(2)}) collective-permute-start(f32[6,72,128]{2,1,0:T(8,128)S(1)} %pack.1.refs_1_.refs_0_.refs_3_), channel_id=1, source_target_pairs={{0,1},{1,0},{2,3},{3,2},{4,5},{5,4},{6,7},{7,6},{8,9},{9,8},{10,11... | collective-permute-start | bytes 663560 | tf_op jit(solution)/shard_map/ppermute | solution.py:175
  16.1 9.8 %collective-permute-start.5 = (f32[6,72,128]{2,1,0:T(8,128)S(1)}, f32[6,72,128]{2,1,0:T(8,128)S(1)}, u32[]{:S(2)}, u32[]{:S(2)}) collective-permute-start(f32[6,72,128]{2,1,0:T(8,128)S(1)} %collective-permute-done.refs_0_._.refs_2_), channel_id=1, source_target_pairs={{0,4},{4,0},{8,12},{12,8},{1,5},{5,1},{9,13},{13,9},{2,6},{6,2},{1... | collective-permute-start | bytes 663560 | tf_op jit(solution)/shard_map/ppermute | solution.py:175
  16.8 3.4 %collective-permute-start.7 = (f32[6,72,128]{2,1,0:T(8,128)S(1)}, f32[6,72,128]{2,1,0:T(8,128)S(1)}, u32[]{:S(2)}, u32[]{:S(2)}) collective-permute-start(f32[6,72,128]{2,1,0:T(8,128)S(1)} %collective-permute-done.1.refs_2_.refs_4_), channel_id=1, source_target_pairs={{0,1},{1,0},{2,3},{3,2},{4,5},{5,4},{6,7},{7,6},{8,9},{9,8},{10,11... | collective-permute-start | bytes 663560 | tf_op jit(solution)/shard_map/ppermute | solution.py:175
  19.4 1.5 %collective-permute-start.8 = (f32[6,72,128]{2,1,0:T(8,128)S(1)}, f32[6,72,128]{2,1,0:T(8,128)S(1)}, u32[]{:S(2)}, u32[]{:S(2)}) collective-permute-start(f32[6,72,128]{2,1,0:T(8,128)S(1)} %collective-permute-done.2.refs_3_.refs_5_), channel_id=1, source_target_pairs={{0,1},{1,0},{2,3},{3,2},{4,5},{5,4},{6,7},{7,6},{8,9},{9,8},{10,11... | collective-permute-start | bytes 663560 | tf_op jit(solution)/shard_map/ppermute | solution.py:175
  20.2 5.8 %collective-permute-start.9 = (f32[6,72,128]{2,1,0:T(8,128)S(1)}, f32[6,72,128]{2,1,0:T(8,128)S(1)}, u32[]{:S(2)}, u32[]{:S(2)}) collective-permute-start(f32[6,72,128]{2,1,0:T(8,128)S(1)} %collective-permute-done.3.refs_4_), channel_id=1, source_target_pairs={{0,1},{1,0},{2,3},{3,2},{4,5},{5,4},{6,7},{7,6},{8,9},{9,8},{10,11... | collective-permute-start | bytes 663560 | tf_op jit(solution)/shard_map/ppermute | solution.py:175
  23.0 10.1 %all-to-all-start = ((f32[32,1,128]{2,1,0:T(1,128)}), f32[32,1,128]{2,1,0:T(1,128)S(1)}, u32[]{:S(2)}, u32[]{:S(2)}) async-start(f32[32,1,128]{2,1,0:T(1,128)} %trace_terms.1), calls=%async_computation | async-start | bytes 32768 | tf_op jit(solution)/shard_map/all_to_all | solution.py:261

commit v11 on v10

--- a/solution.py
+++ b/solution.py
@@ -75,8 +75,11 @@
 
 
 def stack(share_refs, out_ref):
-    for n, ref in enumerate(share_refs):
-        out_ref[n * ref.shape[0]:(n + 1) * ref.shape[0]] = ref[...]
+    first = 0
+    for ref in share_refs:
+        for part in [ref] if len(ref.shape) == 3 else [ref.at[n] for n in range(ref.shape[0])]:
+            out_ref[first:first + part.shape[0]] = part[...]
+            first += part.shape[0]
 
 
 def group_at(sizes, here, own_group, values):
@@ -92,12 +95,21 @@
     return index, valid & stored & (target >= 0)
 
 
+def copy_kernel(x_ref, _, out_ref):
+    out_ref[...] = x_ref[...]
+
+
+def pair_kernel(x_ref, y_ref, out_ref):
+    out_ref[0] = x_ref[...]
+    out_ref[1] = y_ref[...]
+
+
 def mark_kernel(_, out_ref):
     out_ref[...] = jnp.zeros(out_ref.shape, jnp.float32)
 
 
 def trace_kernel(sizes, rows, size, groups, shares, code_ref, *refs):
-    strip_refs, share_refs = refs[:len(groups)], refs[len(groups):len(groups) + 2 * shares]
+    strip_refs, share_refs = refs[:len(groups)], refs[len(groups):len(groups) + 2 * shares - 1]
     total_ref, column_ref = refs[-2:]
     slots = code_ref.shape[0]
     pair, here, own_group, number, per_group = place(sizes)
@@ -134,7 +146,7 @@
 def product_kernel(sizes, groups, strip_at, share_at, code_ref, *refs):
     count = len(groups)
     strip_refs, share_refs = [refs[n] for n in strip_at], [refs[n] for n in share_at]
-    shares = len(share_at) // 2
+    shares = (len(share_at) + 1) // 2
     out_ref, column_ref, a_ref, *w_refs = refs[-6:]
     rows, _, slots, size, _ = out_ref.shape
     pair, here, own_group, _, per_group = place(sizes)
@@ -231,7 +243,15 @@
         mine = [packed] + [in_plane([(n // chips, n % chips)] * 2) for n in range(1, n_row * chips)]
         needed = len(mine)
     early = [(exchanged(packed, "col", 1) if share is None else share, *rest) for share, *rest in early]
-    others = [exchanged(share, "layer", 1) for share in mine]
+    both = pl.pallas_call(
+        pair_kernel,
+        out_shape=jax.ShapeDtypeStruct((2,) + packed.shape, jnp.float32),
+        in_specs=[VMEM, VMEM],
+        out_specs=VMEM,
+        compiler_params=LIMIT,
+        name="pair",
+    )(*mine[:2])
+    others = [exchanged(both, "layer", 1)] + [exchanged(share, "layer", 1) for share in mine[2:needed]]
 
     def column(count):
         return jax.ShapeDtypeStruct((2 * count * rows * slots, tall, LANES), jnp.float32)
@@ -252,18 +272,28 @@
     trace = pl.pallas_call(
         functools.partial(trace_kernel, sizes, rows, size, [tuple(rest) for _, *rest in early], needed),
         out_shape=jax.ShapeDtypeStruct((n_row * n_col * n_layer, 1, LANES), jnp.float32),
-        in_specs=[SMEM] + [VMEM] * (len(early) + 2 * needed) + [UNREAD] * len(marks),
+        in_specs=[SMEM] + [VMEM] * (len(early) + 2 * needed - 1) + [UNREAD] * len(marks),
         out_specs=VMEM,
         scratch_shapes=[pltpu.VMEM(column(needed).shape, jnp.float32)],
         compiler_params=LIMIT,
         name="trace_terms",
-    )(code, *[share for share, *_ in early], *mine[:needed], *others[:needed], *marks)
+    )(code, *[share for share, *_ in early], *mine[:needed], *others[:needed - 1], *marks)
+    for share in mine[needed:]:
+        held = pl.pallas_call(
+            copy_kernel,
+            out_shape=jax.ShapeDtypeStruct(share.shape, jnp.float32),
+            in_specs=[VMEM, UNREAD],
+            out_specs=VMEM,
+            compiler_params=LIMIT,
+            name="copy",
+        )(share, trace)
+        others.append(exchanged(held, "layer", 1))
     trace = lax.all_to_all(trace, AXES, 0, 0, tiled=True)
 
     strip = early + late
     inner = len(strip) * slots * LANES
     near = [share for share, value, _, _ in early if value == 1]
-    operands = far + mine + near + [share for share, *_ in late] + others
+    operands = mine[::-1] + near + far + [share for share, *_ in late] + others
 
     def at(share):
         return next(n for n, operand in enumerate(operands) if operand is share)

time: 33.8 us -> 37.5 us (1.11)
  blocking collectives: 0 us -> 11.7 us
  waiting for transfers between devices: 11.7 us -> 6.76 us
  starting transfers between devices: 13 us -> 10.4 us
  Pallas kernels: 7.29 us -> 6.76 us
    all_to_all x0 -> x1, blocking collectives: none -> 11.7 us  [body(): trace = lax.all_to_all(trace, AXES, 0, 0, tiled=True)]
    ppermute x1, waiting for transfers between devices: 5.2 us -> 0.01 us  [row_strip(): far = lax.ppermute(packed, AXES, route)]
    ppermute x3, waiting for transfers between devices: 2.4 us -> 6.28 us  [in_plane(): return lax.ppermute(packed, AXES, route)]
    all_to_all x1 -> x0, starting transfers between devices: 2.91 us -> none  [body(): trace = lax.all_to_all(trace, AXES, 0, 0, tiled=True)]
    all_to_all x1 -> x0, waiting for transfers between devices: 2.65 us -> none  [body(): trace = lax.all_to_all(trace, AXES, 0, 0, tiled=True)]
    ppermute x6 -> x5, waiting for transfers between devices: 1.46 us -> 0.48 us  [exchanged(): lax.ppermute(value, axis, [(n, n ^ mask) for n in range(lax.axis_size(axi...]
    ppermute x6 -> x5, starting transfers between devices: 1.94 us -> 2.84 us  [exchanged(): lax.ppermute(value, axis, [(n, n ^ mask) for n in range(lax.axis_size(axi...]
    pallas_call x1, Pallas kernels: 2.16 us -> 1.57 us  [body(): pl.pallas_call(functools.partial(trace_kernel, sizes, rows, size, [tuple(...]
  transfers between devices with their start and end apart: 11 -> 9, of which waited for: 5 -> 3; matrix products, arithmetic and copies ran while one was open for 0% -> 0% of each run, Pallas kernels for 20% -> 6%
where the time goes in v11:
time: 37.5 us; the launch traced here: 37.4 us
  blocking collectives  11.7 us (31%)
  starting transfers between devices  10.4 us (28%)
  Pallas kernels  6.76 us (18%)
  waiting for transfers between devices  6.76 us (18%)
  local copies, waits for them, and re-layouts  0.96 us (3%)
  between operations  0.7 us (2%)
    all_to_all x1, blocking collectives, body(): trace = lax.all_to_all(trace, AXES, 0, 0, tiled=True)  11.7 us
    ppermute x3, waiting for transfers between devices, in_plane(): return lax.ppermute(packed, AXES, route)  6.28 us
    pallas_call x1, Pallas kernels, body(): pl.pallas_call(functools.partial(product_kernel, sizes, [tuple(rest) for...  4.49 us
    ppermute x1, starting transfers between devices, row_strip(): far = lax.ppermute(packed, AXES, route)  4.1 us
    ppermute x3, starting transfers between devices, in_plane(): return lax.ppermute(packed, AXES, route)  3.49 us
    ppermute x5, starting transfers between devices, exchanged(): lax.ppermute(value, axis, [(n, n ^ mask) for n in range(lax.axis_size(axi...  2.84 us
    pallas_call x1, Pallas kernels, body(): pl.pallas_call(functools.partial(trace_kernel, sizes, rows, size, [tuple(...  1.57 us
    unnamed x6, local copies, waits for them, and re-layouts  0.96 us
  transfers between devices with their start and end apart: 9, of which 3 were waited for; matrix products, arithmetic and copies ran while one was open for 0% of the time, Pallas kernels for 6%

profile of v11, /device:TPU:0, one launch (start us, length us, event | category | flops | bytes accessed | tf_op | source)
XLA Modules:
  0.0 37.4 jit_solution(12476542412577715209)
XLA Ops:
  0.6 0.0 copy-start
  0.6 1.0 %copy-done = f32[2,1,3,96,96]{4,3,2,1,0:T(8,128)S(1)} copy-done((f32[2,1,3,96,96]{4,3,2,1,0:T(8,128)S(1)}, f32[2,1,3,96,96]{4,3,2,1,0:T(8,128)}, u32[]{:S(2)}) %copy-start) | copy-done | bytes 221208
  1.6 0.0 copy-start.1
  1.6 0.0 copy-start.2
  1.6 0.1 pack.1.x_ref.refs_0_.refs_3_
  1.7 4.1 %collective-permute-start.4 = (f32[6,72,128]{2,1,0:T(8,128)S(1)}, f32[6,72,128]{2,1,0:T(8,128)S(1)}, u32[]{:S(2)}, u32[]{:S(2)}) collective-permute-start(f32[6,72,128]{2,1,0:T(8,128)S(1)} %pack.1.x_ref.refs_0_.refs_3_), channel_id=1, source_target_pairs={{0,8},{1,9},{2,10},{3,11},{4,12},{5,13},{6,14},{7,15},{8,0},{9,1},... | collective-permute-start | bytes 663560 | tf_op jit(solution)/shard_map/ppermute | solution.py:207
  5.8 1.6 %collective-permute-start.3 = (f32[6,72,128]{2,1,0:T(8,128)S(1)}, f32[6,72,128]{2,1,0:T(8,128)S(1)}, u32[]{:S(2)}, u32[]{:S(2)}) collective-permute-start(f32[6,72,128]{2,1,0:T(8,128)S(1)} %pack.1.x_ref.refs_0_.refs_3_), channel_id=1, source_target_pairs={{0,4},{4,0},{8,12},{12,8},{1,5},{5,1},{9,13},{13,9},{2,6},{6,2},{1... | collective-permute-start | bytes 663560 | tf_op jit(solution)/shard_map/ppermute | solution.py:187
  7.4 1.5 %collective-permute-start.2 = (f32[6,72,128]{2,1,0:T(8,128)S(1)}, f32[6,72,128]{2,1,0:T(8,128)S(1)}, u32[]{:S(2)}, u32[]{:S(2)}) collective-permute-start(f32[6,72,128]{2,1,0:T(8,128)S(1)} %pack.1.x_ref.refs_0_.refs_3_), channel_id=1, source_target_pairs={{0,2},{1,3},{2,0},{3,1},{4,6},{5,7},{6,4},{7,5},{8,10},{9,11},{10,... | collective-permute-start | bytes 663560 | tf_op jit(solution)/shard_map/ppermute | solution.py:237
  8.9 0.9 %collective-permute-start.1 = (f32[6,72,128]{2,1,0:T(8,128)S(1)}, f32[6,72,128]{2,1,0:T(8,128)S(1)}, u32[]{:S(2)}, u32[]{:S(2)}) collective-permute-start(f32[6,72,128]{2,1,0:T(8,128)S(1)} %pack.1.x_ref.refs_0_.refs_3_), channel_id=1, source_target_pairs={{0,16},{1,17},{2,18},{3,19},{4,20},{5,21},{6,22},{7,23},{8,26},{9,... | collective-permute-start | bytes 663560 | tf_op jit(solution)/shard_map/ppermute | solution.py:237
  9.8 1.0 %collective-permute-start = (f32[6,72,128]{2,1,0:T(8,128)S(1)}, f32[6,72,128]{2,1,0:T(8,128)S(1)}, u32[]{:S(2)}, u32[]{:S(2)}) collective-permute-start(f32[6,72,128]{2,1,0:T(8,128)S(1)} %pack.1.x_ref.refs_0_.refs_3_), channel_id=1, source_target_pairs={{0,18},{1,19},{2,16},{3,17},{4,22},{5,23},{6,20},{7,21},{8,24},{9,... | collective-permute-start | bytes 663560 | tf_op jit(solution)/shard_map/ppermute | solution.py:237
  10.9 0.0 copy-done.1
  10.9 0.0 copy-done.2
  10.9 4.0 %collective-permute-done.2.y_ref.refs_4_.refs_2_ = f32[6,72,128]{2,1,0:T(8,128)S(1)} collective-permute-done((f32[6,72,128]{2,1,0:T(8,128)S(1)}, f32[6,72,128]{2,1,0:T(8,128)S(1)}, u32[]{:S(2)}, u32[]{:S(2)}) %collective-permute-start.2) | collective-permute-done | bytes 221216 | tf_op jit(solution)/shard_map/ppermute | solution.py:237
  14.9 0.1 collective-permute-start.6
  15.0 2.3 %collective-permute-done.1.refs_5_.refs_1_ = f32[6,72,128]{2,1,0:T(8,128)S(1)} collective-permute-done((f32[6,72,128]{2,1,0:T(8,128)S(1)}, f32[6,72,128]{2,1,0:T(8,128)S(1)}, u32[]{:S(2)}, u32[]{:S(2)}) %collective-permute-start.1) | collective-permute-done | bytes 221216 | tf_op jit(solution)/shard_map/ppermute | solution.py:237
  17.3 0.0 collective-permute-start.7
  17.3 0.0 collective-permute-done.4._.refs_2_.refs_5_
  17.3 1.0 %collective-permute-start.5 = (f32[6,72,128]{2,1,0:T(8,128)S(1)}, f32[6,72,128]{2,1,0:T(8,128)S(1)}, u32[]{:S(2)}, u32[]{:S(2)}) collective-permute-start(f32[6,72,128]{2,1,0:T(8,128)S(1)} %collective-permute-done.4._.refs_2_.refs_5_), channel_id=1, source_target_pairs={{0,4},{4,0},{8,12},{12,8},{1,5},{5,1},{9,13},{13,9},{2,6},{6,2},{1... | collective-permute-start | bytes 663560 | tf_op jit(solution)/shard_map/ppermute | solution.py:187
  18.3 0.0 collective-permute-done.3.refs_1_.refs_4_
  18.3 0.5 %collective-permute-done.7.refs_7_.refs_8_ = f32[6,72,128]{2,1,0:T(8,128)S(1)} collective-permute-done((f32[6,72,128]{2,1,0:T(8,128)S(1)}, f32[6,72,128]{2,1,0:T(8,128)S(1)}, u32[]{:S(2)}, u32[]{:S(2)}) %collective-permute-start.7) | collective-permute-done | bytes 221216 | tf_op jit(solution)/shard_map/ppermute | solution.py:187
  18.8 0.0 collective-permute-done.6.refs_6_.refs_7_
  18.8 1.6 %trace_terms.1._ = f32[32,1,128]{2,1,0:T(1,128)S(1)} custom-call(s32[3,4,16]{2,1,0:T(4,128)S(1)} %select_bitcast_fusion.code_ref, f32[6,72,128]{2,1,0:T(8,128)S(1)} %pack.1.x_ref.refs_0_.refs_3_, f32[6,72,128]{2,1,0:T(8,128)S(1)} %collective-permute-done.3.refs_1_.refs_4_, f32[6,72,128]{2,1,0:T(8,128)S(1)} %collective-permute-done.4._.refs_2_.refs_5_, ...), custom_call_target="tpu_custom_call" | custom-call | tf_op jit(solution)/shard_map/trace_terms/pallas_call | solution.py:272
  20.3 0.0 collective-permute-done.x_ref.refs_0_
  20.4 0.2 collective-permute-start.8
  20.6 11.7 %all_to_all.5.terms_ref = f32[32,1,128]{2,1,0:T(1,128)S(1)} all-to-all(f32[32,1,128]{2,1,0:T(1,128)S(1)} %trace_terms.1._), channel_id=1, replica_groups=mesh['row'=2,'col'=4,'layer'=4] {'row','col','layer'}, dimensions={0} | all-to-all | bytes 32768 | tf_op jit(solution)/shard_map/all_to_all | solution.py:291
  32.3 0.5 %sum.1 = f32[1,1]{1,0:T(1,128)} custom-call(f32[32,1,128]{2,1,0:T(1,128)S(1)} %all_to_all.5.terms_ref), custom_call_target="tpu_custom_call" | custom-call | tf_op jit(solution)/shard_map/sum/pallas_call | solution.py:315
  32.9 0.0 collective-permute-done.5.refs_6_
  32.9 0.0 collective-permute-done.8.refs_9_
  32.9 4.5 %multiply.1 = f32[2,1,3,96,96]{4,3,2,1,0:T(8,128)} custom-call(s32[3,4,16]{2,1,0:T(4,128)S(1)} %select_bitcast_fusion.code_ref, f32[6,72,128]{2,1,0:T(8,128)S(1)} %collective-permute-done.x_ref.refs_0_, f32[6,72,128]{2,1,0:T(8,128)S(1)} %collective-permute-done.1.refs_5_.refs_1_, f32[6,72,128]{2,1,0:T(8,128)S(1)} %collective-permute-done.2.y_ref.refs_4_.refs_2_, ...), custom_call_target="tpu_custom_call" | custom-call | tf_op jit(solution)/shard_map/multiply/pallas_call | solution.py:302
  (4 shorter events, 0.1 us)
Async XLA Ops:
  0.6 1.0 %copy-start = (f32[2,1,3,96,96]{4,3,2,1,0:T(8,128)S(1)}, f32[2,1,3,96,96]{4,3,2,1,0:T(8,128)}, u32[]{:S(2)}) copy-start(f32[2,1,3,96,96]{4,3,2,1,0:T(8,128)} %x_ref.1) | copy-start | bytes 663556
  1.6 9.3 %copy-start.1 = (s32[16,4,3]{0,1,2:T(4,128)S(1)}, s32[16,4,3]{0,1,2:T(4,128)}, u32[]{:S(2)}) copy-start(s32[16,4,3]{0,1,2:T(4,128)} %param.4) | copy-start | bytes 2308
  1.6 9.3 %copy-start.2 = (s32[16,4,3]{0,1,2:T(4,128)S(1)}, s32[16,4,3]{0,1,2:T(4,128)}, u32[]{:S(2)}) copy-start(s32[16,4,3]{0,1,2:T(4,128)} %param.5) | copy-start | bytes 2308
  1.7 15.6 %collective-permute-start.4 = (f32[6,72,128]{2,1,0:T(8,128)S(1)}, f32[6,72,128]{2,1,0:T(8,128)S(1)}, u32[]{:S(2)}, u32[]{:S(2)}) collective-permute-start(f32[6,72,128]{2,1,0:T(8,128)S(1)} %pack.1.x_ref.refs_0_.refs_3_), channel_id=1, source_target_pairs={{0,8},{1,9},{2,10},{3,11},{4,12},{5,13},{6,14},{7,15},{8,0},{9,1},... | collective-permute-start | bytes 663560 | tf_op jit(solution)/shard_map/ppermute | solution.py:207
  5.8 12.5 %collective-permute-start.3 = (f32[6,72,128]{2,1,0:T(8,128)S(1)}, f32[6,72,128]{2,1,0:T(8,128)S(1)}, u32[]{:S(2)}, u32[]{:S(2)}) collective-permute-start(f32[6,72,128]{2,1,0:T(8,128)S(1)} %pack.1.x_ref.refs_0_.refs_3_), channel_id=1, source_target_pairs={{0,4},{4,0},{8,12},{12,8},{1,5},{5,1},{9,13},{13,9},{2,6},{6,2},{1... | collective-permute-start | bytes 663560 | tf_op jit(solution)/shard_map/ppermute | solution.py:187
  7.4 7.5 %collective-permute-start.2 = (f32[6,72,128]{2,1,0:T(8,128)S(1)}, f32[6,72,128]{2,1,0:T(8,128)S(1)}, u32[]{:S(2)}, u32[]{:S(2)}) collective-permute-start(f32[6,72,128]{2,1,0:T(8,128)S(1)} %pack.1.x_ref.refs_0_.refs_3_), channel_id=1, source_target_pairs={{0,2},{1,3},{2,0},{3,1},{4,6},{5,7},{6,4},{7,5},{8,10},{9,11},{10,... | collective-permute-start | bytes 663560 | tf_op jit(solution)/shard_map/ppermute | solution.py:237
  8.9 8.4 %collective-permute-start.1 = (f32[6,72,128]{2,1,0:T(8,128)S(1)}, f32[6,72,128]{2,1,0:T(8,128)S(1)}, u32[]{:S(2)}, u32[]{:S(2)}) collective-permute-start(f32[6,72,128]{2,1,0:T(8,128)S(1)} %pack.1.x_ref.refs_0_.refs_3_), channel_id=1, source_target_pairs={{0,16},{1,17},{2,18},{3,19},{4,20},{5,21},{6,22},{7,23},{8,26},{9,... | collective-permute-start | bytes 663560 | tf_op jit(solution)/shard_map/ppermute | solution.py:237
  9.8 10.5 %collective-permute-start = (f32[6,72,128]{2,1,0:T(8,128)S(1)}, f32[6,72,128]{2,1,0:T(8,128)S(1)}, u32[]{:S(2)}, u32[]{:S(2)}) collective-permute-start(f32[6,72,128]{2,1,0:T(8,128)S(1)} %pack.1.x_ref.refs_0_.refs_3_), channel_id=1, source_target_pairs={{0,18},{1,19},{2,16},{3,17},{4,22},{5,23},{6,20},{7,21},{8,24},{9,... | collective-permute-start | bytes 663560 | tf_op jit(solution)/shard_map/ppermute | solution.py:237
  14.9 3.9 %collective-permute-start.6 = (f32[2,6,72,128]{3,2,1,0:T(8,128)S(1)}, f32[2,6,72,128]{3,2,1,0:T(8,128)S(1)}, u32[]{:S(2)}, u32[]{:S(2)}) collective-permute-start(f32[2,6,72,128]{3,2,1,0:T(8,128)S(1)} %pair.1), channel_id=1, source_target_pairs={{0,1},{1,0},{2,3},{3,2},{4,5},{5,4},{6,7},{7,6},{8,9},{9,8},{10,11... | collective-permute-start | bytes 1327112 | tf_op jit(solution)/shard_map/ppermute | solution.py:187
  17.3 1.5 %collective-permute-start.7 = (f32[6,72,128]{2,1,0:T(8,128)S(1)}, f32[6,72,128]{2,1,0:T(8,128)S(1)}, u32[]{:S(2)}, u32[]{:S(2)}) collective-permute-start(f32[6,72,128]{2,1,0:T(8,128)S(1)} %collective-permute-done.1.refs_5_.refs_1_), channel_id=1, source_target_pairs={{0,1},{1,0},{2,3},{3,2},{4,5},{5,4},{6,7},{7,6},{8,9},{9,8},{10,11... | collective-permute-start | bytes 663560 | tf_op jit(solution)/shard_map/ppermute | solution.py:187
  17.3 15.6 %collective-permute-start.5 = (f32[6,72,128]{2,1,0:T(8,128)S(1)}, f32[6,72,128]{2,1,0:T(8,128)S(1)}, u32[]{:S(2)}, u32[]{:S(2)}) collective-permute-start(f32[6,72,128]{2,1,0:T(8,128)S(1)} %collective-permute-done.4._.refs_2_.refs_5_), channel_id=1, source_target_pairs={{0,4},{4,0},{8,12},{12,8},{1,5},{5,1},{9,13},{13,9},{2,6},{6,2},{1... | collective-permute-start | bytes 663560 | tf_op jit(solution)/shard_map/ppermute | solution.py:187
  20.4 12.5 %collective-permute-start.8 = (f32[6,72,128]{2,1,0:T(8,128)S(1)}, f32[6,72,128]{2,1,0:T(8,128)S(1)}, u32[]{:S(2)}, u32[]{:S(2)}) collective-permute-start(f32[6,72,128]{2,1,0:T(8,128)S(1)} %copy.6), channel_id=1, source_target_pairs={{0,1},{1,0},{2,3},{3,2},{4,5},{5,4},{6,7},{7,6},{8,9},{9,8},{10,11... | collective-permute-start | bytes 663560 | tf_op jit(solution)/shard_map/ppermute | solution.py:187

commit v12 on v11

--- a/solution.py
+++ b/solution.py
@@ -139,7 +139,7 @@
         total_ref[...] = jnp.zeros(total_ref.shape, jnp.float32)
 
 
-def sum_kernel(terms_ref, out_ref):
+def sum_kernel(terms_ref, _, out_ref):
     out_ref[...] = jnp.sum(terms_ref[...], axis=0)[:, :1]
 
 
@@ -315,11 +315,11 @@
     trace = pl.pallas_call(
         sum_kernel,
         out_shape=jax.ShapeDtypeStruct((1, 1), jnp.float32),
-        in_specs=[VMEM],
+        in_specs=[VMEM, UNREAD],
         out_specs=VMEM,
         compiler_params=LIMIT,
         name="sum",
-    )(trace)
+    )(trace, product)
     return product, trace.reshape(())
 
 

time: 37.5 us -> 34.8 us (0.928)
  blocking collectives: 11.7 us -> 0 us
  starting transfers between devices: 10.4 us -> 15.2 us
  waiting for transfers between devices: 6.76 us -> 9.4 us
  local copies, waits for them, and re-layouts: 0.96 us -> 1.92 us
  Pallas kernels: 6.76 us -> 7.35 us
    all_to_all x1 -> x0, blocking collectives: 11.7 us -> none  [body(): trace = lax.all_to_all(trace, AXES, 0, 0, tiled=True)]
    all_to_all x0 -> x1, starting transfers between devices: none -> 4.79 us  [body(): trace = lax.all_to_all(trace, AXES, 0, 0, tiled=True)]
    all_to_all x0 -> x1, waiting for transfers between devices: none -> 2.64 us  [body(): trace = lax.all_to_all(trace, AXES, 0, 0, tiled=True)]
    unnamed x6 -> x8, local copies, waits for them, and re-layouts: 0.96 us -> 1.92 us
    pallas_call x1, Pallas kernels: 1.57 us -> 2.16 us  [body(): pl.pallas_call(functools.partial(trace_kernel, sizes, rows, size, [tuple(...]
  transfers between devices with their start and end apart: 9 -> 10, of which waited for: 3 -> 4; matrix products, arithmetic and copies ran while one was open for 0% -> 0% of each run, Pallas kernels for 6% -> 19%
where the time goes in v12:
time: 34.8 us; the launch traced here: 34.6 us
  starting transfers between devices  15.2 us (44%)
  waiting for transfers between devices  9.4 us (27%)
  Pallas kernels  7.35 us (21%)
  local copies, waits for them, and re-layouts  1.92 us (6%)
  between operations  0.7 us (2%)
    ppermute x3, waiting for transfers between devices, in_plane(): return lax.ppermute(packed, AXES, route)  6.28 us
    all_to_all x1, starting transfers between devices, body(): trace = lax.all_to_all(trace, AXES, 0, 0, tiled=True)  4.79 us
    pallas_call x1, Pallas kernels, body(): pl.pallas_call(functools.partial(product_kernel, sizes, [tuple(rest) for...  4.48 us
    ppermute x1, starting transfers between devices, row_strip(): far = lax.ppermute(packed, AXES, route)  4.1 us
    ppermute x3, starting transfers between devices, in_plane(): return lax.ppermute(packed, AXES, route)  3.49 us
    ppermute x5, starting transfers between devices, exchanged(): lax.ppermute(value, axis, [(n, n ^ mask) for n in range(lax.axis_size(axi...  2.85 us
    all_to_all x1, waiting for transfers between devices, body(): trace = lax.all_to_all(trace, AXES, 0, 0, tiled=True)  2.64 us
    pallas_call x1, Pallas kernels, body(): pl.pallas_call(functools.partial(trace_kernel, sizes, rows, size, [tuple(...  2.16 us
  transfers between devices with their start and end apart: 10, of which 4 were waited for; matrix products, arithmetic and copies ran while one was open for 0% of the time, Pallas kernels for 19%

profile of v12, /device:TPU:0, one launch (start us, length us, event | category | flops | bytes accessed | tf_op | source)
XLA Modules:
  0.0 34.6 jit_solution(2507767965914644321)
XLA Ops:
  0.6 0.0 copy-start.1
  0.6 1.0 %copy-done.1 = f32[2,1,3,96,96]{4,3,2,1,0:T(8,128)S(1)} copy-done((f32[2,1,3,96,96]{4,3,2,1,0:T(8,128)S(1)}, f32[2,1,3,96,96]{4,3,2,1,0:T(8,128)}, u32[]{:S(2)}) %copy-start.1) | copy-done | bytes 221208
  1.6 0.0 copy-start.2
  1.6 0.0 copy-start.3
  1.6 0.1 pack.1.x_ref.refs_0_.refs_3_
  1.7 4.1 %collective-permute-start.4 = (f32[6,72,128]{2,1,0:T(8,128)S(1)}, f32[6,72,128]{2,1,0:T(8,128)S(1)}, u32[]{:S(2)}, u32[]{:S(2)}) collective-permute-start(f32[6,72,128]{2,1,0:T(8,128)S(1)} %pack.1.x_ref.refs_0_.refs_3_), channel_id=1, source_target_pairs={{0,8},{1,9},{2,10},{3,11},{4,12},{5,13},{6,14},{7,15},{8,0},{9,1},... | collective-permute-start | bytes 663560 | tf_op jit(solution)/shard_map/ppermute | solution.py:207
  5.8 1.6 %collective-permute-start.3 = (f32[6,72,128]{2,1,0:T(8,128)S(1)}, f32[6,72,128]{2,1,0:T(8,128)S(1)}, u32[]{:S(2)}, u32[]{:S(2)}) collective-permute-start(f32[6,72,128]{2,1,0:T(8,128)S(1)} %pack.1.x_ref.refs_0_.refs_3_), channel_id=1, source_target_pairs={{0,4},{4,0},{8,12},{12,8},{1,5},{5,1},{9,13},{13,9},{2,6},{6,2},{1... | collective-permute-start | bytes 663560 | tf_op jit(solution)/shard_map/ppermute | solution.py:187
  7.4 1.5 %collective-permute-start.2 = (f32[6,72,128]{2,1,0:T(8,128)S(1)}, f32[6,72,128]{2,1,0:T(8,128)S(1)}, u32[]{:S(2)}, u32[]{:S(2)}) collective-permute-start(f32[6,72,128]{2,1,0:T(8,128)S(1)} %pack.1.x_ref.refs_0_.refs_3_), channel_id=1, source_target_pairs={{0,2},{1,3},{2,0},{3,1},{4,6},{5,7},{6,4},{7,5},{8,10},{9,11},{10,... | collective-permute-start | bytes 663560 | tf_op jit(solution)/shard_map/ppermute | solution.py:237
  8.9 0.9 %collective-permute-start.1 = (f32[6,72,128]{2,1,0:T(8,128)S(1)}, f32[6,72,128]{2,1,0:T(8,128)S(1)}, u32[]{:S(2)}, u32[]{:S(2)}) collective-permute-start(f32[6,72,128]{2,1,0:T(8,128)S(1)} %pack.1.x_ref.refs_0_.refs_3_), channel_id=1, source_target_pairs={{0,16},{1,17},{2,18},{3,19},{4,20},{5,21},{6,22},{7,23},{8,26},{9,... | collective-permute-start | bytes 663560 | tf_op jit(solution)/shard_map/ppermute | solution.py:237
  9.8 1.0 %collective-permute-start = (f32[6,72,128]{2,1,0:T(8,128)S(1)}, f32[6,72,128]{2,1,0:T(8,128)S(1)}, u32[]{:S(2)}, u32[]{:S(2)}) collective-permute-start(f32[6,72,128]{2,1,0:T(8,128)S(1)} %pack.1.x_ref.refs_0_.refs_3_), channel_id=1, source_target_pairs={{0,18},{1,19},{2,16},{3,17},{4,22},{5,23},{6,20},{7,21},{8,24},{9,... | collective-permute-start | bytes 663560 | tf_op jit(solution)/shard_map/ppermute | solution.py:237
  10.9 0.0 copy-done.2
  10.9 0.0 copy-done.3
  10.9 4.0 %collective-permute-done.2.y_ref.refs_4_.refs_2_ = f32[6,72,128]{2,1,0:T(8,128)S(1)} collective-permute-done((f32[6,72,128]{2,1,0:T(8,128)S(1)}, f32[6,72,128]{2,1,0:T(8,128)S(1)}, u32[]{:S(2)}, u32[]{:S(2)}) %collective-permute-start.2) | collective-permute-done | bytes 221216 | tf_op jit(solution)/shard_map/ppermute | solution.py:237
  14.9 0.1 collective-permute-start.6
  15.0 2.3 %collective-permute-done.1.refs_5_.refs_1_ = f32[6,72,128]{2,1,0:T(8,128)S(1)} collective-permute-done((f32[6,72,128]{2,1,0:T(8,128)S(1)}, f32[6,72,128]{2,1,0:T(8,128)S(1)}, u32[]{:S(2)}, u32[]{:S(2)}) %collective-permute-start.1) | collective-permute-done | bytes 221216 | tf_op jit(solution)/shard_map/ppermute | solution.py:237
  17.3 0.0 collective-permute-start.7
  17.3 0.0 collective-permute-done.4._.refs_2_.refs_5_
  17.3 1.0 %collective-permute-start.5 = (f32[6,72,128]{2,1,0:T(8,128)S(1)}, f32[6,72,128]{2,1,0:T(8,128)S(1)}, u32[]{:S(2)}, u32[]{:S(2)}) collective-permute-start(f32[6,72,128]{2,1,0:T(8,128)S(1)} %collective-permute-done.4._.refs_2_.refs_5_), channel_id=1, source_target_pairs={{0,4},{4,0},{8,12},{12,8},{1,5},{5,1},{9,13},{13,9},{2,6},{6,2},{1... | collective-permute-start | bytes 663560 | tf_op jit(solution)/shard_map/ppermute | solution.py:187
  18.3 0.0 collective-permute-done.3.refs_1_.refs_4_
  18.3 0.5 %collective-permute-done.7.refs_7_.refs_8_ = f32[6,72,128]{2,1,0:T(8,128)S(1)} collective-permute-done((f32[6,72,128]{2,1,0:T(8,128)S(1)}, f32[6,72,128]{2,1,0:T(8,128)S(1)}, u32[]{:S(2)}, u32[]{:S(2)}) %collective-permute-start.7) | collective-permute-done | bytes 221216 | tf_op jit(solution)/shard_map/ppermute | solution.py:187
  18.8 0.0 collective-permute-done.6.refs_6_.refs_7_
  18.8 2.2 %trace_terms.1._ = f32[32,1,128]{2,1,0:T(1,128)} custom-call(s32[3,4,16]{2,1,0:T(4,128)S(1)} %select_bitcast_fusion.code_ref, f32[6,72,128]{2,1,0:T(8,128)S(1)} %pack.1.x_ref.refs_0_.refs_3_, f32[6,72,128]{2,1,0:T(8,128)S(1)} %collective-permute-done.3.refs_1_.refs_4_, f32[6,72,128]{2,1,0:T(8,128)S(1)} %collective-permute-done.4._.refs_2_.refs_5_, ...), custom_call_target="tpu_custom_call" | custom-call | tf_op jit(solution)/shard_map/trace_terms/pallas_call | solution.py:272
  20.9 0.0 collective-permute-done.x_ref.refs_0_
  21.0 0.2 collective-permute-start.8
  21.2 4.8 %all-to-all-start = ((f32[32,1,128]{2,1,0:T(1,128)}), f32[32,1,128]{2,1,0:T(1,128)S(1)}, u32[]{:S(2)}, u32[]{:S(2)}) async-start(f32[32,1,128]{2,1,0:T(1,128)} %trace_terms.1._), calls=%async_computation | async-start | bytes 32768 | tf_op jit(solution)/shard_map/all_to_all | solution.py:291
  26.0 0.0 collective-permute-done.5.refs_6_
  26.0 0.0 collective-permute-done.8.refs_9_
  26.0 4.5 %multiply.1._ = f32[2,1,3,96,96]{4,3,2,1,0:T(8,128)} custom-call(s32[3,4,16]{2,1,0:T(4,128)S(1)} %select_bitcast_fusion.code_ref, f32[6,72,128]{2,1,0:T(8,128)S(1)} %collective-permute-done.x_ref.refs_0_, f32[6,72,128]{2,1,0:T(8,128)S(1)} %collective-permute-done.1.refs_5_.refs_1_, f32[6,72,128]{2,1,0:T(8,128)S(1)} %collective-permute-done.2.y_ref.refs_4_.refs_2_, ...), custom_call_target="tpu_custom_call" | custom-call | tf_op jit(solution)/shard_map/multiply/pallas_call | solution.py:302
  30.5 2.6 %all-to-all-done.terms_ref = f32[32,1,128]{2,1,0:T(1,128)S(1)} async-done(((f32[32,1,128]{2,1,0:T(1,128)}), f32[32,1,128]{2,1,0:T(1,128)S(1)}, u32[]{:S(2)}, u32[]{:S(2)}) %all-to-all-start) | async-done | bytes 16416 | tf_op jit(solution)/shard_map/all_to_all | solution.py:291
  33.1 0.0 copy-start
  33.1 1.0 %copy-done = f32[2,1,3,96,96]{4,3,2,1,0:T(8,128)S(1)} copy-done((f32[2,1,3,96,96]{4,3,2,1,0:T(8,128)S(1)}, f32[2,1,3,96,96]{4,3,2,1,0:T(8,128)}, u32[]{:S(2)}) %copy-start) | copy-done | bytes 221208
  34.1 0.5 %sum.1 = f32[1,1]{1,0:T(1,128)} custom-call(f32[32,1,128]{2,1,0:T(1,128)S(1)} %all-to-all-done.terms_ref, f32[2,1,3,96,96]{4,3,2,1,0:T(8,128)S(1)} %copy-done), custom_call_target="tpu_custom_call" | custom-call | tf_op jit(solution)/shard_map/sum/pallas_call | solution.py:315
  (4 shorter events, 0.0 us)
Async XLA Ops:
  0.6 1.0 %copy-start.1 = (f32[2,1,3,96,96]{4,3,2,1,0:T(8,128)S(1)}, f32[2,1,3,96,96]{4,3,2,1,0:T(8,128)}, u32[]{:S(2)}) copy-start(f32[2,1,3,96,96]{4,3,2,1,0:T(8,128)} %x_ref.1) | copy-start | bytes 663556
  1.6 9.3 %copy-start.2 = (s32[16,4,3]{0,1,2:T(4,128)S(1)}, s32[16,4,3]{0,1,2:T(4,128)}, u32[]{:S(2)}) copy-start(s32[16,4,3]{0,1,2:T(4,128)} %param.4) | copy-start | bytes 2308
  1.6 9.3 %copy-start.3 = (s32[16,4,3]{0,1,2:T(4,128)S(1)}, s32[16,4,3]{0,1,2:T(4,128)}, u32[]{:S(2)}) copy-start(s32[16,4,3]{0,1,2:T(4,128)} %param.5) | copy-start | bytes 2308
  1.7 15.6 %collective-permute-start.4 = (f32[6,72,128]{2,1,0:T(8,128)S(1)}, f32[6,72,128]{2,1,0:T(8,128)S(1)}, u32[]{:S(2)}, u32[]{:S(2)}) collective-permute-start(f32[6,72,128]{2,1,0:T(8,128)S(1)} %pack.1.x_ref.refs_0_.refs_3_), channel_id=1, source_target_pairs={{0,8},{1,9},{2,10},{3,11},{4,12},{5,13},{6,14},{7,15},{8,0},{9,1},... | collective-permute-start | bytes 663560 | tf_op jit(solution)/shard_map/ppermute | solution.py:207
  5.8 12.5 %collective-permute-start.3 = (f32[6,72,128]{2,1,0:T(8,128)S(1)}, f32[6,72,128]{2,1,0:T(8,128)S(1)}, u32[]{:S(2)}, u32[]{:S(2)}) collective-permute-start(f32[6,72,128]{2,1,0:T(8,128)S(1)} %pack.1.x_ref.refs_0_.refs_3_), channel_id=1, source_target_pairs={{0,4},{4,0},{8,12},{12,8},{1,5},{5,1},{9,13},{13,9},{2,6},{6,2},{1... | collective-permute-start | bytes 663560 | tf_op jit(solution)/shard_map/ppermute | solution.py:187
  7.4 7.5 %collective-permute-start.2 = (f32[6,72,128]{2,1,0:T(8,128)S(1)}, f32[6,72,128]{2,1,0:T(8,128)S(1)}, u32[]{:S(2)}, u32[]{:S(2)}) collective-permute-start(f32[6,72,128]{2,1,0:T(8,128)S(1)} %pack.1.x_ref.refs_0_.refs_3_), channel_id=1, source_target_pairs={{0,2},{1,3},{2,0},{3,1},{4,6},{5,7},{6,4},{7,5},{8,10},{9,11},{10,... | collective-permute-start | bytes 663560 | tf_op jit(solution)/shard_map/ppermute | solution.py:237
  8.9 8.4 %collective-permute-start.1 = (f32[6,72,128]{2,1,0:T(8,128)S(1)}, f32[6,72,128]{2,1,0:T(8,128)S(1)}, u32[]{:S(2)}, u32[]{:S(2)}) collective-permute-start(f32[6,72,128]{2,1,0:T(8,128)S(1)} %pack.1.x_ref.refs_0_.refs_3_), channel_id=1, source_target_pairs={{0,16},{1,17},{2,18},{3,19},{4,20},{5,21},{6,22},{7,23},{8,26},{9,... | collective-permute-start | bytes 663560 | tf_op jit(solution)/shard_map/ppermute | solution.py:237
  9.8 11.1 %collective-permute-start = (f32[6,72,128]{2,1,0:T(8,128)S(1)}, f32[6,72,128]{2,1,0:T(8,128)S(1)}, u32[]{:S(2)}, u32[]{:S(2)}) collective-permute-start(f32[6,72,128]{2,1,0:T(8,128)S(1)} %pack.1.x_ref.refs_0_.refs_3_), channel_id=1, source_target_pairs={{0,18},{1,19},{2,16},{3,17},{4,22},{5,23},{6,20},{7,21},{8,24},{9,... | collective-permute-start | bytes 663560 | tf_op jit(solution)/shard_map/ppermute | solution.py:237
  14.9 3.9 %collective-permute-start.6 = (f32[2,6,72,128]{3,2,1,0:T(8,128)S(1)}, f32[2,6,72,128]{3,2,1,0:T(8,128)S(1)}, u32[]{:S(2)}, u32[]{:S(2)}) collective-permute-start(f32[2,6,72,128]{3,2,1,0:T(8,128)S(1)} %pair.1), channel_id=1, source_target_pairs={{0,1},{1,0},{2,3},{3,2},{4,5},{5,4},{6,7},{7,6},{8,9},{9,8},{10,11... | collective-permute-start | bytes 1327112 | tf_op jit(solution)/shard_map/ppermute | solution.py:187
  17.3 1.5 %collective-permute-start.7 = (f32[6,72,128]{2,1,0:T(8,128)S(1)}, f32[6,72,128]{2,1,0:T(8,128)S(1)}, u32[]{:S(2)}, u32[]{:S(2)}) collective-permute-start(f32[6,72,128]{2,1,0:T(8,128)S(1)} %collective-permute-done.1.refs_5_.refs_1_), channel_id=1, source_target_pairs={{0,1},{1,0},{2,3},{3,2},{4,5},{5,4},{6,7},{7,6},{8,9},{9,8},{10,11... | collective-permute-start | bytes 663560 | tf_op jit(solution)/shard_map/ppermute | solution.py:187
  17.3 8.7 %collective-permute-start.5 = (f32[6,72,128]{2,1,0:T(8,128)S(1)}, f32[6,72,128]{2,1,0:T(8,128)S(1)}, u32[]{:S(2)}, u32[]{:S(2)}) collective-permute-start(f32[6,72,128]{2,1,0:T(8,128)S(1)} %collective-permute-done.4._.refs_2_.refs_5_), channel_id=1, source_target_pairs={{0,4},{4,0},{8,12},{12,8},{1,5},{5,1},{9,13},{13,9},{2,6},{6,2},{1... | collective-permute-start | bytes 663560 | tf_op jit(solution)/shard_map/ppermute | solution.py:187
  21.0 5.0 %collective-permute-start.8 = (f32[6,72,128]{2,1,0:T(8,128)S(1)}, f32[6,72,128]{2,1,0:T(8,128)S(1)}, u32[]{:S(2)}, u32[]{:S(2)}) collective-permute-start(f32[6,72,128]{2,1,0:T(8,128)S(1)} %copy.6), channel_id=1, source_target_pairs={{0,1},{1,0},{2,3},{3,2},{4,5},{5,4},{6,7},{7,6},{8,9},{9,8},{10,11... | collective-permute-start | bytes 663560 | tf_op jit(solution)/shard_map/ppermute | solution.py:187
  21.2 11.9 %all-to-all-start = ((f32[32,1,128]{2,1,0:T(1,128)}), f32[32,1,128]{2,1,0:T(1,128)S(1)}, u32[]{:S(2)}, u32[]{:S(2)}) async-start(f32[32,1,128]{2,1,0:T(1,128)} %trace_terms.1._), calls=%async_computation | async-start | bytes 32768 | tf_op jit(solution)/shard_map/all_to_all | solution.py:291
  33.1 1.0 %copy-start = (f32[2,1,3,96,96]{4,3,2,1,0:T(8,128)S(1)}, f32[2,1,3,96,96]{4,3,2,1,0:T(8,128)}, u32[]{:S(2)}) copy-start(f32[2,1,3,96,96]{4,3,2,1,0:T(8,128)} %multiply.1._) | copy-start | bytes 663556

commit v13 on v12

--- a/solution.py
+++ b/solution.py
@@ -147,7 +147,8 @@
     count = len(groups)
     strip_refs, share_refs = [refs[n] for n in strip_at], [refs[n] for n in share_at]
     shares = (len(share_at) + 1) // 2
-    out_ref, column_ref, a_ref, *w_refs = refs[-6:]
+    out_ref, end_ref, column_ref, a_ref, *w_refs = refs[-7:]
+    end_ref[...] = jnp.zeros(end_ref.shape, jnp.float32)
     rows, _, slots, size, _ = out_ref.shape
     pair, here, own_group, _, per_group = place(sizes)
     width = per_group * rows
@@ -271,7 +272,7 @@
     ]
     trace = pl.pallas_call(
         functools.partial(trace_kernel, sizes, rows, size, [tuple(rest) for _, *rest in early], needed),
-        out_shape=jax.ShapeDtypeStruct((n_row * n_col * n_layer, 1, LANES), jnp.float32),
+        out_shape=jax.ShapeDtypeStruct((n_row * n_col * chips, 1, LANES), jnp.float32),
         in_specs=[SMEM] + [VMEM] * (len(early) + 2 * needed - 1) + [UNREAD] * len(marks),
         out_specs=VMEM,
         scratch_shapes=[pltpu.VMEM(column(needed).shape, jnp.float32)],
@@ -288,7 +289,9 @@
             name="copy",
         )(share, trace)
         others.append(exchanged(held, "layer", 1))
-    trace = lax.all_to_all(trace, AXES, 0, 0, tiled=True)
+    trace = trace + exchanged(trace, "layer", 1)
+    like = [list(range(core, n_row * n_col * n_layer, 2)) for core in range(2)]
+    trace = lax.all_to_all(trace, AXES, 0, 0, axis_index_groups=like, tiled=True)
 
     strip = early + late
     inner = len(strip) * slots * LANES
@@ -299,11 +302,14 @@
         return next(n for n, operand in enumerate(operands) if operand is share)
 
     strip_at, share_at = [at(share) for share, *_ in strip], [at(share) for share in mine + others]
-    product = pl.pallas_call(
+    product, end = pl.pallas_call(
         functools.partial(product_kernel, sizes, [tuple(rest) for _, *rest in strip], strip_at, share_at),
-        out_shape=jax.ShapeDtypeStruct(blocks.shape, jnp.float32),
+        out_shape=(
+            jax.ShapeDtypeStruct(blocks.shape, jnp.float32),
+            jax.ShapeDtypeStruct((8, LANES), jnp.float32),
+        ),
         in_specs=[SMEM] + [VMEM] * len(operands),
-        out_specs=VMEM,
+        out_specs=(VMEM, VMEM),
         scratch_shapes=[
             pltpu.VMEM(column(len(mine)).shape, jnp.float32),
             pltpu.VMEM((3 * size, inner), jnp.bfloat16),
@@ -319,7 +325,7 @@
         out_specs=VMEM,
         compiler_params=LIMIT,
         name="sum",
-    )(trace, product)
+    )(trace, end)
     return product, trace.reshape(())
 
 

time: 34.8 us -> 36.3 us (1.043)
  starting transfers between devices: 15.2 us -> 16.6 us
  waiting for transfers between devices: 9.4 us -> 10.5 us
  local copies, waits for them, and re-layouts: 1.92 us -> 0.96 us
  Pallas kernels: 7.35 us -> 6.71 us
  other arithmetic: 0.01 us -> 0.6 us
    all_to_all x1, starting transfers between devices: 4.79 us -> 5.79 us  [body(): lax.all_to_all(trace, AXES, 0, 0, axis_index_groups=like, tiled=True)]
    ppermute x5 -> x6, waiting for transfers between devices: 0.48 us -> 1.46 us  [exchanged(): lax.ppermute(value, axis, [(n, n ^ mask) for n in range(lax.axis_size(axi...]
    unnamed x8 -> x6, local copies, waits for them, and re-layouts: 1.92 us -> 0.96 us
    pallas_call x1, Pallas kernels: 2.16 us -> 1.56 us  [body(): pl.pallas_call(functools.partial(trace_kernel, sizes, rows, size, [tuple(...]
    add x0 -> x1, other arithmetic: none -> 0.6 us  [body(): trace = trace + exchanged(trace, 'layer', 1)]
    ppermute x5 -> x6, starting transfers between devices: 2.85 us -> 3.22 us  [exchanged(): lax.ppermute(value, axis, [(n, n ^ mask) for n in range(lax.axis_size(axi...]
  transfers between devices with their start and end apart: 10 -> 11, of which waited for: 4 -> 5; matrix products, arithmetic and copies ran while one was open for 0% -> 2% of each run, Pallas kernels for 19% -> 17%
where the time goes in v13:
time: 36.3 us; the launch traced here: 36.1 us
  starting transfers between devices  16.6 us (46%)
  waiting for transfers between devices  10.5 us (29%)
  Pallas kernels  6.71 us (18%)
  local copies, waits for them, and re-layouts  0.96 us (3%)
  between operations  0.72 us (2%)
  other arithmetic  0.6 us (2%)
    ppermute x3, waiting for transfers between devices, in_plane(): return lax.ppermute(packed, AXES, route)  6.28 us
    all_to_all x1, starting transfers between devices, body(): lax.all_to_all(trace, AXES, 0, 0, axis_index_groups=like, tiled=True)  5.79 us
    pallas_call x1, Pallas kernels, body(): pl.pallas_call(functools.partial(product_kernel, sizes, [tuple(rest) for...  4.47 us
    ppermute x1, starting transfers between devices, row_strip(): far = lax.ppermute(packed, AXES, route)  4.1 us
    ppermute x3, starting transfers between devices, in_plane(): return lax.ppermute(packed, AXES, route)  3.49 us
    ppermute x6, starting transfers between devices, exchanged(): lax.ppermute(value, axis, [(n, n ^ mask) for n in range(lax.axis_size(axi...  3.22 us
    all_to_all x1, waiting for transfers between devices, body(): lax.all_to_all(trace, AXES, 0, 0, axis_index_groups=like, tiled=True)  2.77 us
    pallas_call x1, Pallas kernels, body(): pl.pallas_call(functools.partial(trace_kernel, sizes, rows, size, [tuple(...  1.56 us
  transfers between devices with their start and end apart: 11, of which 5 were waited for; matrix products, arithmetic and copies ran while one was open for 2% of the time, Pallas kernels for 17%

profile of v13, /device:TPU:0, one launch (start us, length us, event | category | flops | bytes accessed | tf_op | source)
XLA Modules:
  0.0 36.1 jit_solution(10969550501975448446)
XLA Ops:
  0.6 0.0 copy-start
  0.6 1.0 %copy-done = f32[2,1,3,96,96]{4,3,2,1,0:T(8,128)S(1)} copy-done((f32[2,1,3,96,96]{4,3,2,1,0:T(8,128)S(1)}, f32[2,1,3,96,96]{4,3,2,1,0:T(8,128)}, u32[]{:S(2)}) %copy-start) | copy-done | bytes 221208
  1.6 0.0 copy-start.1
  1.6 0.1 pack.1.x_ref.refs_0_.refs_3_
  1.7 4.1 %collective-permute-start.4 = (f32[6,72,128]{2,1,0:T(8,128)S(1)}, f32[6,72,128]{2,1,0:T(8,128)S(1)}, u32[]{:S(2)}, u32[]{:S(2)}) collective-permute-start(f32[6,72,128]{2,1,0:T(8,128)S(1)} %pack.1.x_ref.refs_0_.refs_3_), channel_id=1, source_target_pairs={{0,8},{1,9},{2,10},{3,11},{4,12},{5,13},{6,14},{7,15},{8,0},{9,1},... | collective-permute-start | bytes 663560 | tf_op jit(solution)/shard_map/ppermute | solution.py:208
  5.8 1.6 %collective-permute-start.3 = (f32[6,72,128]{2,1,0:T(8,128)S(1)}, f32[6,72,128]{2,1,0:T(8,128)S(1)}, u32[]{:S(2)}, u32[]{:S(2)}) collective-permute-start(f32[6,72,128]{2,1,0:T(8,128)S(1)} %pack.1.x_ref.refs_0_.refs_3_), channel_id=1, source_target_pairs={{0,4},{4,0},{8,12},{12,8},{1,5},{5,1},{9,13},{13,9},{2,6},{6,2},{1... | collective-permute-start | bytes 663560 | tf_op jit(solution)/shard_map/ppermute | solution.py:188
  7.4 1.5 %collective-permute-start.2 = (f32[6,72,128]{2,1,0:T(8,128)S(1)}, f32[6,72,128]{2,1,0:T(8,128)S(1)}, u32[]{:S(2)}, u32[]{:S(2)}) collective-permute-start(f32[6,72,128]{2,1,0:T(8,128)S(1)} %pack.1.x_ref.refs_0_.refs_3_), channel_id=1, source_target_pairs={{0,2},{1,3},{2,0},{3,1},{4,6},{5,7},{6,4},{7,5},{8,10},{9,11},{10,... | collective-permute-start | bytes 663560 | tf_op jit(solution)/shard_map/ppermute | solution.py:238
  8.9 0.9 %collective-permute-start.1 = (f32[6,72,128]{2,1,0:T(8,128)S(1)}, f32[6,72,128]{2,1,0:T(8,128)S(1)}, u32[]{:S(2)}, u32[]{:S(2)}) collective-permute-start(f32[6,72,128]{2,1,0:T(8,128)S(1)} %pack.1.x_ref.refs_0_.refs_3_), channel_id=1, source_target_pairs={{0,16},{1,17},{2,18},{3,19},{4,20},{5,21},{6,22},{7,23},{8,26},{9,... | collective-permute-start | bytes 663560 | tf_op jit(solution)/shard_map/ppermute | solution.py:238
  9.8 1.0 %collective-permute-start = (f32[6,72,128]{2,1,0:T(8,128)S(1)}, f32[6,72,128]{2,1,0:T(8,128)S(1)}, u32[]{:S(2)}, u32[]{:S(2)}) collective-permute-start(f32[6,72,128]{2,1,0:T(8,128)S(1)} %pack.1.x_ref.refs_0_.refs_3_), channel_id=1, source_target_pairs={{0,18},{1,19},{2,16},{3,17},{4,22},{5,23},{6,20},{7,21},{8,24},{9,... | collective-permute-start | bytes 663560 | tf_op jit(solution)/shard_map/ppermute | solution.py:238
  10.9 0.0 copy-done.1
  10.9 0.0 copy-done.2
  10.9 4.0 %collective-permute-done.2.y_ref.refs_4_.refs_2_ = f32[6,72,128]{2,1,0:T(8,128)S(1)} collective-permute-done((f32[6,72,128]{2,1,0:T(8,128)S(1)}, f32[6,72,128]{2,1,0:T(8,128)S(1)}, u32[]{:S(2)}, u32[]{:S(2)}) %collective-permute-start.2) | collective-permute-done | bytes 221216 | tf_op jit(solution)/shard_map/ppermute | solution.py:238
  14.9 0.1 collective-permute-start.6
  15.0 2.3 %collective-permute-done.1.refs_5_.refs_1_ = f32[6,72,128]{2,1,0:T(8,128)S(1)} collective-permute-done((f32[6,72,128]{2,1,0:T(8,128)S(1)}, f32[6,72,128]{2,1,0:T(8,128)S(1)}, u32[]{:S(2)}, u32[]{:S(2)}) %collective-permute-start.1) | collective-permute-done | bytes 221216 | tf_op jit(solution)/shard_map/ppermute | solution.py:238
  17.3 0.0 collective-permute-start.7
  17.3 0.0 collective-permute-done.4._.refs_2_.refs_5_
  17.3 1.0 %collective-permute-start.5 = (f32[6,72,128]{2,1,0:T(8,128)S(1)}, f32[6,72,128]{2,1,0:T(8,128)S(1)}, u32[]{:S(2)}, u32[]{:S(2)}) collective-permute-start(f32[6,72,128]{2,1,0:T(8,128)S(1)} %collective-permute-done.4._.refs_2_.refs_5_), channel_id=1, source_target_pairs={{0,4},{4,0},{8,12},{12,8},{1,5},{5,1},{9,13},{13,9},{2,6},{6,2},{1... | collective-permute-start | bytes 663560 | tf_op jit(solution)/shard_map/ppermute | solution.py:188
  18.3 0.0 collective-permute-done.3.refs_1_.refs_4_
  18.3 0.5 %collective-permute-done.7.refs_7_.refs_8_ = f32[6,72,128]{2,1,0:T(8,128)S(1)} collective-permute-done((f32[6,72,128]{2,1,0:T(8,128)S(1)}, f32[6,72,128]{2,1,0:T(8,128)S(1)}, u32[]{:S(2)}, u32[]{:S(2)}) %collective-permute-start.7) | collective-permute-done | bytes 221216 | tf_op jit(solution)/shard_map/ppermute | solution.py:188
  18.8 0.0 collective-permute-done.6.refs_6_.refs_7_
  18.8 1.6 %trace_terms.1._ = f32[16,1,128]{2,1,0:T(1,128)S(1)} custom-call(s32[3,4,16]{2,1,0:T(4,128)S(1)} %select_bitcast_fusion.code_ref, f32[6,72,128]{2,1,0:T(8,128)S(1)} %pack.1.x_ref.refs_0_.refs_3_, f32[6,72,128]{2,1,0:T(8,128)S(1)} %collective-permute-done.3.refs_1_.refs_4_, f32[6,72,128]{2,1,0:T(8,128)S(1)} %collective-permute-done.4._.refs_2_.refs_5_, ...), custom_call_target="tpu_custom_call" | custom-call | tf_op jit(solution)/shard_map/trace_terms/pallas_call | solution.py:273
  20.3 0.0 collective-permute-done.x_ref.refs_0_
  20.4 0.2 collective-permute-start.8
  20.6 0.4 %collective-permute-start.9 = (f32[16,1,128]{2,1,0:T(1,128)S(1)}, f32[16,1,128]{2,1,0:T(1,128)S(1)}, u32[]{:S(2)}, u32[]{:S(2)}) collective-permute-start(f32[16,1,128]{2,1,0:T(1,128)S(1)} %trace_terms.1._), channel_id=1, source_target_pairs={{0,1},{1,0},{2,3},{3,2},{4,5},{5,4},{6,7},{7,6},{8,9},{9,8},{10,11... | collective-permute-start | bytes 24584 | tf_op jit(solution)/shard_map/ppermute | solution.py:188
  20.9 1.0 %collective-permute-done.9 = f32[16,1,128]{2,1,0:T(1,128)S(1)} collective-permute-done((f32[16,1,128]{2,1,0:T(1,128)S(1)}, f32[16,1,128]{2,1,0:T(1,128)S(1)}, u32[]{:S(2)}, u32[]{:S(2)}) %collective-permute-start.9) | collective-permute-done | bytes 8224 | tf_op jit(solution)/shard_map/ppermute | solution.py:188
  21.9 0.6 %add.3 = f32[16,1,128]{2,1,0:T(1,128)} add(f32[16,1,128]{2,1,0:T(1,128)S(1)} %trace_terms.1._, f32[16,1,128]{2,1,0:T(1,128)S(1)} %collective-permute-done.9) | non-fusion elementwise | flops 2048 | bytes 24576 | tf_op jit(solution)/shard_map/add | solution.py:292
  22.5 5.8 %all-to-all-start = ((f32[16,1,128]{2,1,0:T(1,128)}), f32[16,1,128]{2,1,0:T(1,128)S(1)}, u32[]{:S(2)}, u32[]{:S(2)}) async-start(f32[16,1,128]{2,1,0:T(1,128)} %add.3), calls=%async_computation | async-start | bytes 16384 | tf_op jit(solution)/shard_map/all_to_all | solution.py:294
  28.3 0.0 collective-permute-done.5.refs_6_
  28.3 0.0 collective-permute-done.8.refs_9_
  28.3 4.5 %multiply.1 = (f32[2,1,3,96,96]{4,3,2,1,0:T(8,128)}, f32[8,128]{1,0:T(8,128)S(1)}) custom-call(s32[3,4,16]{2,1,0:T(4,128)S(1)} %select_bitcast_fusion.code_ref, f32[6,72,128]{2,1,0:T(8,128)S(1)} %collective-permute-done.x_ref.refs_0_, f32[6,72,128]{2,1,0:T(8,128)S(1)} %collective-permute-done.1.refs_5_.refs_1_, ...), custom_call_target="tpu_custom_call" | custom-call | tf_op jit(solution)/shard_map/multiply/pallas_call | solution.py:305
  32.8 2.8 %all-to-all-done.terms_ref = f32[16,1,128]{2,1,0:T(1,128)S(1)} async-done(((f32[16,1,128]{2,1,0:T(1,128)}), f32[16,1,128]{2,1,0:T(1,128)S(1)}, u32[]{:S(2)}, u32[]{:S(2)}) %all-to-all-start) | async-done | bytes 8224 | tf_op jit(solution)/shard_map/all_to_all | solution.py:294
  35.6 0.5 %sum.1 = f32[1,1]{1,0:T(1,128)} custom-call(f32[16,1,128]{2,1,0:T(1,128)S(1)} %all-to-all-done.terms_ref, f32[8,128]{1,0:T(8,128)S(1)} %get-tuple-element.5._), custom_call_target="tpu_custom_call" | custom-call | tf_op jit(solution)/shard_map/sum/pallas_call | solution.py:321
  (5 shorter events, 0.1 us)
Async XLA Ops:
  0.6 1.0 %copy-start = (f32[2,1,3,96,96]{4,3,2,1,0:T(8,128)S(1)}, f32[2,1,3,96,96]{4,3,2,1,0:T(8,128)}, u32[]{:S(2)}) copy-start(f32[2,1,3,96,96]{4,3,2,1,0:T(8,128)} %x_ref.1) | copy-start | bytes 663556
  1.6 9.3 %copy-start.1 = (s32[16,4,3]{0,1,2:T(4,128)S(1)}, s32[16,4,3]{0,1,2:T(4,128)}, u32[]{:S(2)}) copy-start(s32[16,4,3]{0,1,2:T(4,128)} %param.4) | copy-start | bytes 2308
  1.6 9.3 %copy-start.2 = (s32[16,4,3]{0,1,2:T(4,128)S(1)}, s32[16,4,3]{0,1,2:T(4,128)}, u32[]{:S(2)}) copy-start(s32[16,4,3]{0,1,2:T(4,128)} %param.5) | copy-start | bytes 2308
  1.7 15.6 %collective-permute-start.4 = (f32[6,72,128]{2,1,0:T(8,128)S(1)}, f32[6,72,128]{2,1,0:T(8,128)S(1)}, u32[]{:S(2)}, u32[]{:S(2)}) collective-permute-start(f32[6,72,128]{2,1,0:T(8,128)S(1)} %pack.1.x_ref.refs_0_.refs_3_), channel_id=1, source_target_pairs={{0,8},{1,9},{2,10},{3,11},{4,12},{5,13},{6,14},{7,15},{8,0},{9,1},... | collective-permute-start | bytes 663560 | tf_op jit(solution)/shard_map/ppermute | solution.py:208
  5.8 12.5 %collective-permute-start.3 = (f32[6,72,128]{2,1,0:T(8,128)S(1)}, f32[6,72,128]{2,1,0:T(8,128)S(1)}, u32[]{:S(2)}, u32[]{:S(2)}) collective-permute-start(f32[6,72,128]{2,1,0:T(8,128)S(1)} %pack.1.x_ref.refs_0_.refs_3_), channel_id=1, source_target_pairs={{0,4},{4,0},{8,12},{12,8},{1,5},{5,1},{9,13},{13,9},{2,6},{6,2},{1... | collective-permute-start | bytes 663560 | tf_op jit(solution)/shard_map/ppermute | solution.py:188
  7.4 7.5 %collective-permute-start.2 = (f32[6,72,128]{2,1,0:T(8,128)S(1)}, f32[6,72,128]{2,1,0:T(8,128)S(1)}, u32[]{:S(2)}, u32[]{:S(2)}) collective-permute-start(f32[6,72,128]{2,1,0:T(8,128)S(1)} %pack.1.x_ref.refs_0_.refs_3_), channel_id=1, source_target_pairs={{0,2},{1,3},{2,0},{3,1},{4,6},{5,7},{6,4},{7,5},{8,10},{9,11},{10,... | collective-permute-start | bytes 663560 | tf_op jit(solution)/shard_map/ppermute | solution.py:238
  8.9 8.4 %collective-permute-start.1 = (f32[6,72,128]{2,1,0:T(8,128)S(1)}, f32[6,72,128]{2,1,0:T(8,128)S(1)}, u32[]{:S(2)}, u32[]{:S(2)}) collective-permute-start(f32[6,72,128]{2,1,0:T(8,128)S(1)} %pack.1.x_ref.refs_0_.refs_3_), channel_id=1, source_target_pairs={{0,16},{1,17},{2,18},{3,19},{4,20},{5,21},{6,22},{7,23},{8,26},{9,... | collective-permute-start | bytes 663560 | tf_op jit(solution)/shard_map/ppermute | solution.py:238
  9.8 10.5 %collective-permute-start = (f32[6,72,128]{2,1,0:T(8,128)S(1)}, f32[6,72,128]{2,1,0:T(8,128)S(1)}, u32[]{:S(2)}, u32[]{:S(2)}) collective-permute-start(f32[6,72,128]{2,1,0:T(8,128)S(1)} %pack.1.x_ref.refs_0_.refs_3_), channel_id=1, source_target_pairs={{0,18},{1,19},{2,16},{3,17},{4,22},{5,23},{6,20},{7,21},{8,24},{9,... | collective-permute-start | bytes 663560 | tf_op jit(solution)/shard_map/ppermute | solution.py:238
  14.9 3.9 %collective-permute-start.6 = (f32[2,6,72,128]{3,2,1,0:T(8,128)S(1)}, f32[2,6,72,128]{3,2,1,0:T(8,128)S(1)}, u32[]{:S(2)}, u32[]{:S(2)}) collective-permute-start(f32[2,6,72,128]{3,2,1,0:T(8,128)S(1)} %pair.1), channel_id=1, source_target_pairs={{0,1},{1,0},{2,3},{3,2},{4,5},{5,4},{6,7},{7,6},{8,9},{9,8},{10,11... | collective-permute-start | bytes 1327112 | tf_op jit(solution)/shard_map/ppermute | solution.py:188
  17.3 1.5 %collective-permute-start.7 = (f32[6,72,128]{2,1,0:T(8,128)S(1)}, f32[6,72,128]{2,1,0:T(8,128)S(1)}, u32[]{:S(2)}, u32[]{:S(2)}) collective-permute-start(f32[6,72,128]{2,1,0:T(8,128)S(1)} %collective-permute-done.1.refs_5_.refs_1_), channel_id=1, source_target_pairs={{0,1},{1,0},{2,3},{3,2},{4,5},{5,4},{6,7},{7,6},{8,9},{9,8},{10,11... | collective-permute-start | bytes 663560 | tf_op jit(solution)/shard_map/ppermute | solution.py:188
  17.3 11.0 %collective-permute-start.5 = (f32[6,72,128]{2,1,0:T(8,128)S(1)}, f32[6,72,128]{2,1,0:T(8,128)S(1)}, u32[]{:S(2)}, u32[]{:S(2)}) collective-permute-start(f32[6,72,128]{2,1,0:T(8,128)S(1)} %collective-permute-done.4._.refs_2_.refs_5_), channel_id=1, source_target_pairs={{0,4},{4,0},{8,12},{12,8},{1,5},{5,1},{9,13},{13,9},{2,6},{6,2},{1... | collective-permute-start | bytes 663560 | tf_op jit(solution)/shard_map/ppermute | solution.py:188
  20.4 8.0 %collective-permute-start.8 = (f32[6,72,128]{2,1,0:T(8,128)S(1)}, f32[6,72,128]{2,1,0:T(8,128)S(1)}, u32[]{:S(2)}, u32[]{:S(2)}) collective-permute-start(f32[6,72,128]{2,1,0:T(8,128)S(1)} %copy.6), channel_id=1, source_target_pairs={{0,1},{1,0},{2,3},{3,2},{4,5},{5,4},{6,7},{7,6},{8,9},{9,8},{10,11... | collective-permute-start | bytes 663560 | tf_op jit(solution)/shard_map/ppermute | solution.py:188
  20.6 1.4 %collective-permute-start.9 = (f32[16,1,128]{2,1,0:T(1,128)S(1)}, f32[16,1,128]{2,1,0:T(1,128)S(1)}, u32[]{:S(2)}, u32[]{:S(2)}) collective-permute-start(f32[16,1,128]{2,1,0:T(1,128)S(1)} %trace_terms.1._), channel_id=1, source_target_pairs={{0,1},{1,0},{2,3},{3,2},{4,5},{5,4},{6,7},{7,6},{8,9},{9,8},{10,11... | collective-permute-start | bytes 24584 | tf_op jit(solution)/shard_map/ppermute | solution.py:188
  22.5 13.1 %all-to-all-start = ((f32[16,1,128]{2,1,0:T(1,128)}), f32[16,1,128]{2,1,0:T(1,128)S(1)}, u32[]{:S(2)}, u32[]{:S(2)}) async-start(f32[16,1,128]{2,1,0:T(1,128)} %add.3), calls=%async_computation | async-start | bytes 16384 | tf_op jit(solution)/shard_map/all_to_all | solution.py:294

commit v14 on v13

--- a/solution.py
+++ b/solution.py
@@ -227,7 +227,17 @@
     )(blocks)
 
     early, late = row_strip(packed, sizes)
-    def in_plane(steps):
+    def copied(share, after):
+        return pl.pallas_call(
+            copy_kernel,
+            out_shape=jax.ShapeDtypeStruct(share.shape, jnp.float32),
+            in_specs=[VMEM, UNREAD],
+            out_specs=VMEM,
+            compiler_params=LIMIT,
+            name="copy",
+        )(share, after)
+
+    def in_plane(steps, value=packed):
         route = []
         for a in range(n_row):
             for c in range(n_col):
@@ -235,10 +245,11 @@
                     row_bits, chip_bits = steps[c >= n_col // 2]
                     target = ((a ^ row_bits) * n_col + c) * n_layer + (b ^ (2 * chip_bits))
                     route.append(((a * n_col + c) * n_layer + b, target))
-        return lax.ppermute(packed, AXES, route)
+        return lax.ppermute(value, AXES, route)
 
     if four_by_four(sizes):
-        mine = [packed, in_plane([(0, 1)] * 2), in_plane([(1, 0), (1, 1)]), in_plane([(1, 1), (1, 0)])]
+        mine = [packed, in_plane([(0, 1)] * 2), in_plane([(1, 0), (1, 1)])]
+        mine.append(in_plane([(1, 1), (1, 0)], copied(packed, mine[1])))
         needed = 3
     else:
         mine = [packed] + [in_plane([(n // chips, n % chips)] * 2) for n in range(1, n_row * chips)]
@@ -272,7 +283,7 @@
     ]
     trace = pl.pallas_call(
         functools.partial(trace_kernel, sizes, rows, size, [tuple(rest) for _, *rest in early], needed),
-        out_shape=jax.ShapeDtypeStruct((n_row * n_col * chips, 1, LANES), jnp.float32),
+        out_shape=jax.ShapeDtypeStruct((n_row * n_col * n_layer, 1, LANES), jnp.float32),
         in_specs=[SMEM] + [VMEM] * (len(early) + 2 * needed - 1) + [UNREAD] * len(marks),
         out_specs=VMEM,
         scratch_shapes=[pltpu.VMEM(column(needed).shape, jnp.float32)],
@@ -280,18 +291,8 @@
         name="trace_terms",
     )(code, *[share for share, *_ in early], *mine[:needed], *others[:needed - 1], *marks)
     for share in mine[needed:]:
-        held = pl.pallas_call(
-            copy_kernel,
-            out_shape=jax.ShapeDtypeStruct(share.shape, jnp.float32),
-            in_specs=[VMEM, UNREAD],
-            out_specs=VMEM,
-            compiler_params=LIMIT,
-            name="copy",
-        )(share, trace)
-        others.append(exchanged(held, "layer", 1))
-    trace = trace + exchanged(trace, "layer", 1)
-    like = [list(range(core, n_row * n_col * n_layer, 2)) for core in range(2)]
-    trace = lax.all_to_all(trace, AXES, 0, 0, axis_index_groups=like, tiled=True)
+        others.append(exchanged(copied(share, trace), "layer", 1))
+    trace = lax.all_to_all(trace, AXES, 0, 0, tiled=True)
 
     strip = early + late
     inner = len(strip) * slots * LANES

time: 36.3 us -> 36.8 us (1.014)
  starting transfers between devices: 16.6 us -> 18.8 us
  waiting for transfers between devices: 10.5 us -> 8.79 us
  Pallas kernels: 6.71 us -> 7.36 us
  other arithmetic: 0.6 us -> 0.01 us
    all_to_all x1, starting transfers between devices: 5.79 us -> 7.01 us  [body(): trace = lax.all_to_all(trace, AXES, 0, 0, tiled=True)]
    ppermute x6 -> x5, waiting for transfers between devices: 1.46 us -> 0.39 us  [exchanged(): lax.ppermute(value, axis, [(n, n ^ mask) for n in range(lax.axis_size(axi...]
    ppermute x3, starting transfers between devices: 3.49 us -> 4.29 us  [in_plane(): return lax.ppermute(value, AXES, route)]
    pallas_call x1, Pallas kernels: 1.56 us -> 2.17 us  [body(): pl.pallas_call(functools.partial(trace_kernel, sizes, rows, size, [tuple(...]
    add x1 -> x0, other arithmetic: 0.6 us -> none  [body(): trace = trace + exchanged(trace, 'layer', 1)]
    ppermute x3, waiting for transfers between devices: 6.28 us -> 5.76 us  [in_plane(): return lax.ppermute(value, AXES, route)]
    ppermute x6 -> x5, starting transfers between devices: 3.22 us -> 3.42 us  [exchanged(): lax.ppermute(value, axis, [(n, n ^ mask) for n in range(lax.axis_size(axi...]
  transfers between devices with their start and end apart: 11 -> 10, of which waited for: 5 -> 4; matrix products, arithmetic and copies ran while one was open for 2% -> 0% of each run, Pallas kernels for 17% -> 18%
where the time goes in v14:
time: 36.8 us; the launch traced here: 36.6 us
  starting transfers between devices  18.8 us (51%)
  waiting for transfers between devices  8.79 us (24%)
  Pallas kernels  7.36 us (20%)
  local copies, waits for them, and re-layouts  0.96 us (3%)
  between operations  0.72 us (2%)
    all_to_all x1, starting transfers between devices, body(): trace = lax.all_to_all(trace, AXES, 0, 0, tiled=True)  7.01 us
    ppermute x3, waiting for transfers between devices, in_plane(): return lax.ppermute(value, AXES, route)  5.76 us
    pallas_call x1, Pallas kernels, body(): pl.pallas_call(functools.partial(product_kernel, sizes, [tuple(rest) for...  4.48 us
    ppermute x3, starting transfers between devices, in_plane(): return lax.ppermute(value, AXES, route)  4.29 us
    ppermute x1, starting transfers between devices, row_strip(): far = lax.ppermute(packed, AXES, route)  4.1 us
    ppermute x5, starting transfers between devices, exchanged(): lax.ppermute(value, axis, [(n, n ^ mask) for n in range(lax.axis_size(axi...  3.42 us
    all_to_all x1, waiting for transfers between devices, body(): trace = lax.all_to_all(trace, AXES, 0, 0, tiled=True)  2.64 us
    pallas_call x1, Pallas kernels, body(): pl.pallas_call(functools.partial(trace_kernel, sizes, rows, size, [tuple(...  2.17 us
  transfers between devices with their start and end apart: 10, of which 4 were waited for; matrix products, arithmetic and copies ran while one was open for 0% of the time, Pallas kernels for 18%

profile of v14, /device:TPU:0, one launch (start us, length us, event | category | flops | bytes accessed | tf_op | source)
XLA Modules:
  0.0 36.6 jit_solution(13676497730991911448)
XLA Ops:
  0.6 0.0 copy-start
  0.6 1.0 %copy-done = f32[2,1,3,96,96]{4,3,2,1,0:T(8,128)S(1)} copy-done((f32[2,1,3,96,96]{4,3,2,1,0:T(8,128)S(1)}, f32[2,1,3,96,96]{4,3,2,1,0:T(8,128)}, u32[]{:S(2)}) %copy-start) | copy-done | bytes 221208
  1.6 0.0 copy-start.1
  1.6 0.0 copy-start.2
  1.6 0.1 pack.1.x_ref.refs_0_.refs_3_
  1.7 4.1 %collective-permute-start.4 = (f32[6,72,128]{2,1,0:T(8,128)S(1)}, f32[6,72,128]{2,1,0:T(8,128)S(1)}, u32[]{:S(2)}, u32[]{:S(2)}) collective-permute-start(f32[6,72,128]{2,1,0:T(8,128)S(1)} %pack.1.x_ref.refs_0_.refs_3_), channel_id=1, source_target_pairs={{0,8},{1,9},{2,10},{3,11},{4,12},{5,13},{6,14},{7,15},{8,0},{9,1},... | collective-permute-start | bytes 663560 | tf_op jit(solution)/shard_map/ppermute | solution.py:208
  5.8 1.6 %collective-permute-start.3 = (f32[6,72,128]{2,1,0:T(8,128)S(1)}, f32[6,72,128]{2,1,0:T(8,128)S(1)}, u32[]{:S(2)}, u32[]{:S(2)}) collective-permute-start(f32[6,72,128]{2,1,0:T(8,128)S(1)} %pack.1.x_ref.refs_0_.refs_3_), channel_id=1, source_target_pairs={{0,4},{4,0},{8,12},{12,8},{1,5},{5,1},{9,13},{13,9},{2,6},{6,2},{1... | collective-permute-start | bytes 663560 | tf_op jit(solution)/shard_map/ppermute | solution.py:188
  7.4 0.9 %collective-permute-start.2 = (f32[6,72,128]{2,1,0:T(8,128)S(1)}, f32[6,72,128]{2,1,0:T(8,128)S(1)}, u32[]{:S(2)}, u32[]{:S(2)}) collective-permute-start(f32[6,72,128]{2,1,0:T(8,128)S(1)} %pack.1.x_ref.refs_0_.refs_3_), channel_id=1, source_target_pairs={{0,16},{1,17},{2,18},{3,19},{4,20},{5,21},{6,22},{7,23},{8,26},{9,... | collective-permute-start | bytes 663560 | tf_op jit(solution)/shard_map/ppermute | solution.py:248
  8.3 1.5 %collective-permute-start = (f32[6,72,128]{2,1,0:T(8,128)S(1)}, f32[6,72,128]{2,1,0:T(8,128)S(1)}, u32[]{:S(2)}, u32[]{:S(2)}) collective-permute-start(f32[6,72,128]{2,1,0:T(8,128)S(1)} %pack.1.x_ref.refs_0_.refs_3_), channel_id=1, source_target_pairs={{0,2},{1,3},{2,0},{3,1},{4,6},{5,7},{6,4},{7,5},{8,10},{9,11},{10,... | collective-permute-start | bytes 663560 | tf_op jit(solution)/shard_map/ppermute | solution.py:248
  9.8 0.0 copy-done.1
  9.8 0.0 copy-done.2
  9.9 5.1 %collective-permute-done._.y_ref.refs_4_.refs_2_ = f32[6,72,128]{2,1,0:T(8,128)S(1)} collective-permute-done((f32[6,72,128]{2,1,0:T(8,128)S(1)}, f32[6,72,128]{2,1,0:T(8,128)S(1)}, u32[]{:S(2)}, u32[]{:S(2)}) %collective-permute-start) | collective-permute-done | bytes 221216 | tf_op jit(solution)/shard_map/ppermute | solution.py:248
  15.0 1.8 %collective-permute-start.1 = (f32[6,72,128]{2,1,0:T(8,128)S(1)}, f32[6,72,128]{2,1,0:T(8,128)S(1)}, u32[]{:S(2)}, u32[]{:S(2)}) collective-permute-start(f32[6,72,128]{2,1,0:T(8,128)S(1)} %copy.7), channel_id=1, source_target_pairs={{0,18},{1,19},{2,16},{3,17},{4,22},{5,23},{6,20},{7,21},{8,24},{9,... | collective-permute-start | bytes 663560 | tf_op jit(solution)/shard_map/ppermute | solution.py:248
  16.8 0.1 collective-permute-start.6
  16.9 0.0 collective-permute-done.2.refs_5_.refs_1_
  16.9 0.5 %collective-permute-start.7 = (f32[6,72,128]{2,1,0:T(8,128)S(1)}, f32[6,72,128]{2,1,0:T(8,128)S(1)}, u32[]{:S(2)}, u32[]{:S(2)}) collective-permute-start(f32[6,72,128]{2,1,0:T(8,128)S(1)} %collective-permute-done.2.refs_5_.refs_1_), channel_id=1, source_target_pairs={{0,1},{1,0},{2,3},{3,2},{4,5},{5,4},{6,7},{7,6},{8,9},{9,8},{10,11... | collective-permute-start | bytes 663560 | tf_op jit(solution)/shard_map/ppermute | solution.py:188
  17.4 0.0 collective-permute-done.4._.refs_2_.refs_5_
  17.4 1.2 %collective-permute-start.5 = (f32[6,72,128]{2,1,0:T(8,128)S(1)}, f32[6,72,128]{2,1,0:T(8,128)S(1)}, u32[]{:S(2)}, u32[]{:S(2)}) collective-permute-start(f32[6,72,128]{2,1,0:T(8,128)S(1)} %collective-permute-done.4._.refs_2_.refs_5_), channel_id=1, source_target_pairs={{0,4},{4,0},{8,12},{12,8},{1,5},{5,1},{9,13},{13,9},{2,6},{6,2},{1... | collective-permute-start | bytes 663560 | tf_op jit(solution)/shard_map/ppermute | solution.py:188
  18.6 0.0 collective-permute-done.3.refs_1_.refs_4_
  18.6 0.4 %collective-permute-done.7.refs_7_.refs_8_ = f32[6,72,128]{2,1,0:T(8,128)S(1)} collective-permute-done((f32[6,72,128]{2,1,0:T(8,128)S(1)}, f32[6,72,128]{2,1,0:T(8,128)S(1)}, u32[]{:S(2)}, u32[]{:S(2)}) %collective-permute-start.7) | collective-permute-done | bytes 221216 | tf_op jit(solution)/shard_map/ppermute | solution.py:188
  19.0 0.0 collective-permute-done.6.refs_6_.refs_7_
  19.0 2.2 %trace_terms.1._ = f32[32,1,128]{2,1,0:T(1,128)} custom-call(s32[3,4,16]{2,1,0:T(4,128)S(1)} %select_bitcast_fusion.code_ref, f32[6,72,128]{2,1,0:T(8,128)S(1)} %pack.1.x_ref.refs_0_.refs_3_, f32[6,72,128]{2,1,0:T(8,128)S(1)} %collective-permute-done.3.refs_1_.refs_4_, f32[6,72,128]{2,1,0:T(8,128)S(1)} %collective-permute-done.4._.refs_2_.refs_5_, ...), custom_call_target="tpu_custom_call" | custom-call | tf_op jit(solution)/shard_map/trace_terms/pallas_call | solution.py:284
  21.2 0.7 %collective-permute-done.1.x_ref.refs_0_ = f32[6,72,128]{2,1,0:T(8,128)S(1)} collective-permute-done((f32[6,72,128]{2,1,0:T(8,128)S(1)}, f32[6,72,128]{2,1,0:T(8,128)S(1)}, u32[]{:S(2)}, u32[]{:S(2)}) %collective-permute-start.1) | collective-permute-done | bytes 221216 | tf_op jit(solution)/shard_map/ppermute | solution.py:248
  21.9 0.1 collective-permute-start.8
  21.9 7.0 %all-to-all-start = ((f32[32,1,128]{2,1,0:T(1,128)}), f32[32,1,128]{2,1,0:T(1,128)S(1)}, u32[]{:S(2)}, u32[]{:S(2)}) async-start(f32[32,1,128]{2,1,0:T(1,128)} %trace_terms.1._), calls=%async_computation | async-start | bytes 32768 | tf_op jit(solution)/shard_map/all_to_all | solution.py:295
  29.0 0.0 collective-permute-done.5.refs_6_
  29.0 0.0 collective-permute-done.8.refs_9_
  29.0 4.5 %multiply.1 = (f32[2,1,3,96,96]{4,3,2,1,0:T(8,128)}, f32[8,128]{1,0:T(8,128)S(1)}) custom-call(s32[3,4,16]{2,1,0:T(4,128)S(1)} %select_bitcast_fusion.code_ref, f32[6,72,128]{2,1,0:T(8,128)S(1)} %collective-permute-done.1.x_ref.refs_0_, f32[6,72,128]{2,1,0:T(8,128)S(1)} %collective-permute-done.2.refs_5_.refs_1_, ...), custom_call_target="tpu_custom_call" | custom-call | tf_op jit(solution)/shard_map/multiply/pallas_call | solution.py:306
  33.5 2.6 %all-to-all-done.terms_ref = f32[32,1,128]{2,1,0:T(1,128)S(1)} async-done(((f32[32,1,128]{2,1,0:T(1,128)}), f32[32,1,128]{2,1,0:T(1,128)S(1)}, u32[]{:S(2)}, u32[]{:S(2)}) %all-to-all-start) | async-done | bytes 16416 | tf_op jit(solution)/shard_map/all_to_all | solution.py:295
  36.1 0.5 %sum.1 = f32[1,1]{1,0:T(1,128)} custom-call(f32[32,1,128]{2,1,0:T(1,128)S(1)} %all-to-all-done.terms_ref, f32[8,128]{1,0:T(8,128)S(1)} %get-tuple-element.5._), custom_call_target="tpu_custom_call" | custom-call | tf_op jit(solution)/shard_map/sum/pallas_call | solution.py:322
  (5 shorter events, 0.1 us)
Async XLA Ops:
  0.6 1.0 %copy-start = (f32[2,1,3,96,96]{4,3,2,1,0:T(8,128)S(1)}, f32[2,1,3,96,96]{4,3,2,1,0:T(8,128)}, u32[]{:S(2)}) copy-start(f32[2,1,3,96,96]{4,3,2,1,0:T(8,128)} %x_ref.1) | copy-start | bytes 663556
  1.6 8.3 %copy-start.1 = (s32[16,4,3]{0,1,2:T(4,128)S(1)}, s32[16,4,3]{0,1,2:T(4,128)}, u32[]{:S(2)}) copy-start(s32[16,4,3]{0,1,2:T(4,128)} %param.4) | copy-start | bytes 2308
  1.6 8.3 %copy-start.2 = (s32[16,4,3]{0,1,2:T(4,128)S(1)}, s32[16,4,3]{0,1,2:T(4,128)}, u32[]{:S(2)}) copy-start(s32[16,4,3]{0,1,2:T(4,128)} %param.5) | copy-start | bytes 2308
  1.7 15.7 %collective-permute-start.4 = (f32[6,72,128]{2,1,0:T(8,128)S(1)}, f32[6,72,128]{2,1,0:T(8,128)S(1)}, u32[]{:S(2)}, u32[]{:S(2)}) collective-permute-start(f32[6,72,128]{2,1,0:T(8,128)S(1)} %pack.1.x_ref.refs_0_.refs_3_), channel_id=1, source_target_pairs={{0,8},{1,9},{2,10},{3,11},{4,12},{5,13},{6,14},{7,15},{8,0},{9,1},... | collective-permute-start | bytes 663560 | tf_op jit(solution)/shard_map/ppermute | solution.py:208
  5.8 12.8 %collective-permute-start.3 = (f32[6,72,128]{2,1,0:T(8,128)S(1)}, f32[6,72,128]{2,1,0:T(8,128)S(1)}, u32[]{:S(2)}, u32[]{:S(2)}) collective-permute-start(f32[6,72,128]{2,1,0:T(8,128)S(1)} %pack.1.x_ref.refs_0_.refs_3_), channel_id=1, source_target_pairs={{0,4},{4,0},{8,12},{12,8},{1,5},{5,1},{9,13},{13,9},{2,6},{6,2},{1... | collective-permute-start | bytes 663560 | tf_op jit(solution)/shard_map/ppermute | solution.py:188
  7.4 9.5 %collective-permute-start.2 = (f32[6,72,128]{2,1,0:T(8,128)S(1)}, f32[6,72,128]{2,1,0:T(8,128)S(1)}, u32[]{:S(2)}, u32[]{:S(2)}) collective-permute-start(f32[6,72,128]{2,1,0:T(8,128)S(1)} %pack.1.x_ref.refs_0_.refs_3_), channel_id=1, source_target_pairs={{0,16},{1,17},{2,18},{3,19},{4,20},{5,21},{6,22},{7,23},{8,26},{9,... | collective-permute-start | bytes 663560 | tf_op jit(solution)/shard_map/ppermute | solution.py:248
  8.3 6.6 %collective-permute-start = (f32[6,72,128]{2,1,0:T(8,128)S(1)}, f32[6,72,128]{2,1,0:T(8,128)S(1)}, u32[]{:S(2)}, u32[]{:S(2)}) collective-permute-start(f32[6,72,128]{2,1,0:T(8,128)S(1)} %pack.1.x_ref.refs_0_.refs_3_), channel_id=1, source_target_pairs={{0,2},{1,3},{2,0},{3,1},{4,6},{5,7},{6,4},{7,5},{8,10},{9,11},{10,... | collective-permute-start | bytes 663560 | tf_op jit(solution)/shard_map/ppermute | solution.py:248
  15.0 6.9 %collective-permute-start.1 = (f32[6,72,128]{2,1,0:T(8,128)S(1)}, f32[6,72,128]{2,1,0:T(8,128)S(1)}, u32[]{:S(2)}, u32[]{:S(2)}) collective-permute-start(f32[6,72,128]{2,1,0:T(8,128)S(1)} %copy.7), channel_id=1, source_target_pairs={{0,18},{1,19},{2,16},{3,17},{4,22},{5,23},{6,20},{7,21},{8,24},{9,... | collective-permute-start | bytes 663560 | tf_op jit(solution)/shard_map/ppermute | solution.py:248
  16.8 2.2 %collective-permute-start.6 = (f32[2,6,72,128]{3,2,1,0:T(8,128)S(1)}, f32[2,6,72,128]{3,2,1,0:T(8,128)S(1)}, u32[]{:S(2)}, u32[]{:S(2)}) collective-permute-start(f32[2,6,72,128]{3,2,1,0:T(8,128)S(1)} %pair.1), channel_id=1, source_target_pairs={{0,1},{1,0},{2,3},{3,2},{4,5},{5,4},{6,7},{7,6},{8,9},{9,8},{10,11... | collective-permute-start | bytes 1327112 | tf_op jit(solution)/shard_map/ppermute | solution.py:188
  16.9 2.1 %collective-permute-start.7 = (f32[6,72,128]{2,1,0:T(8,128)S(1)}, f32[6,72,128]{2,1,0:T(8,128)S(1)}, u32[]{:S(2)}, u32[]{:S(2)}) collective-permute-start(f32[6,72,128]{2,1,0:T(8,128)S(1)} %collective-permute-done.2.refs_5_.refs_1_), channel_id=1, source_target_pairs={{0,1},{1,0},{2,3},{3,2},{4,5},{5,4},{6,7},{7,6},{8,9},{9,8},{10,11... | collective-permute-start | bytes 663560 | tf_op jit(solution)/shard_map/ppermute | solution.py:188
  17.4 11.6 %collective-permute-start.5 = (f32[6,72,128]{2,1,0:T(8,128)S(1)}, f32[6,72,128]{2,1,0:T(8,128)S(1)}, u32[]{:S(2)}, u32[]{:S(2)}) collective-permute-start(f32[6,72,128]{2,1,0:T(8,128)S(1)} %collective-permute-done.4._.refs_2_.refs_5_), channel_id=1, source_target_pairs={{0,4},{4,0},{8,12},{12,8},{1,5},{5,1},{9,13},{13,9},{2,6},{6,2},{1... | collective-permute-start | bytes 663560 | tf_op jit(solution)/shard_map/ppermute | solution.py:188
  21.9 7.1 %collective-permute-start.8 = (f32[6,72,128]{2,1,0:T(8,128)S(1)}, f32[6,72,128]{2,1,0:T(8,128)S(1)}, u32[]{:S(2)}, u32[]{:S(2)}) collective-permute-start(f32[6,72,128]{2,1,0:T(8,128)S(1)} %copy.8), channel_id=1, source_target_pairs={{0,1},{1,0},{2,3},{3,2},{4,5},{5,4},{6,7},{7,6},{8,9},{9,8},{10,11... | collective-permute-start | bytes 663560 | tf_op jit(solution)/shard_map/ppermute | solution.py:188
  21.9 14.2 %all-to-all-start = ((f32[32,1,128]{2,1,0:T(1,128)}), f32[32,1,128]{2,1,0:T(1,128)S(1)}, u32[]{:S(2)}, u32[]{:S(2)}) async-start(f32[32,1,128]{2,1,0:T(1,128)} %trace_terms.1._), calls=%async_computation | async-start | bytes 32768 | tf_op jit(solution)/shard_map/all_to_all | solution.py:295

commit v15 on v13

--- a/solution.py
+++ b/solution.py
@@ -93,10 +93,6 @@
         index = jnp.where(hit, u, index)
         valid = valid | hit
     return index, valid & stored & (target >= 0)
-
-
-def copy_kernel(x_ref, _, out_ref):
-    out_ref[...] = x_ref[...]
 
 
 def pair_kernel(x_ref, y_ref, out_ref):
@@ -252,7 +248,7 @@
         compiler_params=LIMIT,
         name="pair",
     )(*mine[:2])
-    others = [exchanged(both, "layer", 1)] + [exchanged(share, "layer", 1) for share in mine[2:needed]]
+    others = [exchanged(both, "layer", 1)] + [exchanged(share, "layer", 1) for share in mine[2:]]
 
     def column(count):
         return jax.ShapeDtypeStruct((2 * count * rows * slots, tall, LANES), jnp.float32)
@@ -272,31 +268,19 @@
     ]
     trace = pl.pallas_call(
         functools.partial(trace_kernel, sizes, rows, size, [tuple(rest) for _, *rest in early], needed),
-        out_shape=jax.ShapeDtypeStruct((n_row * n_col * chips, 1, LANES), jnp.float32),
+        out_shape=jax.ShapeDtypeStruct((n_row * n_col * n_layer, 1, LANES), jnp.float32),
         in_specs=[SMEM] + [VMEM] * (len(early) + 2 * needed - 1) + [UNREAD] * len(marks),
         out_specs=VMEM,
         scratch_shapes=[pltpu.VMEM(column(needed).shape, jnp.float32)],
         compiler_params=LIMIT,
         name="trace_terms",
     )(code, *[share for share, *_ in early], *mine[:needed], *others[:needed - 1], *marks)
-    for share in mine[needed:]:
-        held = pl.pallas_call(
-            copy_kernel,
-            out_shape=jax.ShapeDtypeStruct(share.shape, jnp.float32),
-            in_specs=[VMEM, UNREAD],
-            out_specs=VMEM,
-            compiler_params=LIMIT,
-            name="copy",
-        )(share, trace)
-        others.append(exchanged(held, "layer", 1))
-    trace = trace + exchanged(trace, "layer", 1)
-    like = [list(range(core, n_row * n_col * n_layer, 2)) for core in range(2)]
-    trace = lax.all_to_all(trace, AXES, 0, 0, axis_index_groups=like, tiled=True)
+    trace = lax.all_to_all(trace, AXES, 0, 0, tiled=True)
 
     strip = early + late
     inner = len(strip) * slots * LANES
     near = [share for share, value, _, _ in early if value == 1]
-    operands = mine[::-1] + near + far + [share for share, *_ in late] + others
+    operands = far + near + mine + [share for share, *_ in late] + others
 
     def at(share):
         return next(n for n, operand in enumerate(operands) if operand is share)

time: 36.3 us -> 34.5 us (0.950)
  starting transfers between devices: 16.6 us -> 14.4 us
  Pallas kernels: 6.71 us -> 7.34 us
  other arithmetic: 0.6 us -> 0.01 us
  waiting for transfers between devices: 10.5 us -> 10.9 us
    ppermute x6 -> x5, waiting for transfers between devices: 1.46 us -> 0.01 us  [exchanged(): lax.ppermute(value, axis, [(n, n ^ mask) for n in range(lax.axis_size(axi...]
    all_to_all x1, starting transfers between devices: 5.79 us -> 4.52 us  [body(): trace = lax.all_to_all(trace, AXES, 0, 0, tiled=True)]
    ppermute x1, waiting for transfers between devices: 0.01 us -> 1.12 us  [row_strip(): far = lax.ppermute(packed, AXES, route)]
    ppermute x6 -> x5, starting transfers between devices: 3.22 us -> 2.27 us  [exchanged(): lax.ppermute(value, axis, [(n, n ^ mask) for n in range(lax.axis_size(axi...]
    ppermute x3, waiting for transfers between devices: 6.28 us -> 7.18 us  [in_plane(): return lax.ppermute(packed, AXES, route)]
    pallas_call x1, Pallas kernels: 1.56 us -> 2.17 us  [body(): pl.pallas_call(functools.partial(trace_kernel, sizes, rows, size, [tuple(...]
    add x1 -> x0, other arithmetic: 0.6 us -> none  [body(): trace = trace + exchanged(trace, 'layer', 1)]
  transfers between devices with their start and end apart: 11 -> 10, of which waited for: 5 -> 5; matrix products, arithmetic and copies ran while one was open for 2% -> 0% of each run, Pallas kernels for 17% -> 19%
where the time goes in v15:
time: 34.5 us; the launch traced here: 34.3 us
  starting transfers between devices  14.4 us (42%)
  waiting for transfers between devices  10.9 us (32%)
  Pallas kernels  7.34 us (21%)
  local copies, waits for them, and re-layouts  0.96 us (3%)
  between operations  0.71 us (2%)
    ppermute x3, waiting for transfers between devices, in_plane(): return lax.ppermute(packed, AXES, route)  7.18 us
    all_to_all x1, starting transfers between devices, body(): trace = lax.all_to_all(trace, AXES, 0, 0, tiled=True)  4.52 us
    pallas_call x1, Pallas kernels, body(): pl.pallas_call(functools.partial(product_kernel, sizes, [tuple(rest) for...  4.48 us
    ppermute x1, starting transfers between devices, row_strip(): far = lax.ppermute(packed, AXES, route)  4.1 us
    ppermute x3, starting transfers between devices, in_plane(): return lax.ppermute(packed, AXES, route)  3.49 us
    all_to_all x1, waiting for transfers between devices, body(): trace = lax.all_to_all(trace, AXES, 0, 0, tiled=True)  2.64 us
    ppermute x5, starting transfers between devices, exchanged(): lax.ppermute(value, axis, [(n, n ^ mask) for n in range(lax.axis_size(axi...  2.27 us
    pallas_call x1, Pallas kernels, body(): pl.pallas_call(functools.partial(trace_kernel, sizes, rows, size, [tuple(...  2.17 us
  transfers between devices with their start and end apart: 10, of which 5 were waited for; matrix products, arithmetic and copies ran while one was open for 0% of the time, Pallas kernels for 19%

profile of v15, /device:TPU:0, one launch (start us, length us, event | category | flops | bytes accessed | tf_op | source)
XLA Modules:
  0.0 34.3 jit_solution(9670184986432726087)
XLA Ops:
  0.6 0.0 copy-start
  0.6 1.0 %copy-done = f32[2,1,3,96,96]{4,3,2,1,0:T(8,128)S(1)} copy-done((f32[2,1,3,96,96]{4,3,2,1,0:T(8,128)S(1)}, f32[2,1,3,96,96]{4,3,2,1,0:T(8,128)}, u32[]{:S(2)}) %copy-start) | copy-done | bytes 221208
  1.6 0.0 copy-start.1
  1.6 0.0 copy-start.2
  1.6 0.1 pack.1.x_ref.refs_2_.refs_0_.refs_3_
  1.7 4.1 %collective-permute-start = (f32[6,72,128]{2,1,0:T(8,128)S(1)}, f32[6,72,128]{2,1,0:T(8,128)S(1)}, u32[]{:S(2)}, u32[]{:S(2)}) collective-permute-start(f32[6,72,128]{2,1,0:T(8,128)S(1)} %pack.1.x_ref.refs_2_.refs_0_.refs_3_), channel_id=1, source_target_pairs={{0,8},{1,9},{2,10},{3,11},{4,12},{5,13},{6,14},{7,15},{8,0},{9,1},... | collective-permute-start | bytes 663560 | tf_op jit(solution)/shard_map/ppermute | solution.py:204
  5.8 1.6 %collective-permute-start.1 = (f32[6,72,128]{2,1,0:T(8,128)S(1)}, f32[6,72,128]{2,1,0:T(8,128)S(1)}, u32[]{:S(2)}, u32[]{:S(2)}) collective-permute-start(f32[6,72,128]{2,1,0:T(8,128)S(1)} %pack.1.x_ref.refs_2_.refs_0_.refs_3_), channel_id=1, source_target_pairs={{0,4},{4,0},{8,12},{12,8},{1,5},{5,1},{9,13},{13,9},{2,6},{6,2},{1... | collective-permute-start | bytes 663560 | tf_op jit(solution)/shard_map/ppermute | solution.py:184
  7.4 1.5 %collective-permute-start.2 = (f32[6,72,128]{2,1,0:T(8,128)S(1)}, f32[6,72,128]{2,1,0:T(8,128)S(1)}, u32[]{:S(2)}, u32[]{:S(2)}) collective-permute-start(f32[6,72,128]{2,1,0:T(8,128)S(1)} %pack.1.x_ref.refs_2_.refs_0_.refs_3_), channel_id=1, source_target_pairs={{0,2},{1,3},{2,0},{3,1},{4,6},{5,7},{6,4},{7,5},{8,10},{9,11},{10,... | collective-permute-start | bytes 663560 | tf_op jit(solution)/shard_map/ppermute | solution.py:234
  8.9 0.9 %collective-permute-start.3 = (f32[6,72,128]{2,1,0:T(8,128)S(1)}, f32[6,72,128]{2,1,0:T(8,128)S(1)}, u32[]{:S(2)}, u32[]{:S(2)}) collective-permute-start(f32[6,72,128]{2,1,0:T(8,128)S(1)} %pack.1.x_ref.refs_2_.refs_0_.refs_3_), channel_id=1, source_target_pairs={{0,16},{1,17},{2,18},{3,19},{4,20},{5,21},{6,22},{7,23},{8,26},{9,... | collective-permute-start | bytes 663560 | tf_op jit(solution)/shard_map/ppermute | solution.py:234
  9.8 1.0 %collective-permute-start.4 = (f32[6,72,128]{2,1,0:T(8,128)S(1)}, f32[6,72,128]{2,1,0:T(8,128)S(1)}, u32[]{:S(2)}, u32[]{:S(2)}) collective-permute-start(f32[6,72,128]{2,1,0:T(8,128)S(1)} %pack.1.x_ref.refs_2_.refs_0_.refs_3_), channel_id=1, source_target_pairs={{0,18},{1,19},{2,16},{3,17},{4,22},{5,23},{6,20},{7,21},{8,24},{9,... | collective-permute-start | bytes 663560 | tf_op jit(solution)/shard_map/ppermute | solution.py:234
  10.9 0.0 copy-done.1
  10.9 0.0 copy-done.2
  10.9 4.0 %collective-permute-done.2.y_ref.refs_3_.refs_4_ = f32[6,72,128]{2,1,0:T(8,128)S(1)} collective-permute-done((f32[6,72,128]{2,1,0:T(8,128)S(1)}, f32[6,72,128]{2,1,0:T(8,128)S(1)}, u32[]{:S(2)}, u32[]{:S(2)}) %collective-permute-start.2) | collective-permute-done | bytes 221216 | tf_op jit(solution)/shard_map/ppermute | solution.py:234
  14.9 0.1 collective-permute-start.6
  15.0 1.1 %collective-permute-done.refs_0_._.refs_2_ = f32[6,72,128]{2,1,0:T(8,128)S(1)} collective-permute-done((f32[6,72,128]{2,1,0:T(8,128)S(1)}, f32[6,72,128]{2,1,0:T(8,128)S(1)}, u32[]{:S(2)}, u32[]{:S(2)}) %collective-permute-start) | collective-permute-done | bytes 221216 | tf_op jit(solution)/shard_map/ppermute | solution.py:204
  16.1 0.6 %collective-permute-start.5 = (f32[6,72,128]{2,1,0:T(8,128)S(1)}, f32[6,72,128]{2,1,0:T(8,128)S(1)}, u32[]{:S(2)}, u32[]{:S(2)}) collective-permute-start(f32[6,72,128]{2,1,0:T(8,128)S(1)} %collective-permute-done.refs_0_._.refs_2_), channel_id=1, source_target_pairs={{0,4},{4,0},{8,12},{12,8},{1,5},{5,1},{9,13},{13,9},{2,6},{6,2},{1... | collective-permute-start | bytes 663560 | tf_op jit(solution)/shard_map/ppermute | solution.py:184
  16.7 0.6 %collective-permute-done.3.refs_4_.refs_5_ = f32[6,72,128]{2,1,0:T(8,128)S(1)} collective-permute-done((f32[6,72,128]{2,1,0:T(8,128)S(1)}, f32[6,72,128]{2,1,0:T(8,128)S(1)}, u32[]{:S(2)}, u32[]{:S(2)}) %collective-permute-start.3) | collective-permute-done | bytes 221216 | tf_op jit(solution)/shard_map/ppermute | solution.py:234
  17.3 0.0 collective-permute-start.7
  17.3 2.6 %collective-permute-done.4.refs_5_ = f32[6,72,128]{2,1,0:T(8,128)S(1)} collective-permute-done((f32[6,72,128]{2,1,0:T(8,128)S(1)}, f32[6,72,128]{2,1,0:T(8,128)S(1)}, u32[]{:S(2)}, u32[]{:S(2)}) %collective-permute-start.4) | collective-permute-done | bytes 221216 | tf_op jit(solution)/shard_map/ppermute | solution.py:234
  19.9 0.0 collective-permute-start.8
  19.9 0.0 collective-permute-done.1.refs_1_
  19.9 0.0 collective-permute-done.7.refs_8_.refs_7_
  19.9 0.0 collective-permute-done.6.refs_7_.refs_6_
  20.0 2.2 %trace_terms.1 = f32[32,1,128]{2,1,0:T(1,128)} custom-call(s32[3,4,16]{2,1,0:T(4,128)S(1)} %select_bitcast_fusion.code_ref, f32[6,72,128]{2,1,0:T(8,128)S(1)} %pack.1.x_ref.refs_2_.refs_0_.refs_3_, f32[6,72,128]{2,1,0:T(8,128)S(1)} %collective-permute-done.1.refs_1_, f32[6,72,128]{2,1,0:T(8,128)S(1)} %collective-permute-done.refs_0_._.refs_2_, ...), custom_call_target="tpu_custom_call" | custom-call | tf_op jit(solution)/shard_map/trace_terms/pallas_call | solution.py:269
  22.1 4.5 %all-to-all-start = ((f32[32,1,128]{2,1,0:T(1,128)}), f32[32,1,128]{2,1,0:T(1,128)S(1)}, u32[]{:S(2)}, u32[]{:S(2)}) async-start(f32[32,1,128]{2,1,0:T(1,128)} %trace_terms.1), calls=%async_computation | async-start | bytes 32768 | tf_op jit(solution)/shard_map/all_to_all | solution.py:278
  26.7 0.0 collective-permute-done.5.refs_6_
  26.7 0.0 collective-permute-done.8.refs_9_
  26.7 4.5 %multiply.1 = (f32[2,1,3,96,96]{4,3,2,1,0:T(8,128)}, f32[8,128]{1,0:T(8,128)S(1)}) custom-call(s32[3,4,16]{2,1,0:T(4,128)S(1)} %select_bitcast_fusion.code_ref, f32[6,72,128]{2,1,0:T(8,128)S(1)} %collective-permute-done.refs_0_._.refs_2_, f32[6,72,128]{2,1,0:T(8,128)S(1)} %collective-permute-done.1.refs_1_, ...), custom_call_target="tpu_custom_call" | custom-call | tf_op jit(solution)/shard_map/multiply/pallas_call | solution.py:289
  31.2 2.6 %all-to-all-done.terms_ref = f32[32,1,128]{2,1,0:T(1,128)S(1)} async-done(((f32[32,1,128]{2,1,0:T(1,128)}), f32[32,1,128]{2,1,0:T(1,128)S(1)}, u32[]{:S(2)}, u32[]{:S(2)}) %all-to-all-start) | async-done | bytes 16416 | tf_op jit(solution)/shard_map/all_to_all | solution.py:278
  33.8 0.5 %sum.1 = f32[1,1]{1,0:T(1,128)} custom-call(f32[32,1,128]{2,1,0:T(1,128)S(1)} %all-to-all-done.terms_ref, f32[8,128]{1,0:T(8,128)S(1)} %get-tuple-element.5._), custom_call_target="tpu_custom_call" | custom-call | tf_op jit(solution)/shard_map/sum/pallas_call | solution.py:305
  (3 shorter events, 0.0 us)
Async XLA Ops:
  0.6 1.0 %copy-start = (f32[2,1,3,96,96]{4,3,2,1,0:T(8,128)S(1)}, f32[2,1,3,96,96]{4,3,2,1,0:T(8,128)}, u32[]{:S(2)}) copy-start(f32[2,1,3,96,96]{4,3,2,1,0:T(8,128)} %x_ref.1) | copy-start | bytes 663556
  1.6 9.3 %copy-start.1 = (s32[16,4,3]{0,1,2:T(4,128)S(1)}, s32[16,4,3]{0,1,2:T(4,128)}, u32[]{:S(2)}) copy-start(s32[16,4,3]{0,1,2:T(4,128)} %param.4) | copy-start | bytes 2308
  1.6 9.3 %copy-start.2 = (s32[16,4,3]{0,1,2:T(4,128)S(1)}, s32[16,4,3]{0,1,2:T(4,128)}, u32[]{:S(2)}) copy-start(s32[16,4,3]{0,1,2:T(4,128)} %param.5) | copy-start | bytes 2308
  1.7 14.4 %collective-permute-start = (f32[6,72,128]{2,1,0:T(8,128)S(1)}, f32[6,72,128]{2,1,0:T(8,128)S(1)}, u32[]{:S(2)}, u32[]{:S(2)}) collective-permute-start(f32[6,72,128]{2,1,0:T(8,128)S(1)} %pack.1.x_ref.refs_2_.refs_0_.refs_3_), channel_id=1, source_target_pairs={{0,8},{1,9},{2,10},{3,11},{4,12},{5,13},{6,14},{7,15},{8,0},{9,1},... | collective-permute-start | bytes 663560 | tf_op jit(solution)/shard_map/ppermute | solution.py:204
  5.8 14.1 %collective-permute-start.1 = (f32[6,72,128]{2,1,0:T(8,128)S(1)}, f32[6,72,128]{2,1,0:T(8,128)S(1)}, u32[]{:S(2)}, u32[]{:S(2)}) collective-permute-start(f32[6,72,128]{2,1,0:T(8,128)S(1)} %pack.1.x_ref.refs_2_.refs_0_.refs_3_), channel_id=1, source_target_pairs={{0,4},{4,0},{8,12},{12,8},{1,5},{5,1},{9,13},{13,9},{2,6},{6,2},{1... | collective-permute-start | bytes 663560 | tf_op jit(solution)/shard_map/ppermute | solution.py:184
  7.4 7.5 %collective-permute-start.2 = (f32[6,72,128]{2,1,0:T(8,128)S(1)}, f32[6,72,128]{2,1,0:T(8,128)S(1)}, u32[]{:S(2)}, u32[]{:S(2)}) collective-permute-start(f32[6,72,128]{2,1,0:T(8,128)S(1)} %pack.1.x_ref.refs_2_.refs_0_.refs_3_), channel_id=1, source_target_pairs={{0,2},{1,3},{2,0},{3,1},{4,6},{5,7},{6,4},{7,5},{8,10},{9,11},{10,... | collective-permute-start | bytes 663560 | tf_op jit(solution)/shard_map/ppermute | solution.py:234
  8.9 8.4 %collective-permute-start.3 = (f32[6,72,128]{2,1,0:T(8,128)S(1)}, f32[6,72,128]{2,1,0:T(8,128)S(1)}, u32[]{:S(2)}, u32[]{:S(2)}) collective-permute-start(f32[6,72,128]{2,1,0:T(8,128)S(1)} %pack.1.x_ref.refs_2_.refs_0_.refs_3_), channel_id=1, source_target_pairs={{0,16},{1,17},{2,18},{3,19},{4,20},{5,21},{6,22},{7,23},{8,26},{9,... | collective-permute-start | bytes 663560 | tf_op jit(solution)/shard_map/ppermute | solution.py:234
  9.8 10.1 %collective-permute-start.4 = (f32[6,72,128]{2,1,0:T(8,128)S(1)}, f32[6,72,128]{2,1,0:T(8,128)S(1)}, u32[]{:S(2)}, u32[]{:S(2)}) collective-permute-start(f32[6,72,128]{2,1,0:T(8,128)S(1)} %pack.1.x_ref.refs_2_.refs_0_.refs_3_), channel_id=1, source_target_pairs={{0,18},{1,19},{2,16},{3,17},{4,22},{5,23},{6,20},{7,21},{8,24},{9,... | collective-permute-start | bytes 663560 | tf_op jit(solution)/shard_map/ppermute | solution.py:234
  14.9 5.1 %collective-permute-start.6 = (f32[2,6,72,128]{3,2,1,0:T(8,128)S(1)}, f32[2,6,72,128]{3,2,1,0:T(8,128)S(1)}, u32[]{:S(2)}, u32[]{:S(2)}) collective-permute-start(f32[2,6,72,128]{3,2,1,0:T(8,128)S(1)} %pair.1), channel_id=1, source_target_pairs={{0,1},{1,0},{2,3},{3,2},{4,5},{5,4},{6,7},{7,6},{8,9},{9,8},{10,11... | collective-permute-start | bytes 1327112 | tf_op jit(solution)/shard_map/ppermute | solution.py:184
  16.1 10.6 %collective-permute-start.5 = (f32[6,72,128]{2,1,0:T(8,128)S(1)}, f32[6,72,128]{2,1,0:T(8,128)S(1)}, u32[]{:S(2)}, u32[]{:S(2)}) collective-permute-start(f32[6,72,128]{2,1,0:T(8,128)S(1)} %collective-permute-done.refs_0_._.refs_2_), channel_id=1, source_target_pairs={{0,4},{4,0},{8,12},{12,8},{1,5},{5,1},{9,13},{13,9},{2,6},{6,2},{1... | collective-permute-start | bytes 663560 | tf_op jit(solution)/shard_map/ppermute | solution.py:184
  17.3 2.7 %collective-permute-start.7 = (f32[6,72,128]{2,1,0:T(8,128)S(1)}, f32[6,72,128]{2,1,0:T(8,128)S(1)}, u32[]{:S(2)}, u32[]{:S(2)}) collective-permute-start(f32[6,72,128]{2,1,0:T(8,128)S(1)} %collective-permute-done.3.refs_4_.refs_5_), channel_id=1, source_target_pairs={{0,1},{1,0},{2,3},{3,2},{4,5},{5,4},{6,7},{7,6},{8,9},{9,8},{10,11... | collective-permute-start | bytes 663560 | tf_op jit(solution)/shard_map/ppermute | solution.py:184
  19.9 6.7 %collective-permute-start.8 = (f32[6,72,128]{2,1,0:T(8,128)S(1)}, f32[6,72,128]{2,1,0:T(8,128)S(1)}, u32[]{:S(2)}, u32[]{:S(2)}) collective-permute-start(f32[6,72,128]{2,1,0:T(8,128)S(1)} %collective-permute-done.4.refs_5_), channel_id=1, source_target_pairs={{0,1},{1,0},{2,3},{3,2},{4,5},{5,4},{6,7},{7,6},{8,9},{9,8},{10,11... | collective-permute-start | bytes 663560 | tf_op jit(solution)/shard_map/ppermute | solution.py:184
  22.1 11.7 %all-to-all-start = ((f32[32,1,128]{2,1,0:T(1,128)}), f32[32,1,128]{2,1,0:T(1,128)S(1)}, u32[]{:S(2)}, u32[]{:S(2)}) async-start(f32[32,1,128]{2,1,0:T(1,128)} %trace_terms.1), calls=%async_computation | async-start | bytes 32768 | tf_op jit(solution)/shard_map/all_to_all | solution.py:278

commit v16 on v14

--- a/solution.py
+++ b/solution.py
@@ -110,7 +110,7 @@
 
 def trace_kernel(sizes, rows, size, groups, shares, code_ref, *refs):
     strip_refs, share_refs = refs[:len(groups)], refs[len(groups):len(groups) + 2 * shares - 1]
-    total_ref, column_ref = refs[-2:]
+    total_ref, column_ref, sum_ref = refs[-3:]
     slots = code_ref.shape[0]
     pair, here, own_group, number, per_group = place(sizes)
     width = per_group * rows
@@ -120,7 +120,7 @@
     @pl.when(own_group == here)
     def _():
         stack(share_refs, column_ref)
-        total = jnp.zeros((size, size), jnp.float32)
+        sum_ref[...] = jnp.zeros(sum_ref.shape, jnp.float32)
         for i in range(rows):
             row = pair * rows + i
             for strip_ref, (value, value_upper, weight) in zip(strip_refs, groups):
@@ -129,10 +129,14 @@
                     column = code_ref[t, group, row]
                     contracted = group * width + jnp.maximum(column, 0)
                     index, valid = matched(code_ref, here, contracted, column >= 0, number * rows + i)
-                    block = column_ref[strip_base(sizes, rows, slots, shares, contracted) + index]
-                    term = straight(strip_ref[i * slots + t]) * straight(block).T
-                    total = total + jnp.where(valid, weight * term, 0.0)
-        total_ref[...] = jnp.full(total_ref.shape, jnp.sum(total), jnp.float32)
+                    left = strip_ref.at[i * slots + t]
+                    right = column_ref.at[strip_base(sizes, rows, slots, shares, contracted) + index]
+
+                    @pl.when(valid)
+                    def _(left=left, right=right, weight=weight):
+                        sum_ref[...] += weight * (straight(left[...]) * straight(right[...]).T)
+
+        total_ref[...] = jnp.full(total_ref.shape, jnp.sum(sum_ref[...]), jnp.float32)
 
     @pl.when(own_group != here)
     def _():
@@ -237,7 +241,7 @@
             name="copy",
         )(share, after)
 
-    def in_plane(steps, value=packed):
+    def in_plane(steps):
         route = []
         for a in range(n_row):
             for c in range(n_col):
@@ -245,11 +249,10 @@
                     row_bits, chip_bits = steps[c >= n_col // 2]
                     target = ((a ^ row_bits) * n_col + c) * n_layer + (b ^ (2 * chip_bits))
                     route.append(((a * n_col + c) * n_layer + b, target))
-        return lax.ppermute(value, AXES, route)
+        return lax.ppermute(packed, AXES, route)
 
     if four_by_four(sizes):
-        mine = [packed, in_plane([(0, 1)] * 2), in_plane([(1, 0), (1, 1)])]
-        mine.append(in_plane([(1, 1), (1, 0)], copied(packed, mine[1])))
+        mine = [packed, in_plane([(0, 1)] * 2), in_plane([(1, 0), (1, 1)]), in_plane([(1, 1), (1, 0)])]
         needed = 3
     else:
         mine = [packed] + [in_plane([(n // chips, n % chips)] * 2) for n in range(1, n_row * chips)]
@@ -286,7 +289,7 @@
         out_shape=jax.ShapeDtypeStruct((n_row * n_col * n_layer, 1, LANES), jnp.float32),
         in_specs=[SMEM] + [VMEM] * (len(early) + 2 * needed - 1) + [UNREAD] * len(marks),
         out_specs=VMEM,
-        scratch_shapes=[pltpu.VMEM(column(needed).shape, jnp.float32)],
+        scratch_shapes=[pltpu.VMEM(column(needed).shape, jnp.float32), pltpu.VMEM((size, size), jnp.float32)],
         compiler_params=LIMIT,
         name="trace_terms",
     )(code, *[share for share, *_ in early], *mine[:needed], *others[:needed - 1], *marks)

time: 36.8 us -> 34.4 us (0.935)
  starting transfers between devices: 18.8 us -> 15.2 us
  waiting for transfers between devices: 8.79 us -> 9.41 us
  Pallas kernels: 7.36 us -> 7.96 us
    all_to_all x1, starting transfers between devices: 7.01 us -> 4.9 us  [body(): trace = lax.all_to_all(trace, AXES, 0, 0, tiled=True)]
    ppermute x3, starting transfers between devices: 4.29 us -> 3.49 us  [in_plane(): return lax.ppermute(packed, AXES, route)]
    ppermute x5, starting transfers between devices: 3.42 us -> 2.72 us  [exchanged(): lax.ppermute(value, axis, [(n, n ^ mask) for n in range(lax.axis_size(axi...]
    pallas_call x1, Pallas kernels: 2.17 us -> 2.8 us  [body(): pl.pallas_call(functools.partial(trace_kernel, sizes, rows, size, [tuple(...]
    ppermute x3, waiting for transfers between devices: 5.76 us -> 6.28 us  [in_plane(): return lax.ppermute(packed, AXES, route)]
  transfers between devices with their start and end apart: 10 -> 10, of which waited for: 4 -> 4; matrix products, arithmetic and copies ran while one was open for 0% -> 0% of each run, Pallas kernels for 18% -> 21%
where the time goes in v16:
time: 34.4 us; the launch traced here: 34.3 us
  starting transfers between devices  15.2 us (44%)
  waiting for transfers between devices  9.41 us (27%)
  Pallas kernels  7.96 us (23%)
  local copies, waits for them, and re-layouts  0.96 us (3%)
  between operations  0.71 us (2%)
    ppermute x3, waiting for transfers between devices, in_plane(): return lax.ppermute(packed, AXES, route)  6.28 us
    all_to_all x1, starting transfers between devices, body(): trace = lax.all_to_all(trace, AXES, 0, 0, tiled=True)  4.9 us
    pallas_call x1, Pallas kernels, body(): pl.pallas_call(functools.partial(product_kernel, sizes, [tuple(rest) for...  4.46 us
    ppermute x1, starting transfers between devices, row_strip(): far = lax.ppermute(packed, AXES, route)  4.1 us
    ppermute x3, starting transfers between devices, in_plane(): return lax.ppermute(packed, AXES, route)  3.49 us
    pallas_call x1, Pallas kernels, body(): pl.pallas_call(functools.partial(trace_kernel, sizes, rows, size, [tuple(...  2.8 us
    ppermute x5, starting transfers between devices, exchanged(): lax.ppermute(value, axis, [(n, n ^ mask) for n in range(lax.axis_size(axi...  2.72 us
    all_to_all x1, waiting for transfers between devices, body(): trace = lax.all_to_all(trace, AXES, 0, 0, tiled=True)  2.65 us
  transfers between devices with their start and end apart: 10, of which 4 were waited for; matrix products, arithmetic and copies ran while one was open for 0% of the time, Pallas kernels for 21%

profile of v16, /device:TPU:0, one launch (start us, length us, event | category | flops | bytes accessed | tf_op | source)
XLA Modules:
  0.0 34.3 jit_solution(14233097000447349945)
XLA Ops:
  0.6 0.0 copy-start
  0.6 1.0 %copy-done = f32[2,1,3,96,96]{4,3,2,1,0:T(8,128)S(1)} copy-done((f32[2,1,3,96,96]{4,3,2,1,0:T(8,128)S(1)}, f32[2,1,3,96,96]{4,3,2,1,0:T(8,128)}, u32[]{:S(2)}) %copy-start) | copy-done | bytes 221208
  1.6 0.0 copy-start.1
  1.6 0.0 copy-start.2
  1.6 0.1 pack.1.x_ref.refs_0_.refs_3_
  1.7 4.1 %collective-permute-start.4 = (f32[6,72,128]{2,1,0:T(8,128)S(1)}, f32[6,72,128]{2,1,0:T(8,128)S(1)}, u32[]{:S(2)}, u32[]{:S(2)}) collective-permute-start(f32[6,72,128]{2,1,0:T(8,128)S(1)} %pack.1.x_ref.refs_0_.refs_3_), channel_id=1, source_target_pairs={{0,8},{1,9},{2,10},{3,11},{4,12},{5,13},{6,14},{7,15},{8,0},{9,1},... | collective-permute-start | bytes 663560 | tf_op jit(solution)/shard_map/ppermute | solution.py:212
  5.8 1.6 %collective-permute-start.3 = (f32[6,72,128]{2,1,0:T(8,128)S(1)}, f32[6,72,128]{2,1,0:T(8,128)S(1)}, u32[]{:S(2)}, u32[]{:S(2)}) collective-permute-start(f32[6,72,128]{2,1,0:T(8,128)S(1)} %pack.1.x_ref.refs_0_.refs_3_), channel_id=1, source_target_pairs={{0,4},{4,0},{8,12},{12,8},{1,5},{5,1},{9,13},{13,9},{2,6},{6,2},{1... | collective-permute-start | bytes 663560 | tf_op jit(solution)/shard_map/ppermute | solution.py:192
  7.4 1.5 %collective-permute-start.2 = (f32[6,72,128]{2,1,0:T(8,128)S(1)}, f32[6,72,128]{2,1,0:T(8,128)S(1)}, u32[]{:S(2)}, u32[]{:S(2)}) collective-permute-start(f32[6,72,128]{2,1,0:T(8,128)S(1)} %pack.1.x_ref.refs_0_.refs_3_), channel_id=1, source_target_pairs={{0,2},{1,3},{2,0},{3,1},{4,6},{5,7},{6,4},{7,5},{8,10},{9,11},{10,... | collective-permute-start | bytes 663560 | tf_op jit(solution)/shard_map/ppermute | solution.py:252
  8.9 0.9 %collective-permute-start.1 = (f32[6,72,128]{2,1,0:T(8,128)S(1)}, f32[6,72,128]{2,1,0:T(8,128)S(1)}, u32[]{:S(2)}, u32[]{:S(2)}) collective-permute-start(f32[6,72,128]{2,1,0:T(8,128)S(1)} %pack.1.x_ref.refs_0_.refs_3_), channel_id=1, source_target_pairs={{0,16},{1,17},{2,18},{3,19},{4,20},{5,21},{6,22},{7,23},{8,26},{9,... | collective-permute-start | bytes 663560 | tf_op jit(solution)/shard_map/ppermute | solution.py:252
  9.8 1.0 %collective-permute-start = (f32[6,72,128]{2,1,0:T(8,128)S(1)}, f32[6,72,128]{2,1,0:T(8,128)S(1)}, u32[]{:S(2)}, u32[]{:S(2)}) collective-permute-start(f32[6,72,128]{2,1,0:T(8,128)S(1)} %pack.1.x_ref.refs_0_.refs_3_), channel_id=1, source_target_pairs={{0,18},{1,19},{2,16},{3,17},{4,22},{5,23},{6,20},{7,21},{8,24},{9,... | collective-permute-start | bytes 663560 | tf_op jit(solution)/shard_map/ppermute | solution.py:252
  10.9 0.0 copy-done.1
  10.9 0.0 copy-done.2
  10.9 4.0 %collective-permute-done.2.y_ref.refs_4_.refs_2_ = f32[6,72,128]{2,1,0:T(8,128)S(1)} collective-permute-done((f32[6,72,128]{2,1,0:T(8,128)S(1)}, f32[6,72,128]{2,1,0:T(8,128)S(1)}, u32[]{:S(2)}, u32[]{:S(2)}) %collective-permute-start.2) | collective-permute-done | bytes 221216 | tf_op jit(solution)/shard_map/ppermute | solution.py:252
  14.9 0.1 collective-permute-start.6
  15.0 2.3 %collective-permute-done.1.refs_5_.refs_1_ = f32[6,72,128]{2,1,0:T(8,128)S(1)} collective-permute-done((f32[6,72,128]{2,1,0:T(8,128)S(1)}, f32[6,72,128]{2,1,0:T(8,128)S(1)}, u32[]{:S(2)}, u32[]{:S(2)}) %collective-permute-start.1) | collective-permute-done | bytes 221216 | tf_op jit(solution)/shard_map/ppermute | solution.py:252
  17.3 0.0 collective-permute-start.7
  17.3 0.0 collective-permute-done.4._.refs_2_.refs_5_
  17.3 1.0 %collective-permute-start.5 = (f32[6,72,128]{2,1,0:T(8,128)S(1)}, f32[6,72,128]{2,1,0:T(8,128)S(1)}, u32[]{:S(2)}, u32[]{:S(2)}) collective-permute-start(f32[6,72,128]{2,1,0:T(8,128)S(1)} %collective-permute-done.4._.refs_2_.refs_5_), channel_id=1, source_target_pairs={{0,4},{4,0},{8,12},{12,8},{1,5},{5,1},{9,13},{13,9},{2,6},{6,2},{1... | collective-permute-start | bytes 663560 | tf_op jit(solution)/shard_map/ppermute | solution.py:192
  18.3 0.0 collective-permute-done.3.refs_1_.refs_4_
  18.3 0.5 %collective-permute-done.7.refs_7_.refs_8_ = f32[6,72,128]{2,1,0:T(8,128)S(1)} collective-permute-done((f32[6,72,128]{2,1,0:T(8,128)S(1)}, f32[6,72,128]{2,1,0:T(8,128)S(1)}, u32[]{:S(2)}, u32[]{:S(2)}) %collective-permute-start.7) | collective-permute-done | bytes 221216 | tf_op jit(solution)/shard_map/ppermute | solution.py:192
  18.8 0.0 collective-permute-done.6.refs_6_.refs_7_
  18.8 2.8 %trace_terms.1._ = f32[32,1,128]{2,1,0:T(1,128)} custom-call(s32[3,4,16]{2,1,0:T(4,128)S(1)} %select_bitcast_fusion.code_ref, f32[6,72,128]{2,1,0:T(8,128)S(1)} %pack.1.x_ref.refs_0_.refs_3_, f32[6,72,128]{2,1,0:T(8,128)S(1)} %collective-permute-done.3.refs_1_.refs_4_, f32[6,72,128]{2,1,0:T(8,128)S(1)} %collective-permute-done.4._.refs_2_.refs_5_, ...), custom_call_target="tpu_custom_call" | custom-call | tf_op jit(solution)/shard_map/trace_terms/pallas_call | solution.py:287
  21.6 0.0 collective-permute-done.x_ref.refs_0_
  21.6 0.1 collective-permute-start.8
  21.7 4.9 %all-to-all-start = ((f32[32,1,128]{2,1,0:T(1,128)}), f32[32,1,128]{2,1,0:T(1,128)S(1)}, u32[]{:S(2)}, u32[]{:S(2)}) async-start(f32[32,1,128]{2,1,0:T(1,128)} %trace_terms.1._), calls=%async_computation | async-start | bytes 32768 | tf_op jit(solution)/shard_map/all_to_all | solution.py:298
  26.6 0.0 collective-permute-done.5.refs_6_
  26.6 0.0 collective-permute-done.8.refs_9_
  26.6 4.5 %multiply.1 = (f32[2,1,3,96,96]{4,3,2,1,0:T(8,128)}, f32[8,128]{1,0:T(8,128)S(1)}) custom-call(s32[3,4,16]{2,1,0:T(4,128)S(1)} %select_bitcast_fusion.code_ref, f32[6,72,128]{2,1,0:T(8,128)S(1)} %collective-permute-done.x_ref.refs_0_, f32[6,72,128]{2,1,0:T(8,128)S(1)} %collective-permute-done.1.refs_5_.refs_1_, ...), custom_call_target="tpu_custom_call" | custom-call | tf_op jit(solution)/shard_map/multiply/pallas_call | solution.py:309
  31.1 2.7 %all-to-all-done.terms_ref = f32[32,1,128]{2,1,0:T(1,128)S(1)} async-done(((f32[32,1,128]{2,1,0:T(1,128)}), f32[32,1,128]{2,1,0:T(1,128)S(1)}, u32[]{:S(2)}, u32[]{:S(2)}) %all-to-all-start) | async-done | bytes 16416 | tf_op jit(solution)/shard_map/all_to_all | solution.py:298
  33.7 0.5 %sum.1 = f32[1,1]{1,0:T(1,128)} custom-call(f32[32,1,128]{2,1,0:T(1,128)S(1)} %all-to-all-done.terms_ref, f32[8,128]{1,0:T(8,128)S(1)} %get-tuple-element.5._), custom_call_target="tpu_custom_call" | custom-call | tf_op jit(solution)/shard_map/sum/pallas_call | solution.py:325
  (4 shorter events, 0.0 us)
Async XLA Ops:
  0.6 1.0 %copy-start = (f32[2,1,3,96,96]{4,3,2,1,0:T(8,128)S(1)}, f32[2,1,3,96,96]{4,3,2,1,0:T(8,128)}, u32[]{:S(2)}) copy-start(f32[2,1,3,96,96]{4,3,2,1,0:T(8,128)} %x_ref.1) | copy-start | bytes 663556
  1.6 9.3 %copy-start.1 = (s32[16,4,3]{0,1,2:T(4,128)S(1)}, s32[16,4,3]{0,1,2:T(4,128)}, u32[]{:S(2)}) copy-start(s32[16,4,3]{0,1,2:T(4,128)} %param.4) | copy-start | bytes 2308
  1.6 9.3 %copy-start.2 = (s32[16,4,3]{0,1,2:T(4,128)S(1)}, s32[16,4,3]{0,1,2:T(4,128)}, u32[]{:S(2)}) copy-start(s32[16,4,3]{0,1,2:T(4,128)} %param.5) | copy-start | bytes 2308
  1.7 15.6 %collective-permute-start.4 = (f32[6,72,128]{2,1,0:T(8,128)S(1)}, f32[6,72,128]{2,1,0:T(8,128)S(1)}, u32[]{:S(2)}, u32[]{:S(2)}) collective-permute-start(f32[6,72,128]{2,1,0:T(8,128)S(1)} %pack.1.x_ref.refs_0_.refs_3_), channel_id=1, source_target_pairs={{0,8},{1,9},{2,10},{3,11},{4,12},{5,13},{6,14},{7,15},{8,0},{9,1},... | collective-permute-start | bytes 663560 | tf_op jit(solution)/shard_map/ppermute | solution.py:212
  5.8 12.5 %collective-permute-start.3 = (f32[6,72,128]{2,1,0:T(8,128)S(1)}, f32[6,72,128]{2,1,0:T(8,128)S(1)}, u32[]{:S(2)}, u32[]{:S(2)}) collective-permute-start(f32[6,72,128]{2,1,0:T(8,128)S(1)} %pack.1.x_ref.refs_0_.refs_3_), channel_id=1, source_target_pairs={{0,4},{4,0},{8,12},{12,8},{1,5},{5,1},{9,13},{13,9},{2,6},{6,2},{1... | collective-permute-start | bytes 663560 | tf_op jit(solution)/shard_map/ppermute | solution.py:192
  7.4 7.5 %collective-permute-start.2 = (f32[6,72,128]{2,1,0:T(8,128)S(1)}, f32[6,72,128]{2,1,0:T(8,128)S(1)}, u32[]{:S(2)}, u32[]{:S(2)}) collective-permute-start(f32[6,72,128]{2,1,0:T(8,128)S(1)} %pack.1.x_ref.refs_0_.refs_3_), channel_id=1, source_target_pairs={{0,2},{1,3},{2,0},{3,1},{4,6},{5,7},{6,4},{7,5},{8,10},{9,11},{10,... | collective-permute-start | bytes 663560 | tf_op jit(solution)/shard_map/ppermute | solution.py:252
  8.9 8.4 %collective-permute-start.1 = (f32[6,72,128]{2,1,0:T(8,128)S(1)}, f32[6,72,128]{2,1,0:T(8,128)S(1)}, u32[]{:S(2)}, u32[]{:S(2)}) collective-permute-start(f32[6,72,128]{2,1,0:T(8,128)S(1)} %pack.1.x_ref.refs_0_.refs_3_), channel_id=1, source_target_pairs={{0,16},{1,17},{2,18},{3,19},{4,20},{5,21},{6,22},{7,23},{8,26},{9,... | collective-permute-start | bytes 663560 | tf_op jit(solution)/shard_map/ppermute | solution.py:252
  9.8 11.7 %collective-permute-start = (f32[6,72,128]{2,1,0:T(8,128)S(1)}, f32[6,72,128]{2,1,0:T(8,128)S(1)}, u32[]{:S(2)}, u32[]{:S(2)}) collective-permute-start(f32[6,72,128]{2,1,0:T(8,128)S(1)} %pack.1.x_ref.refs_0_.refs_3_), channel_id=1, source_target_pairs={{0,18},{1,19},{2,16},{3,17},{4,22},{5,23},{6,20},{7,21},{8,24},{9,... | collective-permute-start | bytes 663560 | tf_op jit(solution)/shard_map/ppermute | solution.py:252
  14.9 3.9 %collective-permute-start.6 = (f32[2,6,72,128]{3,2,1,0:T(8,128)S(1)}, f32[2,6,72,128]{3,2,1,0:T(8,128)S(1)}, u32[]{:S(2)}, u32[]{:S(2)}) collective-permute-start(f32[2,6,72,128]{3,2,1,0:T(8,128)S(1)} %pair.1), channel_id=1, source_target_pairs={{0,1},{1,0},{2,3},{3,2},{4,5},{5,4},{6,7},{7,6},{8,9},{9,8},{10,11... | collective-permute-start | bytes 1327112 | tf_op jit(solution)/shard_map/ppermute | solution.py:192
  17.3 1.5 %collective-permute-start.7 = (f32[6,72,128]{2,1,0:T(8,128)S(1)}, f32[6,72,128]{2,1,0:T(8,128)S(1)}, u32[]{:S(2)}, u32[]{:S(2)}) collective-permute-start(f32[6,72,128]{2,1,0:T(8,128)S(1)} %collective-permute-done.1.refs_5_.refs_1_), channel_id=1, source_target_pairs={{0,1},{1,0},{2,3},{3,2},{4,5},{5,4},{6,7},{7,6},{8,9},{9,8},{10,11... | collective-permute-start | bytes 663560 | tf_op jit(solution)/shard_map/ppermute | solution.py:192
  17.3 9.3 %collective-permute-start.5 = (f32[6,72,128]{2,1,0:T(8,128)S(1)}, f32[6,72,128]{2,1,0:T(8,128)S(1)}, u32[]{:S(2)}, u32[]{:S(2)}) collective-permute-start(f32[6,72,128]{2,1,0:T(8,128)S(1)} %collective-permute-done.4._.refs_2_.refs_5_), channel_id=1, source_target_pairs={{0,4},{4,0},{8,12},{12,8},{1,5},{5,1},{9,13},{13,9},{2,6},{6,2},{1... | collective-permute-start | bytes 663560 | tf_op jit(solution)/shard_map/ppermute | solution.py:192
  21.6 5.0 %collective-permute-start.8 = (f32[6,72,128]{2,1,0:T(8,128)S(1)}, f32[6,72,128]{2,1,0:T(8,128)S(1)}, u32[]{:S(2)}, u32[]{:S(2)}) collective-permute-start(f32[6,72,128]{2,1,0:T(8,128)S(1)} %copy.6), channel_id=1, source_target_pairs={{0,1},{1,0},{2,3},{3,2},{4,5},{5,4},{6,7},{7,6},{8,9},{9,8},{10,11... | collective-permute-start | bytes 663560 | tf_op jit(solution)/shard_map/ppermute | solution.py:192
  21.7 12.0 %all-to-all-start = ((f32[32,1,128]{2,1,0:T(1,128)}), f32[32,1,128]{2,1,0:T(1,128)S(1)}, u32[]{:S(2)}, u32[]{:S(2)}) async-start(f32[32,1,128]{2,1,0:T(1,128)} %trace_terms.1._), calls=%async_computation | async-start | bytes 32768 | tf_op jit(solution)/shard_map/all_to_all | solution.py:298

commit v17 on v14

--- a/solution.py
+++ b/solution.py
@@ -130,8 +130,8 @@
                     contracted = group * width + jnp.maximum(column, 0)
                     index, valid = matched(code_ref, here, contracted, column >= 0, number * rows + i)
                     block = column_ref[strip_base(sizes, rows, slots, shares, contracted) + index]
-                    term = straight(strip_ref[i * slots + t]) * straight(block).T
-                    total = total + jnp.where(valid, weight * term, 0.0)
+                    factor = jnp.where(valid, jnp.float32(weight), jnp.float32(0))
+                    total = total + factor * (straight(strip_ref[i * slots + t]) * straight(block).T)
         total_ref[...] = jnp.full(total_ref.shape, jnp.sum(total), jnp.float32)
 
     @pl.when(own_group != here)
@@ -237,7 +237,7 @@
             name="copy",
         )(share, after)
 
-    def in_plane(steps, value=packed):
+    def in_plane(steps):
         route = []
         for a in range(n_row):
             for c in range(n_col):
@@ -245,11 +245,10 @@
                     row_bits, chip_bits = steps[c >= n_col // 2]
                     target = ((a ^ row_bits) * n_col + c) * n_layer + (b ^ (2 * chip_bits))
                     route.append(((a * n_col + c) * n_layer + b, target))
-        return lax.ppermute(value, AXES, route)
+        return lax.ppermute(packed, AXES, route)
 
     if four_by_four(sizes):
-        mine = [packed, in_plane([(0, 1)] * 2), in_plane([(1, 0), (1, 1)])]
-        mine.append(in_plane([(1, 1), (1, 0)], copied(packed, mine[1])))
+        mine = [packed, in_plane([(0, 1)] * 2), in_plane([(1, 0), (1, 1)]), in_plane([(1, 1), (1, 0)])]
         needed = 3
     else:
         mine = [packed] + [in_plane([(n // chips, n % chips)] * 2) for n in range(1, n_row * chips)]

time: 36.8 us -> 33.8 us (0.918)
  starting transfers between devices: 18.8 us -> 15.2 us
  waiting for transfers between devices: 8.79 us -> 9.42 us
    all_to_all x1, starting transfers between devices: 7.01 us -> 4.79 us  [body(): trace = lax.all_to_all(trace, AXES, 0, 0, tiled=True)]
    ppermute x3, starting transfers between devices: 4.29 us -> 3.49 us  [in_plane(): return lax.ppermute(packed, AXES, route)]
    ppermute x5, starting transfers between devices: 3.42 us -> 2.85 us  [exchanged(): lax.ppermute(value, axis, [(n, n ^ mask) for n in range(lax.axis_size(axi...]
    ppermute x3, waiting for transfers between devices: 5.76 us -> 6.28 us  [in_plane(): return lax.ppermute(packed, AXES, route)]
  transfers between devices with their start and end apart: 10 -> 10, of which waited for: 4 -> 4; matrix products, arithmetic and copies ran while one was open for 0% -> 0% of each run, Pallas kernels for 18% -> 20%
where the time goes in v17:
time: 33.8 us; the launch traced here: 33.7 us
  starting transfers between devices  15.2 us (45%)
  waiting for transfers between devices  9.42 us (28%)
  Pallas kernels  7.34 us (22%)
  local copies, waits for them, and re-layouts  0.96 us (3%)
  between operations  0.7 us (2%)
    ppermute x3, waiting for transfers between devices, in_plane(): return lax.ppermute(packed, AXES, route)  6.28 us
    all_to_all x1, starting transfers between devices, body(): trace = lax.all_to_all(trace, AXES, 0, 0, tiled=True)  4.79 us
    pallas_call x1, Pallas kernels, body(): pl.pallas_call(functools.partial(product_kernel, sizes, [tuple(rest) for...  4.46 us
    ppermute x1, starting transfers between devices, row_strip(): far = lax.ppermute(packed, AXES, route)  4.1 us
    ppermute x3, starting transfers between devices, in_plane(): return lax.ppermute(packed, AXES, route)  3.49 us
    ppermute x5, starting transfers between devices, exchanged(): lax.ppermute(value, axis, [(n, n ^ mask) for n in range(lax.axis_size(axi...  2.85 us
    all_to_all x1, waiting for transfers between devices, body(): trace = lax.all_to_all(trace, AXES, 0, 0, tiled=True)  2.66 us
    pallas_call x1, Pallas kernels, body(): pl.pallas_call(functools.partial(trace_kernel, sizes, rows, size, [tuple(...  2.18 us
  transfers between devices with their start and end apart: 10, of which 4 were waited for; matrix products, arithmetic and copies ran while one was open for 0% of the time, Pallas kernels for 20%

profile of v17, /device:TPU:0, one launch (start us, length us, event | category | flops | bytes accessed | tf_op | source)
XLA Modules:
  0.0 33.7 jit_solution(1448275585485097869)
XLA Ops:
  0.6 0.0 copy-start
  0.6 1.0 %copy-done = f32[2,1,3,96,96]{4,3,2,1,0:T(8,128)S(1)} copy-done((f32[2,1,3,96,96]{4,3,2,1,0:T(8,128)S(1)}, f32[2,1,3,96,96]{4,3,2,1,0:T(8,128)}, u32[]{:S(2)}) %copy-start) | copy-done | bytes 221208
  1.6 0.0 copy-start.1
  1.6 0.0 copy-start.2
  1.6 0.1 pack.1.x_ref.refs_0_.refs_3_
  1.7 4.1 %collective-permute-start.4 = (f32[6,72,128]{2,1,0:T(8,128)S(1)}, f32[6,72,128]{2,1,0:T(8,128)S(1)}, u32[]{:S(2)}, u32[]{:S(2)}) collective-permute-start(f32[6,72,128]{2,1,0:T(8,128)S(1)} %pack.1.x_ref.refs_0_.refs_3_), channel_id=1, source_target_pairs={{0,8},{1,9},{2,10},{3,11},{4,12},{5,13},{6,14},{7,15},{8,0},{9,1},... | collective-permute-start | bytes 663560 | tf_op jit(solution)/shard_map/ppermute | solution.py:208
  5.8 1.6 %collective-permute-start.3 = (f32[6,72,128]{2,1,0:T(8,128)S(1)}, f32[6,72,128]{2,1,0:T(8,128)S(1)}, u32[]{:S(2)}, u32[]{:S(2)}) collective-permute-start(f32[6,72,128]{2,1,0:T(8,128)S(1)} %pack.1.x_ref.refs_0_.refs_3_), channel_id=1, source_target_pairs={{0,4},{4,0},{8,12},{12,8},{1,5},{5,1},{9,13},{13,9},{2,6},{6,2},{1... | collective-permute-start | bytes 663560 | tf_op jit(solution)/shard_map/ppermute | solution.py:188
  7.4 1.5 %collective-permute-start.2 = (f32[6,72,128]{2,1,0:T(8,128)S(1)}, f32[6,72,128]{2,1,0:T(8,128)S(1)}, u32[]{:S(2)}, u32[]{:S(2)}) collective-permute-start(f32[6,72,128]{2,1,0:T(8,128)S(1)} %pack.1.x_ref.refs_0_.refs_3_), channel_id=1, source_target_pairs={{0,2},{1,3},{2,0},{3,1},{4,6},{5,7},{6,4},{7,5},{8,10},{9,11},{10,... | collective-permute-start | bytes 663560 | tf_op jit(solution)/shard_map/ppermute | solution.py:248
  8.9 0.9 %collective-permute-start.1 = (f32[6,72,128]{2,1,0:T(8,128)S(1)}, f32[6,72,128]{2,1,0:T(8,128)S(1)}, u32[]{:S(2)}, u32[]{:S(2)}) collective-permute-start(f32[6,72,128]{2,1,0:T(8,128)S(1)} %pack.1.x_ref.refs_0_.refs_3_), channel_id=1, source_target_pairs={{0,16},{1,17},{2,18},{3,19},{4,20},{5,21},{6,22},{7,23},{8,26},{9,... | collective-permute-start | bytes 663560 | tf_op jit(solution)/shard_map/ppermute | solution.py:248
  9.8 1.0 %collective-permute-start = (f32[6,72,128]{2,1,0:T(8,128)S(1)}, f32[6,72,128]{2,1,0:T(8,128)S(1)}, u32[]{:S(2)}, u32[]{:S(2)}) collective-permute-start(f32[6,72,128]{2,1,0:T(8,128)S(1)} %pack.1.x_ref.refs_0_.refs_3_), channel_id=1, source_target_pairs={{0,18},{1,19},{2,16},{3,17},{4,22},{5,23},{6,20},{7,21},{8,24},{9,... | collective-permute-start | bytes 663560 | tf_op jit(solution)/shard_map/ppermute | solution.py:248
  10.9 0.0 copy-done.1
  10.9 0.0 copy-done.2
  10.9 4.0 %collective-permute-done.2.y_ref.refs_4_.refs_2_ = f32[6,72,128]{2,1,0:T(8,128)S(1)} collective-permute-done((f32[6,72,128]{2,1,0:T(8,128)S(1)}, f32[6,72,128]{2,1,0:T(8,128)S(1)}, u32[]{:S(2)}, u32[]{:S(2)}) %collective-permute-start.2) | collective-permute-done | bytes 221216 | tf_op jit(solution)/shard_map/ppermute | solution.py:248
  14.9 0.1 collective-permute-start.6
  15.0 2.3 %collective-permute-done.1.refs_5_.refs_1_ = f32[6,72,128]{2,1,0:T(8,128)S(1)} collective-permute-done((f32[6,72,128]{2,1,0:T(8,128)S(1)}, f32[6,72,128]{2,1,0:T(8,128)S(1)}, u32[]{:S(2)}, u32[]{:S(2)}) %collective-permute-start.1) | collective-permute-done | bytes 221216 | tf_op jit(solution)/shard_map/ppermute | solution.py:248
  17.3 0.0 collective-permute-start.7
  17.3 0.0 collective-permute-done.4._.refs_2_.refs_5_
  17.3 1.0 %collective-permute-start.5 = (f32[6,72,128]{2,1,0:T(8,128)S(1)}, f32[6,72,128]{2,1,0:T(8,128)S(1)}, u32[]{:S(2)}, u32[]{:S(2)}) collective-permute-start(f32[6,72,128]{2,1,0:T(8,128)S(1)} %collective-permute-done.4._.refs_2_.refs_5_), channel_id=1, source_target_pairs={{0,4},{4,0},{8,12},{12,8},{1,5},{5,1},{9,13},{13,9},{2,6},{6,2},{1... | collective-permute-start | bytes 663560 | tf_op jit(solution)/shard_map/ppermute | solution.py:188
  18.3 0.0 collective-permute-done.3.refs_1_.refs_4_
  18.3 0.5 %collective-permute-done.7.refs_7_.refs_8_ = f32[6,72,128]{2,1,0:T(8,128)S(1)} collective-permute-done((f32[6,72,128]{2,1,0:T(8,128)S(1)}, f32[6,72,128]{2,1,0:T(8,128)S(1)}, u32[]{:S(2)}, u32[]{:S(2)}) %collective-permute-start.7) | collective-permute-done | bytes 221216 | tf_op jit(solution)/shard_map/ppermute | solution.py:188
  18.8 0.0 collective-permute-done.6.refs_6_.refs_7_
  18.8 2.2 %trace_terms.1._ = f32[32,1,128]{2,1,0:T(1,128)} custom-call(s32[3,4,16]{2,1,0:T(4,128)S(1)} %select_bitcast_fusion.code_ref, f32[6,72,128]{2,1,0:T(8,128)S(1)} %pack.1.x_ref.refs_0_.refs_3_, f32[6,72,128]{2,1,0:T(8,128)S(1)} %collective-permute-done.3.refs_1_.refs_4_, f32[6,72,128]{2,1,0:T(8,128)S(1)} %collective-permute-done.4._.refs_2_.refs_5_, ...), custom_call_target="tpu_custom_call" | custom-call | tf_op jit(solution)/shard_map/trace_terms/pallas_call | solution.py:283
  20.9 0.0 collective-permute-done.x_ref.refs_0_
  21.0 0.2 collective-permute-start.8
  21.2 4.8 %all-to-all-start = ((f32[32,1,128]{2,1,0:T(1,128)}), f32[32,1,128]{2,1,0:T(1,128)S(1)}, u32[]{:S(2)}, u32[]{:S(2)}) async-start(f32[32,1,128]{2,1,0:T(1,128)} %trace_terms.1._), calls=%async_computation | async-start | bytes 32768 | tf_op jit(solution)/shard_map/all_to_all | solution.py:294
  26.0 0.0 collective-permute-done.5.refs_6_
  26.0 0.0 collective-permute-done.8.refs_9_
  26.0 4.5 %multiply.1 = (f32[2,1,3,96,96]{4,3,2,1,0:T(8,128)}, f32[8,128]{1,0:T(8,128)S(1)}) custom-call(s32[3,4,16]{2,1,0:T(4,128)S(1)} %select_bitcast_fusion.code_ref, f32[6,72,128]{2,1,0:T(8,128)S(1)} %collective-permute-done.x_ref.refs_0_, f32[6,72,128]{2,1,0:T(8,128)S(1)} %collective-permute-done.1.refs_5_.refs_1_, ...), custom_call_target="tpu_custom_call" | custom-call | tf_op jit(solution)/shard_map/multiply/pallas_call | solution.py:305
  30.4 2.7 %all-to-all-done.terms_ref = f32[32,1,128]{2,1,0:T(1,128)S(1)} async-done(((f32[32,1,128]{2,1,0:T(1,128)}), f32[32,1,128]{2,1,0:T(1,128)S(1)}, u32[]{:S(2)}, u32[]{:S(2)}) %all-to-all-start) | async-done | bytes 16416 | tf_op jit(solution)/shard_map/all_to_all | solution.py:294
  33.1 0.5 %sum.1 = f32[1,1]{1,0:T(1,128)} custom-call(f32[32,1,128]{2,1,0:T(1,128)S(1)} %all-to-all-done.terms_ref, f32[8,128]{1,0:T(8,128)S(1)} %get-tuple-element.5._), custom_call_target="tpu_custom_call" | custom-call | tf_op jit(solution)/shard_map/sum/pallas_call | solution.py:321
  (4 shorter events, 0.0 us)
Async XLA Ops:
  0.6 1.0 %copy-start = (f32[2,1,3,96,96]{4,3,2,1,0:T(8,128)S(1)}, f32[2,1,3,96,96]{4,3,2,1,0:T(8,128)}, u32[]{:S(2)}) copy-start(f32[2,1,3,96,96]{4,3,2,1,0:T(8,128)} %x_ref.1) | copy-start | bytes 663556
  1.6 9.3 %copy-start.1 = (s32[16,4,3]{0,1,2:T(4,128)S(1)}, s32[16,4,3]{0,1,2:T(4,128)}, u32[]{:S(2)}) copy-start(s32[16,4,3]{0,1,2:T(4,128)} %param.4) | copy-start | bytes 2308
  1.6 9.3 %copy-start.2 = (s32[16,4,3]{0,1,2:T(4,128)S(1)}, s32[16,4,3]{0,1,2:T(4,128)}, u32[]{:S(2)}) copy-start(s32[16,4,3]{0,1,2:T(4,128)} %param.5) | copy-start | bytes 2308
  1.7 15.6 %collective-permute-start.4 = (f32[6,72,128]{2,1,0:T(8,128)S(1)}, f32[6,72,128]{2,1,0:T(8,128)S(1)}, u32[]{:S(2)}, u32[]{:S(2)}) collective-permute-start(f32[6,72,128]{2,1,0:T(8,128)S(1)} %pack.1.x_ref.refs_0_.refs_3_), channel_id=1, source_target_pairs={{0,8},{1,9},{2,10},{3,11},{4,12},{5,13},{6,14},{7,15},{8,0},{9,1},... | collective-permute-start | bytes 663560 | tf_op jit(solution)/shard_map/ppermute | solution.py:208
  5.8 12.5 %collective-permute-start.3 = (f32[6,72,128]{2,1,0:T(8,128)S(1)}, f32[6,72,128]{2,1,0:T(8,128)S(1)}, u32[]{:S(2)}, u32[]{:S(2)}) collective-permute-start(f32[6,72,128]{2,1,0:T(8,128)S(1)} %pack.1.x_ref.refs_0_.refs_3_), channel_id=1, source_target_pairs={{0,4},{4,0},{8,12},{12,8},{1,5},{5,1},{9,13},{13,9},{2,6},{6,2},{1... | collective-permute-start | bytes 663560 | tf_op jit(solution)/shard_map/ppermute | solution.py:188
  7.4 7.5 %collective-permute-start.2 = (f32[6,72,128]{2,1,0:T(8,128)S(1)}, f32[6,72,128]{2,1,0:T(8,128)S(1)}, u32[]{:S(2)}, u32[]{:S(2)}) collective-permute-start(f32[6,72,128]{2,1,0:T(8,128)S(1)} %pack.1.x_ref.refs_0_.refs_3_), channel_id=1, source_target_pairs={{0,2},{1,3},{2,0},{3,1},{4,6},{5,7},{6,4},{7,5},{8,10},{9,11},{10,... | collective-permute-start | bytes 663560 | tf_op jit(solution)/shard_map/ppermute | solution.py:248
  8.9 8.4 %collective-permute-start.1 = (f32[6,72,128]{2,1,0:T(8,128)S(1)}, f32[6,72,128]{2,1,0:T(8,128)S(1)}, u32[]{:S(2)}, u32[]{:S(2)}) collective-permute-start(f32[6,72,128]{2,1,0:T(8,128)S(1)} %pack.1.x_ref.refs_0_.refs_3_), channel_id=1, source_target_pairs={{0,16},{1,17},{2,18},{3,19},{4,20},{5,21},{6,22},{7,23},{8,26},{9,... | collective-permute-start | bytes 663560 | tf_op jit(solution)/shard_map/ppermute | solution.py:248
  9.8 11.1 %collective-permute-start = (f32[6,72,128]{2,1,0:T(8,128)S(1)}, f32[6,72,128]{2,1,0:T(8,128)S(1)}, u32[]{:S(2)}, u32[]{:S(2)}) collective-permute-start(f32[6,72,128]{2,1,0:T(8,128)S(1)} %pack.1.x_ref.refs_0_.refs_3_), channel_id=1, source_target_pairs={{0,18},{1,19},{2,16},{3,17},{4,22},{5,23},{6,20},{7,21},{8,24},{9,... | collective-permute-start | bytes 663560 | tf_op jit(solution)/shard_map/ppermute | solution.py:248
  14.9 3.9 %collective-permute-start.6 = (f32[2,6,72,128]{3,2,1,0:T(8,128)S(1)}, f32[2,6,72,128]{3,2,1,0:T(8,128)S(1)}, u32[]{:S(2)}, u32[]{:S(2)}) collective-permute-start(f32[2,6,72,128]{3,2,1,0:T(8,128)S(1)} %pair.1), channel_id=1, source_target_pairs={{0,1},{1,0},{2,3},{3,2},{4,5},{5,4},{6,7},{7,6},{8,9},{9,8},{10,11... | collective-permute-start | bytes 1327112 | tf_op jit(solution)/shard_map/ppermute | solution.py:188
  17.3 1.5 %collective-permute-start.7 = (f32[6,72,128]{2,1,0:T(8,128)S(1)}, f32[6,72,128]{2,1,0:T(8,128)S(1)}, u32[]{:S(2)}, u32[]{:S(2)}) collective-permute-start(f32[6,72,128]{2,1,0:T(8,128)S(1)} %collective-permute-done.1.refs_5_.refs_1_), channel_id=1, source_target_pairs={{0,1},{1,0},{2,3},{3,2},{4,5},{5,4},{6,7},{7,6},{8,9},{9,8},{10,11... | collective-permute-start | bytes 663560 | tf_op jit(solution)/shard_map/ppermute | solution.py:188
  17.3 8.7 %collective-permute-start.5 = (f32[6,72,128]{2,1,0:T(8,128)S(1)}, f32[6,72,128]{2,1,0:T(8,128)S(1)}, u32[]{:S(2)}, u32[]{:S(2)}) collective-permute-start(f32[6,72,128]{2,1,0:T(8,128)S(1)} %collective-permute-done.4._.refs_2_.refs_5_), channel_id=1, source_target_pairs={{0,4},{4,0},{8,12},{12,8},{1,5},{5,1},{9,13},{13,9},{2,6},{6,2},{1... | collective-permute-start | bytes 663560 | tf_op jit(solution)/shard_map/ppermute | solution.py:188
  21.0 5.0 %collective-permute-start.8 = (f32[6,72,128]{2,1,0:T(8,128)S(1)}, f32[6,72,128]{2,1,0:T(8,128)S(1)}, u32[]{:S(2)}, u32[]{:S(2)}) collective-permute-start(f32[6,72,128]{2,1,0:T(8,128)S(1)} %copy.6), channel_id=1, source_target_pairs={{0,1},{1,0},{2,3},{3,2},{4,5},{5,4},{6,7},{7,6},{8,9},{9,8},{10,11... | collective-permute-start | bytes 663560 | tf_op jit(solution)/shard_map/ppermute | solution.py:188
  21.2 11.9 %all-to-all-start = ((f32[32,1,128]{2,1,0:T(1,128)}), f32[32,1,128]{2,1,0:T(1,128)S(1)}, u32[]{:S(2)}, u32[]{:S(2)}) async-start(f32[32,1,128]{2,1,0:T(1,128)} %trace_terms.1._), calls=%async_computation | async-start | bytes 32768 | tf_op jit(solution)/shard_map/all_to_all | solution.py:294

commit v18 on v10

--- a/solution.py
+++ b/solution.py
@@ -118,8 +118,8 @@
                     contracted = group * width + jnp.maximum(column, 0)
                     index, valid = matched(code_ref, here, contracted, column >= 0, number * rows + i)
                     block = column_ref[strip_base(sizes, rows, slots, shares, contracted) + index]
-                    term = straight(strip_ref[i * slots + t]) * straight(block).T
-                    total = total + jnp.where(valid, weight * term, 0.0)
+                    factor = jnp.where(valid, jnp.float32(weight), jnp.float32(0))
+                    total = total + factor * (straight(strip_ref[i * slots + t]) * straight(block).T)
         total_ref[...] = jnp.full(total_ref.shape, jnp.sum(total), jnp.float32)
 
     @pl.when(own_group != here)

time: 33.8 us -> 33.8 us (level)
  no operation moved by 1% of the time
where the time goes in v18:
time: 33.8 us; the launch traced here: 33.6 us
  starting transfers between devices  13 us (38%)
  waiting for transfers between devices  11.7 us (35%)
  Pallas kernels  7.32 us (22%)
  local copies, waits for them, and re-layouts  0.96 us (3%)
  between operations  0.7 us (2%)
    ppermute x1, waiting for transfers between devices, row_strip(): far = lax.ppermute(packed, AXES, route)  5.2 us
    pallas_call x1, Pallas kernels, body(): pl.pallas_call(functools.partial(product_kernel, sizes, [tuple(rest) for...  4.49 us
    ppermute x1, starting transfers between devices, row_strip(): far = lax.ppermute(packed, AXES, route)  4.1 us
    ppermute x3, starting transfers between devices, in_plane(): return lax.ppermute(packed, AXES, route)  4.03 us
    all_to_all x1, starting transfers between devices, body(): trace = lax.all_to_all(trace, AXES, 0, 0, tiled=True)  2.9 us
    all_to_all x1, waiting for transfers between devices, body(): trace = lax.all_to_all(trace, AXES, 0, 0, tiled=True)  2.63 us
    ppermute x3, waiting for transfers between devices, in_plane(): return lax.ppermute(packed, AXES, route)  2.4 us
    pallas_call x1, Pallas kernels, body(): pl.pallas_call(functools.partial(trace_kernel, sizes, rows, size, [tuple(...  2.18 us
  transfers between devices with their start and end apart: 11, of which 5 were waited for; matrix products, arithmetic and copies ran while one was open for 0% of the time, Pallas kernels for 20%

profile of v18, /device:TPU:0, one launch (start us, length us, event | category | flops | bytes accessed | tf_op | source)
XLA Modules:
  0.0 33.6 jit_solution(7694637665462256073)
XLA Ops:
  0.6 0.0 copy-start
  0.6 1.0 %copy-done = f32[2,1,3,96,96]{4,3,2,1,0:T(8,128)S(1)} copy-done((f32[2,1,3,96,96]{4,3,2,1,0:T(8,128)S(1)}, f32[2,1,3,96,96]{4,3,2,1,0:T(8,128)}, u32[]{:S(2)}) %copy-start) | copy-done | bytes 221208
  1.6 0.0 copy-start.1
  1.6 0.0 copy-start.2
  1.6 0.1 pack.1.refs_1_.refs_0_.refs_3_
  1.7 4.1 %collective-permute-start = (f32[6,72,128]{2,1,0:T(8,128)S(1)}, f32[6,72,128]{2,1,0:T(8,128)S(1)}, u32[]{:S(2)}, u32[]{:S(2)}) collective-permute-start(f32[6,72,128]{2,1,0:T(8,128)S(1)} %pack.1.refs_1_.refs_0_.refs_3_), channel_id=1, source_target_pairs={{0,8},{1,9},{2,10},{3,11},{4,12},{5,13},{6,14},{7,15},{8,0},{9,1},... | collective-permute-start | bytes 663560 | tf_op jit(solution)/shard_map/ppermute | solution.py:195
  5.8 1.5 %collective-permute-start.1 = (f32[6,72,128]{2,1,0:T(8,128)S(1)}, f32[6,72,128]{2,1,0:T(8,128)S(1)}, u32[]{:S(2)}, u32[]{:S(2)}) collective-permute-start(f32[6,72,128]{2,1,0:T(8,128)S(1)} %pack.1.refs_1_.refs_0_.refs_3_), channel_id=1, source_target_pairs={{0,2},{1,3},{2,0},{3,1},{4,6},{5,7},{6,4},{7,5},{8,10},{9,11},{10,... | collective-permute-start | bytes 663560 | tf_op jit(solution)/shard_map/ppermute | solution.py:225
  7.3 2.5 %collective-permute-start.2 = (f32[6,72,128]{2,1,0:T(8,128)S(1)}, f32[6,72,128]{2,1,0:T(8,128)S(1)}, u32[]{:S(2)}, u32[]{:S(2)}) collective-permute-start(f32[6,72,128]{2,1,0:T(8,128)S(1)} %pack.1.refs_1_.refs_0_.refs_3_), channel_id=1, source_target_pairs={{0,16},{1,17},{2,18},{3,19},{4,20},{5,21},{6,22},{7,23},{8,26},{9,... | collective-permute-start | bytes 663560 | tf_op jit(solution)/shard_map/ppermute | solution.py:225
  9.8 0.0 collective-permute-start.3
  9.8 1.0 %collective-permute-start.4 = (f32[6,72,128]{2,1,0:T(8,128)S(1)}, f32[6,72,128]{2,1,0:T(8,128)S(1)}, u32[]{:S(2)}, u32[]{:S(2)}) collective-permute-start(f32[6,72,128]{2,1,0:T(8,128)S(1)} %pack.1.refs_1_.refs_0_.refs_3_), channel_id=1, source_target_pairs={{0,4},{4,0},{8,12},{12,8},{1,5},{5,1},{9,13},{13,9},{2,6},{6,2},{1... | collective-permute-start | bytes 663560 | tf_op jit(solution)/shard_map/ppermute | solution.py:175
  10.9 0.0 copy-done.1
  10.9 0.0 copy-done.2
  10.9 5.2 %collective-permute-done.refs_0_._.refs_2_ = f32[6,72,128]{2,1,0:T(8,128)S(1)} collective-permute-done((f32[6,72,128]{2,1,0:T(8,128)S(1)}, f32[6,72,128]{2,1,0:T(8,128)S(1)}, u32[]{:S(2)}, u32[]{:S(2)}) %collective-permute-start) | collective-permute-done | bytes 221216 | tf_op jit(solution)/shard_map/ppermute | solution.py:195
  16.1 0.0 collective-permute-start.6
  16.1 0.0 collective-permute-done.1.refs_2_.refs_4_
  16.1 0.7 %collective-permute-start.5 = (f32[6,72,128]{2,1,0:T(8,128)S(1)}, f32[6,72,128]{2,1,0:T(8,128)S(1)}, u32[]{:S(2)}, u32[]{:S(2)}) collective-permute-start(f32[6,72,128]{2,1,0:T(8,128)S(1)} %collective-permute-done.refs_0_._.refs_2_), channel_id=1, source_target_pairs={{0,4},{4,0},{8,12},{12,8},{1,5},{5,1},{9,13},{13,9},{2,6},{6,2},{1... | collective-permute-start | bytes 663560 | tf_op jit(solution)/shard_map/ppermute | solution.py:175
  16.8 0.0 collective-permute-done.2.refs_3_.refs_5_
  16.8 0.2 collective-permute-start.7
  17.0 2.4 %collective-permute-done.3.refs_4_ = f32[6,72,128]{2,1,0:T(8,128)S(1)} collective-permute-done((f32[6,72,128]{2,1,0:T(8,128)S(1)}, f32[6,72,128]{2,1,0:T(8,128)S(1)}, u32[]{:S(2)}, u32[]{:S(2)}) %collective-permute-start.3) | collective-permute-done | bytes 221216 | tf_op jit(solution)/shard_map/ppermute | solution.py:225
  19.4 0.0 collective-permute-start.8
  19.4 0.8 %collective-permute-done.4.refs_5_.refs_1_ = f32[6,72,128]{2,1,0:T(8,128)S(1)} collective-permute-done((f32[6,72,128]{2,1,0:T(8,128)S(1)}, f32[6,72,128]{2,1,0:T(8,128)S(1)}, u32[]{:S(2)}, u32[]{:S(2)}) %collective-permute-start.4) | collective-permute-done | bytes 221216 | tf_op jit(solution)/shard_map/ppermute | solution.py:175
  20.2 0.0 collective-permute-start.9
  20.2 0.0 collective-permute-done.6.refs_7_.refs_6_
  20.2 0.0 collective-permute-done.7.refs_8_.refs_7_
  20.2 0.7 %collective-permute-done.8.refs_9_.refs_8_ = f32[6,72,128]{2,1,0:T(8,128)S(1)} collective-permute-done((f32[6,72,128]{2,1,0:T(8,128)S(1)}, f32[6,72,128]{2,1,0:T(8,128)S(1)}, u32[]{:S(2)}, u32[]{:S(2)}) %collective-permute-start.8) | collective-permute-done | bytes 221216 | tf_op jit(solution)/shard_map/ppermute | solution.py:175
  20.9 2.2 %trace_terms.1 = f32[32,1,128]{2,1,0:T(1,128)} custom-call(s32[3,4,16]{2,1,0:T(4,128)S(1)} %select_bitcast_fusion.code_ref, f32[6,72,128]{2,1,0:T(8,128)S(1)} %pack.1.refs_1_.refs_0_.refs_3_, f32[6,72,128]{2,1,0:T(8,128)S(1)} %collective-permute-done.4.refs_5_.refs_1_, f32[6,72,128]{2,1,0:T(8,128)S(1)} %collective-permute-done.refs_0_._.refs_2_, ...), custom_call_target="tpu_custom_call" | custom-call | tf_op jit(solution)/shard_map/trace_terms/pallas_call | solution.py:252
  23.0 2.9 %all-to-all-start = ((f32[32,1,128]{2,1,0:T(1,128)}), f32[32,1,128]{2,1,0:T(1,128)S(1)}, u32[]{:S(2)}, u32[]{:S(2)}) async-start(f32[32,1,128]{2,1,0:T(1,128)} %trace_terms.1), calls=%async_computation | async-start | bytes 32768 | tf_op jit(solution)/shard_map/all_to_all | solution.py:261
  26.0 0.0 collective-permute-done.5.refs_6_
  26.0 0.0 collective-permute-done.9.refs_10_
  26.0 4.5 %multiply.1 = f32[2,1,3,96,96]{4,3,2,1,0:T(8,128)} custom-call(s32[3,4,16]{2,1,0:T(4,128)S(1)} %select_bitcast_fusion.code_ref, f32[6,72,128]{2,1,0:T(8,128)S(1)} %collective-permute-done.refs_0_._.refs_2_, f32[6,72,128]{2,1,0:T(8,128)S(1)} %pack.1.refs_1_.refs_0_.refs_3_, f32[6,72,128]{2,1,0:T(8,128)S(1)} %collective-permute-done.1.refs_2_.refs_4_, ...), custom_call_target="tpu_custom_call" | custom-call | tf_op jit(solution)/shard_map/multiply/pallas_call | solution.py:272
  30.5 2.6 %all-to-all-done.terms_ref = f32[32,1,128]{2,1,0:T(1,128)S(1)} async-done(((f32[32,1,128]{2,1,0:T(1,128)}), f32[32,1,128]{2,1,0:T(1,128)S(1)}, u32[]{:S(2)}, u32[]{:S(2)}) %all-to-all-start) | async-done | bytes 16416 | tf_op jit(solution)/shard_map/all_to_all | solution.py:261
  33.1 0.5 %sum.1 = f32[1,1]{1,0:T(1,128)} custom-call(f32[32,1,128]{2,1,0:T(1,128)S(1)} %all-to-all-done.terms_ref), custom_call_target="tpu_custom_call" | custom-call | tf_op jit(solution)/shard_map/sum/pallas_call | solution.py:285
  (2 shorter events, 0.0 us)
Async XLA Ops:
  0.6 1.0 %copy-start = (f32[2,1,3,96,96]{4,3,2,1,0:T(8,128)S(1)}, f32[2,1,3,96,96]{4,3,2,1,0:T(8,128)}, u32[]{:S(2)}) copy-start(f32[2,1,3,96,96]{4,3,2,1,0:T(8,128)} %x_ref.1) | copy-start | bytes 663556
  1.6 9.3 %copy-start.1 = (s32[16,4,3]{0,1,2:T(4,128)S(1)}, s32[16,4,3]{0,1,2:T(4,128)}, u32[]{:S(2)}) copy-start(s32[16,4,3]{0,1,2:T(4,128)} %param.4) | copy-start | bytes 2308
  1.6 9.3 %copy-start.2 = (s32[16,4,3]{0,1,2:T(4,128)S(1)}, s32[16,4,3]{0,1,2:T(4,128)}, u32[]{:S(2)}) copy-start(s32[16,4,3]{0,1,2:T(4,128)} %param.5) | copy-start | bytes 2308
  1.7 14.4 %collective-permute-start = (f32[6,72,128]{2,1,0:T(8,128)S(1)}, f32[6,72,128]{2,1,0:T(8,128)S(1)}, u32[]{:S(2)}, u32[]{:S(2)}) collective-permute-start(f32[6,72,128]{2,1,0:T(8,128)S(1)} %pack.1.refs_1_.refs_0_.refs_3_), channel_id=1, source_target_pairs={{0,8},{1,9},{2,10},{3,11},{4,12},{5,13},{6,14},{7,15},{8,0},{9,1},... | collective-permute-start | bytes 663560 | tf_op jit(solution)/shard_map/ppermute | solution.py:195
  5.8 10.3 %collective-permute-start.1 = (f32[6,72,128]{2,1,0:T(8,128)S(1)}, f32[6,72,128]{2,1,0:T(8,128)S(1)}, u32[]{:S(2)}, u32[]{:S(2)}) collective-permute-start(f32[6,72,128]{2,1,0:T(8,128)S(1)} %pack.1.refs_1_.refs_0_.refs_3_), channel_id=1, source_target_pairs={{0,2},{1,3},{2,0},{3,1},{4,6},{5,7},{6,4},{7,5},{8,10},{9,11},{10,... | collective-permute-start | bytes 663560 | tf_op jit(solution)/shard_map/ppermute | solution.py:225
  7.3 9.4 %collective-permute-start.2 = (f32[6,72,128]{2,1,0:T(8,128)S(1)}, f32[6,72,128]{2,1,0:T(8,128)S(1)}, u32[]{:S(2)}, u32[]{:S(2)}) collective-permute-start(f32[6,72,128]{2,1,0:T(8,128)S(1)} %pack.1.refs_1_.refs_0_.refs_3_), channel_id=1, source_target_pairs={{0,16},{1,17},{2,18},{3,19},{4,20},{5,21},{6,22},{7,23},{8,26},{9,... | collective-permute-start | bytes 663560 | tf_op jit(solution)/shard_map/ppermute | solution.py:225
  9.8 9.5 %collective-permute-start.3 = (f32[6,72,128]{2,1,0:T(8,128)S(1)}, f32[6,72,128]{2,1,0:T(8,128)S(1)}, u32[]{:S(2)}, u32[]{:S(2)}) collective-permute-start(f32[6,72,128]{2,1,0:T(8,128)S(1)} %pack.1.refs_1_.refs_0_.refs_3_), channel_id=1, source_target_pairs={{0,18},{1,19},{2,16},{3,17},{4,22},{5,23},{6,20},{7,21},{8,24},{9,... | collective-permute-start | bytes 663560 | tf_op jit(solution)/shard_map/ppermute | solution.py:225
  9.8 10.3 %collective-permute-start.4 = (f32[6,72,128]{2,1,0:T(8,128)S(1)}, f32[6,72,128]{2,1,0:T(8,128)S(1)}, u32[]{:S(2)}, u32[]{:S(2)}) collective-permute-start(f32[6,72,128]{2,1,0:T(8,128)S(1)} %pack.1.refs_1_.refs_0_.refs_3_), channel_id=1, source_target_pairs={{0,4},{4,0},{8,12},{12,8},{1,5},{5,1},{9,13},{13,9},{2,6},{6,2},{1... | collective-permute-start | bytes 663560 | tf_op jit(solution)/shard_map/ppermute | solution.py:175
  16.1 4.1 %collective-permute-start.6 = (f32[6,72,128]{2,1,0:T(8,128)S(1)}, f32[6,72,128]{2,1,0:T(8,128)S(1)}, u32[]{:S(2)}, u32[]{:S(2)}) collective-permute-start(f32[6,72,128]{2,1,0:T(8,128)S(1)} %pack.1.refs_1_.refs_0_.refs_3_), channel_id=1, source_target_pairs={{0,1},{1,0},{2,3},{3,2},{4,5},{5,4},{6,7},{7,6},{8,9},{9,8},{10,11... | collective-permute-start | bytes 663560 | tf_op jit(solution)/shard_map/ppermute | solution.py:175
  16.1 9.9 %collective-permute-start.5 = (f32[6,72,128]{2,1,0:T(8,128)S(1)}, f32[6,72,128]{2,1,0:T(8,128)S(1)}, u32[]{:S(2)}, u32[]{:S(2)}) collective-permute-start(f32[6,72,128]{2,1,0:T(8,128)S(1)} %collective-permute-done.refs_0_._.refs_2_), channel_id=1, source_target_pairs={{0,4},{4,0},{8,12},{12,8},{1,5},{5,1},{9,13},{13,9},{2,6},{6,2},{1... | collective-permute-start | bytes 663560 | tf_op jit(solution)/shard_map/ppermute | solution.py:175
  16.8 3.4 %collective-permute-start.7 = (f32[6,72,128]{2,1,0:T(8,128)S(1)}, f32[6,72,128]{2,1,0:T(8,128)S(1)}, u32[]{:S(2)}, u32[]{:S(2)}) collective-permute-start(f32[6,72,128]{2,1,0:T(8,128)S(1)} %collective-permute-done.1.refs_2_.refs_4_), channel_id=1, source_target_pairs={{0,1},{1,0},{2,3},{3,2},{4,5},{5,4},{6,7},{7,6},{8,9},{9,8},{10,11... | collective-permute-start | bytes 663560 | tf_op jit(solution)/shard_map/ppermute | solution.py:175
  19.4 1.5 %collective-permute-start.8 = (f32[6,72,128]{2,1,0:T(8,128)S(1)}, f32[6,72,128]{2,1,0:T(8,128)S(1)}, u32[]{:S(2)}, u32[]{:S(2)}) collective-permute-start(f32[6,72,128]{2,1,0:T(8,128)S(1)} %collective-permute-done.2.refs_3_.refs_5_), channel_id=1, source_target_pairs={{0,1},{1,0},{2,3},{3,2},{4,5},{5,4},{6,7},{7,6},{8,9},{9,8},{10,11... | collective-permute-start | bytes 663560 | tf_op jit(solution)/shard_map/ppermute | solution.py:175
  20.2 5.8 %collective-permute-start.9 = (f32[6,72,128]{2,1,0:T(8,128)S(1)}, f32[6,72,128]{2,1,0:T(8,128)S(1)}, u32[]{:S(2)}, u32[]{:S(2)}) collective-permute-start(f32[6,72,128]{2,1,0:T(8,128)S(1)} %collective-permute-done.3.refs_4_), channel_id=1, source_target_pairs={{0,1},{1,0},{2,3},{3,2},{4,5},{5,4},{6,7},{7,6},{8,9},{9,8},{10,11... | collective-permute-start | bytes 663560 | tf_op jit(solution)/shard_map/ppermute | solution.py:175
  23.0 10.0 %all-to-all-start = ((f32[32,1,128]{2,1,0:T(1,128)}), f32[32,1,128]{2,1,0:T(1,128)S(1)}, u32[]{:S(2)}, u32[]{:S(2)}) async-start(f32[32,1,128]{2,1,0:T(1,128)} %trace_terms.1), calls=%async_computation | async-start | bytes 32768 | tf_op jit(solution)/shard_map/all_to_all | solution.py:261
